TPU v7x, 128 devices: a whole 4x4x4 slice. The times are simulated.
128 devices in a mesh: frame: 8 (over y_hi, x), head: 16 (over y_lo, z, core).
Axes of the slice: x: 4, y: 4 (y_hi: 2, y_lo: 2; y = y_hi * 2 + y_lo), z: 4, core: 2. Of those that a mesh axis runs over, the one named last changes fastest.
Arguments:
- tokens: bfloat16 [8192, 5120], P('frame', 'head'), may hold values from -16 to 16
- qkv_weight: bfloat16 [3, 5120, 4096], P(None, None, 'head'), may hold values from -0.1118034 to 0.1118034
- out_weight: bfloat16 [4096, 5120], P('head'), may hold values from -0.125 to 0.125
- modulation: float32 [3, 5120], replicated, may hold values from -3 to 3
- block_mask: int32 [32, 64, 64], P('head', 'frame'), may hold values from 0 to 1, as said below
Outputs:
- mixed: bfloat16 [8192, 5120], P('frame', 'head')
Inputs may be any that keep to these rules, and one draw needn't show every extreme that they name: `block_mask`: 1 keeps a pair of 128-token blocks; every query block keeps its own block.
All inputs are finite; a program needn't handle non-finite values.
Results may differ from a plain program's by a relative error of at most 0.0085.
Values may be sent and summed in bfloat16 or wider, within the bound.
No kernel may reach another device: no remote copies, remote signals or barrier semaphores. Data moves between devices by JAX's collectives and lax.ppermute only.
A program may use at most 256 MiB of HBM per device.

v0:
```python
import math

import jax
import jax.numpy as jnp
from jax import lax
from jax.sharding import PartitionSpec as P

BLK = 128


NEGATIVE = -1e30
EPSILON = 1e-06


def update_heads(state, query, keys, values, keep, scale):
    top, total, summed = state
    scores = jnp.einsum("qhd,khd->hqk", query, keys, preferred_element_type=jnp.float32) * scale
    masked = jnp.where(keep, scores, NEGATIVE)
    new_top = jnp.maximum(top, jnp.max(masked, axis=2))
    weights = jnp.where(keep, jnp.exp(scores - new_top[:, :, None]), 0.0)
    total = jnp.sum(weights, axis=2)
    summed = jnp.einsum(
        "hqk,khd->hqd", weights.astype(jnp.bfloat16), values, preferred_element_type=jnp.float32
    )
    return (new_top, total, summed)


def shards(tokens, qkv_weight, out_weight, modulation, block_mask):
    local_rows, local_cols = tokens.shape
    heads_here = block_mask.shape[0]
    inner = qkv_weight.shape[2]
    head_size = inner // heads_here
    scale = 1.0 / math.sqrt(head_size)
    col_start = lax.axis_index("head") * local_cols
    own_mod = lax.dynamic_slice_in_dim(modulation, col_start, local_cols, 1)
    whole = lax.all_gather(tokens, "head", axis=1, tiled=True)
    wide = whole.astype(jnp.float32)
    center = jnp.mean(wide, axis=1, keepdims=True)
    spread = jnp.mean(jnp.square(wide - center), axis=1, keepdims=True)
    normed = (
        (wide - center) * lax.rsqrt(spread + EPSILON) * (1.0 + modulation[1]) + modulation[0]
    ).astype(jnp.bfloat16)
    projected = jnp.einsum("td,jdc->jtc", normed, qkv_weight, preferred_element_type=jnp.float32)
    query = projected[0].astype(jnp.bfloat16).reshape(local_rows, heads_here, head_size)
    keyed = projected[1].astype(jnp.bfloat16)
    valued = projected[2].astype(jnp.bfloat16)
    start_state = (
        jnp.full((heads_here, local_rows), NEGATIVE, jnp.float32),
        jnp.zeros((heads_here, local_rows), jnp.float32),
        jnp.zeros((heads_here, local_rows, head_size), jnp.float32),
    )
    key_piece = lax.all_gather(keyed, "frame", axis=0, tiled=True)
    value_piece = lax.all_gather(valued, "frame", axis=0, tiled=True)
    count = key_piece.shape[0]
    keys = key_piece.reshape(count, heads_here, head_size)
    values = value_piece.reshape(count, heads_here, head_size)
    blocks = block_mask > 0
    keep = jnp.repeat(jnp.repeat(blocks, BLK, axis=1), BLK, axis=2)
    top, total, summed = update_heads(start_state, query, keys, values, keep, scale)
    heads_done = (
        (summed / total[:, :, None])
        .astype(jnp.bfloat16)
        .transpose(1, 0, 2)
        .reshape(local_rows, inner)
    )
    mixed_cols = lax.psum_scatter(
        lax.dot_general(
            out_weight, heads_done, (((0,), (1,)), ((), ())), preferred_element_type=jnp.float32
        ).astype(jnp.bfloat16),
        "head",
        scatter_dimension=0,
        tiled=True,
    ).astype(jnp.float32)
    mixed = mixed_cols.T
    return (tokens.astype(jnp.float32) + own_mod[2] * mixed).astype(jnp.bfloat16)


def solution(mesh):
    placed = (
        P("frame", "head"),
        P(None, None, "head"),
        P("head", None),
        P(),
        P("head", "frame", None),
    )
    return jax.shard_map(
        shards, mesh=mesh, in_specs=placed, out_specs=P("frame", "head"), check_vma=False
    )
```

profile of v0, /device:TPU:1, one launch (start us, length us, event | category | flops | bytes accessed | tf_op | source)
XLA Modules:
  0.0 381.8 jit_solution(10321196492068253965)
XLA Ops:
  6.5 0.0 copy-start
  6.5 0.0 all-gather.6.cloned.1.call-start
  6.5 0.7 all-gather.6.cloned.1.call-update
  7.3 0.0 all-gather.8.cloned.1.call-start
  7.3 1.0 slice_add_fusion
  8.3 66.4 %all-gather.6.cloned.1.call-done = bf16[1024,5120]{0,1:T(8,128)(2,1)} async-done(((bf16[1024,320]{0,1:T(8,128)(2,1)}), bf16[1024,5120]{0,1:T(8,128)(2,1)}) %all-gather.6.cloned.1.call-update) | async-done | bytes 10485776 | tf_op jit(solution)/shard_map/all_gather | solution.py:36
  74.8 5.7 %convert_reduce_fusion = f32[1024]{0:T(1024)S(1)} fusion(bf16[1024,5120]{0,1:T(8,128)(2,1)} %all-gather.6.cloned.1.call-done), kind=kLoop, calls=%fused_computation.6 | loop fusion | flops 10484736 | bytes 10489856 | tf_op jit(solution)/shard_map/reduce_sum | solution.py:38
  80.4 1.3 copy-done.1
  81.7 2.8 fusion.6
  84.5 17.4 %fusion.16 = bf16[3,1024,256]{1,2,0:T(8,128)(2,1)} fusion(bf16[3,5120,256]{2,1,0:T(8,128)(2,1)} %param.6, bf16[1024,5120]{0,1:T(8,128)(2,1)} %all-gather.6.cloned.1.call-done, f32[5120]{0:T(1024)S(1)} %bitcast.41, f32[5120]{0:T(1024)S(1)} %bitcast.40, f32[1024]{0:T(1024)S(1)} %add_rsqrt_fusion, f32[1024]{0:T(1024)S(1)} %broadcast_multiply_fusion), kind=kOutput, calls=%fused_computation.17 | convolution fusion | flops 8085307392 | bytes 19972096 | tf_op jit(solution)/shard_map/td,jdc->jtc/dot_general | solution.py:43
  102.0 2.5 fusion.27
  104.4 0.0 all-gather.8.cloned.1.call-update
  104.5 0.0 all-gather.10.cloned.1.call-start
  104.5 0.7 all-gather.10.cloned.1.call-update
  105.2 0.0 reduce-scatter.4.cloned.1.call-start
  105.2 0.0 copy-done.3
  105.3 0.1 broadcast_in_dim.21
  105.3 23.4 %broadcast_in_dim.22 = pred[2,1024,64,128]{3,2,1,0:T(32,128)(4,1)} broadcast(pred[2,1024,64]{2,1,0:T(8,128)(4,1)S(1)} %bitcast.38), dimensions={0,1,2} | broadcast | bytes 16908288 | tf_op jit(solution)/shard_map/broadcast_in_dim | solution.py:58
  128.7 44.5 %reshape.37 = pred[2,1024,8192]{2,1,0:T(32,128)(4,1)} reshape(pred[2,1024,64,128]{3,2,1,0:T(32,128)(4,1)} %broadcast_in_dim.22) | data formatting | bytes 33554432 | tf_op jit(solution)/shard_map/reshape | solution.py:58
  173.2 3.1 all-gather.8.cloned.1.call-done
  176.3 32.5 %select_reduce_fusion = (f32[2,1024]{1,0:T(2,128)S(1)}, f32[2,1024,8192]{2,1,0:T(8,128)}) fusion(pred[2,1024,8192]{2,1,0:T(32,128)(4,1)} %reshape.37, bf16[1024,2,128]{0,2,1:T(8,128)(2,1)S(1)} %bitcast.37, bf16[8192,2,128]{0,2,1:T(8,128)(2,1)} %bitcast.36), kind=kOutput, calls=%fused_computation.1 | convolution fusion | flops 4345296896 | bytes 88612864 | tf_op jit(solution)/shard_map/qhd,khd->hqk/dot_general | solution.py:17
  208.8 27.1 %fusion = f32[2,1024]{1,0:T(2,128)S(1)} fusion(pred[2,1024,8192]{2,1,0:T(32,128)(4,1)} %reshape.37, f32[2,1024,8192]{2,1,0:T(8,128)} %get-tuple-element.11, f32[2,1024]{1,0:T(2,128)S(1)} %broadcast_maximum_fusion), kind=kLoop, calls=%fused_computation.2 | loop fusion | flops 67106816 | bytes 83902464 | tf_op jit(solution)/shard_map/reduce_sum | solution.py:21
  235.9 12.2 %all-gather.10.cloned.1.call-done = bf16[1,8192,256]{1,2,0:T(8,128)(2,1)} async-done(((bf16[1,1024,256]{1,2,0:T(8,128)(2,1)}), bf16[1,8192,256]{1,2,0:T(8,128)(2,1)}) %all-gather.10.cloned.1.call-update) | async-done | bytes 4194320 | tf_op jit(solution)/shard_map/all_gather | solution.py:53
  248.0 30.9 %divide_convert_fusion = bf16[1024,2,128]{0,2,1:T(8,128)(2,1)S(1)} fusion(bf16[8192,2,128]{0,2,1:T(8,128)(2,1)} %bitcast.43, pred[2,1024,8192]{2,1,0:T(32,128)(4,1)} %reshape.37, f32[2,1024,8192]{2,1,0:T(8,128)} %get-tuple-element.11, f32[2,1024]{1,0:T(2,128)S(1)} %broadcast_maximum_fusion, f32[1024,2]{0,1:T(2,128)S(1)} %bitcast.42), kind=kOutput, calls=%fused_computation.21 | convolution fusion | flops 4362600448 | bytes 88621056 | tf_op jit(solution)/shard_map/hqk,khd->hqd/dot_general | solution.py:22
  278.9 0.0 copy-done
  278.9 5.5 %convert_bitcast_fusion = bf16[5120,1024]{0,1:T(8,128)(2,1)} fusion(bf16[1024,256]{0,1:T(8,128)(2,1)S(1)} %bitcast.39, bf16[256,5120]{1,0:T(8,128)(2,1)S(1)} %copy-done), kind=kOutput, calls=%fused_computation.14 | convolution fusion | flops 2689597440 | bytes 13631488 | tf_op jit(solution)/shard_map/dot_general | solution.py:67
  284.4 14.5 %copy.28 = bf16[5120,1024]{1,0:T(8,128)(2,1)} copy(bf16[5120,1024]{0,1:T(8,128)(2,1)} %convert_bitcast_fusion) | data formatting | bytes 20971520
  298.9 0.0 reduce-scatter.4.cloned.1.call-update
  298.9 0.8 dynamic-slice_reduce_fusion
  299.7 73.4 %reduce-scatter.4.cloned.1.call-done = bf16[320,1024]{1,0:T(8,128)(2,1)} async-done(((bf16[5120,1024]{1,0:T(8,128)(2,1)}), bf16[320,1024]{1,0:T(8,128)(2,1)}) %reduce-scatter.4.cloned.1.call-update) | async-done | bytes 655376 | tf_op jit(solution)/shard_map/reduce_scatter | solution.py:66
  373.1 0.0 copy-done.2
  373.1 2.2 fusion.22
  (7 shorter events, 0.0 us)
Async XLA Ops:
  6.5 272.4 %copy-start = (bf16[256,5120]{1,0:T(8,128)(2,1)S(1)}, bf16[256,5120]{1,0:T(8,128)(2,1)}, u32[]{:S(2)}) copy-start(bf16[256,5120]{1,0:T(8,128)(2,1)} %param.7) | copy-start | bytes 7864324
  6.5 68.2 %all-gather.6.cloned.1.call-start = ((), (), s32[]{:S(2)}) async-start(), calls=%async_computation.1 | async-start | bytes 11141120 | tf_op jit(solution)/shard_map/all_gather | solution.py:36
  7.3 169.0 %all-gather.8.cloned.1.call-start = ((), (), s32[]{:S(2)}) async-start(), calls=%async_computation.2 | async-start | bytes 4718592 | tf_op jit(solution)/shard_map/all_gather | solution.py:52
  74.8 7.0 %copy-start.1 = (bf16[1024,5120]{0,1:T(8,128)(2,1)S(1)}, bf16[1024,5120]{0,1:T(8,128)(2,1)}, u32[]{:S(2)}) copy-start(bf16[1024,5120]{0,1:T(8,128)(2,1)} %all-gather.6.cloned.1.call-done) | copy-start | bytes 31457284
  84.5 20.7 %copy-start.3 = (s32[2,8,64]{2,1,0:T(8,128)S(1)}, s32[2,8,64]{2,1,0:T(8,128)}, u32[]{:S(2)}) copy-start(s32[2,8,64]{2,1,0:T(8,128)} %param.9) | copy-start | bytes 12292
  104.5 143.6 %all-gather.10.cloned.1.call-start = ((), (), s32[]{:S(2)}) async-start(), calls=%async_computation.3 | async-start | bytes 4718592 | tf_op jit(solution)/shard_map/all_gather | solution.py:53
  105.2 267.9 %reduce-scatter.4.cloned.1.call-start = ((), (), s32[]{:S(2)}) async-start(), calls=%async_computation.4 | async-start | bytes 11141120 | tf_op jit(solution)/shard_map/reduce_scatter | solution.py:66
  284.4 88.7 %copy-start.2 = (bf16[1024,320]{0,1:T(8,128)(2,1)S(1)}, bf16[1024,320]{0,1:T(8,128)(2,1)}, u32[]{:S(2)}) copy-start(bf16[1024,320]{0,1:T(8,128)(2,1)} %param.5) | copy-start | bytes 1966084
Sparse Core Ops, SparseCore 0:
  9.1 65.6 all-gather.5
  104.6 71.6 all-gather.7
  178.6 69.3 all-gather.9
  299.0 74.0 reduce-scatter.3
where the time goes:
time: 386 us; the launch traced here: 382 us
  waiting for transfers between devices  156 us (40%)
  local copies, waits for them, and re-layouts  87 us (23%)
  matrix products  86.3 us (22%)
  other arithmetic  38.7 us (10%)
  between operations  13.2 us (3%)
    reduce_scatter x1, waiting for transfers between devices, shards(): lax.psum_scatter(lax.dot_general(out_weight, heads_done, (((0,), (1,)), (...  73.4 us
    all_gather x1, waiting for transfers between devices, shards(): whole = lax.all_gather(tokens, 'head', axis=1, tiled=True)  66.4 us
    reshape x1, local copies, waits for them, and re-layouts, shards(): keep = jnp.repeat(jnp.repeat(blocks, BLK, axis=1), BLK, axis=2)  44.5 us
    dot_general x1, matrix products, update_heads(): jnp.einsum('qhd,khd->hqk', query, keys, preferred_element_type=jnp.float32)  32.5 us
    dot_general x1, matrix products, update_heads(): jnp.einsum('hqk,khd->hqd', weights.astype(jnp.bfloat16), values, preferre...  30.9 us
    reduce_sum x1, other arithmetic, update_heads(): total = jnp.sum(weights, axis=2)  27.1 us
    broadcast_in_dim x2, local copies, waits for them, and re-layouts, shards(): keep = jnp.repeat(jnp.repeat(blocks, BLK, axis=1), BLK, axis=2)  23.4 us
    dot_general x1, matrix products, shards(): jnp.einsum('td,jdc->jtc', normed, qkv_weight, preferred_element_type=jnp....  17.4 us
  transfers between devices with their start and end apart: 4, of which 4 were waited for; matrix products, arithmetic and copies ran while one was open for 34% of the time, Pallas kernels for 0%

commit v1 on v0

v1 whole, which is shorter than its diff:
```python
import math

import jax
import jax.numpy as jnp
from jax import lax
from jax.experimental import pallas as pl
from jax.experimental.pallas import tpu as pltpu
from jax.sharding import Mesh
from jax.sharding import PartitionSpec as P

BLK = 128
EPSILON = 1e-06
NEGATIVE = -1e30
FRAME = ("yh", "x")
CHIP = ("yl", "z")
HEAD = ("yl", "z", "core")
SWAP = [(0, 1), (1, 0)]
MIB = 1 << 20


def project_kernel(x0, x1, x2, x3, weight, gain, shift, center, rate, q_out, k0, k1, v0, v1, total):
    step = pl.program_id(0)

    @pl.when(step == 0)
    def _():
        total[...] = jnp.zeros_like(total)

    wide_gain = gain[...]
    wide_shift = shift[...]
    for chunk, x in enumerate((x0, x1, x2, x3)):
        width = x.shape[1]
        parts = []
        for part in range(width // BLK):
            columns = slice(chunk * width + part * BLK, chunk * width + (part + 1) * BLK)
            wide = x[:, part * BLK : (part + 1) * BLK].astype(jnp.float32)
            part_normed = (wide - center[:, columns]) * rate[:, columns] * wide_gain + wide_shift
            parts.append(part_normed.astype(jnp.bfloat16))
        normed = jnp.concatenate(parts, axis=1)
        columns = slice(chunk * width, (chunk + 1) * width)
        total[:, columns] += jnp.dot(weight[...], normed, preferred_element_type=jnp.float32)

    @pl.when(step == pl.num_programs(0) - 1)
    def _():
        inner = q_out.shape[0]
        half = inner // 2
        q_out[...] = total[:inner].astype(jnp.bfloat16)
        k0[...] = total[inner : inner + half].T.astype(jnp.bfloat16)
        k1[...] = total[inner + half : 2 * inner].T.astype(jnp.bfloat16)
        v0[...] = total[2 * inner : 2 * inner + half].astype(jnp.bfloat16)
        v1[...] = total[2 * inner + half :].astype(jnp.bfloat16)


def project(xs, weight, gain, shift, center, rate):
    features, width = xs[0].shape
    count = width * len(xs)
    outs = weight.shape[0]
    inner = outs // 3
    half = inner // 2
    deep = 512
    whole = lambda shape: pl.BlockSpec(shape, lambda k: (0, 0))
    return pl.pallas_call(
        project_kernel,
        grid=(features // deep,),
        in_specs=[pl.BlockSpec((deep, width), lambda k: (k, 0))] * len(xs)
        + [
            pl.BlockSpec((outs, deep), lambda k: (0, k)),
            pl.BlockSpec((deep, BLK), lambda k: (k, 0)),
            pl.BlockSpec((deep, BLK), lambda k: (k, 0)),
            whole((1, count)),
            whole((1, count)),
        ],
        out_specs=[
            whole((inner, count)),
            whole((count, half)),
            whole((count, half)),
            whole((half, count)),
            whole((half, count)),
        ],
        out_shape=[
            jax.ShapeDtypeStruct((inner, count), jnp.bfloat16),
            jax.ShapeDtypeStruct((count, half), jnp.bfloat16),
            jax.ShapeDtypeStruct((count, half), jnp.bfloat16),
            jax.ShapeDtypeStruct((half, count), jnp.bfloat16),
            jax.ShapeDtypeStruct((half, count), jnp.bfloat16),
        ],
        scratch_shapes=[pltpu.VMEM((outs, count), jnp.float32)],
        compiler_params=pltpu.CompilerParams(vmem_limit_bytes=40 * MIB),
        cost_estimate=pl.CostEstimate(
            flops=2 * outs * features * count,
            bytes_accessed=2 * features * (count + outs),
            transcendentals=0,
        ),
        name="project",
    )(*xs, weight, gain, shift, center, rate)


GROUP = 4


def attend_kernel(factor, places, counts, q_ref, k0, k1, v0, v1, out, scores):
    head_size = k0.shape[1]
    per_head = q_ref.shape[1] // BLK
    per_frame = v0.shape[1] // BLK

    for head, (keys, values) in enumerate(((k0, v0), (k1, v1))):

        def one(block, _):
            row = head * per_head + block
            column = pl.multiple_of(block * BLK, BLK)
            query = q_ref[head * head_size : (head + 1) * head_size, pl.ds(column, BLK)]
            count = counts[row]
            groups = (count + GROUP - 1) // GROUP

            def rate(group, top):
                for item in range(GROUP):
                    place = group * GROUP + item
                    start = pl.multiple_of(places[row, place] * BLK, BLK)
                    score = jnp.dot(
                        keys[pl.ds(start, BLK), :], query, preferred_element_type=jnp.float32
                    )
                    scores[pl.ds(pl.multiple_of(place * BLK, BLK), BLK), :] = score
                    best = jnp.max(score.reshape(BLK // 8, 8, BLK), axis=0)
                    top = jnp.maximum(top, best + jnp.where(place < count, 0.0, NEGATIVE))
                return top

            top = lax.fori_loop(0, groups, rate, jnp.full((8, BLK), NEGATIVE, jnp.float32))
            top = jnp.max(top, axis=0, keepdims=True) * factor

            def gather(group, state):
                total, summed = state
                weights, held = [], []
                for item in range(GROUP):
                    place = group * GROUP + item
                    score = scores[pl.ds(pl.multiple_of(place * BLK, BLK), BLK), :]
                    offset = top + jnp.where(place < count, 0.0, -NEGATIVE)
                    weight = jnp.exp2(score * factor - offset)
                    total = total + jnp.sum(weight.reshape(BLK // 8, 8, BLK), axis=0)
                    weights.append(weight.astype(jnp.bfloat16))
                    where = places[row, place]
                    first = pl.multiple_of((where // per_frame) * head_size, head_size)
                    start = pl.multiple_of((where % per_frame) * BLK, BLK)
                    held.append(values[pl.ds(first, head_size), pl.ds(start, BLK)])
                summed = summed + jnp.dot(
                    jnp.concatenate(held, axis=1),
                    jnp.concatenate(weights, axis=0),
                    preferred_element_type=jnp.float32,
                )
                return total, summed

            total, summed = lax.fori_loop(
                0,
                groups,
                gather,
                (jnp.zeros((8, BLK), jnp.float32), jnp.zeros((head_size, BLK), jnp.float32)),
            )
            total = jnp.sum(total, axis=0, keepdims=True)
            out[head * head_size : (head + 1) * head_size, pl.ds(column, BLK)] = (
                summed / total
            ).astype(jnp.bfloat16)
            return 0

        lax.fori_loop(0, per_head, one, 0)


def attend(factor, places, counts, query, k0, k1, v0, v1):
    def kernel(*refs):
        attend_kernel(factor, *refs)

    return pl.pallas_call(
        kernel,
        in_specs=[pl.BlockSpec(memory_space=pltpu.SMEM)] * 2
        + [pl.BlockSpec(memory_space=pltpu.VMEM)] * 5,
        out_specs=pl.BlockSpec(memory_space=pltpu.VMEM),
        out_shape=jax.ShapeDtypeStruct(query.shape, jnp.bfloat16),
        scratch_shapes=[pltpu.VMEM((k0.shape[0], BLK), jnp.float32)],
        compiler_params=pltpu.CompilerParams(vmem_limit_bytes=40 * MIB),
        cost_estimate=pl.CostEstimate(
            flops=query.shape[0] * query.shape[1] * k0.shape[0],
            bytes_accessed=4 * 2 * k0.shape[0] * k0.shape[1],
            transcendentals=query.shape[1] * k0.shape[0] // 2,
        ),
        name="attend",
    )(places, counts, query, k0, k1, v0, v1)


def leave_kernel(own_weight, other_weight, own, other, *outs):
    summed = jnp.dot(own_weight[...], own[...], preferred_element_type=jnp.float32)
    summed += jnp.dot(other_weight[...], other[...], preferred_element_type=jnp.float32)
    summed = summed.astype(jnp.bfloat16)
    width = outs[0].shape[1]
    for index, out in enumerate(outs):
        out[...] = summed[:, index * width : (index + 1) * width]


def leave(own_weight, other_weight, own, other, pieces):
    features, inner = own_weight.shape
    count = own.shape[1]
    width = count // pieces
    high = 512
    return pl.pallas_call(
        leave_kernel,
        grid=(features // high,),
        in_specs=[pl.BlockSpec((high, inner), lambda i: (i, 0))] * 2
        + [pl.BlockSpec((inner, count), lambda i: (0, 0))] * 2,
        out_specs=[pl.BlockSpec((high, width), lambda i: (i, 0))] * pieces,
        out_shape=[jax.ShapeDtypeStruct((features, width), jnp.bfloat16)] * pieces,
        compiler_params=pltpu.CompilerParams(vmem_limit_bytes=40 * MIB),
        cost_estimate=pl.CostEstimate(
            flops=4 * features * inner * count,
            bytes_accessed=4 * features * (inner + count),
            transcendentals=0,
        ),
        name="leave",
    )(own_weight, other_weight, own, other)


def shards(tokens, qkv_weight, out_weight, modulation, block_mask):
    rows, local = tokens.shape
    features = modulation.shape[1]
    heads_here = block_mask.shape[0]
    inner = qkv_weight.shape[2]
    head_size = inner // heads_here
    factor = math.log2(math.e) / math.sqrt(head_size)
    core = lax.axis_index("core")
    across = tokens.T

    wide = across.astype(jnp.float32)
    own_center = jnp.mean(wide, axis=0, keepdims=True)
    own_spread = jnp.sum(jnp.square(wide - own_center), axis=0, keepdims=True)
    stats = lax.all_gather(jnp.concatenate([own_center, own_spread], axis=0), HEAD, axis=0)
    center = jnp.mean(stats[:, 0], axis=0, keepdims=True)
    spread = (
        jnp.sum(stats[:, 1], axis=0, keepdims=True)
        + local * jnp.sum(jnp.square(stats[:, 0] - center), axis=0, keepdims=True)
    ) / features
    rate = lax.rsqrt(spread + EPSILON)

    quarter = rows // 4
    xs = [
        lax.all_gather(across[:, i * quarter : (i + 1) * quarter], HEAD, axis=0, tiled=True)
        for i in range(4)
    ]
    weight = jnp.transpose(qkv_weight, (0, 2, 1)).reshape(3 * inner, features)
    gain = jnp.broadcast_to((1.0 + modulation[1])[:, None], (features, BLK))
    shift = jnp.broadcast_to(modulation[0][:, None], (features, BLK))
    own_weight = out_weight.T
    other_weight = lax.ppermute(own_weight, "core", SWAP)

    keep = (block_mask != 0).astype(jnp.int32).reshape(-1, block_mask.shape[2])
    counts = jnp.sum(keep, axis=1)
    blocks = jnp.arange(keep.shape[1], dtype=jnp.int32)
    earlier = blocks[None, :] < blocks[:, None]
    rank = jnp.sum(jnp.where(earlier[None], keep[:, None, :], 0), axis=2)
    chosen = (keep[:, None, :] != 0) & (rank[:, None, :] == blocks[None, :, None])
    places = jnp.sum(jnp.where(chosen, blocks[None, None, :], 0), axis=2)

    query, k0, k1, v0, v1 = project(xs, weight, gain, shift, center, rate)
    k0, k1, v0, v1 = [
        lax.all_gather(part, FRAME, axis=0, tiled=True) for part in (k0, k1, v0, v1)
    ]
    heads = attend(factor, places, counts, query, k0, k1, v0, v1)

    half = rows // 2
    mine = lax.dynamic_slice_in_dim(heads, core * half, half, 1)
    given = lax.dynamic_slice_in_dim(heads, (1 - core) * half, half, 1)
    other = lax.ppermute(given, "core", SWAP)
    shares = leave(own_weight, other_weight, mine, other, 4)
    sums = [lax.psum_scatter(s, CHIP, scatter_dimension=0, tiled=True) for s in shares]
    summed = jnp.concatenate(sums, axis=1)
    kept = lax.dynamic_slice_in_dim(summed, core * local, local, 0)
    given = lax.dynamic_slice_in_dim(summed, (1 - core) * local, local, 0)
    other = lax.ppermute(given, "core", SWAP)
    left = jnp.where(core == 0, kept, other)
    right = jnp.where(core == 0, other, kept)
    projected = jnp.concatenate([left, right], axis=1).astype(jnp.float32)
    first = lax.axis_index(HEAD) * local
    gate = lax.dynamic_slice_in_dim(modulation, first, local, 1)[2][:, None]
    mixed = (wide + gate * projected).astype(jnp.bfloat16)
    return mixed.T


def solution(mesh):
    fine = Mesh(mesh.devices.reshape(2, 4, 2, 4, 2), ("yh", "x", "yl", "z", "core"))
    placed = (
        P(FRAME, HEAD),
        P(None, None, HEAD),
        P(HEAD, None),
        P(),
        P(HEAD, FRAME, None),
    )
    return jax.shard_map(
        shards, mesh=fine, in_specs=placed, out_specs=P(FRAME, HEAD), check_vma=False
    )
```

time: 386 us -> 634 us (1.64)
  waiting for transfers between devices: 156 us -> 504 us
  matrix products: 86.3 us -> 0 us
  local copies, waits for them, and re-layouts: 87 us -> 37.2 us
  Pallas kernels: 0 us -> 47.5 us
  other arithmetic: 38.7 us -> 2.66 us
  blocking collectives: 0 us -> 22.7 us
    all_gather x3 -> x8, waiting for transfers between devices: 81.7 us -> 329 us  [the longest x4 215 us: shards(): lax.all_gather(part, FRAME, axis=0, tiled=True)]
    reduce_scatter x1 -> x4, waiting for transfers between devices: 73.4 us -> 167 us  [shards(): lax.psum_scatter(s, CHIP, scatter_dimension=0, tiled=True)]
    dot_general x4 -> x0, matrix products: 86.3 us -> none  [the longest x1 32.5 us: update_heads(): jnp.einsum('qhd,khd->hqk', query, keys, preferred_element_type=jnp.float32)]
    pallas_call x0 -> x3, Pallas kernels: none -> 47.5 us  [the longest x1 24.1 us: attend(): pl.pallas_call(kernel, in_specs=[pl.BlockSpec(memory_space=pltpu.SMEM)] *...]
    reshape x1 -> x0, local copies, waits for them, and re-layouts: 44.5 us -> none  [shards(): keep = jnp.repeat(jnp.repeat(blocks, BLK, axis=1), BLK, axis=2)]
    reduce_sum x3 -> x7, other arithmetic: 35.5 us -> 1.32 us  [the longest x1 0.35 us: shards(): places = jnp.sum(jnp.where(chosen, blocks[None, None, :], 0), axis=2)]
    all_gather x0 -> x1, blocking collectives: none -> 22.7 us  [shards(): lax.all_gather(jnp.concatenate([own_center, own_spread], axis=0), HEAD, a...]
    broadcast_in_dim x2, local copies, waits for them, and re-layouts: 23.4 us -> 6.41 us  [the longest x1 3.21 us: shards(): gain = jnp.broadcast_to((1.0 + modulation[1])[:, None], (features, BLK))]
  transfers between devices with their start and end apart: 4 -> 15, of which waited for: 4 -> 14; matrix products, arithmetic and copies ran while one was open for 34% -> 3% of each run, Pallas kernels for 0% -> 4%
where the time goes in v1:
time: 634 us
  waiting for transfers between devices  504 us (79%)
  Pallas kernels  47.5 us (7%)
  local copies, waits for them, and re-layouts  37.2 us (6%)
  blocking collectives  22.7 us (4%)
  between operations  13.8 us (2%)
  starting transfers between devices  6.38 us (1%)
    all_gather x4, waiting for transfers between devices, shards(): lax.all_gather(part, FRAME, axis=0, tiled=True)  215 us
    reduce_scatter x4, waiting for transfers between devices, shards(): lax.psum_scatter(s, CHIP, scatter_dimension=0, tiled=True)  167 us
    all_gather x4, waiting for transfers between devices, shards(): lax.all_gather(across[:, i * quarter:(i + 1) * quarter], HEAD, axis=0, ti...  114 us
    pallas_call x1, Pallas kernels, attend(): pl.pallas_call(kernel, in_specs=[pl.BlockSpec(memory_space=pltpu.SMEM)] *...  24.1 us
    all_gather x1, blocking collectives, shards(): lax.all_gather(jnp.concatenate([own_center, own_spread], axis=0), HEAD, a...  22.7 us
    unnamed x30, local copies, waits for them, and re-layouts  16.8 us
    pallas_call x1, Pallas kernels, project(): pl.pallas_call(project_kernel, grid=(features // deep,), in_specs=[pl.Blo...  14.4 us
  transfers between devices with their start and end apart: 15, of which 14 were waited for; matrix products, arithmetic and copies ran while one was open for 3% of the time, Pallas kernels for 4%

profile of v1, /device:TPU:1, one launch (start us, length us, event | category | flops | bytes accessed | tf_op | source)
XLA Modules:
  0.0 634.1 jit_solution(3956119940871933869)
XLA Ops:
  6.5 2.0 fusion.7
  10.7 10.8 %copy.11 = bf16[3,256,5120]{2,1,0:T(8,128)(2,1)} copy(bf16[3,256,5120]{1,2,0:T(8,128)(2,1)} %bitcast.32) | data formatting | bytes 15728640 | tf_op jit(solution)/shard_map/transpose | solution.py:243
  21.8 22.7 %all-gather.1 = f32[16,2,1024]{2,1,0:T(2,128)S(1)} all-gather(f32[1,2,1024]{2,1,0:T(2,128)S(1)} %maximum_bitcast_fusion), channel_id=2, replica_groups=mesh['yh'=2,'x'=4,'yl'=2,'z'=4,'core'=2] {'yl','z','core'}, dimensions={0}, use_global_device_ids=true | all-gather | bytes 139264 | tf_op jit(solution)/shard_map/all_gather | solution.py:230
  44.7 3.0 all-gather.11.cloned.1.call-done.x0
  47.8 36.9 %all-gather.13.cloned.1.call-done.x1 = bf16[5120,256]{1,0:T(8,128)(2,1)} async-done(((bf16[320,256]{1,0:T(8,128)(2,1)}), bf16[5120,256]{1,0:T(8,128)(2,1)}) %all-gather.13.cloned.1.call-update) | async-done | bytes 2621456 | tf_op jit(solution)/shard_map/all_gather | solution.py:240
  84.7 36.9 %all-gather.15.cloned.1.call-done.x2 = bf16[5120,256]{1,0:T(8,128)(2,1)} async-done(((bf16[320,256]{1,0:T(8,128)(2,1)}), bf16[5120,256]{1,0:T(8,128)(2,1)}) %all-gather.15.cloned.1.call-update) | async-done | bytes 2621456 | tf_op jit(solution)/shard_map/all_gather | solution.py:240
  121.6 36.7 %all-gather.17.cloned.1.call-done.x3 = bf16[5120,256]{1,0:T(8,128)(2,1)} async-done(((bf16[320,256]{1,0:T(8,128)(2,1)}), bf16[5120,256]{1,0:T(8,128)(2,1)}) %all-gather.17.cloned.1.call-update) | async-done | bytes 2621456 | tf_op jit(solution)/shard_map/all_gather | solution.py:240
  158.3 3.2 broadcast_in_dim.60.gain
  161.5 3.2 broadcast_in_dim.62.shift
  164.7 1.7 copy-done.7
  166.4 1.7 copy-done.8
  168.2 14.4 %project.1 = (bf16[256,1024]{1,0:T(8,128)(2,1)S(1)}, bf16[1024,128]{1,0:T(8,128)(2,1)}, bf16[1024,128]{1,0:T(8,128)(2,1)}, bf16[128,1024]{1,0:T(8,128)(2,1)}, bf16[128,1024]{1,0:T(8,128)(2,1)}) custom-call(bf16[5120,256]{1,0:T(8,128)(2,1)S(1)} %copy-done.5, bf16[5120,256]{1,0:T(8,128)(2,1)S(1)} %copy-done.6, bf16[5120,256]{1,0:T(8,128)(2,1)S(1)} %copy-done.7, ...), custom_call_target="tpu_custom_call" | custom-call | flops 8053063680 | bytes 18350080 | tf_op jit(solution)/shard_map/project/pallas_call | solution.py:61
  184.7 3.0 copy.10
  189.0 46.9 %all-gather.19.cloned.1.call-done.refs_3_ = bf16[8192,128]{1,0:T(8,128)(2,1)} async-done(((bf16[1024,128]{1,0:T(8,128)(2,1)}), bf16[8192,128]{1,0:T(8,128)(2,1)}) %all-gather.19.cloned.1.call-update) | async-done | bytes 2097168 | tf_op jit(solution)/shard_map/all_gather | solution.py:259
  235.9 56.0 %all-gather.21.cloned.1.call-done.refs_4_ = bf16[8192,128]{1,0:T(8,128)(2,1)} async-done(((bf16[1024,128]{1,0:T(8,128)(2,1)}), bf16[8192,128]{1,0:T(8,128)(2,1)}) %all-gather.21.cloned.1.call-update) | async-done | bytes 2097168 | tf_op jit(solution)/shard_map/all_gather | solution.py:259
  291.9 56.1 %all-gather.23.cloned.1.call-done.refs_5_ = bf16[1024,1024]{1,0:T(8,128)(2,1)} async-done(((bf16[128,1024]{1,0:T(8,128)(2,1)}), bf16[1024,1024]{1,0:T(8,128)(2,1)}) %all-gather.23.cloned.1.call-update) | async-done | bytes 2097168 | tf_op jit(solution)/shard_map/all_gather | solution.py:259
  348.0 56.1 %all-gather.25.cloned.1.call-done.refs_6_ = bf16[1024,1024]{1,0:T(8,128)(2,1)} async-done(((bf16[128,1024]{1,0:T(8,128)(2,1)}), bf16[1024,1024]{1,0:T(8,128)(2,1)}) %all-gather.25.cloned.1.call-update) | async-done | bytes 2097168 | tf_op jit(solution)/shard_map/all_gather | solution.py:259
  404.2 1.6 copy-done
  405.7 1.6 copy-done.1
  407.3 1.6 copy-done.2
  408.9 1.6 copy-done.3
  410.5 24.1 %attend.1 = bf16[256,1024]{1,0:T(8,128)(2,1)S(1)} custom-call(s32[16,64]{1,0:T(8,128)S(1)} %select_reduce_fusion.refs_0_, s32[16]{0:T(128)S(1)} %reduce_sum.77.refs_1_, bf16[256,1024]{1,0:T(8,128)(2,1)S(1)} %get-tuple-element.14.refs_2_, bf16[8192,128]{1,0:T(8,128)(2,1)S(1)} %copy-done, bf16[8192,128]{1,0:T(8,128)(2,1)S(1)} %copy-done.1, ...), custom_call_target="tpu_custom_call" | custom-call | flops 2147483648 | bytes 8388608 | tf_op jit(solution)/shard_map/attend/pallas_call | solution.py:169
  434.8 1.5 collective-permute-done.1.other
  436.3 9.0 %leave.1 = (bf16[5120,128]{1,0:T(8,128)(2,1)S(1)}, bf16[5120,128]{1,0:T(8,128)(2,1)}, bf16[5120,128]{1,0:T(8,128)(2,1)}, bf16[5120,128]{1,0:T(8,128)(2,1)}) custom-call(bf16[5120,256]{1,0:T(8,128)(2,1)S(1)} %bitcast.28, bf16[5120,256]{1,0:T(8,128)(2,1)} %collective-permute-done.other_weight, bf16[256,512]{1,0:T(8,128)(2,1)S(1)} %get-tuple-element.34.own, ...), custom_call_target="tpu_custom_call" | custom-call | flops 2684354560 | bytes 15728640 | tf_op jit(solution)/shard_map/leave/pallas_call | solution.py:200
  445.3 1.1 copy-done.4
  448.3 47.0 %reduce-scatter.5.cloned.1.call-done = bf16[640,128]{1,0:T(8,128)(2,1)} async-done(((bf16[5120,128]{1,0:T(8,128)(2,1)}), bf16[640,128]{1,0:T(8,128)(2,1)}) %reduce-scatter.5.cloned.1.call-update) | async-done | bytes 163856 | tf_op jit(solution)/shard_map/reduce_scatter | solution.py:268
  496.3 40.0 %reduce-scatter.7.cloned.1.call-done = bf16[640,128]{1,0:T(8,128)(2,1)} async-done(((bf16[5120,128]{1,0:T(8,128)(2,1)}), bf16[640,128]{1,0:T(8,128)(2,1)}) %reduce-scatter.7.cloned.1.call-update) | async-done | bytes 163856 | tf_op jit(solution)/shard_map/reduce_scatter | solution.py:268
  537.2 40.1 %reduce-scatter.9.cloned.1.call-done = bf16[640,128]{1,0:T(8,128)(2,1)} async-done(((bf16[5120,128]{1,0:T(8,128)(2,1)}), bf16[640,128]{1,0:T(8,128)(2,1)}) %reduce-scatter.9.cloned.1.call-update) | async-done | bytes 163856 | tf_op jit(solution)/shard_map/reduce_scatter | solution.py:268
  578.3 40.0 %reduce-scatter.11.cloned.1.call-done = bf16[640,128]{1,0:T(8,128)(2,1)} async-done(((bf16[5120,128]{1,0:T(8,128)(2,1)}), bf16[640,128]{1,0:T(8,128)(2,1)}) %reduce-scatter.11.cloned.1.call-update) | async-done | bytes 163856 | tf_op jit(solution)/shard_map/reduce_scatter | solution.py:268
  619.2 5.5 collective-permute-start.2
  624.8 1.2 collective-permute-done.2
  626.2 1.1 fusion.3
  (70 shorter events, 12.1 us)
Async XLA Ops:
  6.5 41.3 %all-gather.11.cloned.1.call-start = ((), (), s32[]{:S(2)}) async-start(), calls=%async_computation.4 | async-start | bytes 2785280 | tf_op jit(solution)/shard_map/all_gather | solution.py:240
  8.5 76.2 %all-gather.13.cloned.1.call-start = ((), (), s32[]{:S(2)}) async-start(), calls=%async_computation.5 | async-start | bytes 2785280 | tf_op jit(solution)/shard_map/all_gather | solution.py:240
  9.3 112.3 %all-gather.15.cloned.1.call-start = ((), (), s32[]{:S(2)}) async-start(), calls=%async_computation.6 | async-start | bytes 2785280 | tf_op jit(solution)/shard_map/all_gather | solution.py:240
  10.0 148.2 %all-gather.17.cloned.1.call-start = ((), (), s32[]{:S(2)}) async-start(), calls=%async_computation.7 | async-start | bytes 2785280 | tf_op jit(solution)/shard_map/all_gather | solution.py:240
  10.6 225.3 %all-gather.19.cloned.1.call-start = ((), (), s32[]{:S(2)}) async-start(), calls=%async_computation.8 | async-start | bytes 2359296 | tf_op jit(solution)/shard_map/all_gather | solution.py:259
  10.7 10.8 %copy-start.9 = (bf16[1024,320]{0,1:T(8,128)(2,1)S(1)}, bf16[1024,320]{0,1:T(8,128)(2,1)}, u32[]{:S(2)}) copy-start(bf16[1024,320]{0,1:T(8,128)(2,1)} %param.5) | copy-start | bytes 1966084
  21.5 23.2 %copy-start.11 = (f32[3,5120]{1,0:T(4,128)S(1)}, f32[3,5120]{1,0:T(4,128)}, u32[]{:S(2)}) copy-start(f32[3,5120]{1,0:T(4,128)} %param.8) | copy-start | bytes 184324
  158.3 6.4 %copy-start.6 = (bf16[5120,256]{1,0:T(8,128)(2,1)S(1)}, bf16[5120,256]{1,0:T(8,128)(2,1)}, u32[]{:S(2)}) copy-start(bf16[5120,256]{1,0:T(8,128)(2,1)} %all-gather.13.cloned.1.call-done.x1) | copy-start | bytes 7864324
  161.5 3.2 copy-start.5
  164.7 1.7 copy-start.7
  166.4 1.7 copy-start.8
  182.6 109.3 %all-gather.21.cloned.1.call-start = ((), (), s32[]{:S(2)}) async-start(), calls=%async_computation.9 | async-start | bytes 2359296 | tf_op jit(solution)/shard_map/all_gather | solution.py:259
  183.1 164.9 %all-gather.23.cloned.1.call-start = ((), (), s32[]{:S(2)}) async-start(), calls=%async_computation.10 | async-start | bytes 2359296 | tf_op jit(solution)/shard_map/all_gather | solution.py:259
  183.9 220.3 %all-gather.25.cloned.1.call-start = ((), (), s32[]{:S(2)}) async-start(), calls=%async_computation.11 | async-start | bytes 2359296 | tf_op jit(solution)/shard_map/all_gather | solution.py:259
  184.6 3.4 copy-start.12
  184.7 310.7 %reduce-scatter.5.cloned.1.call-start = ((), (), s32[]{:S(2)}) async-start(), calls=%async_computation.12 | async-start | bytes 1474560 | tf_op jit(solution)/shard_map/reduce_scatter | solution.py:268
  187.7 247.1 %collective-permute-start = (bf16[5120,256]{1,0:T(8,128)(2,1)S(1)}, bf16[5120,256]{1,0:T(8,128)(2,1)}, u32[]{:S(2)}, u32[]{:S(2)}) collective-permute-start(bf16[5120,256]{1,0:T(8,128)(2,1)S(1)} %bitcast.27), channel_id=1, source_target_pairs={{0,1},{1,0},{2,3},{3,2},{4,5},{5,4},{6,7},{7,6},{8,9},{9,8},{10,11... | collective-permute-start | bytes 7864328 | tf_op jit(solution)/shard_map/ppermute | solution.py:247
  404.2 1.6 copy-start
  405.7 1.6 copy-start.1
  407.3 1.6 copy-start.2
  408.9 1.6 copy-start.3
  434.7 1.6 collective-permute-start.1
  445.3 1.1 copy-start.4
  446.4 89.8 %reduce-scatter.7.cloned.1.call-start = ((), (), s32[]{:S(2)}) async-start(), calls=%async_computation.13 | async-start | bytes 1474560 | tf_op jit(solution)/shard_map/reduce_scatter | solution.py:268
  447.0 130.3 %reduce-scatter.9.cloned.1.call-start = ((), (), s32[]{:S(2)}) async-start(), calls=%async_computation.14 | async-start | bytes 1474560 | tf_op jit(solution)/shard_map/reduce_scatter | solution.py:268
  447.7 170.5 %reduce-scatter.11.cloned.1.call-start = ((), (), s32[]{:S(2)}) async-start(), calls=%async_computation.15 | async-start | bytes 1474560 | tf_op jit(solution)/shard_map/reduce_scatter | solution.py:268
  537.2 88.9 %copy-start.10 = (bf16[1024,320]{0,1:T(8,128)(2,1)S(1)}, bf16[1024,320]{0,1:T(8,128)(2,1)}, u32[]{:S(2)}) copy-start(bf16[1024,320]{0,1:T(8,128)(2,1)} %param.5) | copy-start | bytes 1966084
  619.2 6.8 %collective-permute-start.2 = (bf16[320,512]{1,0:T(8,128)(2,1)S(1)}, bf16[320,512]{1,0:T(8,128)(2,1)S(1)}, u32[]{:S(2)}, u32[]{:S(2)}) collective-permute-start(bf16[320,512]{1,0:T(8,128)(2,1)S(1)} %constant_dynamic-slice_fusion), channel_id=1, source_target_pairs={{0,1},{1,0},{2,3},{3,2},{4,5},{5,4},{6,7},{7,6},{8,9},{9,8},{10,11... | collective-permute-start | bytes 983048 | tf_op jit(solution)/shard_map/ppermute | solution.py:272
Sparse Core Ops, SparseCore 0:
  9.1 38.6 all-gather.10
  49.5 35.1 all-gather.12
  86.4 35.0 all-gather.14
  123.1 35.0 all-gather.16
  182.7 53.2 all-gather.18
  238.1 53.7 all-gather.20
  294.2 53.7 all-gather.22
  350.4 53.7 all-gather.24
  446.5 48.7 reduce-scatter.4
  497.6 38.6 reduce-scatter.6
  538.7 38.6 reduce-scatter.8
  579.6 38.6 reduce-scatter.10

commit v2 on v0

v2 whole, which is shorter than its diff:
```python
import math

import jax
import jax.numpy as jnp
from jax import lax
from jax.experimental import pallas as pl
from jax.experimental.pallas import tpu as pltpu
from jax.sharding import Mesh
from jax.sharding import PartitionSpec as P

BLK = 128
EPSILON = 1e-06
NEGATIVE = -1e30
FRAME = ("yh", "x")
HEAD = ("yl", "z", "core")
MIB = 1 << 20
GROUP = 4
CUTS = ((0, 224), (224, 432), (432, 640))


def shift(value, axis, steps):
    count = lax.axis_size(axis)
    return lax.ppermute(value, axis, [(i, (i + steps) % count) for i in range(count)])


def swap(value, axis):
    return shift(value, axis, 1)


def tile_of(rows):
    return {640: 128, 224: 112}.get(rows, rows)


def project_kernel(
    chips, heads, *refs
):
    xs, (own, other, gain, bias), outs, (normed, total) = (
        refs[:10],
        refs[10:14],
        refs[14:22],
        refs[22:],
    )
    step = pl.program_id(0)
    features = normed.shape[0] * normed.shape[1]
    count = normed.shape[2]
    lay = [(piece, 0, x) for piece, x in enumerate(xs[:7])]
    lay += [(7, cut[0], x) for cut, x in zip(CUTS, xs[7:])]

    def fold(values):
        return jnp.sum(values.reshape(values.shape[0] // 8, 8, count), axis=0)

    @pl.when(step == 0)
    def _():
        total[...] = jnp.zeros_like(total)
        summed = jnp.zeros((8, count), jnp.float32)
        for _, _, x in lay:
            tile = tile_of(x.shape[0])

            def add(i, state, x=x, tile=tile):
                wide = x[pl.ds(pl.multiple_of(i * tile, 16), tile), :].astype(jnp.float32)
                return state + fold(wide)

            summed = lax.fori_loop(0, x.shape[0] // tile, add, summed)
        center = jnp.sum(summed, axis=0, keepdims=True) / features
        summed = jnp.zeros((8, count), jnp.float32)
        for _, _, x in lay:
            tile = tile_of(x.shape[0])

            def square(i, state, x=x, tile=tile):
                wide = x[pl.ds(pl.multiple_of(i * tile, 16), tile), :].astype(jnp.float32)
                return state + fold(jnp.square(wide - center))

            summed = lax.fori_loop(0, x.shape[0] // tile, square, summed)
        rate = lax.rsqrt(jnp.sum(summed, axis=0, keepdims=True) / features + EPSILON)
        for piece, first, x in lay:
            tile = tile_of(x.shape[0])

            def norm(i, _, x=x, tile=tile, piece=piece, first=first):
                start = pl.multiple_of(i * tile, 16)
                row = pl.multiple_of(chips[piece] * normed.shape[1] + first + start, 16)
                part_gain = gain[pl.ds(row, tile), :]
                part_bias = bias[pl.ds(row, tile), :]
                for part in range(count // BLK):
                    columns = slice(part * BLK, (part + 1) * BLK)
                    wide = x[pl.ds(start, tile), columns].astype(jnp.float32)
                    value = (wide - center[:, columns]) * rate[:, columns] * part_gain + part_bias
                    normed[
                        piece, pl.ds(pl.multiple_of(first + start, 16), tile), columns
                    ] = value.astype(jnp.bfloat16)
                return 0

            lax.fori_loop(0, x.shape[0] // tile, norm, 0)

    held = normed[step]
    outs_own = own.shape[0]
    total[:outs_own] += jnp.dot(own[...], held, preferred_element_type=jnp.float32)
    total[outs_own:] += jnp.dot(other[...], held, preferred_element_type=jnp.float32)

    @pl.when(step == pl.num_programs(0) - 1)
    def _():
        for index in range(4):
            kv, q = outs[2 * index], outs[2 * index + 1]
            base = pl.multiple_of(heads[index] * BLK, BLK)
            q[...] = total[pl.ds(base, BLK), :].astype(jnp.bfloat16)
            keys = total[pl.ds(base + 2 * BLK, BLK), :]
            for part in range(count // BLK):
                columns = slice(part * BLK, (part + 1) * BLK)
                kv[:BLK, columns] = keys[:, columns].T.astype(jnp.bfloat16)
            kv[BLK:, :] = total[pl.ds(base + 4 * BLK, BLK), :].astype(jnp.bfloat16)


def project(chips, heads, xs, own, other, gain, bias):
    outs, features = own.shape
    deep, count = xs[0].shape
    whole = lambda shape: pl.BlockSpec(shape, lambda k, *_: (0, 0))
    block = pl.BlockSpec((outs, deep), lambda k, chips, heads: (0, chips[k]))
    shapes = [(2 * BLK, count), (BLK, count)] * 4
    return pl.pallas_call(
        project_kernel,
        grid_spec=pltpu.PrefetchScalarGridSpec(
            num_scalar_prefetch=2,
            grid=(features // deep,),
            in_specs=[whole(x.shape) for x in xs]
            + [block, block, whole(gain.shape), whole(bias.shape)],
            out_specs=[whole(s) for s in shapes],
            scratch_shapes=[
                pltpu.VMEM((features // deep, deep, count), jnp.bfloat16),
                pltpu.VMEM((2 * outs, count), jnp.float32),
            ],
        ),
        out_shape=[jax.ShapeDtypeStruct(s, jnp.bfloat16) for s in shapes],
        compiler_params=pltpu.CompilerParams(vmem_limit_bytes=50 * MIB),
        cost_estimate=pl.CostEstimate(
            flops=4 * outs * features * count,
            bytes_accessed=2 * features * (count + 2 * outs),
            transcendentals=0,
        ),
        name="project",
    )(chips, heads, *xs, own, other, gain, bias)


def attend_kernel(factor, places, counts, *refs):
    queries, pieces, outs, (kv, scores, arrived) = refs[:4], refs[4:20], refs[20:24], refs[24:]
    copies = [
        pltpu.make_async_copy(piece, kv.at[index], arrived.at[index])
        for index, piece in enumerate(pieces)
    ]
    for copy in copies:
        copy.start()
    for copy in copies:
        copy.wait()
    per_piece = kv.shape[2] // BLK

    for index, (query_ref, out) in enumerate(zip(queries, outs)):

        def one(block, _):
            row = index * per_piece + block
            column = pl.multiple_of(block * BLK, BLK)
            query = query_ref[:, pl.ds(column, BLK)]
            count = counts[row]
            groups = (count + GROUP - 1) // GROUP

            def rate(group, top):
                for item in range(GROUP):
                    place = group * GROUP + item
                    where = places[row, place]
                    start = pl.multiple_of((where % per_piece) * BLK, BLK)
                    score = jnp.dot(
                        kv[where // per_piece, :BLK, pl.ds(start, BLK)],
                        query,
                        preferred_element_type=jnp.float32,
                    )
                    scores[pl.ds(pl.multiple_of(place * BLK, BLK), BLK), :] = score
                    best = jnp.max(score.reshape(BLK // 8, 8, BLK), axis=0)
                    top = jnp.maximum(top, best + jnp.where(place < count, 0.0, NEGATIVE))
                return top

            top = lax.fori_loop(0, groups, rate, jnp.full((8, BLK), NEGATIVE, jnp.float32))
            top = jnp.max(top, axis=0, keepdims=True) * factor

            def gather(group, state):
                total, summed = state
                weights, held = [], []
                for item in range(GROUP):
                    place = group * GROUP + item
                    score = scores[pl.ds(pl.multiple_of(place * BLK, BLK), BLK), :]
                    offset = top + jnp.where(place < count, 0.0, -NEGATIVE)
                    weight = jnp.exp2(score * factor - offset)
                    total = total + jnp.sum(weight.reshape(BLK // 8, 8, BLK), axis=0)
                    weights.append(weight.astype(jnp.bfloat16))
                    where = places[row, place]
                    start = pl.multiple_of((where % per_piece) * BLK, BLK)
                    held.append(kv[where // per_piece, BLK:, pl.ds(start, BLK)])
                summed = summed + jnp.dot(
                    jnp.concatenate(held, axis=1),
                    jnp.concatenate(weights, axis=0),
                    preferred_element_type=jnp.float32,
                )
                return total, summed

            total, summed = lax.fori_loop(
                0,
                groups,
                gather,
                (jnp.zeros((8, BLK), jnp.float32), jnp.zeros((BLK, BLK), jnp.float32)),
            )
            total = jnp.sum(total, axis=0, keepdims=True)
            out[:, pl.ds(column, BLK)] = (summed / total).astype(jnp.bfloat16)
            return 0

        lax.fori_loop(0, per_piece, one, 0)


def attend(factor, places, counts, queries, pieces):
    def kernel(*refs):
        attend_kernel(factor, *refs)

    shape = queries[0].shape
    tokens = len(pieces) * shape[1]
    return pl.pallas_call(
        kernel,
        in_specs=[pl.BlockSpec(memory_space=pltpu.SMEM)] * 2
        + [pl.BlockSpec(memory_space=pltpu.VMEM)] * len(queries)
        + [pl.BlockSpec(memory_space=pl.ANY)] * len(pieces),
        out_specs=[pl.BlockSpec(memory_space=pltpu.VMEM)] * len(queries),
        out_shape=[jax.ShapeDtypeStruct(shape, jnp.bfloat16)] * len(queries),
        scratch_shapes=[
            pltpu.VMEM((len(pieces), *pieces[0].shape), jnp.bfloat16),
            pltpu.VMEM((tokens, BLK), jnp.float32),
            pltpu.SemaphoreType.DMA((len(pieces),)),
        ],
        compiler_params=pltpu.CompilerParams(vmem_limit_bytes=40 * MIB),
        cost_estimate=pl.CostEstimate(
            flops=tokens * BLK * shape[1] * len(queries),
            bytes_accessed=4 * tokens * BLK,
            transcendentals=tokens * shape[1],
        ),
        name="attend",
    )(places, counts, *queries, *pieces)


def leave_kernel(plan, chips, columns, *refs):
    weights, heads, rest = refs[:4], refs[4:8], refs[8:]
    step = pl.program_id(0)
    summed = jnp.dot(
        jnp.concatenate([weight[...] for weight in weights], axis=1),
        jnp.concatenate([head[...] for head in heads], axis=0),
        preferred_element_type=jnp.float32,
    )
    adds = sum(len(given) for given, _ in plan)
    taken, outs = rest[:adds], list(rest[adds:])
    at = 0
    for index, (given, cuts) in enumerate(plan):
        here = taken[at : at + len(given)]
        at += len(given)
        mine = [outs.pop(0) for _ in cuts]

        @pl.when(step == index)
        def _():
            for cut, out in zip(cuts, mine):
                value = summed[cut[0] : cut[1]]
                parts = []
                for (first, last), ref in zip(given, here):
                    if (first, last) == cut:
                        value = value + ref[...].astype(jnp.float32)
                    else:
                        parts.append((first, last, ref))
                if parts:
                    ((first, last, ref),) = parts
                    middle = value[first:last] + ref[...].astype(jnp.float32)
                    pieces = [value[:first]] if first else []
                    pieces.append(middle)
                    pieces += [value[last:]] if last < cut[1] else []
                    value = jnp.concatenate(pieces, axis=0)
                out[...] = value.astype(out.dtype)


def leave(chips, columns, weight, heads, plan, taken):
    high = CUTS[-1][1]
    count = heads[0].shape[1]
    steps = len(plan)

    def block(index):
        return pl.BlockSpec((high, BLK), lambda i, chips, columns: (chips[i], columns[index]))

    whole = lambda shape: pl.BlockSpec(shape, lambda i, *_: (0, 0))
    shapes = [(cut[1] - cut[0], count) for _, cuts in plan for cut in cuts]

    def kernel(*refs):
        leave_kernel(plan, *refs)

    return pl.pallas_call(
        kernel,
        grid_spec=pltpu.PrefetchScalarGridSpec(
            num_scalar_prefetch=2,
            grid=(steps,),
            in_specs=[block(i) for i in range(4)]
            + [whole(h.shape) for h in heads]
            + [whole(t.shape) for t in taken],
            out_specs=[whole(s) for s in shapes],
        ),
        out_shape=[jax.ShapeDtypeStruct(s, jnp.bfloat16) for s in shapes],
        compiler_params=pltpu.CompilerParams(vmem_limit_bytes=40 * MIB),
        cost_estimate=pl.CostEstimate(
            flops=2 * steps * high * 4 * BLK * count,
            bytes_accessed=2 * steps * high * (4 * BLK + count),
            transcendentals=0,
        ),
        name="leave",
    )(chips, columns, *[weight] * 4, *heads, *taken)


def gather_tokens(own):
    below = shift(own, "z", 1)
    above = shift(own, "z", -1)
    beside = swap(own, "yl")
    far = shift(below, "z", 1)
    beside_below = swap(below, "yl")
    beside_above = shift(beside, "z", -1)
    first, second, third = [slice(*cut) for cut in CUTS]
    parts = [
        swap(far[first], "yl"),
        shift(beside_above[second], "z", -1),
        shift(beside_below[third], "z", 1),
    ]
    places = [(0, 0), (0, -1), (0, 1), (1, 0), (0, 2), (1, -1), (1, 1), (1, 2)]
    return places, [own, below, above, beside, far, beside_below, beside_above, *parts]


def shards(tokens, qkv_weight, out_weight, modulation, block_mask):
    rows, local = tokens.shape
    features = modulation.shape[1]
    heads_here = block_mask.shape[0]
    inner = qkv_weight.shape[2]
    head_size = inner // heads_here
    factor = math.log2(math.e) / math.sqrt(head_size)
    half = rows // 2
    core = lax.axis_index("core")
    frame_x, frame_y = lax.axis_index("x"), lax.axis_index("yh")
    chip_y, chip_z = lax.axis_index("yl"), lax.axis_index("z")
    across = tokens.T

    def chip(dy, dz):
        return ((chip_y + dy) % 2) * 4 + (chip_z + dz) % 4

    def mine_and_given(value, axis):
        size = value.shape[axis] // 2
        mine = lax.dynamic_slice_in_dim(value, core * size, size, axis)
        return mine, lax.dynamic_slice_in_dim(value, (1 - core) * size, size, axis)

    def head_slot(steps):
        head = (frame_x + steps) % 4
        return jnp.where(head // 2 == core, 0, 1), head % 2

    mine, given = mine_and_given(across, 1)
    other = swap(given, "core")
    own = jnp.concatenate(
        [jnp.where(core == 0, mine, other), jnp.where(core == 0, other, mine)], axis=0
    )
    places, xs = gather_tokens(own)

    own_weight = jnp.transpose(qkv_weight, (0, 2, 1)).reshape(3 * inner, features)
    other_weight = swap(own_weight, "core")
    gain = jnp.broadcast_to((1.0 + modulation[1])[:, None], (features, BLK))
    bias = jnp.broadcast_to(modulation[0][:, None], (features, BLK))
    leaving = jnp.concatenate([out_weight, swap(out_weight, "core")], axis=0).T

    mask_mine, mask_given = mine_and_given(block_mask, 1)
    mask_heads = jnp.stack([mask_mine, swap(mask_given, "core")])
    mask_rows = []
    for steps in range(4):
        side, slot = head_slot(steps)
        part = lax.dynamic_slice(
            mask_heads, (side, slot, 0, 0), (1, 1, *mask_heads.shape[2:])
        )[0, 0]
        mask_rows.append(shift(part, "x", steps) if steps else part)
    keep = jnp.concatenate(mask_rows, axis=0) != 0
    blocks = jnp.arange(keep.shape[1], dtype=jnp.int32)
    per_core = half // BLK
    piece, inside = blocks // per_core, blocks % per_core
    from_core, from_y, from_x = core ^ (piece // 8), frame_y ^ (piece // 4 % 2), (frame_x - piece % 4) % 4
    origin = (from_y * 4 + from_x) * (2 * per_core) + from_core * per_core + inside
    same = origin[:, None] == blocks[None, :]
    keep = jnp.sum(jnp.where(same[None] & keep[:, None, :], 1, 0), axis=2)
    counts = jnp.sum(keep, axis=1)
    earlier = blocks[None, :] < blocks[:, None]
    rank = jnp.sum(jnp.where(earlier[None], keep[:, None, :], 0), axis=2)
    chosen = (keep[:, None, :] != 0) & (rank[:, None, :] == blocks[None, :, None])
    listed = jnp.sum(jnp.where(chosen, blocks[None, None, :], 0), axis=2)

    chips = jnp.stack([chip(*place) for place in places]).astype(jnp.int32)
    slots = [head_slot(steps) for steps in range(4)]
    bases = jnp.stack([side * 3 * heads_here + slot for side, slot in slots]).astype(jnp.int32)
    made = project(chips, bases, xs, own_weight, other_weight, gain, bias)
    order = (0, 1, 3, 2)
    kv = {0: made[0]}
    for steps in order[1:]:
        kv[steps] = shift(made[2 * steps], "x", steps)
    queries = [made[1]] + [shift(made[2 * steps + 1], "x", steps) for steps in (1, 2, 3)]
    away = {steps: swap(kv[steps], "yh") for steps in order}
    pieces = [kv[i] for i in range(4)] + [away[i] for i in range(4)]
    pieces += [swap(p, "core") for p in pieces]
    heads = attend(factor, listed, counts, queries, pieces)
    heads = [heads[0]] + [shift(heads[steps], "x", -steps) for steps in (1, 2, 3)]

    columns = jnp.stack([side * heads_here + slot for side, slot in slots]).astype(jnp.int32)
    whole = CUTS[0][0], CUTS[-1][1]

    def shares(targets, plan, *taken):
        chips = jnp.stack([chip(*target) for target in targets]).astype(jnp.int32)
        return leave(chips, columns, leaving, heads, plan, taken)

    parts = shares([(1, 2)], [((), CUTS)])
    first = swap(parts[0], "yl")
    second = shift(parts[1], "z", 1)
    third = shift(parts[2], "z", -1)
    down, up, side = shares(
        [(0, 2), (1, 1), (1, -1)],
        [((CUTS[0],), (whole,)), ((CUTS[1],), (whole,)), ((CUTS[2],), (whole,))],
        first,
        second,
        third,
    )
    down, up, side = shift(down, "z", -1), shift(up, "z", 1), swap(side, "yl")
    down, up, side = shares(
        [(0, -1), (0, 1), (1, 0)],
        [((whole, whole), (whole,)), ((), (whole,)), ((whole,), (whole,))],
        down,
        side,
        up,
    )
    down, up, side = shift(down, "z", -1), shift(up, "z", 1), swap(side, "yl")
    (summed,) = shares([(0, 0)], [((whole, whole, whole), (whole,))], down, up, side)

    kept, given = mine_and_given(summed, 0)
    other = swap(given, "core")
    projected = jnp.concatenate(
        [jnp.where(core == 0, kept, other), jnp.where(core == 0, other, kept)], axis=1
    ).astype(jnp.float32)
    start = lax.axis_index(HEAD) * local
    gate = lax.dynamic_slice_in_dim(modulation, start, local, 1)[2][:, None]
    return (across.astype(jnp.float32) + gate * projected).astype(jnp.bfloat16).T


def solution(mesh):
    fine = Mesh(mesh.devices.reshape(2, 4, 2, 4, 2), ("yh", "x", "yl", "z", "core"))
    placed = (
        P(FRAME, HEAD),
        P(None, None, HEAD),
        P(HEAD, None),
        P(),
        P(HEAD, FRAME, None),
    )
    return jax.shard_map(
        shards, mesh=fine, in_specs=placed, out_specs=P(FRAME, HEAD), check_vma=False
    )
```

time: 386 us -> 263 us (0.68)
  matrix products: 86.3 us -> 0 us
  starting transfers between devices: 0.12 us -> 74 us
  local copies, waits for them, and re-layouts: 87 us -> 25.6 us
  waiting for transfers between devices: 156 us -> 101 us
  Pallas kernels: 0 us -> 51.5 us
  other arithmetic: 38.7 us -> 6.48 us
  between operations: 13.2 us -> 0.44 us
    ppermute x0 -> x47, waiting for transfers between devices: none -> 101 us  [shift(): lax.ppermute(value, axis, [(i, (i + steps) % count) for i in range(count)])]
    dot_general x4 -> x0, matrix products: 86.3 us -> none  [the longest x1 32.5 us: update_heads(): jnp.einsum('qhd,khd->hqk', query, keys, preferred_element_type=jnp.float32)]
    all_gather x3 -> x0, waiting for transfers between devices: 81.7 us -> none  [the longest x1 66.4 us: shards(): whole = lax.all_gather(tokens, 'head', axis=1, tiled=True)]
    ppermute x0 -> x47, starting transfers between devices: none -> 74 us  [shift(): lax.ppermute(value, axis, [(i, (i + steps) % count) for i in range(count)])]
    reduce_scatter x1 -> x0, waiting for transfers between devices: 73.4 us -> none  [shards(): lax.psum_scatter(lax.dot_general(out_weight, heads_done, (((0,), (1,)), (...]
    pallas_call x0 -> x6, Pallas kernels: none -> 51.5 us  [the longest x1 22 us: project(): pl.pallas_call(project_kernel, grid_spec=pltpu.PrefetchScalarGridSpec(num...]
    reshape x1 -> x0, local copies, waits for them, and re-layouts: 44.5 us -> none  [shards(): keep = jnp.repeat(jnp.repeat(blocks, BLK, axis=1), BLK, axis=2)]
    reduce_sum x3, other arithmetic: 35.5 us -> 1.35 us  [the longest x1 0.65 us: shards(): counts = jnp.sum(keep, axis=1)]
  transfers between devices with their start and end apart: 4 -> 47, of which waited for: 4 -> 25; matrix products, arithmetic and copies ran while one was open for 34% -> 6% of each run, Pallas kernels for 0% -> 16%
where the time goes in v2:
time: 263 us; the launch traced here: 259 us
  waiting for transfers between devices  101 us (38%)
  starting transfers between devices  74 us (28%)
  Pallas kernels  51.5 us (20%)
  local copies, waits for them, and re-layouts  25.6 us (10%)
  other arithmetic  6.48 us (2%)
    ppermute x47, waiting for transfers between devices, shift(): lax.ppermute(value, axis, [(i, (i + steps) % count) for i in range(count)])  101 us
    ppermute x47, starting transfers between devices, shift(): lax.ppermute(value, axis, [(i, (i + steps) % count) for i in range(count)])  74 us
    pallas_call x1, Pallas kernels, project(): pl.pallas_call(project_kernel, grid_spec=pltpu.PrefetchScalarGridSpec(num...  22 us
    pallas_call x1, Pallas kernels, attend(): pl.pallas_call(kernel, in_specs=[pl.BlockSpec(memory_space=pltpu.SMEM)] *...  20.4 us
    transpose x1, local copies, waits for them, and re-layouts, shards(): jnp.transpose(qkv_weight, (0, 2, 1)).reshape(3 * inner, features)  10.4 us
    pallas_call x4, Pallas kernels, leave(): pl.pallas_call(kernel, grid_spec=pltpu.PrefetchScalarGridSpec(num_scalar_...  9.11 us
    unnamed x23, local copies, waits for them, and re-layouts  7.78 us
  transfers between devices with their start and end apart: 47, of which 25 were waited for; matrix products, arithmetic and copies ran while one was open for 6% of the time, Pallas kernels for 16%

profile of v2, /device:TPU:1, one launch (start us, length us, event | category | flops | bytes accessed | tf_op | source)
XLA Modules:
  0.0 259.3 jit_solution(8366382113089635717)
XLA Ops:
  0.0 10.4 %copy.11 = bf16[3,256,5120]{2,1,0:T(8,128)(2,1)} copy(bf16[3,256,5120]{1,2,0:T(8,128)(2,1)} %bitcast.46) | data formatting | bytes 15728640 | tf_op jit(solution)/shard_map/transpose | solution.py:362
  12.0 7.6 %collective-permute-done.5 = bf16[320,512]{1,0:T(8,128)(2,1)S(1)} collective-permute-done((bf16[320,512]{1,0:T(8,128)(2,1)S(1)}, bf16[320,512]{1,0:T(8,128)(2,1)S(1)}, u32[]{:S(2)}, u32[]{:S(2)}) %collective-permute-start.5) | collective-permute-done | bytes 327712 | tf_op jit(solution)/shard_map/ppermute | solution.py:23
  22.9 15.8 %collective-permute-done.6.refs_1_ = bf16[640,512]{1,0:T(8,128)(2,1)S(1)} collective-permute-done((bf16[640,512]{1,0:T(8,128)(2,1)S(1)}, bf16[640,512]{1,0:T(8,128)(2,1)S(1)}, u32[]{:S(2)}, u32[]{:S(2)}) %collective-permute-start.6) | collective-permute-done | bytes 655392 | tf_op jit(solution)/shard_map/ppermute | solution.py:23
  40.0 2.7 %collective-permute-start.11 = (bf16[640,512]{1,0:T(8,128)(2,1)S(1)}, bf16[640,512]{1,0:T(8,128)(2,1)S(1)}, u32[]{:S(2)}, u32[]{:S(2)}) collective-permute-start(bf16[640,512]{1,0:T(8,128)(2,1)S(1)} %collective-permute-done.8.refs_3_), channel_id=1, source_target_pairs={{0,6},{2,0},{4,2},{6,4},{1,7},{3,1},{5,3},{7,5},{8,14},{10,8},{12,... | collective-permute-start | bytes 1966088 | tf_op jit(solution)/shard_map/ppermute | solution.py:23
  42.8 12.7 %collective-permute-done.9.refs_4_ = bf16[640,512]{1,0:T(8,128)(2,1)S(1)} collective-permute-done((bf16[640,512]{1,0:T(8,128)(2,1)S(1)}, bf16[640,512]{1,0:T(8,128)(2,1)S(1)}, u32[]{:S(2)}, u32[]{:S(2)}) %collective-permute-start.9) | collective-permute-done | bytes 655392 | tf_op jit(solution)/shard_map/ppermute | solution.py:23
  57.9 2.7 %collective-permute-start.13 = (bf16[208,512]{1,0:T(8,128)(2,1)S(1)}, bf16[208,512]{1,0:T(8,128)(2,1)S(1)}, u32[]{:S(2)}, u32[]{:S(2)}) collective-permute-start(bf16[208,512]{1,0:T(8,128)(2,1)S(1)} %slice.25), channel_id=1, source_target_pairs={{0,6},{2,0},{4,2},{6,4},{1,7},{3,1},{5,3},{7,5},{8,14},{10,8},{12,... | collective-permute-start | bytes 638984 | tf_op jit(solution)/shard_map/ppermute | solution.py:23
  60.8 4.4 %copy.10 = bf16[256,5120]{0,1:T(8,128)(2,1)} copy(bf16[256,5120]{1,0:T(8,128)(2,1)} %param.7) | data formatting | bytes 5242880 | tf_op args[2]
  65.2 4.3 %collective-permute-done.7.refs_2_ = bf16[640,512]{1,0:T(8,128)(2,1)S(1)} collective-permute-done((bf16[640,512]{1,0:T(8,128)(2,1)S(1)}, bf16[640,512]{1,0:T(8,128)(2,1)S(1)}, u32[]{:S(2)}, u32[]{:S(2)}) %collective-permute-start.7) | collective-permute-done | bytes 655392 | tf_op jit(solution)/shard_map/ppermute | solution.py:23
  69.5 4.0 %collective-permute-start = (bf16[256,5120]{0,1:T(8,128)(2,1)}, bf16[256,5120]{0,1:T(8,128)(2,1)}, u32[]{:S(2)}, u32[]{:S(2)}) collective-permute-start(bf16[256,5120]{0,1:T(8,128)(2,1)} %copy.10), channel_id=1, source_target_pairs={{0,1},{1,0},{2,3},{3,2},{4,5},{5,4},{6,7},{7,6},{8,9},{9,8},{10,11... | collective-permute-start | bytes 7864328 | tf_op jit(solution)/shard_map/ppermute | solution.py:23
  74.1 3.2 %broadcast_in_dim.66.refs_12_ = f32[5120,128]{1,0:T(8,128)} broadcast(f32[5120]{0:T(1024)S(1)} %bitcast.50), dimensions={0} | broadcast | bytes 2641920 | tf_op jit(solution)/shard_map/broadcast_in_dim | solution.py:364
  77.3 3.2 %broadcast_in_dim.68.refs_13_ = f32[5120,128]{1,0:T(8,128)} broadcast(f32[5120]{0:T(1024)S(1)} %bitcast.49), dimensions={0} | broadcast | bytes 2641920 | tf_op jit(solution)/shard_map/broadcast_in_dim | solution.py:365
  80.5 22.0 %project.1 = (bf16[256,512]{1,0:T(8,128)(2,1)S(1)}, bf16[128,512]{1,0:T(8,128)(2,1)S(1)}, bf16[256,512]{1,0:T(8,128)(2,1)S(1)}, bf16[128,512]{1,0:T(8,128)(2,1)S...) custom-call(s32[8]{0:T(128)S(1)} %stack.96.chips, ...), custom_call_target="tpu_custom_call" | custom-call | flops 8053063680 | bytes 20971520 | tf_op jit(solution)/shard_map/project/pallas_call | solution.py:118
  103.8 2.5 collective-permute-start.1
  117.2 12.6 %collective-permute-done.18.refs_5_ = bf16[128,512]{1,0:T(8,128)(2,1)S(1)} collective-permute-done((bf16[128,512]{1,0:T(8,128)(2,1)S(1)}, bf16[128,512]{1,0:T(8,128)(2,1)S(1)}, u32[]{:S(2)}, u32[]{:S(2)}) %collective-permute-start.18) | collective-permute-done | bytes 131104 | tf_op jit(solution)/shard_map/ppermute | solution.py:23
  129.8 2.6 %collective-permute-start.22 = (bf16[256,512]{1,0:T(8,128)(2,1)S(1)}, bf16[256,512]{1,0:T(8,128)(2,1)S(1)}, u32[]{:S(2)}, u32[]{:S(2)}) collective-permute-start(bf16[256,512]{1,0:T(8,128)(2,1)S(1)} %get-tuple-element.30.refs_6_), channel_id=1, source_target_pairs={{0,64},{64,0},{1,65},{65,1},{2,66},{66,2},{3,67},{67,3},{4,68},{68... | collective-permute-start | bytes 786440 | tf_op jit(solution)/shard_map/ppermute | solution.py:23
  135.0 2.6 %collective-permute-start.24 = (bf16[256,512]{1,0:T(8,128)(2,1)S(1)}, bf16[256,512]{1,0:T(8,128)(2,1)S(1)}, u32[]{:S(2)}, u32[]{:S(2)}) collective-permute-start(bf16[256,512]{1,0:T(8,128)(2,1)S(1)} %collective-permute-done.20.refs_8_), channel_id=1, source_target_pairs={{0,64},{64,0},{1,65},{65,1},{2,66},{66,2},{3,67},{67,3},{4,68},{68... | collective-permute-start | bytes 786440 | tf_op jit(solution)/shard_map/ppermute | solution.py:23
  137.7 3.6 %collective-permute-start.27 = (bf16[256,512]{1,0:T(8,128)(2,1)S(1)}, bf16[256,512]{1,0:T(8,128)(2,1)S(1)}, u32[]{:S(2)}, u32[]{:S(2)}) collective-permute-start(bf16[256,512]{1,0:T(8,128)(2,1)S(1)} %collective-permute-done.19.refs_7_), channel_id=1, source_target_pairs={{0,1},{1,0},{2,3},{3,2},{4,5},{5,4},{6,7},{7,6},{8,9},{9,8},{10,11... | collective-permute-start | bytes 786440 | tf_op jit(solution)/shard_map/ppermute | solution.py:23
  141.4 3.1 %collective-permute-done.23.refs_11_ = bf16[256,512]{1,0:T(8,128)(2,1)S(1)} collective-permute-done((bf16[256,512]{1,0:T(8,128)(2,1)S(1)}, bf16[256,512]{1,0:T(8,128)(2,1)S(1)}, u32[]{:S(2)}, u32[]{:S(2)}) %collective-permute-start.23) | collective-permute-done | bytes 262176 | tf_op jit(solution)/shard_map/ppermute | solution.py:23
  145.5 4.7 %collective-permute-done.24.refs_12_ = bf16[256,512]{1,0:T(8,128)(2,1)S(1)} collective-permute-done((bf16[256,512]{1,0:T(8,128)(2,1)S(1)}, bf16[256,512]{1,0:T(8,128)(2,1)S(1)}, u32[]{:S(2)}, u32[]{:S(2)}) %collective-permute-start.24) | collective-permute-done | bytes 262176 | tf_op jit(solution)/shard_map/ppermute | solution.py:23
  150.1 2.5 collective-permute-start.29
  159.2 20.4 %attend.1 = (bf16[128,512]{1,0:T(8,128)(2,1)S(1)}, bf16[128,512]{1,0:T(8,128)(2,1)S(1)}, bf16[128,512]{1,0:T(8,128)(2,1)S(1)}, bf16[128,512]{1,0:T(8,128)(2,1)S(1)}) custom-call(s32[16,64]{1,0:T(8,128)S(1)} %select_reduce_fusion.2.refs_0_, s32[16]{0:T(128)S(1)} %get-tuple-element.47.refs_1_, bf16[128,512]{1,0:T(8,128)(2,1)S(1)} %get-tuple-element.26.refs_2_, ...), custom_call_target="tpu_custom_call" | custom-call | flops 2147483648 | bytes 4194304 | tf_op jit(solution)/shard_map/attend/pallas_call | solution.py:220
  179.6 3.5 %collective-permute-start.34 = (bf16[128,512]{1,0:T(8,128)(2,1)S(1)}, bf16[128,512]{1,0:T(8,128)(2,1)S(1)}, u32[]{:S(2)}, u32[]{:S(2)}) collective-permute-start(bf16[128,512]{1,0:T(8,128)(2,1)S(1)} %get-tuple-element.35), channel_id=1, source_target_pairs={{0,48},{16,0},{32,16},{48,32},{1,49},{17,1},{33,17},{49,33},{2,50}... | collective-permute-start | bytes 393224 | tf_op jit(solution)/shard_map/ppermute | solution.py:23
  189.0 3.8 %collective-permute-done.36.refs_9_ = bf16[128,512]{1,0:T(8,128)(2,1)S(1)} collective-permute-done((bf16[128,512]{1,0:T(8,128)(2,1)S(1)}, bf16[128,512]{1,0:T(8,128)(2,1)S(1)}, u32[]{:S(2)}, u32[]{:S(2)}) %collective-permute-start.36) | collective-permute-done | bytes 131104 | tf_op jit(solution)/shard_map/ppermute | solution.py:23
  193.9 4.3 %collective-permute-start.37 = (bf16[224,512]{1,0:T(8,128)(2,1)S(1)}, bf16[224,512]{1,0:T(8,128)(2,1)S(1)}, u32[]{:S(2)}, u32[]{:S(2)}) collective-permute-start(bf16[224,512]{1,0:T(8,128)(2,1)S(1)} %get-tuple-element.38), channel_id=1, source_target_pairs={{0,8},{8,0},{1,9},{9,1},{2,10},{10,2},{3,11},{11,3},{4,12},{12,4},... | collective-permute-start | bytes 688136 | tf_op jit(solution)/shard_map/ppermute | solution.py:23
  198.2 6.8 %collective-permute-start.38 = (bf16[208,512]{1,0:T(8,128)(2,1)S(1)}, bf16[208,512]{1,0:T(8,128)(2,1)S(1)}, u32[]{:S(2)}, u32[]{:S(2)}) collective-permute-start(bf16[208,512]{1,0:T(8,128)(2,1)S(1)} %get-tuple-element.39), channel_id=1, source_target_pairs={{0,2},{2,4},{4,6},{6,0},{1,3},{3,5},{5,7},{7,1},{8,10},{10,12},{12... | collective-permute-start | bytes 638984 | tf_op jit(solution)/shard_map/ppermute | solution.py:23
  205.1 2.7 %collective-permute-done.38.refs_11_ = bf16[208,512]{1,0:T(8,128)(2,1)S(1)} collective-permute-done((bf16[208,512]{1,0:T(8,128)(2,1)S(1)}, bf16[208,512]{1,0:T(8,128)(2,1)S(1)}, u32[]{:S(2)}, u32[]{:S(2)}) %collective-permute-start.38) | collective-permute-done | bytes 213024 | tf_op jit(solution)/shard_map/ppermute | solution.py:23
  209.7 2.8 %leave.5 = (bf16[640,512]{1,0:T(8,128)(2,1)S(1)}, bf16[640,512]{1,0:T(8,128)(2,1)S(1)}, bf16[640,512]{1,0:T(8,128)(2,1)S(1)}) custom-call(s32[3]{0:T(128)S(1)} %pad_add_fusion.3.refs_0_, s32[4]{0:T(128)S(1)} %pad_add_fusion.refs_1_, bf16[5120,512]{1,0:T(8,128)(2,1)S(1)} %maximum_bitcast_fusion.refs_2_.refs_3_.refs_4_.refs_5_, ...), custom_call_target="tpu_custom_call" | custom-call | flops 1006632960 | bytes 3932160 | tf_op jit(solution)/shard_map/leave/pallas_call | solution.py:292
  214.7 11.1 %collective-permute-done.40.refs_10_ = bf16[640,512]{1,0:T(8,128)(2,1)S(1)} collective-permute-done((bf16[640,512]{1,0:T(8,128)(2,1)S(1)}, bf16[640,512]{1,0:T(8,128)(2,1)S(1)}, u32[]{:S(2)}, u32[]{:S(2)}) %collective-permute-start.40) | collective-permute-done | bytes 655392 | tf_op jit(solution)/shard_map/ppermute | solution.py:23
  229.2 4.0 %leave.6 = (bf16[640,512]{1,0:T(8,128)(2,1)}, bf16[640,512]{1,0:T(8,128)(2,1)}, bf16[640,512]{1,0:T(8,128)(2,1)S(1)}) custom-call(s32[3]{0:T(128)S(1)} %pad_add_fusion.2.refs_0_, s32[4]{0:T(128)S(1)} %pad_add_fusion.refs_1_, bf16[5120,512]{1,0:T(8,128)(2,1)S(1)} %maximum_bitcast_fusion.refs_2_.refs_3_.refs_4_.refs_5_, ...), custom_call_target="tpu_custom_call" | custom-call | flops 1006632960 | bytes 3932160 | tf_op jit(solution)/shard_map/leave/pallas_call | solution.py:292
  235.6 10.4 %collective-permute-done.43.refs_10_ = bf16[640,512]{1,0:T(8,128)(2,1)S(1)} collective-permute-done((bf16[640,512]{1,0:T(8,128)(2,1)}, bf16[640,512]{1,0:T(8,128)(2,1)S(1)}, u32[]{:S(2)}, u32[]{:S(2)}) %collective-permute-start.43) | collective-permute-done | bytes 655392 | tf_op jit(solution)/shard_map/ppermute | solution.py:23
  247.2 2.5 copy-done.1
  250.9 4.8 %collective-permute-start.46 = (bf16[320,512]{1,0:T(8,128)(2,1)S(1)}, bf16[320,512]{1,0:T(8,128)(2,1)S(1)}, u32[]{:S(2)}, u32[]{:S(2)}) collective-permute-start(bf16[320,512]{1,0:T(8,128)(2,1)S(1)} %constant_dynamic-slice_fusion), channel_id=1, source_target_pairs={{0,1},{1,0},{2,3},{3,2},{4,5},{5,4},{6,7},{7,6},{8,9},{9,8},{10,11... | collective-permute-start | bytes 983048 | tf_op jit(solution)/shard_map/ppermute | solution.py:23
  (121 shorter events, 54.3 us)
Async XLA Ops:
  10.5 63.6 %collective-permute-start.15 = (bf16[768,5120]{1,0:T(8,128)(2,1)}, bf16[768,5120]{1,0:T(8,128)(2,1)}, u32[]{:S(2)}, u32[]{:S(2)}) collective-permute-start(bf16[768,5120]{1,0:T(8,128)(2,1)} %bitcast.47), channel_id=1, source_target_pairs={{0,1},{1,0},{2,3},{3,2},{4,5},{5,4},{6,7},{7,6},{8,9},{9,8},{10,11... | collective-permute-start | bytes 23592968 | tf_op jit(solution)/shard_map/ppermute | solution.py:23
  19.8 18.9 %collective-permute-start.6 = (bf16[640,512]{1,0:T(8,128)(2,1)S(1)}, bf16[640,512]{1,0:T(8,128)(2,1)S(1)}, u32[]{:S(2)}, u32[]{:S(2)}) collective-permute-start(bf16[640,512]{1,0:T(8,128)(2,1)S(1)} %pad_maximum_fusion.refs_0_), channel_id=1, source_target_pairs={{0,2},{2,4},{4,6},{6,0},{1,3},{3,5},{5,7},{7,1},{8,10},{10,12},{12... | collective-permute-start | bytes 1966088 | tf_op jit(solution)/shard_map/ppermute | solution.py:23
  21.6 18.4 %collective-permute-start.8 = (bf16[640,512]{1,0:T(8,128)(2,1)S(1)}, bf16[640,512]{1,0:T(8,128)(2,1)S(1)}, u32[]{:S(2)}, u32[]{:S(2)}) collective-permute-start(bf16[640,512]{1,0:T(8,128)(2,1)S(1)} %pad_maximum_fusion.refs_0_), channel_id=1, source_target_pairs={{0,8},{8,0},{1,9},{9,1},{2,10},{10,2},{3,11},{11,3},{4,12},{12,4},... | collective-permute-start | bytes 1966088 | tf_op jit(solution)/shard_map/ppermute | solution.py:23
  38.7 16.8 %collective-permute-start.9 = (bf16[640,512]{1,0:T(8,128)(2,1)S(1)}, bf16[640,512]{1,0:T(8,128)(2,1)S(1)}, u32[]{:S(2)}, u32[]{:S(2)}) collective-permute-start(bf16[640,512]{1,0:T(8,128)(2,1)S(1)} %collective-permute-done.6.refs_1_), channel_id=1, source_target_pairs={{0,2},{2,4},{4,6},{6,0},{1,3},{3,5},{5,7},{7,1},{8,10},{10,12},{12... | collective-permute-start | bytes 1966088 | tf_op jit(solution)/shard_map/ppermute | solution.py:23
  38.7 19.0 %collective-permute-start.10 = (bf16[640,512]{1,0:T(8,128)(2,1)S(1)}, bf16[640,512]{1,0:T(8,128)(2,1)S(1)}, u32[]{:S(2)}, u32[]{:S(2)}) collective-permute-start(bf16[640,512]{1,0:T(8,128)(2,1)S(1)} %collective-permute-done.6.refs_1_), channel_id=1, source_target_pairs={{0,8},{8,0},{1,9},{9,1},{2,10},{10,2},{3,11},{11,3},{4,12},{12,4},... | collective-permute-start | bytes 1966088 | tf_op jit(solution)/shard_map/ppermute | solution.py:23
  40.0 17.8 %collective-permute-start.11 = (bf16[640,512]{1,0:T(8,128)(2,1)S(1)}, bf16[640,512]{1,0:T(8,128)(2,1)S(1)}, u32[]{:S(2)}, u32[]{:S(2)}) collective-permute-start(bf16[640,512]{1,0:T(8,128)(2,1)S(1)} %collective-permute-done.8.refs_3_), channel_id=1, source_target_pairs={{0,6},{2,0},{4,2},{6,4},{1,7},{3,1},{5,3},{7,5},{8,14},{10,8},{12,... | collective-permute-start | bytes 1966088 | tf_op jit(solution)/shard_map/ppermute | solution.py:23
  42.7 26.8 %collective-permute-start.7 = (bf16[640,512]{1,0:T(8,128)(2,1)S(1)}, bf16[640,512]{1,0:T(8,128)(2,1)S(1)}, u32[]{:S(2)}, u32[]{:S(2)}) collective-permute-start(bf16[640,512]{1,0:T(8,128)(2,1)S(1)} %pad_maximum_fusion.refs_0_), channel_id=1, source_target_pairs={{0,6},{2,0},{4,2},{6,4},{1,7},{3,1},{5,3},{7,5},{8,14},{10,8},{12,... | collective-permute-start | bytes 1966088 | tf_op jit(solution)/shard_map/ppermute | solution.py:23
  56.4 17.7 %collective-permute-start.12 = (bf16[224,512]{1,0:T(8,128)(2,1)S(1)}, bf16[224,512]{1,0:T(8,128)(2,1)S(1)}, u32[]{:S(2)}, u32[]{:S(2)}) collective-permute-start(bf16[224,512]{1,0:T(8,128)(2,1)S(1)} %slice.24), channel_id=1, source_target_pairs={{0,8},{8,0},{1,9},{9,1},{2,10},{10,2},{3,11},{11,3},{4,12},{12,4},... | collective-permute-start | bytes 688136 | tf_op jit(solution)/shard_map/ppermute | solution.py:23
  57.8 15.9 %collective-permute-start.14 = (bf16[208,512]{1,0:T(8,128)(2,1)S(1)}, bf16[208,512]{1,0:T(8,128)(2,1)S(1)}, u32[]{:S(2)}, u32[]{:S(2)}) collective-permute-start(bf16[208,512]{1,0:T(8,128)(2,1)S(1)} %slice.26), channel_id=1, source_target_pairs={{0,2},{2,4},{4,6},{6,0},{1,3},{3,5},{5,7},{7,1},{8,10},{10,12},{12... | collective-permute-start | bytes 638984 | tf_op jit(solution)/shard_map/ppermute | solution.py:23
  57.9 16.2 %collective-permute-start.13 = (bf16[208,512]{1,0:T(8,128)(2,1)S(1)}, bf16[208,512]{1,0:T(8,128)(2,1)S(1)}, u32[]{:S(2)}, u32[]{:S(2)}) collective-permute-start(bf16[208,512]{1,0:T(8,128)(2,1)S(1)} %slice.25), channel_id=1, source_target_pairs={{0,6},{2,0},{4,2},{6,4},{1,7},{3,1},{5,3},{7,5},{8,14},{10,8},{12,... | collective-permute-start | bytes 638984 | tf_op jit(solution)/shard_map/ppermute | solution.py:23
  69.5 116.5 %collective-permute-start = (bf16[256,5120]{0,1:T(8,128)(2,1)}, bf16[256,5120]{0,1:T(8,128)(2,1)}, u32[]{:S(2)}, u32[]{:S(2)}) collective-permute-start(bf16[256,5120]{0,1:T(8,128)(2,1)} %copy.10), channel_id=1, source_target_pairs={{0,1},{1,0},{2,3},{3,2},{4,5},{5,4},{6,7},{7,6},{8,9},{9,8},{10,11... | collective-permute-start | bytes 7864328 | tf_op jit(solution)/shard_map/ppermute | solution.py:23
  102.5 12.6 %collective-permute-start.16 = (bf16[128,512]{1,0:T(8,128)(2,1)S(1)}, bf16[128,512]{1,0:T(8,128)(2,1)S(1)}, u32[]{:S(2)}, u32[]{:S(2)}) collective-permute-start(bf16[128,512]{1,0:T(8,128)(2,1)S(1)} %get-tuple-element.27), channel_id=1, source_target_pairs={{0,16},{16,32},{32,48},{48,0},{1,17},{17,33},{33,49},{49,1},{2,18}... | collective-permute-start | bytes 393224 | tf_op jit(solution)/shard_map/ppermute | solution.py:23
  112.4 20.0 %collective-permute-start.19 = (bf16[256,512]{1,0:T(8,128)(2,1)S(1)}, bf16[256,512]{1,0:T(8,128)(2,1)S(1)}, u32[]{:S(2)}, u32[]{:S(2)}) collective-permute-start(bf16[256,512]{1,0:T(8,128)(2,1)S(1)} %get-tuple-element.31), channel_id=1, source_target_pairs={{0,16},{16,32},{32,48},{48,0},{1,17},{17,33},{33,49},{49,1},{2,18}... | collective-permute-start | bytes 786440 | tf_op jit(solution)/shard_map/ppermute | solution.py:23
  113.3 21.3 %collective-permute-start.20 = (bf16[256,512]{1,0:T(8,128)(2,1)S(1)}, bf16[256,512]{1,0:T(8,128)(2,1)S(1)}, u32[]{:S(2)}, u32[]{:S(2)}) collective-permute-start(bf16[256,512]{1,0:T(8,128)(2,1)S(1)} %get-tuple-element.32), channel_id=1, source_target_pairs={{0,32},{16,48},{32,0},{48,16},{1,33},{17,49},{33,1},{49,17},{2,34}... | collective-permute-start | bytes 786440 | tf_op jit(solution)/shard_map/ppermute | solution.py:23
  115.1 19.9 %collective-permute-start.21 = (bf16[256,512]{1,0:T(8,128)(2,1)S(1)}, bf16[256,512]{1,0:T(8,128)(2,1)S(1)}, u32[]{:S(2)}, u32[]{:S(2)}) collective-permute-start(bf16[256,512]{1,0:T(8,128)(2,1)S(1)} %get-tuple-element.33), channel_id=1, source_target_pairs={{0,48},{16,0},{32,16},{48,32},{1,49},{17,1},{33,17},{49,33},{2,50}... | collective-permute-start | bytes 786440 | tf_op jit(solution)/shard_map/ppermute | solution.py:23
  117.2 12.6 %collective-permute-start.18 = (bf16[128,512]{1,0:T(8,128)(2,1)S(1)}, bf16[128,512]{1,0:T(8,128)(2,1)S(1)}, u32[]{:S(2)}, u32[]{:S(2)}) collective-permute-start(bf16[128,512]{1,0:T(8,128)(2,1)S(1)} %get-tuple-element.29), channel_id=1, source_target_pairs={{0,48},{16,0},{32,16},{48,32},{1,49},{17,1},{33,17},{49,33},{2,50}... | collective-permute-start | bytes 393224 | tf_op jit(solution)/shard_map/ppermute | solution.py:23
  129.8 7.9 %collective-permute-start.22 = (bf16[256,512]{1,0:T(8,128)(2,1)S(1)}, bf16[256,512]{1,0:T(8,128)(2,1)S(1)}, u32[]{:S(2)}, u32[]{:S(2)}) collective-permute-start(bf16[256,512]{1,0:T(8,128)(2,1)S(1)} %get-tuple-element.30.refs_6_), channel_id=1, source_target_pairs={{0,64},{64,0},{1,65},{65,1},{2,66},{66,2},{3,67},{67,3},{4,68},{68... | collective-permute-start | bytes 786440 | tf_op jit(solution)/shard_map/ppermute | solution.py:23
  132.4 8.9 %collective-permute-start.26 = (bf16[256,512]{1,0:T(8,128)(2,1)S(1)}, bf16[256,512]{1,0:T(8,128)(2,1)S(1)}, u32[]{:S(2)}, u32[]{:S(2)}) collective-permute-start(bf16[256,512]{1,0:T(8,128)(2,1)S(1)} %get-tuple-element.30.refs_6_), channel_id=1, source_target_pairs={{0,1},{1,0},{2,3},{3,2},{4,5},{5,4},{6,7},{7,6},{8,9},{9,8},{10,11... | collective-permute-start | bytes 786440 | tf_op jit(solution)/shard_map/ppermute | solution.py:23
  134.6 9.9 %collective-permute-start.23 = (bf16[256,512]{1,0:T(8,128)(2,1)S(1)}, bf16[256,512]{1,0:T(8,128)(2,1)S(1)}, u32[]{:S(2)}, u32[]{:S(2)}) collective-permute-start(bf16[256,512]{1,0:T(8,128)(2,1)S(1)} %collective-permute-done.19.refs_7_), channel_id=1, source_target_pairs={{0,64},{64,0},{1,65},{65,1},{2,66},{66,2},{3,67},{67,3},{4,68},{68... | collective-permute-start | bytes 786440 | tf_op jit(solution)/shard_map/ppermute | solution.py:23
  135.0 15.2 %collective-permute-start.24 = (bf16[256,512]{1,0:T(8,128)(2,1)S(1)}, bf16[256,512]{1,0:T(8,128)(2,1)S(1)}, u32[]{:S(2)}, u32[]{:S(2)}) collective-permute-start(bf16[256,512]{1,0:T(8,128)(2,1)S(1)} %collective-permute-done.20.refs_8_), channel_id=1, source_target_pairs={{0,64},{64,0},{1,65},{65,1},{2,66},{66,2},{3,67},{67,3},{4,68},{68... | collective-permute-start | bytes 786440 | tf_op jit(solution)/shard_map/ppermute | solution.py:23
  137.7 19.2 %collective-permute-start.27 = (bf16[256,512]{1,0:T(8,128)(2,1)S(1)}, bf16[256,512]{1,0:T(8,128)(2,1)S(1)}, u32[]{:S(2)}, u32[]{:S(2)}) collective-permute-start(bf16[256,512]{1,0:T(8,128)(2,1)S(1)} %collective-permute-done.19.refs_7_), channel_id=1, source_target_pairs={{0,1},{1,0},{2,3},{3,2},{4,5},{5,4},{6,7},{7,6},{8,9},{9,8},{10,11... | collective-permute-start | bytes 786440 | tf_op jit(solution)/shard_map/ppermute | solution.py:23
  141.4 15.5 %collective-permute-start.28 = (bf16[256,512]{1,0:T(8,128)(2,1)S(1)}, bf16[256,512]{1,0:T(8,128)(2,1)S(1)}, u32[]{:S(2)}, u32[]{:S(2)}) collective-permute-start(bf16[256,512]{1,0:T(8,128)(2,1)S(1)} %collective-permute-done.20.refs_8_), channel_id=1, source_target_pairs={{0,1},{1,0},{2,3},{3,2},{4,5},{5,4},{6,7},{7,6},{8,9},{9,8},{10,11... | collective-permute-start | bytes 786440 | tf_op jit(solution)/shard_map/ppermute | solution.py:23
  144.5 10.7 %collective-permute-start.25 = (bf16[256,512]{1,0:T(8,128)(2,1)S(1)}, bf16[256,512]{1,0:T(8,128)(2,1)S(1)}, u32[]{:S(2)}, u32[]{:S(2)}) collective-permute-start(bf16[256,512]{1,0:T(8,128)(2,1)S(1)} %collective-permute-done.21.refs_9_), channel_id=1, source_target_pairs={{0,64},{64,0},{1,65},{65,1},{2,66},{66,2},{3,67},{67,3},{4,68},{68... | collective-permute-start | bytes 786440 | tf_op jit(solution)/shard_map/ppermute | solution.py:23
  179.6 8.6 %collective-permute-start.34 = (bf16[128,512]{1,0:T(8,128)(2,1)S(1)}, bf16[128,512]{1,0:T(8,128)(2,1)S(1)}, u32[]{:S(2)}, u32[]{:S(2)}) collective-permute-start(bf16[128,512]{1,0:T(8,128)(2,1)S(1)} %get-tuple-element.35), channel_id=1, source_target_pairs={{0,48},{16,0},{32,16},{48,32},{1,49},{17,1},{33,17},{49,33},{2,50}... | collective-permute-start | bytes 393224 | tf_op jit(solution)/shard_map/ppermute | solution.py:23
  193.9 15.8 %collective-permute-start.37 = (bf16[224,512]{1,0:T(8,128)(2,1)S(1)}, bf16[224,512]{1,0:T(8,128)(2,1)S(1)}, u32[]{:S(2)}, u32[]{:S(2)}) collective-permute-start(bf16[224,512]{1,0:T(8,128)(2,1)S(1)} %get-tuple-element.38), channel_id=1, source_target_pairs={{0,8},{8,0},{1,9},{9,1},{2,10},{10,2},{3,11},{11,3},{4,12},{12,4},... | collective-permute-start | bytes 688136 | tf_op jit(solution)/shard_map/ppermute | solution.py:23
  198.2 9.6 %collective-permute-start.38 = (bf16[208,512]{1,0:T(8,128)(2,1)S(1)}, bf16[208,512]{1,0:T(8,128)(2,1)S(1)}, u32[]{:S(2)}, u32[]{:S(2)}) collective-permute-start(bf16[208,512]{1,0:T(8,128)(2,1)S(1)} %get-tuple-element.39), channel_id=1, source_target_pairs={{0,2},{2,4},{4,6},{6,0},{1,3},{3,5},{5,7},{7,1},{8,10},{10,12},{12... | collective-permute-start | bytes 638984 | tf_op jit(solution)/shard_map/ppermute | solution.py:23
  212.5 13.3 %collective-permute-start.40 = (bf16[640,512]{1,0:T(8,128)(2,1)S(1)}, bf16[640,512]{1,0:T(8,128)(2,1)S(1)}, u32[]{:S(2)}, u32[]{:S(2)}) collective-permute-start(bf16[640,512]{1,0:T(8,128)(2,1)S(1)} %get-tuple-element.41), channel_id=1, source_target_pairs={{0,6},{2,0},{4,2},{6,4},{1,7},{3,1},{5,3},{7,5},{8,14},{10,8},{12,... | collective-permute-start | bytes 1966088 | tf_op jit(solution)/shard_map/ppermute | solution.py:23
  214.3 13.4 %collective-permute-start.41 = (bf16[640,512]{1,0:T(8,128)(2,1)S(1)}, bf16[640,512]{1,0:T(8,128)(2,1)S(1)}, u32[]{:S(2)}, u32[]{:S(2)}) collective-permute-start(bf16[640,512]{1,0:T(8,128)(2,1)S(1)} %get-tuple-element.42), channel_id=1, source_target_pairs={{0,8},{8,0},{1,9},{9,1},{2,10},{10,2},{3,11},{11,3},{4,12},{12,4},... | collective-permute-start | bytes 1966088 | tf_op jit(solution)/shard_map/ppermute | solution.py:23
  214.6 14.6 %collective-permute-start.42 = (bf16[640,512]{1,0:T(8,128)(2,1)S(1)}, bf16[640,512]{1,0:T(8,128)(2,1)S(1)}, u32[]{:S(2)}, u32[]{:S(2)}) collective-permute-start(bf16[640,512]{1,0:T(8,128)(2,1)S(1)} %get-tuple-element.43), channel_id=1, source_target_pairs={{0,2},{2,4},{4,6},{6,0},{1,3},{3,5},{5,7},{7,1},{8,10},{10,12},{12... | collective-permute-start | bytes 1966088 | tf_op jit(solution)/shard_map/ppermute | solution.py:23
  233.3 12.7 %collective-permute-start.43 = (bf16[640,512]{1,0:T(8,128)(2,1)}, bf16[640,512]{1,0:T(8,128)(2,1)S(1)}, u32[]{:S(2)}, u32[]{:S(2)}) collective-permute-start(bf16[640,512]{1,0:T(8,128)(2,1)} %get-tuple-element.44), channel_id=1, source_target_pairs={{0,6},{2,0},{4,2},{6,4},{1,7},{3,1},{5,3},{7,5},{8,14},{10,8},{12,... | collective-permute-start | bytes 1966088 | tf_op jit(solution)/shard_map/ppermute | solution.py:23
  233.3 13.9 %collective-permute-start.44 = (bf16[640,512]{1,0:T(8,128)(2,1)}, bf16[640,512]{1,0:T(8,128)(2,1)S(1)}, u32[]{:S(2)}, u32[]{:S(2)}) collective-permute-start(bf16[640,512]{1,0:T(8,128)(2,1)} %get-tuple-element.45), channel_id=1, source_target_pairs={{0,2},{2,4},{4,6},{6,0},{1,3},{3,5},{5,7},{7,1},{8,10},{10,12},{12... | collective-permute-start | bytes 1966088 | tf_op jit(solution)/shard_map/ppermute | solution.py:23
  234.7 12.5 %collective-permute-start.45 = (bf16[640,512]{1,0:T(8,128)(2,1)S(1)}, bf16[640,512]{1,0:T(8,128)(2,1)S(1)}, u32[]{:S(2)}, u32[]{:S(2)}) collective-permute-start(bf16[640,512]{1,0:T(8,128)(2,1)S(1)} %get-tuple-element.46), channel_id=1, source_target_pairs={{0,8},{8,0},{1,9},{9,1},{2,10},{10,2},{3,11},{11,3},{4,12},{12,4},... | collective-permute-start | bytes 1966088 | tf_op jit(solution)/shard_map/ppermute | solution.py:23
  (26 other events, 258.8 us)

commit v3 on v2

--- a/solution.py
+++ b/solution.py
@@ -1,3 +1,4 @@
+import functools
 import math
 
 import jax
@@ -14,8 +15,11 @@
 FRAME = ("yh", "x")
 HEAD = ("yl", "z", "core")
 MIB = 1 << 20
-GROUP = 4
+PAIRS = 8
 CUTS = ((0, 224), (224, 432), (432, 640))
+
+
+DEEP = CUTS[-1][1]
 
 
 def shift(value, axis, steps):
@@ -31,17 +35,68 @@
     return {640: 128, 224: 112}.get(rows, rows)
 
 
+def prepare_kernel(qkv, leaving, modulation, _, weight, gain, bias, leaving_out):
+    inner = qkv.shape[2]
+    for part in range(3):
+        weight[part * inner : (part + 1) * inner, :] = qkv[part].T
+    leaving_out[...] = leaving[...].T
+    for row, out, add in ((1, gain, 1.0), (0, bias, 0.0)):
+        for part in range(out.shape[0] // BLK):
+            rows = slice(part * BLK, (part + 1) * BLK)
+            line = modulation[row : row + 1, rows] + add
+            out[rows, :] = jnp.broadcast_to(line, (BLK, BLK)).T
+
+
+def prepare(qkv_weight, out_weight, modulation, after):
+    _, features, inner = qkv_weight.shape
+    deep = 512
+    return pl.pallas_call(
+        prepare_kernel,
+        grid=(features // deep,),
+        in_specs=[
+            pl.BlockSpec((3, deep, inner), lambda i: (0, i, 0)),
+            pl.BlockSpec((out_weight.shape[0], deep), lambda i: (0, i)),
+            pl.BlockSpec((3, deep), lambda i: (0, i)),
+            pl.BlockSpec(memory_space=pl.ANY),
+        ],
+        out_specs=[
+            pl.BlockSpec((3 * inner, deep), lambda i: (0, i)),
+            pl.BlockSpec((deep, BLK), lambda i: (i, 0)),
+            pl.BlockSpec((deep, BLK), lambda i: (i, 0)),
+            pl.BlockSpec((deep, out_weight.shape[0]), lambda i: (i, 0)),
+        ],
+        out_shape=[
+            jax.ShapeDtypeStruct((3 * inner, features), jnp.bfloat16),
+            jax.ShapeDtypeStruct((features, BLK), jnp.float32),
+            jax.ShapeDtypeStruct((features, BLK), jnp.float32),
+            jax.ShapeDtypeStruct((features, out_weight.shape[0]), jnp.bfloat16),
+        ],
+        compiler_params=pltpu.CompilerParams(vmem_limit_bytes=24 * MIB),
+        cost_estimate=pl.CostEstimate(
+            flops=0, bytes_accessed=16 * features * inner, transcendentals=0
+        ),
+        name="prepare",
+    )(qkv_weight, out_weight, modulation, after)
+
+
+def together(*arrays):
+    return pl.pallas_call(
+        lambda *refs: None,
+        in_specs=[pl.BlockSpec(memory_space=pl.ANY)] * len(arrays),
+        out_specs=[pl.BlockSpec(memory_space=pl.ANY)] * len(arrays),
+        out_shape=[jax.ShapeDtypeStruct(a.shape, a.dtype) for a in arrays],
+        input_output_aliases={i: i for i in range(len(arrays))},
+        name="together",
+    )(*arrays)
+
+
 def project_kernel(
     chips, heads, *refs
 ):
-    xs, (own, other, gain, bias), outs, (normed, total) = (
-        refs[:10],
-        refs[10:14],
-        refs[14:22],
-        refs[22:],
-    )
+    xs, weights, (gain, bias), rest = refs[:10], refs[10:14], refs[14:16], refs[16:]
+    (kv0, q0, *packed), (normed, total) = rest[-7:-2], rest[-2:]
     step = pl.program_id(0)
-    features = normed.shape[0] * normed.shape[1]
+    features = 8 * DEEP
     count = normed.shape[2]
     lay = [(piece, 0, x) for piece, x in enumerate(xs[:7])]
     lay += [(7, cut[0], x) for cut, x in zip(CUTS, xs[7:])]
@@ -77,7 +132,7 @@
 
             def norm(i, _, x=x, tile=tile, piece=piece, first=first):
                 start = pl.multiple_of(i * tile, 16)
-                row = pl.multiple_of(chips[piece] * normed.shape[1] + first + start, 16)
+                row = pl.multiple_of(chips[piece] * DEEP + first + start, 16)
                 part_gain = gain[pl.ds(row, tile), :]
                 part_bias = bias[pl.ds(row, tile), :]
                 for part in range(count // BLK):
@@ -85,46 +140,58 @@
                     wide = x[pl.ds(start, tile), columns].astype(jnp.float32)
                     value = (wide - center[:, columns]) * rate[:, columns] * part_gain + part_bias
                     normed[
-                        piece, pl.ds(pl.multiple_of(first + start, 16), tile), columns
+                        piece // 2,
+                        pl.ds(pl.multiple_of(piece % 2 * DEEP + first + start, 16), tile),
+                        columns,
                     ] = value.astype(jnp.bfloat16)
                 return 0
 
             lax.fori_loop(0, x.shape[0] // tile, norm, 0)
 
     held = normed[step]
-    outs_own = own.shape[0]
-    total[:outs_own] += jnp.dot(own[...], held, preferred_element_type=jnp.float32)
-    total[outs_own:] += jnp.dot(other[...], held, preferred_element_type=jnp.float32)
+    outs = total.shape[0] // 2
+    for side in range(2):
+        weight = jnp.concatenate([w[...] for w in weights[2 * side : 2 * side + 2]], axis=1)
+        total[side * outs : (side + 1) * outs] += jnp.dot(
+            weight, held, preferred_element_type=jnp.float32
+        )
 
     @pl.when(step == pl.num_programs(0) - 1)
     def _():
         for index in range(4):
-            kv, q = outs[2 * index], outs[2 * index + 1]
+            if index:
+                kv, q = packed[index - 1], packed[index - 1].at[2 * BLK :]
+            else:
+                kv, q = kv0, q0
             base = pl.multiple_of(heads[index] * BLK, BLK)
             q[...] = total[pl.ds(base, BLK), :].astype(jnp.bfloat16)
             keys = total[pl.ds(base + 2 * BLK, BLK), :]
             for part in range(count // BLK):
                 columns = slice(part * BLK, (part + 1) * BLK)
                 kv[:BLK, columns] = keys[:, columns].T.astype(jnp.bfloat16)
-            kv[BLK:, :] = total[pl.ds(base + 4 * BLK, BLK), :].astype(jnp.bfloat16)
-
-
-def project(chips, heads, xs, own, other, gain, bias):
+            kv[BLK : 2 * BLK, :] = total[pl.ds(base + 4 * BLK, BLK), :].astype(jnp.bfloat16)
+
+
+def project(chips, heads, xs, own, other, gain, bias, after):
     outs, features = own.shape
     deep, count = xs[0].shape
     whole = lambda shape: pl.BlockSpec(shape, lambda k, *_: (0, 0))
-    block = pl.BlockSpec((outs, deep), lambda k, chips, heads: (0, chips[k]))
-    shapes = [(2 * BLK, count), (BLK, count)] * 4
+    blocks = [
+        pl.BlockSpec((outs, deep), lambda k, chips, heads, i=i: (0, chips[2 * k + i]))
+        for i in range(2)
+    ]
+    shapes = [(2 * BLK, count), (BLK, count)] + [(3 * BLK, count)] * 3
     return pl.pallas_call(
         project_kernel,
         grid_spec=pltpu.PrefetchScalarGridSpec(
             num_scalar_prefetch=2,
-            grid=(features // deep,),
+            grid=(features // deep // 2,),
             in_specs=[whole(x.shape) for x in xs]
-            + [block, block, whole(gain.shape), whole(bias.shape)],
+            + [*blocks, *blocks, whole(gain.shape), whole(bias.shape)]
+            + [pl.BlockSpec(memory_space=pl.ANY)] * len(after),
             out_specs=[whole(s) for s in shapes],
             scratch_shapes=[
-                pltpu.VMEM((features // deep, deep, count), jnp.bfloat16),
+                pltpu.VMEM((features // deep // 2, 2 * deep, count), jnp.bfloat16),
                 pltpu.VMEM((2 * outs, count), jnp.float32),
             ],
         ),
@@ -136,115 +203,162 @@
             transcendentals=0,
         ),
         name="project",
-    )(chips, heads, *xs, own, other, gain, bias)
-
-
-def attend_kernel(factor, places, counts, *refs):
-    queries, pieces, outs, (kv, scores, arrived) = refs[:4], refs[4:20], refs[20:24], refs[24:]
-    copies = [
-        pltpu.make_async_copy(piece, kv.at[index], arrived.at[index])
-        for index, piece in enumerate(pieces)
-    ]
+    )(chips, heads, *xs, own, own, other, other, gain, bias, *after)
+
+
+def attend_kernel(factor, unroll, plan, places, counts, first, owner, *refs):
+    arrays, outs, rest = refs[: -4 - 8], refs[-4 - 8 : -8], refs[-8:]
+    kv, query, asked, scores, tops, totals, sums, arrived = rest
+    copies = []
+    for kind, index, array, start in plan:
+        to = (kv if kind == "kv" else query).at[index]
+        rows = to.shape[0]
+        copies.append(
+            pltpu.make_async_copy(
+                arrays[array].at[start : start + rows], to, arrived.at[len(copies)]
+            )
+        )
     for copy in copies:
         copy.start()
+    per_piece = kv.shape[2] // BLK
+    rows = len(outs) * per_piece
+    tops[...] = jnp.full_like(tops, NEGATIVE)
+    totals[...] = jnp.zeros_like(totals)
+    sums[...] = jnp.zeros_like(sums)
     for copy in copies:
         copy.wait()
-    per_piece = kv.shape[2] // BLK
-
-    for index, (query_ref, out) in enumerate(zip(queries, outs)):
-
-        def one(block, _):
-            row = index * per_piece + block
-            column = pl.multiple_of(block * BLK, BLK)
-            query = query_ref[:, pl.ds(column, BLK)]
-            count = counts[row]
-            groups = (count + GROUP - 1) // GROUP
-
-            def rate(group, top):
-                for item in range(GROUP):
-                    place = group * GROUP + item
-                    where = places[row, place]
-                    start = pl.multiple_of((where % per_piece) * BLK, BLK)
-                    score = jnp.dot(
-                        kv[where // per_piece, :BLK, pl.ds(start, BLK)],
-                        query,
-                        preferred_element_type=jnp.float32,
-                    )
-                    scores[pl.ds(pl.multiple_of(place * BLK, BLK), BLK), :] = score
-                    best = jnp.max(score.reshape(BLK // 8, 8, BLK), axis=0)
-                    top = jnp.maximum(top, best + jnp.where(place < count, 0.0, NEGATIVE))
-                return top
-
-            top = lax.fori_loop(0, groups, rate, jnp.full((8, BLK), NEGATIVE, jnp.float32))
-            top = jnp.max(top, axis=0, keepdims=True) * factor
-
-            def gather(group, state):
-                total, summed = state
-                weights, held = [], []
-                for item in range(GROUP):
-                    place = group * GROUP + item
-                    score = scores[pl.ds(pl.multiple_of(place * BLK, BLK), BLK), :]
-                    offset = top + jnp.where(place < count, 0.0, -NEGATIVE)
-                    weight = jnp.exp2(score * factor - offset)
-                    total = total + jnp.sum(weight.reshape(BLK // 8, 8, BLK), axis=0)
-                    weights.append(weight.astype(jnp.bfloat16))
-                    where = places[row, place]
-                    start = pl.multiple_of((where % per_piece) * BLK, BLK)
-                    held.append(kv[where // per_piece, BLK:, pl.ds(start, BLK)])
-                summed = summed + jnp.dot(
-                    jnp.concatenate(held, axis=1),
-                    jnp.concatenate(weights, axis=0),
-                    preferred_element_type=jnp.float32,
-                )
-                return total, summed
-
-            total, summed = lax.fori_loop(
-                0,
-                groups,
-                gather,
-                (jnp.zeros((8, BLK), jnp.float32), jnp.zeros((BLK, BLK), jnp.float32)),
+    for index in range(len(outs)):
+        for part in range(per_piece):
+            asked[index * per_piece + part] = query[index, :, part * BLK : (part + 1) * BLK]
+
+    def find(pair, low, high):
+        live = pair < high
+        pair = jnp.where(live, pair, low)
+        row = owner[pair]
+        place = 2 * (pair - first[row])
+        wheres = [places[row, place], places[row, place + 1]]
+        offsets = [
+            jnp.where(live, 0.0, NEGATIVE),
+            jnp.where(live & (place + 1 < counts[row]), 0.0, NEGATIVE),
+        ]
+        return row, wheres, offsets
+
+    def held(where, part):
+        start = pl.multiple_of((where & (per_piece - 1)) * BLK, BLK)
+        return kv[where >> 2, part * BLK : (part + 1) * BLK, pl.ds(start, BLK)]
+
+    def fold(op, value):
+        return op(value.reshape(BLK // 8, 8, BLK), axis=0)
+
+    def rate(low, high, step, _):
+        found = []
+        for item in range(unroll):
+            pair = step * unroll + item
+            row, wheres, offsets = find(low + pair, low, high)
+            keys = jnp.concatenate([held(where, 0) for where in wheres], axis=0)
+            score = jnp.dot(keys, asked[row], preferred_element_type=jnp.float32)
+            scores[pair] = score
+            best = jnp.maximum(
+                fold(jnp.max, score[:BLK]) + offsets[0], fold(jnp.max, score[BLK:]) + offsets[1]
             )
-            total = jnp.sum(total, axis=0, keepdims=True)
-            out[:, pl.ds(column, BLK)] = (summed / total).astype(jnp.bfloat16)
-            return 0
-
-        lax.fori_loop(0, per_piece, one, 0)
-
-
-def attend(factor, places, counts, queries, pieces):
+            found.append((row, best))
+        for row, best in found:
+            tops[row] = jnp.maximum(tops[row], best)
+        return 0
+
+    def gather(low, high, step, _):
+        found = []
+        for item in range(unroll):
+            pair = step * unroll + item
+            row, wheres, offsets = find(low + pair, low, high)
+            top = tops[row][:1]
+            score = scores[pair]
+            halves = [
+                jnp.exp2(score[part * BLK : (part + 1) * BLK] * factor - (top - offsets[part]))
+                for part in range(2)
+            ]
+            total = fold(jnp.sum, halves[0]) + fold(jnp.sum, halves[1])
+            weights = jnp.concatenate([half.astype(jnp.bfloat16) for half in halves], axis=0)
+            values = jnp.concatenate([held(where, 1) for where in wheres], axis=1)
+            summed = jnp.dot(values, weights, preferred_element_type=jnp.float32)
+            found.append((row, total, summed))
+        for row, total, summed in found:
+            totals[row] += total
+            sums[row] += summed
+        return 0
+
+    for index in range(len(outs)):
+        low, high = first[index * per_piece], first[(index + 1) * per_piece]
+        steps = (high - low + unroll - 1) // unroll
+        lax.fori_loop(0, steps, functools.partial(rate, low, high), 0)
+        for row in range(index * per_piece, (index + 1) * per_piece):
+            top = jnp.max(tops[row], axis=0, keepdims=True) * factor
+            tops[row] = jnp.broadcast_to(top, tops.shape[1:])
+        lax.fori_loop(0, steps, functools.partial(gather, low, high), 0)
+
+    for index, out in enumerate(outs):
+        for part in range(per_piece):
+            row = index * per_piece + part
+            total = jnp.sum(totals[row], axis=0, keepdims=True)
+            out[:, part * BLK : (part + 1) * BLK] = (sums[row] / total).astype(jnp.bfloat16)
+
+
+def pair_lists(counts, most):
+    twos = (counts + 1) // 2
+    rows = counts.shape[0]
+    order = jnp.arange(rows + 1, dtype=jnp.int32)
+    first = jnp.sum(jnp.where(order[None, :rows] < order[:, None], twos[None, :], 0), axis=1)
+    slots = jnp.arange(rows * most // 2, dtype=jnp.int32)
+    return first, jnp.sum(jnp.where(first[None, 1:] <= slots[:, None], 1, 0), axis=1)
+
+
+def attend(factor, lists, plan, arrays, count):
+    rows, most = lists[0].shape
+    pieces = most * BLK // count
+    asking = rows * BLK // count
+
     def kernel(*refs):
-        attend_kernel(factor, *refs)
-
-    shape = queries[0].shape
-    tokens = len(pieces) * shape[1]
+        attend_kernel(factor, PAIRS, plan, *refs)
+
+    shape = (BLK, count)
     return pl.pallas_call(
         kernel,
-        in_specs=[pl.BlockSpec(memory_space=pltpu.SMEM)] * 2
-        + [pl.BlockSpec(memory_space=pltpu.VMEM)] * len(queries)
-        + [pl.BlockSpec(memory_space=pl.ANY)] * len(pieces),
-        out_specs=[pl.BlockSpec(memory_space=pltpu.VMEM)] * len(queries),
-        out_shape=[jax.ShapeDtypeStruct(shape, jnp.bfloat16)] * len(queries),
+        in_specs=[pl.BlockSpec(memory_space=pltpu.SMEM)] * len(lists)
+        + [pl.BlockSpec(memory_space=pl.ANY)] * len(arrays),
+        out_specs=[pl.BlockSpec(memory_space=pltpu.VMEM)] * asking,
+        out_shape=[jax.ShapeDtypeStruct(shape, jnp.bfloat16)] * asking,
         scratch_shapes=[
-            pltpu.VMEM((len(pieces), *pieces[0].shape), jnp.bfloat16),
-            pltpu.VMEM((tokens, BLK), jnp.float32),
-            pltpu.SemaphoreType.DMA((len(pieces),)),
+            pltpu.VMEM((pieces, 2 * BLK, count), jnp.bfloat16),
+            pltpu.VMEM((asking, *shape), jnp.bfloat16),
+            pltpu.VMEM((rows, BLK, BLK), jnp.bfloat16),
+            pltpu.VMEM((rows * most // 2 // asking + PAIRS, 2 * BLK, BLK), jnp.float32),
+            pltpu.VMEM((rows, 8, BLK), jnp.float32),
+            pltpu.VMEM((rows, 8, BLK), jnp.float32),
+            pltpu.VMEM((rows, BLK, BLK), jnp.float32),
+            pltpu.SemaphoreType.DMA((len(plan),)),
         ],
-        compiler_params=pltpu.CompilerParams(vmem_limit_bytes=40 * MIB),
+        compiler_params=pltpu.CompilerParams(vmem_limit_bytes=32 * MIB),
         cost_estimate=pl.CostEstimate(
-            flops=tokens * BLK * shape[1] * len(queries),
-            bytes_accessed=4 * tokens * BLK,
-            transcendentals=tokens * shape[1],
+            flops=rows * BLK * most * BLK * BLK,
+            bytes_accessed=4 * most * BLK * BLK,
+            transcendentals=rows * BLK * most * BLK // 4,
         ),
         name="attend",
-    )(places, counts, *queries, *pieces)
+    )(*lists, *arrays)
 
 
 def leave_kernel(plan, chips, columns, *refs):
-    weights, heads, rest = refs[:4], refs[4:8], refs[8:]
+    weights, heads, rest, ordered = refs[:2], refs[2:6], refs[6:-1], refs[-1]
     step = pl.program_id(0)
+
+    @pl.when(step == 0)
+    def _():
+        for index, head in enumerate(heads):
+            ordered[pl.ds(pl.multiple_of(columns[index] * BLK, BLK), BLK), :] = head[...]
+
     summed = jnp.dot(
         jnp.concatenate([weight[...] for weight in weights], axis=1),
-        jnp.concatenate([head[...] for head in heads], axis=0),
+        ordered[...],
         preferred_element_type=jnp.float32,
     )
     adds = sum(len(given) for given, _ in plan)
@@ -275,14 +389,12 @@
                 out[...] = value.astype(out.dtype)
 
 
-def leave(chips, columns, weight, heads, plan, taken):
+def leave(chips, columns, weights, heads, plan, taken):
     high = CUTS[-1][1]
     count = heads[0].shape[1]
     steps = len(plan)
-
-    def block(index):
-        return pl.BlockSpec((high, BLK), lambda i, chips, columns: (chips[i], columns[index]))
-
+    inner = weights[0].shape[1]
+    block = pl.BlockSpec((high, inner), lambda i, chips, columns: (chips[i], 0))
     whole = lambda shape: pl.BlockSpec(shape, lambda i, *_: (0, 0))
     shapes = [(cut[1] - cut[0], count) for _, cuts in plan for cut in cuts]
 
@@ -294,26 +406,28 @@
         grid_spec=pltpu.PrefetchScalarGridSpec(
             num_scalar_prefetch=2,
             grid=(steps,),
-            in_specs=[block(i) for i in range(4)]
+            in_specs=[block] * 2
             + [whole(h.shape) for h in heads]
             + [whole(t.shape) for t in taken],
             out_specs=[whole(s) for s in shapes],
+            scratch_shapes=[pltpu.VMEM((2 * inner, count), jnp.bfloat16)],
         ),
         out_shape=[jax.ShapeDtypeStruct(s, jnp.bfloat16) for s in shapes],
-        compiler_params=pltpu.CompilerParams(vmem_limit_bytes=40 * MIB),
+        compiler_params=pltpu.CompilerParams(vmem_limit_bytes=32 * MIB),
         cost_estimate=pl.CostEstimate(
-            flops=2 * steps * high * 4 * BLK * count,
-            bytes_accessed=2 * steps * high * (4 * BLK + count),
+            flops=4 * steps * high * inner * count,
+            bytes_accessed=2 * steps * high * (2 * inner + count),
             transcendentals=0,
         ),
         name="leave",
-    )(chips, columns, *[weight] * 4, *heads, *taken)
+    )(chips, columns, *weights, *heads, *taken)
 
 
 def gather_tokens(own):
     below = shift(own, "z", 1)
     above = shift(own, "z", -1)
     beside = swap(own, "yl")
+    below, above, beside = together(below, above, beside)
     far = shift(below, "z", 1)
     beside_below = swap(below, "yl")
     beside_above = shift(beside, "z", -1)
@@ -359,11 +473,9 @@
     )
     places, xs = gather_tokens(own)
 
-    own_weight = jnp.transpose(qkv_weight, (0, 2, 1)).reshape(3 * inner, features)
+    own_weight, gain, bias, leaving = prepare(qkv_weight, out_weight, modulation, own)
     other_weight = swap(own_weight, "core")
-    gain = jnp.broadcast_to((1.0 + modulation[1])[:, None], (features, BLK))
-    bias = jnp.broadcast_to(modulation[0][:, None], (features, BLK))
-    leaving = jnp.concatenate([out_weight, swap(out_weight, "core")], axis=0).T
+    leaving = leaving, swap(leaving, "core")
 
     mask_mine, mask_given = mine_and_given(block_mask, 1)
     mask_heads = jnp.stack([mask_mine, swap(mask_given, "core")])
@@ -391,16 +503,25 @@
     chips = jnp.stack([chip(*place) for place in places]).astype(jnp.int32)
     slots = [head_slot(steps) for steps in range(4)]
     bases = jnp.stack([side * 3 * heads_here + slot for side, slot in slots]).astype(jnp.int32)
-    made = project(chips, bases, xs, own_weight, other_weight, gain, bias)
-    order = (0, 1, 3, 2)
-    kv = {0: made[0]}
-    for steps in order[1:]:
-        kv[steps] = shift(made[2 * steps], "x", steps)
-    queries = [made[1]] + [shift(made[2 * steps + 1], "x", steps) for steps in (1, 2, 3)]
-    away = {steps: swap(kv[steps], "yh") for steps in order}
-    pieces = [kv[i] for i in range(4)] + [away[i] for i in range(4)]
-    pieces += [swap(p, "core") for p in pieces]
-    heads = attend(factor, listed, counts, queries, pieces)
+    lists = (listed, counts, *pair_lists(counts, listed.shape[1]))
+    kv, query, *packed = project(
+        chips, bases, xs, own_weight, other_weight, gain, bias, (*lists, leaving[1])
+    )
+    two, one, three = [shift(packed[i - 1], "x", i) for i in (2, 1, 3)]
+    both = jnp.concatenate([one[: 2 * BLK], three[: 2 * BLK]], axis=0)
+    last = two[: 2 * BLK]
+    away = [swap(part, "yh") for part in (kv, both, last)]
+    near = jnp.concatenate([kv, both, last], axis=0)
+    arrays = [kv, query, one, two, three, *away, swap(near, "core"), *[swap(a, "core") for a in away]]
+    step = 2 * BLK
+    plan = [("kv", 0, 0, 0), ("q", 0, 1, 0)]
+    for steps, array in ((1, 2), (2, 3), (3, 4)):
+        plan += [("kv", steps, array, 0), ("q", steps, array, step)]
+    for index, array in ((4, 5), (12, 9)):
+        plan += [("kv", index, array, 0), ("kv", index + 1, array + 1, 0)]
+        plan += [("kv", index + 3, array + 1, step), ("kv", index + 2, array + 2, 0)]
+    plan += [("kv", 8 + steps, 8, at * step) for at, steps in enumerate((0, 1, 3, 2))]
+    heads = attend(factor, lists, plan, arrays, half)
     heads = [heads[0]] + [shift(heads[steps], "x", -steps) for steps in (1, 2, 3)]
 
     columns = jnp.stack([side * heads_here + slot for side, slot in slots]).astype(jnp.int32)

time: 263 us -> 238 us (0.905); the launches traced: 259 us -> 237 us
  waiting for transfers between devices: 101 us -> 87.2 us
  local copies, waits for them, and re-layouts: 25.6 us -> 14.6 us
  Pallas kernels: 51.5 us -> 54.6 us
    ppermute x47 -> x39, waiting for transfers between devices: 101 us -> 87.2 us  [shift(): lax.ppermute(value, axis, [(i, (i + steps) % count) for i in range(count)])]
    transpose x1 -> x0, local copies, waits for them, and re-layouts: 10.4 us -> none  [shards(): jnp.transpose(qkv_weight, (0, 2, 1)).reshape(3 * inner, features)]
    pallas_call x0 -> x2, Pallas kernels: none -> 7.52 us  [the longest x1 7.52 us: prepare(): pl.pallas_call(prepare_kernel, grid=(features // deep,), in_specs=[pl.Blo...]
    pallas_call x1, Pallas kernels: 20.4 us -> 12.9 us  [attend(): pl.pallas_call(kernel, in_specs=[pl.BlockSpec(memory_space=pltpu.SMEM)] *...]
    broadcast_in_dim x2 -> x0, local copies, waits for them, and re-layouts: 6.43 us -> none  [the longest x1 3.22 us: shards(): bias = jnp.broadcast_to(modulation[0][:, None], (features, BLK))]
    unnamed x23 -> x38, local copies, waits for them, and re-layouts: 7.78 us -> 12.4 us
    pallas_call x4, Pallas kernels: 9.11 us -> 13.6 us  [leave(): pl.pallas_call(kernel, grid_spec=pltpu.PrefetchScalarGridSpec(num_scalar_...]
    ppermute x47 -> x39, starting transfers between devices: 74 us -> 75.7 us  [shift(): lax.ppermute(value, axis, [(i, (i + steps) % count) for i in range(count)])]
  transfers between devices with their start and end apart: 47 -> 39, of which waited for: 25 -> 21; matrix products, arithmetic and copies ran while one was open for 6% -> 1% of each run, Pallas kernels for 16% -> 0%
where the time goes in v3:
time: 238 us; the launch traced here: 237 us
  waiting for transfers between devices  87.2 us (37%)
  starting transfers between devices  75.7 us (32%)
  Pallas kernels  54.6 us (23%)
  local copies, waits for them, and re-layouts  14.6 us (6%)
  other arithmetic  4.46 us (2%)
    ppermute x39, waiting for transfers between devices, shift(): lax.ppermute(value, axis, [(i, (i + steps) % count) for i in range(count)])  87.2 us
    ppermute x39, starting transfers between devices, shift(): lax.ppermute(value, axis, [(i, (i + steps) % count) for i in range(count)])  75.7 us
    pallas_call x1, Pallas kernels, project(): pl.pallas_call(project_kernel, grid_spec=pltpu.PrefetchScalarGridSpec(num...  20.6 us
    pallas_call x4, Pallas kernels, leave(): pl.pallas_call(kernel, grid_spec=pltpu.PrefetchScalarGridSpec(num_scalar_...  13.6 us
    pallas_call x1, Pallas kernels, attend(): pl.pallas_call(kernel, in_specs=[pl.BlockSpec(memory_space=pltpu.SMEM)] *...  12.9 us
    unnamed x38, local copies, waits for them, and re-layouts  12.4 us
    pallas_call x1, Pallas kernels, prepare(): pl.pallas_call(prepare_kernel, grid=(features // deep,), in_specs=[pl.Blo...  7.52 us
  transfers between devices with their start and end apart: 39, of which 21 were waited for; matrix products, arithmetic and copies ran while one was open for 1% of the time, Pallas kernels for 0%

profile of v3, /device:TPU:1, one launch (start us, length us, event | category | flops | bytes accessed | tf_op | source)
XLA Modules:
  0.0 237.1 jit_solution(8116876738712395005)
XLA Ops:
  5.1 3.2 %copy-done.2 = bf16[3,5120,256]{2,1,0:T(8,128)(2,1)S(1)} copy-done((bf16[3,5120,256]{2,1,0:T(8,128)(2,1)S(1)}, bf16[3,5120,256]{2,1,0:T(8,128)(2,1)}, u32[]{:S(2)}) %copy-start.2) | copy-done | bytes 7864344
  8.3 7.5 %prepare.1 = (bf16[768,5120]{1,0:T(8,128)(2,1)}, f32[5120,128]{1,0:T(8,128)S(1)}, f32[5120,128]{1,0:T(8,128)S(1)}, bf16[5120,256]{1,0:T(8,128)(2,1)}) custom-call(bf16[3,5120,256]{2,1,0:T(8,128)(2,1)S(1)} %copy-done.2, bf16[256,5120]{1,0:T(8,128)(2,1)S(1)} %copy-done.5, f32[3,5120]{1,0:T(4,128)S(1)} %copy-done.12, ...), custom_call_target="tpu_custom_call" | custom-call | bytes 20971520 | tf_op jit(solution)/shard_map/prepare/pallas_call | solution.py:53
  20.0 8.9 %collective-permute-done.2 = s32[2,4,64]{2,1,0:T(4,128)S(1)} collective-permute-done((s32[2,4,64]{2,1,0:T(4,128)S(1)}, s32[2,4,64]{2,1,0:T(4,128)S(1)}, u32[]{:S(2)}, u32[]{:S(2)}) %collective-permute-start.2) | collective-permute-done | bytes 2080 | tf_op jit(solution)/shard_map/ppermute | solution.py:27
  30.3 2.5 %collective-permute-start.4 = (s32[4,64]{1,0:T(4,128)S(1)}, s32[4,64]{1,0:T(4,128)S(1)}, u32[]{:S(2)}, u32[]{:S(2)}) collective-permute-start(s32[4,64]{1,0:T(4,128)S(1)} %get-tuple-element.63), channel_id=1, source_target_pairs={{0,32},{16,48},{32,0},{48,16},{1,33},{17,49},{33,1},{49,17},{2,34}... | collective-permute-start | bytes 3080 | tf_op jit(solution)/shard_map/ppermute | solution.py:27
  35.4 3.8 %collective-permute-start.7 = (bf16[640,512]{1,0:T(8,128)(2,1)S(1)}, bf16[640,512]{1,0:T(8,128)(2,1)S(1)}, u32[]{:S(2)}, u32[]{:S(2)}) collective-permute-start(bf16[640,512]{1,0:T(8,128)(2,1)S(1)} %pad_maximum_fusion.1._.refs_0_), channel_id=1, source_target_pairs={{0,6},{2,0},{4,2},{6,4},{1,7},{3,1},{5,3},{7,5},{8,14},{10,8},{12,... | collective-permute-start | bytes 1966088 | tf_op jit(solution)/shard_map/ppermute | solution.py:27
  40.0 9.2 %collective-permute-done.8.refs_2_ = bf16[640,512]{1,0:T(8,128)(2,1)} collective-permute-done((bf16[640,512]{1,0:T(8,128)(2,1)S(1)}, bf16[640,512]{1,0:T(8,128)(2,1)}, u32[]{:S(2)}, u32[]{:S(2)}) %collective-permute-start.8) | collective-permute-done | bytes 655392 | tf_op jit(solution)/shard_map/ppermute | solution.py:27
  49.2 2.5 %collective-permute-done.7.refs_1_ = bf16[640,512]{1,0:T(8,128)(2,1)S(1)} collective-permute-done((bf16[640,512]{1,0:T(8,128)(2,1)S(1)}, bf16[640,512]{1,0:T(8,128)(2,1)S(1)}, u32[]{:S(2)}, u32[]{:S(2)}) %collective-permute-start.7) | collective-permute-done | bytes 655392 | tf_op jit(solution)/shard_map/ppermute | solution.py:27
  54.9 2.7 %collective-permute-start.11 = (bf16[640,512]{1,0:T(8,128)(2,1)}, bf16[640,512]{1,0:T(8,128)(2,1)S(1)}, u32[]{:S(2)}, u32[]{:S(2)}) collective-permute-start(bf16[640,512]{1,0:T(8,128)(2,1)} %get-tuple-element.33.refs_3_), channel_id=1, source_target_pairs={{0,6},{2,0},{4,2},{6,4},{1,7},{3,1},{5,3},{7,5},{8,14},{10,8},{12,... | collective-permute-start | bytes 1966088 | tf_op jit(solution)/shard_map/ppermute | solution.py:27
  58.1 10.4 %collective-permute-done.11.refs_6_ = bf16[640,512]{1,0:T(8,128)(2,1)S(1)} collective-permute-done((bf16[640,512]{1,0:T(8,128)(2,1)}, bf16[640,512]{1,0:T(8,128)(2,1)S(1)}, u32[]{:S(2)}, u32[]{:S(2)}) %collective-permute-start.11) | collective-permute-done | bytes 655392 | tf_op jit(solution)/shard_map/ppermute | solution.py:27
  68.5 3.4 %collective-permute-start.13 = (bf16[208,512]{1,0:T(8,128)(2,1)S(1)}, bf16[208,512]{1,0:T(8,128)(2,1)S(1)}, u32[]{:S(2)}, u32[]{:S(2)}) collective-permute-start(bf16[208,512]{1,0:T(8,128)(2,1)S(1)} %slice.37), channel_id=1, source_target_pairs={{0,6},{2,0},{4,2},{6,4},{1,7},{3,1},{5,3},{7,5},{8,14},{10,8},{12,... | collective-permute-start | bytes 638984 | tf_op jit(solution)/shard_map/ppermute | solution.py:27
  74.7 3.2 %collective-permute-done.14.refs_9_ = bf16[208,512]{1,0:T(8,128)(2,1)S(1)} collective-permute-done((bf16[208,512]{1,0:T(8,128)(2,1)S(1)}, bf16[208,512]{1,0:T(8,128)(2,1)S(1)}, u32[]{:S(2)}, u32[]{:S(2)}) %collective-permute-start.14) | collective-permute-done | bytes 213024 | tf_op jit(solution)/shard_map/ppermute | solution.py:27
  79.4 20.6 %project.1 = (bf16[256,512]{1,0:T(8,128)(2,1)S(1)}, bf16[128,512]{1,0:T(8,128)(2,1)S(1)}, bf16[384,512]{1,0:T(8,128)(2,1)S(1)}, bf16[384,512]{1,0:T(8,128)(2,1)S(1)}, bf16[384,512]{1,0:T(8,128)(2,1)S(1)}) custom-call(s32[8]{0:T(128)S(1)} %stack.96.chips, s32[4]{0:T(128)S(1)} %pad_add_fusion.1.heads, bf16[640,512]{1,0:T(8,128)(2,1)S(1)} %pad_maximum_fusion.1._.refs_0_, ...), custom_call_target="tpu_custom_call" | custom-call | flops 8053063680 | bytes 20971520 | tf_op jit(solution)/shard_map/project/pallas_call | solution.py:184
  103.7 7.2 %collective-permute-done.16.refs_6_ = bf16[384,512]{1,0:T(8,128)(2,1)S(1)} collective-permute-done((bf16[384,512]{1,0:T(8,128)(2,1)S(1)}, bf16[384,512]{1,0:T(8,128)(2,1)S(1)}, u32[]{:S(2)}, u32[]{:S(2)}) %collective-permute-start.16) | collective-permute-done | bytes 393248 | tf_op jit(solution)/shard_map/ppermute | solution.py:27
  111.1 4.7 %collective-permute-start.20 = (bf16[512,512]{1,0:T(8,128)(2,1)S(1)}, bf16[512,512]{1,0:T(8,128)(2,1)S(1)}, u32[]{:S(2)}, u32[]{:S(2)}) collective-permute-start(bf16[512,512]{1,0:T(8,128)(2,1)S(1)} %pad_maximum_fusion.2), channel_id=1, source_target_pairs={{0,64},{64,0},{1,65},{65,1},{2,66},{66,2},{3,67},{67,3},{4,68},{68... | collective-permute-start | bytes 1572872 | tf_op jit(solution)/shard_map/ppermute | solution.py:27
  115.9 9.2 %collective-permute-start.22 = (bf16[1024,512]{1,0:T(8,128)(2,1)S(1)}, bf16[1024,512]{1,0:T(8,128)(2,1)S(1)}, u32[]{:S(2)}, u32[]{:S(2)}) collective-permute-start(bf16[1024,512]{1,0:T(8,128)(2,1)S(1)} %pad_maximum_fusion), channel_id=1, source_target_pairs={{0,1},{1,0},{2,3},{3,2},{4,5},{5,4},{6,7},{7,6},{8,9},{9,8},{10,11... | collective-permute-start | bytes 3145736 | tf_op jit(solution)/shard_map/ppermute | solution.py:27
  125.1 3.0 %collective-permute-start.21 = (bf16[256,512]{1,0:T(8,128)(2,1)S(1)}, bf16[256,512]{1,0:T(8,128)(2,1)S(1)}, u32[]{:S(2)}, u32[]{:S(2)}) collective-permute-start(bf16[256,512]{1,0:T(8,128)(2,1)S(1)} %slice.41), channel_id=1, source_target_pairs={{0,64},{64,0},{1,65},{65,1},{2,66},{66,2},{3,67},{67,3},{4,68},{68... | collective-permute-start | bytes 786440 | tf_op jit(solution)/shard_map/ppermute | solution.py:27
  128.1 9.1 %collective-permute-start.24 = (bf16[512,512]{1,0:T(8,128)(2,1)S(1)}, bf16[512,512]{1,0:T(8,128)(2,1)S(1)}, u32[]{:S(2)}, u32[]{:S(2)}) collective-permute-start(bf16[512,512]{1,0:T(8,128)(2,1)S(1)} %collective-permute-done.20.refs_10_), channel_id=1, source_target_pairs={{0,1},{1,0},{2,3},{3,2},{4,5},{5,4},{6,7},{7,6},{8,9},{9,8},{10,11... | collective-permute-start | bytes 1572872 | tf_op jit(solution)/shard_map/ppermute | solution.py:27
  137.3 2.8 %collective-permute-start.23 = (bf16[256,512]{1,0:T(8,128)(2,1)S(1)}, bf16[256,512]{1,0:T(8,128)(2,1)S(1)}, u32[]{:S(2)}, u32[]{:S(2)}) collective-permute-start(bf16[256,512]{1,0:T(8,128)(2,1)S(1)} %collective-permute-done.19.refs_9_), channel_id=1, source_target_pairs={{0,1},{1,0},{2,3},{3,2},{4,5},{5,4},{6,7},{7,6},{8,9},{9,8},{10,11... | collective-permute-start | bytes 786440 | tf_op jit(solution)/shard_map/ppermute | solution.py:27
  140.7 2.7 %collective-permute-start.25 = (bf16[256,512]{1,0:T(8,128)(2,1)S(1)}, bf16[256,512]{1,0:T(8,128)(2,1)S(1)}, u32[]{:S(2)}, u32[]{:S(2)}) collective-permute-start(bf16[256,512]{1,0:T(8,128)(2,1)S(1)} %collective-permute-done.21.refs_11_), channel_id=1, source_target_pairs={{0,1},{1,0},{2,3},{3,2},{4,5},{5,4},{6,7},{7,6},{8,9},{9,8},{10,11... | collective-permute-start | bytes 786440 | tf_op jit(solution)/shard_map/ppermute | solution.py:27
  144.5 12.9 %attend.1 = (bf16[128,512]{1,0:T(8,128)(2,1)S(1)}, bf16[128,512]{1,0:T(8,128)(2,1)}, bf16[128,512]{1,0:T(8,128)(2,1)}, bf16[128,512]{1,0:T(8,128)(2,1)}) custom-call(s32[16,64]{1,0:T(8,128)S(1)} %select_reduce_fusion.2.refs_16_.refs_0_, s32[16]{0:T(128)S(1)} %get-tuple-element.55.refs_17_.refs_1_, s32[17]{0:T(128)S(1)} %select_reduce_fusion.5.refs_18_.refs_2_, ...), custom_call_target="tpu_custom_call" | custom-call | flops 2147483648 | bytes 4194304 | tf_op jit(solution)/shard_map/attend/pallas_call | solution.py:324
  159.1 4.0 %collective-permute-done.26.refs_5_ = bf16[128,512]{1,0:T(8,128)(2,1)S(1)} collective-permute-done((bf16[128,512]{1,0:T(8,128)(2,1)}, bf16[128,512]{1,0:T(8,128)(2,1)S(1)}, u32[]{:S(2)}, u32[]{:S(2)}) %collective-permute-start.26) | collective-permute-done | bytes 131104 | tf_op jit(solution)/shard_map/ppermute | solution.py:27
  164.2 3.4 %collective-permute-done.28.refs_7_ = bf16[128,512]{1,0:T(8,128)(2,1)S(1)} collective-permute-done((bf16[128,512]{1,0:T(8,128)(2,1)}, bf16[128,512]{1,0:T(8,128)(2,1)S(1)}, u32[]{:S(2)}, u32[]{:S(2)}) %collective-permute-start.28) | collective-permute-done | bytes 131104 | tf_op jit(solution)/shard_map/ppermute | solution.py:27
  169.7 2.9 %collective-permute-start.29 = (bf16[224,512]{1,0:T(8,128)(2,1)S(1)}, bf16[224,512]{1,0:T(8,128)(2,1)S(1)}, u32[]{:S(2)}, u32[]{:S(2)}) collective-permute-start(bf16[224,512]{1,0:T(8,128)(2,1)S(1)} %get-tuple-element.46), channel_id=1, source_target_pairs={{0,8},{8,0},{1,9},{9,1},{2,10},{10,2},{3,11},{11,3},{4,12},{12,4},... | collective-permute-start | bytes 688136 | tf_op jit(solution)/shard_map/ppermute | solution.py:27
  172.6 6.0 %collective-permute-start.31 = (bf16[208,512]{1,0:T(8,128)(2,1)S(1)}, bf16[208,512]{1,0:T(8,128)(2,1)S(1)}, u32[]{:S(2)}, u32[]{:S(2)}) collective-permute-start(bf16[208,512]{1,0:T(8,128)(2,1)S(1)} %get-tuple-element.48), channel_id=1, source_target_pairs={{0,6},{2,0},{4,2},{6,4},{1,7},{3,1},{5,3},{7,5},{8,14},{10,8},{12,... | collective-permute-start | bytes 638984 | tf_op jit(solution)/shard_map/ppermute | solution.py:27
  178.6 4.4 %collective-permute-done.30.refs_9_ = bf16[208,512]{1,0:T(8,128)(2,1)S(1)} collective-permute-done((bf16[208,512]{1,0:T(8,128)(2,1)S(1)}, bf16[208,512]{1,0:T(8,128)(2,1)S(1)}, u32[]{:S(2)}, u32[]{:S(2)}) %collective-permute-start.30) | collective-permute-done | bytes 213024 | tf_op jit(solution)/shard_map/ppermute | solution.py:27
  183.0 3.8 %leave.5 = (bf16[640,512]{1,0:T(8,128)(2,1)S(1)}, bf16[640,512]{1,0:T(8,128)(2,1)S(1)}, bf16[640,512]{1,0:T(8,128)(2,1)S(1)}) custom-call(s32[3]{0:T(128)S(1)} %pad_add_fusion.3.refs_0_, s32[4]{0:T(128)S(1)} %pad_add_fusion.refs_1_, bf16[5120,256]{1,0:T(8,128)(2,1)} %get-tuple-element.30.refs_2_, bf16[5120,256]{1,0:T(8,128)(2,1)S(1)} %copy-done.1, ...), custom_call_target="tpu_custom_call" | custom-call | flops 1006632960 | bytes 3932160 | tf_op jit(solution)/shard_map/leave/pallas_call | solution.py:404
  186.8 2.4 %collective-permute-start.32 = (bf16[640,512]{1,0:T(8,128)(2,1)S(1)}, bf16[640,512]{1,0:T(8,128)(2,1)S(1)}, u32[]{:S(2)}, u32[]{:S(2)}) collective-permute-start(bf16[640,512]{1,0:T(8,128)(2,1)S(1)} %get-tuple-element.49), channel_id=1, source_target_pairs={{0,6},{2,0},{4,2},{6,4},{1,7},{3,1},{5,3},{7,5},{8,14},{10,8},{12,... | collective-permute-start | bytes 1966088 | tf_op jit(solution)/shard_map/ppermute | solution.py:27
  189.8 11.5 %collective-permute-done.32.refs_8_ = bf16[640,512]{1,0:T(8,128)(2,1)S(1)} collective-permute-done((bf16[640,512]{1,0:T(8,128)(2,1)S(1)}, bf16[640,512]{1,0:T(8,128)(2,1)S(1)}, u32[]{:S(2)}, u32[]{:S(2)}) %collective-permute-start.32) | collective-permute-done | bytes 655392 | tf_op jit(solution)/shard_map/ppermute | solution.py:27
  204.8 5.2 %leave.6 = (bf16[640,512]{1,0:T(8,128)(2,1)}, bf16[640,512]{1,0:T(8,128)(2,1)}, bf16[640,512]{1,0:T(8,128)(2,1)}) custom-call(s32[3]{0:T(128)S(1)} %pad_add_fusion.2.refs_0_, s32[4]{0:T(128)S(1)} %pad_add_fusion.refs_1_, bf16[5120,256]{1,0:T(8,128)(2,1)} %get-tuple-element.30.refs_2_, bf16[5120,256]{1,0:T(8,128)(2,1)S(1)} %copy-done.1, ...), custom_call_target="tpu_custom_call" | custom-call | flops 1006632960 | bytes 3932160 | tf_op jit(solution)/shard_map/leave/pallas_call | solution.py:404
  212.2 11.1 %collective-permute-done.35.refs_8_ = bf16[640,512]{1,0:T(8,128)(2,1)S(1)} collective-permute-done((bf16[640,512]{1,0:T(8,128)(2,1)}, bf16[640,512]{1,0:T(8,128)(2,1)S(1)}, u32[]{:S(2)}, u32[]{:S(2)}) %collective-permute-start.35) | collective-permute-done | bytes 655392 | tf_op jit(solution)/shard_map/ppermute | solution.py:27
  227.4 2.6 %leave.7 = bf16[640,512]{1,0:T(8,128)(2,1)S(1)} custom-call(s32[1]{0:T(128)} %bitcast.1.refs_0_, s32[4]{0:T(128)S(1)} %pad_add_fusion.refs_1_, bf16[5120,256]{1,0:T(8,128)(2,1)} %get-tuple-element.30.refs_2_, bf16[5120,256]{1,0:T(8,128)(2,1)S(1)} %copy-done.1, bf16[128,512]{1,0:T(8,128)(2,1)S(1)} %get-tuple-element.42.refs_4_, ...), custom_call_target="tpu_custom_call" | custom-call | flops 335544320 | bytes 1310720 | tf_op jit(solution)/shard_map/leave/pallas_call | solution.py:404
  230.0 4.5 %collective-permute-start.38 = (bf16[320,512]{1,0:T(8,128)(2,1)S(1)}, bf16[320,512]{1,0:T(8,128)(2,1)S(1)}, u32[]{:S(2)}, u32[]{:S(2)}) collective-permute-start(bf16[320,512]{1,0:T(8,128)(2,1)S(1)} %constant_dynamic-slice_fusion), channel_id=1, source_target_pairs={{0,1},{1,0},{2,3},{3,2},{4,5},{5,4},{6,7},{7,6},{8,9},{9,8},{10,11... | collective-permute-start | bytes 983048 | tf_op jit(solution)/shard_map/ppermute | solution.py:27
  (127 shorter events, 45.4 us)
Async XLA Ops:
  18.9 59.0 %collective-permute-start.15 = (bf16[768,5120]{1,0:T(8,128)(2,1)}, bf16[768,5120]{1,0:T(8,128)(2,1)}, u32[]{:S(2)}, u32[]{:S(2)}) collective-permute-start(bf16[768,5120]{1,0:T(8,128)(2,1)} %get-tuple-element.34.refs_10_.refs_11_), channel_id=1, source_target_pairs={{0,1},{1,0},{2,3},{3,2},{4,5},{5,4},{6,7},{7,6},{8,9},{9,8},{10,11... | collective-permute-start | bytes 23592968 | tf_op jit(solution)/shard_map/ppermute | solution.py:27
  19.2 58.6 %collective-permute-start.1 = (bf16[5120,256]{1,0:T(8,128)(2,1)}, bf16[5120,256]{1,0:T(8,128)(2,1)S(1)}, u32[]{:S(2)}, u32[]{:S(2)}) collective-permute-start(bf16[5120,256]{1,0:T(8,128)(2,1)} %get-tuple-element.30.refs_2_), channel_id=1, source_target_pairs={{0,1},{1,0},{2,3},{3,2},{4,5},{5,4},{6,7},{7,6},{8,9},{9,8},{10,11... | collective-permute-start | bytes 7864328 | tf_op jit(solution)/shard_map/ppermute | solution.py:27
  19.4 9.5 %collective-permute-start.2 = (s32[2,4,64]{2,1,0:T(4,128)S(1)}, s32[2,4,64]{2,1,0:T(4,128)S(1)}, u32[]{:S(2)}, u32[]{:S(2)}) collective-permute-start(s32[2,4,64]{2,1,0:T(4,128)S(1)} %get-tuple-element.65), channel_id=1, source_target_pairs={{0,1},{1,0},{2,3},{3,2},{4,5},{5,4},{6,7},{7,6},{8,9},{9,8},{10,11... | collective-permute-start | bytes 6152 | tf_op jit(solution)/shard_map/ppermute | solution.py:27
  32.7 6.4 %collective-permute-start.5 = (s32[4,64]{1,0:T(4,128)S(1)}, s32[4,64]{1,0:T(4,128)S(1)}, u32[]{:S(2)}, u32[]{:S(2)}) collective-permute-start(s32[4,64]{1,0:T(4,128)S(1)} %get-tuple-element.64), channel_id=1, source_target_pairs={{0,48},{16,0},{32,16},{48,32},{1,49},{17,1},{33,17},{49,33},{2,50}... | collective-permute-start | bytes 3080 | tf_op jit(solution)/shard_map/ppermute | solution.py:27
  34.0 15.2 %collective-permute-start.8 = (bf16[640,512]{1,0:T(8,128)(2,1)S(1)}, bf16[640,512]{1,0:T(8,128)(2,1)}, u32[]{:S(2)}, u32[]{:S(2)}) collective-permute-start(bf16[640,512]{1,0:T(8,128)(2,1)S(1)} %pad_maximum_fusion.1._.refs_0_), channel_id=1, source_target_pairs={{0,8},{8,0},{1,9},{9,1},{2,10},{10,2},{3,11},{11,3},{4,12},{12,4},... | collective-permute-start | bytes 1966088 | tf_op jit(solution)/shard_map/ppermute | solution.py:27
  35.4 16.3 %collective-permute-start.7 = (bf16[640,512]{1,0:T(8,128)(2,1)S(1)}, bf16[640,512]{1,0:T(8,128)(2,1)S(1)}, u32[]{:S(2)}, u32[]{:S(2)}) collective-permute-start(bf16[640,512]{1,0:T(8,128)(2,1)S(1)} %pad_maximum_fusion.1._.refs_0_), channel_id=1, source_target_pairs={{0,6},{2,0},{4,2},{6,4},{1,7},{3,1},{5,3},{7,5},{8,14},{10,8},{12,... | collective-permute-start | bytes 1966088 | tf_op jit(solution)/shard_map/ppermute | solution.py:27
  39.1 15.8 %collective-permute-start.6 = (bf16[640,512]{1,0:T(8,128)(2,1)S(1)}, bf16[640,512]{1,0:T(8,128)(2,1)}, u32[]{:S(2)}, u32[]{:S(2)}) collective-permute-start(bf16[640,512]{1,0:T(8,128)(2,1)S(1)} %pad_maximum_fusion.1._.refs_0_), channel_id=1, source_target_pairs={{0,2},{2,4},{4,6},{6,0},{1,3},{3,5},{5,7},{7,1},{8,10},{10,12},{12... | collective-permute-start | bytes 1966088 | tf_op jit(solution)/shard_map/ppermute | solution.py:27
  54.9 17.0 %collective-permute-start.10 = (bf16[640,512]{1,0:T(8,128)(2,1)}, bf16[640,512]{1,0:T(8,128)(2,1)S(1)}, u32[]{:S(2)}, u32[]{:S(2)}) collective-permute-start(bf16[640,512]{1,0:T(8,128)(2,1)} %get-tuple-element.31.refs_1_), channel_id=1, source_target_pairs={{0,8},{8,0},{1,9},{9,1},{2,10},{10,2},{3,11},{11,3},{4,12},{12,4},... | collective-permute-start | bytes 1966088 | tf_op jit(solution)/shard_map/ppermute | solution.py:27
  54.9 17.1 %collective-permute-start.9 = (bf16[640,512]{1,0:T(8,128)(2,1)}, bf16[640,512]{1,0:T(8,128)(2,1)S(1)}, u32[]{:S(2)}, u32[]{:S(2)}) collective-permute-start(bf16[640,512]{1,0:T(8,128)(2,1)} %get-tuple-element.31.refs_1_), channel_id=1, source_target_pairs={{0,2},{2,4},{4,6},{6,0},{1,3},{3,5},{5,7},{7,1},{8,10},{10,12},{12... | collective-permute-start | bytes 1966088 | tf_op jit(solution)/shard_map/ppermute | solution.py:27
  54.9 13.6 %collective-permute-start.11 = (bf16[640,512]{1,0:T(8,128)(2,1)}, bf16[640,512]{1,0:T(8,128)(2,1)S(1)}, u32[]{:S(2)}, u32[]{:S(2)}) collective-permute-start(bf16[640,512]{1,0:T(8,128)(2,1)} %get-tuple-element.33.refs_3_), channel_id=1, source_target_pairs={{0,6},{2,0},{4,2},{6,4},{1,7},{3,1},{5,3},{7,5},{8,14},{10,8},{12,... | collective-permute-start | bytes 1966088 | tf_op jit(solution)/shard_map/ppermute | solution.py:27
  68.5 6.2 %collective-permute-start.13 = (bf16[208,512]{1,0:T(8,128)(2,1)S(1)}, bf16[208,512]{1,0:T(8,128)(2,1)S(1)}, u32[]{:S(2)}, u32[]{:S(2)}) collective-permute-start(bf16[208,512]{1,0:T(8,128)(2,1)S(1)} %slice.37), channel_id=1, source_target_pairs={{0,6},{2,0},{4,2},{6,4},{1,7},{3,1},{5,3},{7,5},{8,14},{10,8},{12,... | collective-permute-start | bytes 638984 | tf_op jit(solution)/shard_map/ppermute | solution.py:27
  71.9 6.0 %collective-permute-start.14 = (bf16[208,512]{1,0:T(8,128)(2,1)S(1)}, bf16[208,512]{1,0:T(8,128)(2,1)S(1)}, u32[]{:S(2)}, u32[]{:S(2)}) collective-permute-start(bf16[208,512]{1,0:T(8,128)(2,1)S(1)} %slice.38), channel_id=1, source_target_pairs={{0,2},{2,4},{4,6},{6,0},{1,3},{3,5},{5,7},{7,1},{8,10},{10,12},{12... | collective-permute-start | bytes 638984 | tf_op jit(solution)/shard_map/ppermute | solution.py:27
  100.0 10.9 %collective-permute-start.16 = (bf16[384,512]{1,0:T(8,128)(2,1)S(1)}, bf16[384,512]{1,0:T(8,128)(2,1)S(1)}, u32[]{:S(2)}, u32[]{:S(2)}) collective-permute-start(bf16[384,512]{1,0:T(8,128)(2,1)S(1)} %get-tuple-element.39), channel_id=1, source_target_pairs={{0,16},{16,32},{32,48},{48,0},{1,17},{17,33},{33,49},{49,1},{2,18}... | collective-permute-start | bytes 1179656 | tf_op jit(solution)/shard_map/ppermute | solution.py:27
  101.0 10.0 %collective-permute-start.18 = (bf16[384,512]{1,0:T(8,128)(2,1)S(1)}, bf16[384,512]{1,0:T(8,128)(2,1)S(1)}, u32[]{:S(2)}, u32[]{:S(2)}) collective-permute-start(bf16[384,512]{1,0:T(8,128)(2,1)S(1)} %get-tuple-element.41), channel_id=1, source_target_pairs={{0,48},{16,0},{32,16},{48,32},{1,49},{17,1},{33,17},{49,33},{2,50}... | collective-permute-start | bytes 1179656 | tf_op jit(solution)/shard_map/ppermute | solution.py:27
  102.8 13.0 %collective-permute-start.17 = (bf16[384,512]{1,0:T(8,128)(2,1)S(1)}, bf16[384,512]{1,0:T(8,128)(2,1)S(1)}, u32[]{:S(2)}, u32[]{:S(2)}) collective-permute-start(bf16[384,512]{1,0:T(8,128)(2,1)S(1)} %get-tuple-element.40), channel_id=1, source_target_pairs={{0,32},{16,48},{32,0},{48,16},{1,33},{17,49},{33,1},{49,17},{2,34}... | collective-permute-start | bytes 1179656 | tf_op jit(solution)/shard_map/ppermute | solution.py:27
  111.1 17.1 %collective-permute-start.20 = (bf16[512,512]{1,0:T(8,128)(2,1)S(1)}, bf16[512,512]{1,0:T(8,128)(2,1)S(1)}, u32[]{:S(2)}, u32[]{:S(2)}) collective-permute-start(bf16[512,512]{1,0:T(8,128)(2,1)S(1)} %pad_maximum_fusion.2), channel_id=1, source_target_pairs={{0,64},{64,0},{1,65},{65,1},{2,66},{66,2},{3,67},{67,3},{4,68},{68... | collective-permute-start | bytes 1572872 | tf_op jit(solution)/shard_map/ppermute | solution.py:27
  115.9 28.6 %collective-permute-start.22 = (bf16[1024,512]{1,0:T(8,128)(2,1)S(1)}, bf16[1024,512]{1,0:T(8,128)(2,1)S(1)}, u32[]{:S(2)}, u32[]{:S(2)}) collective-permute-start(bf16[1024,512]{1,0:T(8,128)(2,1)S(1)} %pad_maximum_fusion), channel_id=1, source_target_pairs={{0,1},{1,0},{2,3},{3,2},{4,5},{5,4},{6,7},{7,6},{8,9},{9,8},{10,11... | collective-permute-start | bytes 3145736 | tf_op jit(solution)/shard_map/ppermute | solution.py:27
  125.1 12.1 %collective-permute-start.19 = (bf16[256,512]{1,0:T(8,128)(2,1)S(1)}, bf16[256,512]{1,0:T(8,128)(2,1)S(1)}, u32[]{:S(2)}, u32[]{:S(2)}) collective-permute-start(bf16[256,512]{1,0:T(8,128)(2,1)S(1)} %get-tuple-element.37.refs_4_), channel_id=1, source_target_pairs={{0,64},{64,0},{1,65},{65,1},{2,66},{66,2},{3,67},{67,3},{4,68},{68... | collective-permute-start | bytes 786440 | tf_op jit(solution)/shard_map/ppermute | solution.py:27
  125.1 15.5 %collective-permute-start.21 = (bf16[256,512]{1,0:T(8,128)(2,1)S(1)}, bf16[256,512]{1,0:T(8,128)(2,1)S(1)}, u32[]{:S(2)}, u32[]{:S(2)}) collective-permute-start(bf16[256,512]{1,0:T(8,128)(2,1)S(1)} %slice.41), channel_id=1, source_target_pairs={{0,64},{64,0},{1,65},{65,1},{2,66},{66,2},{3,67},{67,3},{4,68},{68... | collective-permute-start | bytes 786440 | tf_op jit(solution)/shard_map/ppermute | solution.py:27
  128.1 16.4 %collective-permute-start.24 = (bf16[512,512]{1,0:T(8,128)(2,1)S(1)}, bf16[512,512]{1,0:T(8,128)(2,1)S(1)}, u32[]{:S(2)}, u32[]{:S(2)}) collective-permute-start(bf16[512,512]{1,0:T(8,128)(2,1)S(1)} %collective-permute-done.20.refs_10_), channel_id=1, source_target_pairs={{0,1},{1,0},{2,3},{3,2},{4,5},{5,4},{6,7},{7,6},{8,9},{9,8},{10,11... | collective-permute-start | bytes 1572872 | tf_op jit(solution)/shard_map/ppermute | solution.py:27
  137.3 6.1 %collective-permute-start.23 = (bf16[256,512]{1,0:T(8,128)(2,1)S(1)}, bf16[256,512]{1,0:T(8,128)(2,1)S(1)}, u32[]{:S(2)}, u32[]{:S(2)}) collective-permute-start(bf16[256,512]{1,0:T(8,128)(2,1)S(1)} %collective-permute-done.19.refs_9_), channel_id=1, source_target_pairs={{0,1},{1,0},{2,3},{3,2},{4,5},{5,4},{6,7},{7,6},{8,9},{9,8},{10,11... | collective-permute-start | bytes 786440 | tf_op jit(solution)/shard_map/ppermute | solution.py:27
  158.1 6.1 %collective-permute-start.27 = (bf16[128,512]{1,0:T(8,128)(2,1)}, bf16[128,512]{1,0:T(8,128)(2,1)S(1)}, u32[]{:S(2)}, u32[]{:S(2)}) collective-permute-start(bf16[128,512]{1,0:T(8,128)(2,1)} %get-tuple-element.44), channel_id=1, source_target_pairs={{0,32},{16,48},{32,0},{48,16},{1,33},{17,49},{33,1},{49,17},{2,34}... | collective-permute-start | bytes 393224 | tf_op jit(solution)/shard_map/ppermute | solution.py:27
  158.1 9.5 %collective-permute-start.28 = (bf16[128,512]{1,0:T(8,128)(2,1)}, bf16[128,512]{1,0:T(8,128)(2,1)S(1)}, u32[]{:S(2)}, u32[]{:S(2)}) collective-permute-start(bf16[128,512]{1,0:T(8,128)(2,1)} %get-tuple-element.45), channel_id=1, source_target_pairs={{0,16},{16,32},{32,48},{48,0},{1,17},{17,33},{33,49},{49,1},{2,18}... | collective-permute-start | bytes 393224 | tf_op jit(solution)/shard_map/ppermute | solution.py:27
  169.7 13.3 %collective-permute-start.29 = (bf16[224,512]{1,0:T(8,128)(2,1)S(1)}, bf16[224,512]{1,0:T(8,128)(2,1)S(1)}, u32[]{:S(2)}, u32[]{:S(2)}) collective-permute-start(bf16[224,512]{1,0:T(8,128)(2,1)S(1)} %get-tuple-element.46), channel_id=1, source_target_pairs={{0,8},{8,0},{1,9},{9,1},{2,10},{10,2},{3,11},{11,3},{4,12},{12,4},... | collective-permute-start | bytes 688136 | tf_op jit(solution)/shard_map/ppermute | solution.py:27
  172.6 10.4 %collective-permute-start.30 = (bf16[208,512]{1,0:T(8,128)(2,1)S(1)}, bf16[208,512]{1,0:T(8,128)(2,1)S(1)}, u32[]{:S(2)}, u32[]{:S(2)}) collective-permute-start(bf16[208,512]{1,0:T(8,128)(2,1)S(1)} %get-tuple-element.47), channel_id=1, source_target_pairs={{0,2},{2,4},{4,6},{6,0},{1,3},{3,5},{5,7},{7,1},{8,10},{10,12},{12... | collective-permute-start | bytes 638984 | tf_op jit(solution)/shard_map/ppermute | solution.py:27
  172.6 10.4 %collective-permute-start.31 = (bf16[208,512]{1,0:T(8,128)(2,1)S(1)}, bf16[208,512]{1,0:T(8,128)(2,1)S(1)}, u32[]{:S(2)}, u32[]{:S(2)}) collective-permute-start(bf16[208,512]{1,0:T(8,128)(2,1)S(1)} %get-tuple-element.48), channel_id=1, source_target_pairs={{0,6},{2,0},{4,2},{6,4},{1,7},{3,1},{5,3},{7,5},{8,14},{10,8},{12,... | collective-permute-start | bytes 638984 | tf_op jit(solution)/shard_map/ppermute | solution.py:27
  186.8 14.5 %collective-permute-start.32 = (bf16[640,512]{1,0:T(8,128)(2,1)S(1)}, bf16[640,512]{1,0:T(8,128)(2,1)S(1)}, u32[]{:S(2)}, u32[]{:S(2)}) collective-permute-start(bf16[640,512]{1,0:T(8,128)(2,1)S(1)} %get-tuple-element.49), channel_id=1, source_target_pairs={{0,6},{2,0},{4,2},{6,4},{1,7},{3,1},{5,3},{7,5},{8,14},{10,8},{12,... | collective-permute-start | bytes 1966088 | tf_op jit(solution)/shard_map/ppermute | solution.py:27
  189.2 13.9 %collective-permute-start.33 = (bf16[640,512]{1,0:T(8,128)(2,1)S(1)}, bf16[640,512]{1,0:T(8,128)(2,1)S(1)}, u32[]{:S(2)}, u32[]{:S(2)}) collective-permute-start(bf16[640,512]{1,0:T(8,128)(2,1)S(1)} %get-tuple-element.50), channel_id=1, source_target_pairs={{0,8},{8,0},{1,9},{9,1},{2,10},{10,2},{3,11},{11,3},{4,12},{12,4},... | collective-permute-start | bytes 1966088 | tf_op jit(solution)/shard_map/ppermute | solution.py:27
  189.7 15.1 %collective-permute-start.34 = (bf16[640,512]{1,0:T(8,128)(2,1)S(1)}, bf16[640,512]{1,0:T(8,128)(2,1)S(1)}, u32[]{:S(2)}, u32[]{:S(2)}) collective-permute-start(bf16[640,512]{1,0:T(8,128)(2,1)S(1)} %get-tuple-element.51), channel_id=1, source_target_pairs={{0,2},{2,4},{4,6},{6,0},{1,3},{3,5},{5,7},{7,1},{8,10},{10,12},{12... | collective-permute-start | bytes 1966088 | tf_op jit(solution)/shard_map/ppermute | solution.py:27
  210.0 13.3 %collective-permute-start.35 = (bf16[640,512]{1,0:T(8,128)(2,1)}, bf16[640,512]{1,0:T(8,128)(2,1)S(1)}, u32[]{:S(2)}, u32[]{:S(2)}) collective-permute-start(bf16[640,512]{1,0:T(8,128)(2,1)} %get-tuple-element.52), channel_id=1, source_target_pairs={{0,6},{2,0},{4,2},{6,4},{1,7},{3,1},{5,3},{7,5},{8,14},{10,8},{12,... | collective-permute-start | bytes 1966088 | tf_op jit(solution)/shard_map/ppermute | solution.py:27
  210.0 14.5 %collective-permute-start.36 = (bf16[640,512]{1,0:T(8,128)(2,1)}, bf16[640,512]{1,0:T(8,128)(2,1)}, u32[]{:S(2)}, u32[]{:S(2)}) collective-permute-start(bf16[640,512]{1,0:T(8,128)(2,1)} %get-tuple-element.53), channel_id=1, source_target_pairs={{0,2},{2,4},{4,6},{6,0},{1,3},{3,5},{5,7},{7,1},{8,10},{10,12},{12... | collective-permute-start | bytes 1966088 | tf_op jit(solution)/shard_map/ppermute | solution.py:27
  211.5 13.0 %collective-permute-start.37 = (bf16[640,512]{1,0:T(8,128)(2,1)}, bf16[640,512]{1,0:T(8,128)(2,1)}, u32[]{:S(2)}, u32[]{:S(2)}) collective-permute-start(bf16[640,512]{1,0:T(8,128)(2,1)} %get-tuple-element.54), channel_id=1, source_target_pairs={{0,8},{8,0},{1,9},{9,1},{2,10},{10,2},{3,11},{11,3},{4,12},{12,4},... | collective-permute-start | bytes 1966088 | tf_op jit(solution)/shard_map/ppermute | solution.py:27
  (26 other events, 195.7 us)

commit v4 on v3

--- a/solution.py
+++ b/solution.py
@@ -35,11 +35,32 @@
     return {640: 128, 224: 112}.get(rows, rows)
 
 
-def prepare_kernel(qkv, leaving, modulation, _, weight, gain, bias, leaving_out):
-    inner = qkv.shape[2]
-    for part in range(3):
-        weight[part * inner : (part + 1) * inner, :] = qkv[part].T
-    leaving_out[...] = leaving[...].T
+def turn_kernel(weight, out):
+    inner = weight.shape[2]
+    for part in range(weight.shape[0]):
+        out[part * inner : (part + 1) * inner, :] = weight[part].T
+
+
+def turn(weight):
+    parts, features, inner = weight.shape
+    deep = 512
+    return pl.pallas_call(
+        turn_kernel,
+        grid=(features // deep,),
+        in_specs=[pl.BlockSpec((parts, deep, inner), lambda i: (0, i, 0))],
+        out_specs=pl.BlockSpec((parts * inner, deep), lambda i: (0, i)),
+        out_shape=jax.ShapeDtypeStruct((parts * inner, features), weight.dtype),
+        compiler_params=pltpu.CompilerParams(vmem_limit_bytes=16 * MIB),
+        cost_estimate=pl.CostEstimate(
+            flops=0, bytes_accessed=4 * weight.size, transcendentals=0
+        ),
+        name="turn",
+    )(weight)
+
+
+def prepare_kernel(own, other, modulation, gain, bias, own_out, other_out):
+    own_out[...] = own[...].T
+    other_out[...] = other[...].T
     for row, out, add in ((1, gain, 1.0), (0, bias, 0.0)):
         for part in range(out.shape[0] // BLK):
             rows = slice(part * BLK, (part + 1) * BLK)
@@ -47,47 +68,39 @@
             out[rows, :] = jnp.broadcast_to(line, (BLK, BLK)).T
 
 
-def prepare(qkv_weight, out_weight, modulation, after):
-    _, features, inner = qkv_weight.shape
+def prepare(own, other, modulation):
+    inner, features = own.shape
     deep = 512
     return pl.pallas_call(
         prepare_kernel,
         grid=(features // deep,),
         in_specs=[
-            pl.BlockSpec((3, deep, inner), lambda i: (0, i, 0)),
-            pl.BlockSpec((out_weight.shape[0], deep), lambda i: (0, i)),
+            pl.BlockSpec((inner, deep), lambda i: (0, i)),
+            pl.BlockSpec((inner, deep), lambda i: (0, i)),
             pl.BlockSpec((3, deep), lambda i: (0, i)),
-            pl.BlockSpec(memory_space=pl.ANY),
         ],
         out_specs=[
-            pl.BlockSpec((3 * inner, deep), lambda i: (0, i)),
             pl.BlockSpec((deep, BLK), lambda i: (i, 0)),
             pl.BlockSpec((deep, BLK), lambda i: (i, 0)),
-            pl.BlockSpec((deep, out_weight.shape[0]), lambda i: (i, 0)),
+            pl.BlockSpec((deep, inner), lambda i: (i, 0)),
+            pl.BlockSpec((deep, inner), lambda i: (i, 0)),
         ],
         out_shape=[
-            jax.ShapeDtypeStruct((3 * inner, features), jnp.bfloat16),
             jax.ShapeDtypeStruct((features, BLK), jnp.float32),
             jax.ShapeDtypeStruct((features, BLK), jnp.float32),
-            jax.ShapeDtypeStruct((features, out_weight.shape[0]), jnp.bfloat16),
+            jax.ShapeDtypeStruct((features, inner), jnp.bfloat16),
+            jax.ShapeDtypeStruct((features, inner), jnp.bfloat16),
         ],
-        compiler_params=pltpu.CompilerParams(vmem_limit_bytes=24 * MIB),
+        compiler_params=pltpu.CompilerParams(vmem_limit_bytes=16 * MIB),
         cost_estimate=pl.CostEstimate(
-            flops=0, bytes_accessed=16 * features * inner, transcendentals=0
+            flops=0, bytes_accessed=12 * features * inner, transcendentals=0
         ),
         name="prepare",
-    )(qkv_weight, out_weight, modulation, after)
-
-
-def together(*arrays):
-    return pl.pallas_call(
-        lambda *refs: None,
-        in_specs=[pl.BlockSpec(memory_space=pl.ANY)] * len(arrays),
-        out_specs=[pl.BlockSpec(memory_space=pl.ANY)] * len(arrays),
-        out_shape=[jax.ShapeDtypeStruct(a.shape, a.dtype) for a in arrays],
-        input_output_aliases={i: i for i in range(len(arrays))},
-        name="together",
-    )(*arrays)
+    )(own, other, modulation)
+
+
+def together(arrays, others=()):
+    return lax.optimization_barrier((*arrays, *others))[: len(arrays)]
 
 
 def project_kernel(
@@ -361,42 +374,24 @@
         ordered[...],
         preferred_element_type=jnp.float32,
     )
-    adds = sum(len(given) for given, _ in plan)
-    taken, outs = rest[:adds], list(rest[adds:])
-    at = 0
-    for index, (given, cuts) in enumerate(plan):
-        here = taken[at : at + len(given)]
-        at += len(given)
+    outs = list(rest)
+    for index, cuts in enumerate(plan):
         mine = [outs.pop(0) for _ in cuts]
 
         @pl.when(step == index)
         def _():
             for cut, out in zip(cuts, mine):
-                value = summed[cut[0] : cut[1]]
-                parts = []
-                for (first, last), ref in zip(given, here):
-                    if (first, last) == cut:
-                        value = value + ref[...].astype(jnp.float32)
-                    else:
-                        parts.append((first, last, ref))
-                if parts:
-                    ((first, last, ref),) = parts
-                    middle = value[first:last] + ref[...].astype(jnp.float32)
-                    pieces = [value[:first]] if first else []
-                    pieces.append(middle)
-                    pieces += [value[last:]] if last < cut[1] else []
-                    value = jnp.concatenate(pieces, axis=0)
-                out[...] = value.astype(out.dtype)
-
-
-def leave(chips, columns, weights, heads, plan, taken):
+                out[...] = summed[cut[0] : cut[1]].astype(out.dtype)
+
+
+def leave(chips, columns, weights, heads, plan):
     high = CUTS[-1][1]
     count = heads[0].shape[1]
     steps = len(plan)
     inner = weights[0].shape[1]
     block = pl.BlockSpec((high, inner), lambda i, chips, columns: (chips[i], 0))
     whole = lambda shape: pl.BlockSpec(shape, lambda i, *_: (0, 0))
-    shapes = [(cut[1] - cut[0], count) for _, cuts in plan for cut in cuts]
+    shapes = [(cut[1] - cut[0], count) for cuts in plan for cut in cuts]
 
     def kernel(*refs):
         leave_kernel(plan, *refs)
@@ -407,8 +402,7 @@
             num_scalar_prefetch=2,
             grid=(steps,),
             in_specs=[block] * 2
-            + [whole(h.shape) for h in heads]
-            + [whole(t.shape) for t in taken],
+            + [whole(h.shape) for h in heads],
             out_specs=[whole(s) for s in shapes],
             scratch_shapes=[pltpu.VMEM((2 * inner, count), jnp.bfloat16)],
         ),
@@ -420,17 +414,55 @@
             transcendentals=0,
         ),
         name="leave",
-    )(chips, columns, *weights, *heads, *taken)
-
-
-def gather_tokens(own):
+    )(chips, columns, *weights, *heads)
+
+
+def arrive_kernel(plan, *refs):
+    outs = refs[-len(plan) :]
+    at = 0
+    for cuts, out in zip(plan, outs):
+        share, arrived = refs[at], refs[at + 1 : at + 1 + len(cuts)]
+        at += 1 + len(cuts)
+        rows = sorted({0, out.shape[0], *[edge for cut in cuts for edge in cut]})
+        for low, high in zip(rows, rows[1:]):
+            value = share[low:high].astype(jnp.float32)
+            for (first, last), ref in zip(cuts, arrived):
+                if first <= low and high <= last:
+                    value += ref[low - first : high - first].astype(jnp.float32)
+            out[low:high] = value.astype(out.dtype)
+
+
+def arrive(plan, *arrays):
+    shares, at = [], 0
+    for cuts in plan:
+        shares.append(arrays[at])
+        at += 1 + len(cuts)
+
+    def kernel(*refs):
+        arrive_kernel(plan, *refs)
+
+    return pl.pallas_call(
+        kernel,
+        in_specs=[pl.BlockSpec(memory_space=pltpu.VMEM)] * len(arrays),
+        out_specs=[pl.BlockSpec(memory_space=pltpu.VMEM)] * len(plan),
+        out_shape=[jax.ShapeDtypeStruct(share.shape, share.dtype) for share in shares],
+        compiler_params=pltpu.CompilerParams(vmem_limit_bytes=24 * MIB),
+        cost_estimate=pl.CostEstimate(
+            flops=0, bytes_accessed=8 * shares[0].size, transcendentals=0
+        ),
+        name="arrive",
+    )(*arrays)
+
+
+def gather_tokens(own, first_others, second_others):
     below = shift(own, "z", 1)
     above = shift(own, "z", -1)
     beside = swap(own, "yl")
-    below, above, beside = together(below, above, beside)
+    below, above, beside = together((below, above, beside), first_others)
     far = shift(below, "z", 1)
     beside_below = swap(below, "yl")
     beside_above = shift(beside, "z", -1)
+    far, beside_below, beside_above = together((far, beside_below, beside_above), second_others)
     first, second, third = [slice(*cut) for cut in CUTS]
     parts = [
         swap(far[first], "yl"),
@@ -471,14 +503,9 @@
     own = jnp.concatenate(
         [jnp.where(core == 0, mine, other), jnp.where(core == 0, other, mine)], axis=0
     )
-    places, xs = gather_tokens(own)
-
-    own_weight, gain, bias, leaving = prepare(qkv_weight, out_weight, modulation, own)
-    other_weight = swap(own_weight, "core")
-    leaving = leaving, swap(leaving, "core")
-
     mask_mine, mask_given = mine_and_given(block_mask, 1)
-    mask_heads = jnp.stack([mask_mine, swap(mask_given, "core")])
+    mask_other = swap(mask_given, "core")
+    mask_heads = jnp.stack([mask_mine, mask_other])
     mask_rows = []
     for steps in range(4):
         side, slot = head_slot(steps)
@@ -486,6 +513,13 @@
             mask_heads, (side, slot, 0, 0), (1, 1, *mask_heads.shape[2:])
         )[0, 0]
         mask_rows.append(shift(part, "x", steps) if steps else part)
+    raw, _ = lax.optimization_barrier((qkv_weight, own))
+    other_raw = swap(raw, "core")
+    own_weight, other_weight = turn(raw), turn(other_raw)
+    places, xs = gather_tokens(own, (own_weight, *mask_rows[1:]), (other_weight,))
+    out_raw, _ = lax.optimization_barrier((out_weight, xs[1]))
+    gain, bias, *leaving = prepare(out_weight, swap(out_raw, "core"), modulation)
+
     keep = jnp.concatenate(mask_rows, axis=0) != 0
     blocks = jnp.arange(keep.shape[1], dtype=jnp.int32)
     per_core = half // BLK
@@ -505,7 +539,7 @@
     bases = jnp.stack([side * 3 * heads_here + slot for side, slot in slots]).astype(jnp.int32)
     lists = (listed, counts, *pair_lists(counts, listed.shape[1]))
     kv, query, *packed = project(
-        chips, bases, xs, own_weight, other_weight, gain, bias, (*lists, leaving[1])
+        chips, bases, xs, own_weight, other_weight, gain, bias, (*lists, *leaving)
     )
     two, one, three = [shift(packed[i - 1], "x", i) for i in (2, 1, 3)]
     both = jnp.concatenate([one[: 2 * BLK], three[: 2 * BLK]], axis=0)
@@ -527,31 +561,26 @@
     columns = jnp.stack([side * heads_here + slot for side, slot in slots]).astype(jnp.int32)
     whole = CUTS[0][0], CUTS[-1][1]
 
-    def shares(targets, plan, *taken):
+    def shares(targets, cuts):
         chips = jnp.stack([chip(*target) for target in targets]).astype(jnp.int32)
-        return leave(chips, columns, leaving, heads, plan, taken)
-
-    parts = shares([(1, 2)], [((), CUTS)])
+        return leave(chips, columns, leaving, heads, [cuts] * len(targets))
+
+    parts = shares([(1, 2)], CUTS)
+    near = [(0, 2), (1, 1), (1, -1), (0, -1), (0, 1), (1, 0), (0, 0)]
+    share = dict(zip(near, shares(near, (whole,))))
     first = swap(parts[0], "yl")
     second = shift(parts[1], "z", 1)
     third = shift(parts[2], "z", -1)
-    down, up, side = shares(
-        [(0, 2), (1, 1), (1, -1)],
-        [((CUTS[0],), (whole,)), ((CUTS[1],), (whole,)), ((CUTS[2],), (whole,))],
-        first,
-        second,
-        third,
+    down, up, side = arrive(
+        [(CUTS[0],), (CUTS[1],), (CUTS[2],)],
+        *[share[0, 2], first, share[1, 1], second, share[1, -1], third],
     )
     down, up, side = shift(down, "z", -1), shift(up, "z", 1), swap(side, "yl")
-    down, up, side = shares(
-        [(0, -1), (0, 1), (1, 0)],
-        [((whole, whole), (whole,)), ((), (whole,)), ((whole,), (whole,))],
-        down,
-        side,
-        up,
+    down, side = arrive(
+        [(whole, whole), (whole,)], share[0, -1], down, side, share[1, 0], up
     )
-    down, up, side = shift(down, "z", -1), shift(up, "z", 1), swap(side, "yl")
-    (summed,) = shares([(0, 0)], [((whole, whole, whole), (whole,))], down, up, side)
+    down, up, side = shift(down, "z", -1), shift(share[0, 1], "z", 1), swap(side, "yl")
+    (summed,) = arrive([(whole, whole, whole)], share[0, 0], down, up, side)
 
     kept, given = mine_and_given(summed, 0)
     other = swap(given, "core")

time: 238 us -> 234 us (0.983)
  starting transfers between devices: 75.7 us -> 54.8 us
  local copies, waits for them, and re-layouts: 14.6 us -> 26.2 us
  Pallas kernels: 54.6 us -> 63.7 us
  waiting for transfers between devices: 87.2 us -> 84.6 us
    ppermute x39, starting transfers between devices: 75.7 us -> 54.8 us  [shift(): lax.ppermute(value, axis, [(i, (i + steps) % count) for i in range(count)])]
    pallas_call x1 -> x5, Pallas kernels: 0.01 us -> 13.2 us  [the longest x2 11.6 us: turn(): pl.pallas_call(turn_kernel, grid=(features // deep,), in_specs=[pl.BlockS...]
    unnamed x38 -> x54, local copies, waits for them, and re-layouts: 12.4 us -> 24 us
    pallas_call x4 -> x2, Pallas kernels: 13.6 us -> 7.26 us  [leave(): pl.pallas_call(kernel, grid_spec=pltpu.PrefetchScalarGridSpec(num_scalar_...]
    pallas_call x1, Pallas kernels: 12.9 us -> 15.5 us  [attend(): pl.pallas_call(kernel, in_specs=[pl.BlockSpec(memory_space=pltpu.SMEM)] *...]
    ppermute x39, waiting for transfers between devices: 87.2 us -> 84.6 us  [shift(): lax.ppermute(value, axis, [(i, (i + steps) % count) for i in range(count)])]
  transfers between devices with their start and end apart: 39 -> 39, of which waited for: 21 -> 20; matrix products, arithmetic and copies ran while one was open for 1% -> 1% of each run, Pallas kernels for 0% -> 11%
where the time goes in v4:
time: 234 us
  waiting for transfers between devices  84.6 us (36%)
  Pallas kernels  63.7 us (27%)
  starting transfers between devices  54.8 us (23%)
  local copies, waits for them, and re-layouts  26.2 us (11%)
  other arithmetic  4.31 us (2%)
    ppermute x39, waiting for transfers between devices, shift(): lax.ppermute(value, axis, [(i, (i + steps) % count) for i in range(count)])  84.6 us
    ppermute x39, starting transfers between devices, shift(): lax.ppermute(value, axis, [(i, (i + steps) % count) for i in range(count)])  54.8 us
    unnamed x54, local copies, waits for them, and re-layouts  24 us
    pallas_call x1, Pallas kernels, project(): pl.pallas_call(project_kernel, grid_spec=pltpu.PrefetchScalarGridSpec(num...  20.6 us
    pallas_call x1, Pallas kernels, attend(): pl.pallas_call(kernel, in_specs=[pl.BlockSpec(memory_space=pltpu.SMEM)] *...  15.5 us
    pallas_call x2, Pallas kernels, turn(): pl.pallas_call(turn_kernel, grid=(features // deep,), in_specs=[pl.BlockS...  11.6 us
    pallas_call x2, Pallas kernels, leave(): pl.pallas_call(kernel, grid_spec=pltpu.PrefetchScalarGridSpec(num_scalar_...  7.26 us
    pallas_call x1, Pallas kernels, prepare(): pl.pallas_call(prepare_kernel, grid=(features // deep,), in_specs=[pl.Blo...  7.04 us
  transfers between devices with their start and end apart: 39, of which 20 were waited for; matrix products, arithmetic and copies ran while one was open for 1% of the time, Pallas kernels for 11%

profile of v4, /device:TPU:1, one launch (start us, length us, event | category | flops | bytes accessed | tf_op | source)
XLA Modules:
  0.0 234.1 jit_solution(11897799675421921742)
XLA Ops:
  7.1 2.1 collective-permute-start.2
  11.3 6.1 %collective-permute-done.4 = s32[2,4,64]{2,1,0:T(4,128)S(1)} collective-permute-done((s32[2,4,64]{2,1,0:T(4,128)S(1)}, s32[2,4,64]{2,1,0:T(4,128)S(1)}, u32[]{:S(2)}, u32[]{:S(2)}) %collective-permute-start.4) | collective-permute-done | bytes 2080 | tf_op jit(solution)/shard_map/ppermute | solution.py:27
  18.8 2.8 %collective-permute-done.5 = s32[4,64]{1,0:T(4,128)S(1)} collective-permute-done((s32[4,64]{1,0:T(4,128)S(1)}, s32[4,64]{1,0:T(4,128)S(1)}, u32[]{:S(2)}, u32[]{:S(2)}) %collective-permute-start.5) | collective-permute-done | bytes 1056 | tf_op jit(solution)/shard_map/ppermute | solution.py:27
  23.2 2.3 collective-permute-done.6
  26.8 3.2 %copy-done.7 = bf16[3,5120,256]{2,1,0:T(8,128)(2,1)S(1)} copy-done((bf16[3,5120,256]{2,1,0:T(8,128)(2,1)S(1)}, bf16[3,5120,256]{2,1,0:T(8,128)(2,1)}, u32[]{:S(2)}) %copy-start.7) | copy-done | bytes 7864344
  30.1 3.7 %turn.2.refs_10_.refs_11_ = bf16[768,5120]{1,0:T(8,128)(2,1)S(1)} custom-call(bf16[3,5120,256]{2,1,0:T(8,128)(2,1)S(1)} %copy-done.7), custom_call_target="tpu_custom_call" | custom-call | bytes 15728640 | tf_op jit(solution)/shard_map/turn/pallas_call | solution.py:47
  33.8 3.1 %copy-done = bf16[768,5120]{1,0:T(8,128)(2,1)} copy-done((bf16[768,5120]{1,0:T(8,128)(2,1)}, bf16[768,5120]{1,0:T(8,128)(2,1)S(1)}, u32[]{:S(2)}) %copy-start) | copy-done | bytes 7864344
  37.0 2.6 %collective-permute-start.8 = (bf16[256,5120]{1,0:T(8,128)(2,1)S(1)}, bf16[256,5120]{1,0:T(8,128)(2,1)}, u32[]{:S(2)}, u32[]{:S(2)}) collective-permute-start(bf16[256,5120]{1,0:T(8,128)(2,1)S(1)} %copy-done.10), channel_id=1, source_target_pairs={{0,1},{1,0},{2,3},{3,2},{4,5},{5,4},{6,7},{7,6},{8,9},{9,8},{10,11... | collective-permute-start | bytes 7864328 | tf_op jit(solution)/shard_map/ppermute | solution.py:27
  46.3 7.9 %turn.3.refs_12_.refs_13_ = bf16[768,5120]{1,0:T(8,128)(2,1)S(1)} custom-call(bf16[3,5120,256]{2,1,0:T(8,128)(2,1)} %collective-permute-done.12.weight), custom_call_target="tpu_custom_call" | custom-call | bytes 15728640 | tf_op jit(solution)/shard_map/turn/pallas_call | solution.py:47
  54.2 3.0 %copy-done.1 = bf16[768,5120]{1,0:T(8,128)(2,1)} copy-done((bf16[768,5120]{1,0:T(8,128)(2,1)}, bf16[768,5120]{1,0:T(8,128)(2,1)S(1)}, u32[]{:S(2)}) %copy-start.1) | copy-done | bytes 7864344
  57.2 2.6 %collective-permute-done.11.refs_6_ = bf16[640,512]{1,0:T(8,128)(2,1)S(1)} collective-permute-done((bf16[640,512]{1,0:T(8,128)(2,1)}, bf16[640,512]{1,0:T(8,128)(2,1)S(1)}, u32[]{:S(2)}, u32[]{:S(2)}) %collective-permute-start.11) | collective-permute-done | bytes 655392 | tf_op jit(solution)/shard_map/ppermute | solution.py:27
  61.1 2.4 %collective-permute-start.14 = (bf16[208,512]{1,0:T(8,128)(2,1)S(1)}, bf16[208,512]{1,0:T(8,128)(2,1)S(1)}, u32[]{:S(2)}, u32[]{:S(2)}) collective-permute-start(bf16[208,512]{1,0:T(8,128)(2,1)S(1)} %slice.31), channel_id=1, source_target_pairs={{0,6},{2,0},{4,2},{6,4},{1,7},{3,1},{5,3},{7,5},{8,14},{10,8},{12,... | collective-permute-start | bytes 638984 | tf_op jit(solution)/shard_map/ppermute | solution.py:27
  64.0 7.0 %prepare.1 = (f32[5120,128]{1,0:T(8,128)S(1)}, f32[5120,128]{1,0:T(8,128)S(1)}, bf16[5120,256]{1,0:T(8,128)(2,1)S(1)}, bf16[5120,256]{1,0:T(8,128)(2,1)S(1)}) custom-call(bf16[256,5120]{1,0:T(8,128)(2,1)S(1)} %copy-done.10, bf16[256,5120]{1,0:T(8,128)(2,1)} %collective-permute-done.8.other, f32[3,5120]{1,0:T(4,128)S(1)} %copy-done.19), custom_call_target="tpu_custom_call" | custom-call | bytes 15728640 | tf_op jit(solution)/shard_map/prepare/pallas_call | solution.py:74
  77.2 20.6 %project.1 = (bf16[256,512]{1,0:T(8,128)(2,1)S(1)}, bf16[128,512]{1,0:T(8,128)(2,1)S(1)}, bf16[384,512]{1,0:T(8,128)(2,1)S(1)}, bf16[384,512]{1,0:T(8,128)(2,1)S(1)}, bf16[384,512]{1,0:T(8,128)(2,1)S(1)}) custom-call(s32[8]{0:T(128)S(1)} %stack.94.chips, s32[4]{0:T(128)S(1)} %pad_add_fusion.1.heads, bf16[640,512]{1,0:T(8,128)(2,1)S(1)} %pad_maximum_fusion.1.refs_0_, ...), custom_call_target="tpu_custom_call" | custom-call | flops 8053063680 | bytes 20971520 | tf_op jit(solution)/shard_map/project/pallas_call | solution.py:197
  98.0 2.5 %collective-permute-start.18 = (bf16[384,512]{1,0:T(8,128)(2,1)S(1)}, bf16[384,512]{1,0:T(8,128)(2,1)S(1)}, u32[]{:S(2)}, u32[]{:S(2)}) collective-permute-start(bf16[384,512]{1,0:T(8,128)(2,1)S(1)} %get-tuple-element.57), channel_id=1, source_target_pairs={{0,48},{16,0},{32,16},{48,32},{1,49},{17,1},{33,17},{49,33},{2,50}... | collective-permute-start | bytes 1179656 | tf_op jit(solution)/shard_map/ppermute | solution.py:27
  100.5 8.3 %collective-permute-done.16.refs_6_ = bf16[384,512]{1,0:T(8,128)(2,1)S(1)} collective-permute-done((bf16[384,512]{1,0:T(8,128)(2,1)S(1)}, bf16[384,512]{1,0:T(8,128)(2,1)S(1)}, u32[]{:S(2)}, u32[]{:S(2)}) %collective-permute-start.16) | collective-permute-done | bytes 393248 | tf_op jit(solution)/shard_map/ppermute | solution.py:27
  109.0 6.5 %collective-permute-done.17.refs_7_ = bf16[384,512]{1,0:T(8,128)(2,1)S(1)} collective-permute-done((bf16[384,512]{1,0:T(8,128)(2,1)S(1)}, bf16[384,512]{1,0:T(8,128)(2,1)S(1)}, u32[]{:S(2)}, u32[]{:S(2)}) %collective-permute-start.17) | collective-permute-done | bytes 393248 | tf_op jit(solution)/shard_map/ppermute | solution.py:27
  115.5 3.8 %collective-permute-start.22 = (bf16[1024,512]{1,0:T(8,128)(2,1)S(1)}, bf16[1024,512]{1,0:T(8,128)(2,1)S(1)}, u32[]{:S(2)}, u32[]{:S(2)}) collective-permute-start(bf16[1024,512]{1,0:T(8,128)(2,1)S(1)} %pad_maximum_fusion), channel_id=1, source_target_pairs={{0,1},{1,0},{2,3},{3,2},{4,5},{5,4},{6,7},{7,6},{8,9},{9,8},{10,11... | collective-permute-start | bytes 3145736 | tf_op jit(solution)/shard_map/ppermute | solution.py:27
  119.3 2.9 %collective-permute-start.20 = (bf16[512,512]{1,0:T(8,128)(2,1)S(1)}, bf16[512,512]{1,0:T(8,128)(2,1)S(1)}, u32[]{:S(2)}, u32[]{:S(2)}) collective-permute-start(bf16[512,512]{1,0:T(8,128)(2,1)S(1)} %pad_maximum_fusion.2), channel_id=1, source_target_pairs={{0,64},{64,0},{1,65},{65,1},{2,66},{66,2},{3,67},{67,3},{4,68},{68... | collective-permute-start | bytes 1572872 | tf_op jit(solution)/shard_map/ppermute | solution.py:27
  122.3 2.9 %collective-permute-start.21 = (bf16[256,512]{1,0:T(8,128)(2,1)S(1)}, bf16[256,512]{1,0:T(8,128)(2,1)S(1)}, u32[]{:S(2)}, u32[]{:S(2)}) collective-permute-start(bf16[256,512]{1,0:T(8,128)(2,1)S(1)} %slice.38), channel_id=1, source_target_pairs={{0,64},{64,0},{1,65},{65,1},{2,66},{66,2},{3,67},{67,3},{4,68},{68... | collective-permute-start | bytes 786440 | tf_op jit(solution)/shard_map/ppermute | solution.py:27
  125.2 9.1 %collective-permute-done.20.refs_10_ = bf16[512,512]{1,0:T(8,128)(2,1)S(1)} collective-permute-done((bf16[512,512]{1,0:T(8,128)(2,1)S(1)}, bf16[512,512]{1,0:T(8,128)(2,1)S(1)}, u32[]{:S(2)}, u32[]{:S(2)}) %collective-permute-start.20) | collective-permute-done | bytes 524320 | tf_op jit(solution)/shard_map/ppermute | solution.py:27
  135.6 4.3 %collective-permute-done.19.refs_9_ = bf16[256,512]{1,0:T(8,128)(2,1)S(1)} collective-permute-done((bf16[256,512]{1,0:T(8,128)(2,1)S(1)}, bf16[256,512]{1,0:T(8,128)(2,1)S(1)}, u32[]{:S(2)}, u32[]{:S(2)}) %collective-permute-start.19) | collective-permute-done | bytes 262176 | tf_op jit(solution)/shard_map/ppermute | solution.py:27
  141.3 4.3 %collective-permute-done.21.refs_11_ = bf16[256,512]{1,0:T(8,128)(2,1)S(1)} collective-permute-done((bf16[256,512]{1,0:T(8,128)(2,1)S(1)}, bf16[256,512]{1,0:T(8,128)(2,1)S(1)}, u32[]{:S(2)}, u32[]{:S(2)}) %collective-permute-start.21) | collective-permute-done | bytes 262176 | tf_op jit(solution)/shard_map/ppermute | solution.py:27
  147.6 15.5 %attend.1 = (bf16[128,512]{1,0:T(8,128)(2,1)S(1)}, bf16[128,512]{1,0:T(8,128)(2,1)}, bf16[128,512]{1,0:T(8,128)(2,1)}, bf16[128,512]{1,0:T(8,128)(2,1)S(1)}) custom-call(s32[16,64]{1,0:T(8,128)S(1)} %select_reduce_fusion.2.refs_16_.refs_0_, s32[16]{0:T(128)S(1)} %get-tuple-element.77.refs_17_.refs_1_, s32[17]{0:T(128)S(1)} %select_reduce_fusion.5.refs_18_.refs_2_, ...), custom_call_target="tpu_custom_call" | custom-call | flops 2147483648 | bytes 4194304 | tf_op jit(solution)/shard_map/attend/pallas_call | solution.py:337
  164.7 4.0 %collective-permute-done.26.refs_5_ = bf16[128,512]{1,0:T(8,128)(2,1)S(1)} collective-permute-done((bf16[128,512]{1,0:T(8,128)(2,1)}, bf16[128,512]{1,0:T(8,128)(2,1)S(1)}, u32[]{:S(2)}, u32[]{:S(2)}) %collective-permute-start.26) | collective-permute-done | bytes 131104 | tf_op jit(solution)/shard_map/ppermute | solution.py:27
  170.4 2.9 %collective-permute-done.28.refs_7_ = bf16[128,512]{1,0:T(8,128)(2,1)S(1)} collective-permute-done((bf16[128,512]{1,0:T(8,128)(2,1)S(1)}, bf16[128,512]{1,0:T(8,128)(2,1)S(1)}, u32[]{:S(2)}, u32[]{:S(2)}) %collective-permute-start.28) | collective-permute-done | bytes 131104 | tf_op jit(solution)/shard_map/ppermute | solution.py:27
  178.1 4.8 %collective-permute-start.29 = (bf16[224,512]{1,0:T(8,128)(2,1)}, bf16[224,512]{1,0:T(8,128)(2,1)S(1)}, u32[]{:S(2)}, u32[]{:S(2)}) collective-permute-start(bf16[224,512]{1,0:T(8,128)(2,1)} %get-tuple-element.65), channel_id=1, source_target_pairs={{0,8},{8,0},{1,9},{9,1},{2,10},{10,2},{3,11},{11,3},{4,12},{12,4},... | collective-permute-start | bytes 688136 | tf_op jit(solution)/shard_map/ppermute | solution.py:27
  183.0 2.7 %collective-permute-start.31 = (bf16[208,512]{1,0:T(8,128)(2,1)}, bf16[208,512]{1,0:T(8,128)(2,1)S(1)}, u32[]{:S(2)}, u32[]{:S(2)}) collective-permute-start(bf16[208,512]{1,0:T(8,128)(2,1)} %copy-done.20), channel_id=1, source_target_pairs={{0,6},{2,0},{4,2},{6,4},{1,7},{3,1},{5,3},{7,5},{8,14},{10,8},{12,... | collective-permute-start | bytes 638984 | tf_op jit(solution)/shard_map/ppermute | solution.py:27
  191.0 5.6 %leave.2 = (bf16[640,512]{1,0:T(8,128)(2,1)S(1)}, bf16[640,512]{1,0:T(8,128)(2,1)S(1)}, bf16[640,512]{1,0:T(8,128)(2,1)S(1)}, bf16[640,512]{1,0:T(8,128)(2,1)S(1...) custom-call(s32[7]{0:T(128)S(1)} %stack.84.refs_0_, ...), custom_call_target="tpu_custom_call" | custom-call | flops 2348810240 | bytes 9175040 | tf_op jit(solution)/shard_map/leave/pallas_call | solution.py:399
  198.4 12.8 %collective-permute-done.32.refs_1_ = bf16[640,512]{1,0:T(8,128)(2,1)S(1)} collective-permute-done((bf16[640,512]{1,0:T(8,128)(2,1)S(1)}, bf16[640,512]{1,0:T(8,128)(2,1)S(1)}, u32[]{:S(2)}, u32[]{:S(2)}) %collective-permute-start.32) | collective-permute-done | bytes 655392 | tf_op jit(solution)/shard_map/ppermute | solution.py:27
  214.8 11.8 %collective-permute-done.36.refs_2_ = bf16[640,512]{1,0:T(8,128)(2,1)S(1)} collective-permute-done((bf16[640,512]{1,0:T(8,128)(2,1)}, bf16[640,512]{1,0:T(8,128)(2,1)S(1)}, u32[]{:S(2)}, u32[]{:S(2)}) %collective-permute-start.36) | collective-permute-done | bytes 655392 | tf_op jit(solution)/shard_map/ppermute | solution.py:27
  227.1 4.5 %collective-permute-start.38 = (bf16[320,512]{1,0:T(8,128)(2,1)S(1)}, bf16[320,512]{1,0:T(8,128)(2,1)S(1)}, u32[]{:S(2)}, u32[]{:S(2)}) collective-permute-start(bf16[320,512]{1,0:T(8,128)(2,1)S(1)} %constant_dynamic-slice_fusion), channel_id=1, source_target_pairs={{0,1},{1,0},{2,3},{3,2},{4,5},{5,4},{6,7},{7,6},{8,9},{9,8},{10,11... | collective-permute-start | bytes 983048 | tf_op jit(solution)/shard_map/ppermute | solution.py:27
  (144 shorter events, 55.0 us)
Async XLA Ops:
  4.9 41.4 %collective-permute-start.12 = (bf16[3,5120,256]{2,1,0:T(8,128)(2,1)}, bf16[3,5120,256]{2,1,0:T(8,128)(2,1)}, u32[]{:S(2)}, u32[]{:S(2)}) collective-permute-start(bf16[3,5120,256]{2,1,0:T(8,128)(2,1)} %weight), channel_id=1, source_target_pairs={{0,1},{1,0},{2,3},{3,2},{4,5},{5,4},{6,7},{7,6},{8,9},{9,8},{10,11... | collective-permute-start | bytes 23592968 | tf_op jit(solution)/shard_map/ppermute | solution.py:27
  5.4 31.6 %collective-permute-start.1 = (bf16[640,512]{1,0:T(8,128)(2,1)S(1)}, bf16[640,512]{1,0:T(8,128)(2,1)}, u32[]{:S(2)}, u32[]{:S(2)}) collective-permute-start(bf16[640,512]{1,0:T(8,128)(2,1)S(1)} %pad_maximum_fusion.1.refs_0_), channel_id=1, source_target_pairs={{0,2},{2,4},{4,6},{6,0},{1,3},{3,5},{5,7},{7,1},{8,10},{10,12},{12... | collective-permute-start | bytes 1966088 | tf_op jit(solution)/shard_map/ppermute | solution.py:27
  7.1 29.9 %collective-permute-start.2 = (bf16[640,512]{1,0:T(8,128)(2,1)S(1)}, bf16[640,512]{1,0:T(8,128)(2,1)}, u32[]{:S(2)}, u32[]{:S(2)}) collective-permute-start(bf16[640,512]{1,0:T(8,128)(2,1)S(1)} %pad_maximum_fusion.1.refs_0_), channel_id=1, source_target_pairs={{0,6},{2,0},{4,2},{6,4},{1,7},{3,1},{5,3},{7,5},{8,14},{10,8},{12,... | collective-permute-start | bytes 1966088 | tf_op jit(solution)/shard_map/ppermute | solution.py:27
  9.2 27.7 %collective-permute-start.3 = (bf16[640,512]{1,0:T(8,128)(2,1)S(1)}, bf16[640,512]{1,0:T(8,128)(2,1)}, u32[]{:S(2)}, u32[]{:S(2)}) collective-permute-start(bf16[640,512]{1,0:T(8,128)(2,1)S(1)} %pad_maximum_fusion.1.refs_0_), channel_id=1, source_target_pairs={{0,8},{8,0},{1,9},{9,1},{2,10},{10,2},{3,11},{11,3},{4,12},{12,4},... | collective-permute-start | bytes 1966088 | tf_op jit(solution)/shard_map/ppermute | solution.py:27
  10.5 6.9 %collective-permute-start.4 = (s32[2,4,64]{2,1,0:T(4,128)S(1)}, s32[2,4,64]{2,1,0:T(4,128)S(1)}, u32[]{:S(2)}, u32[]{:S(2)}) collective-permute-start(s32[2,4,64]{2,1,0:T(4,128)S(1)} %get-tuple-element.87), channel_id=1, source_target_pairs={{0,1},{1,0},{2,3},{3,2},{4,5},{5,4},{6,7},{7,6},{8,9},{9,8},{10,11... | collective-permute-start | bytes 6152 | tf_op jit(solution)/shard_map/ppermute | solution.py:27
  25.5 11.4 %collective-permute-start.7 = (s32[4,64]{1,0:T(4,128)S(1)}, s32[4,64]{1,0:T(4,128)S(1)}, u32[]{:S(2)}, u32[]{:S(2)}) collective-permute-start(s32[4,64]{1,0:T(4,128)S(1)} %get-tuple-element.86), channel_id=1, source_target_pairs={{0,48},{16,0},{32,16},{48,32},{1,49},{17,1},{33,17},{49,33},{2,50}... | collective-permute-start | bytes 3080 | tf_op jit(solution)/shard_map/ppermute | solution.py:27
  37.0 27.0 %collective-permute-start.8 = (bf16[256,5120]{1,0:T(8,128)(2,1)S(1)}, bf16[256,5120]{1,0:T(8,128)(2,1)}, u32[]{:S(2)}, u32[]{:S(2)}) collective-permute-start(bf16[256,5120]{1,0:T(8,128)(2,1)S(1)} %copy-done.10), channel_id=1, source_target_pairs={{0,1},{1,0},{2,3},{3,2},{4,5},{5,4},{6,7},{7,6},{8,9},{9,8},{10,11... | collective-permute-start | bytes 7864328 | tf_op jit(solution)/shard_map/ppermute | solution.py:27
  40.6 16.7 %collective-permute-start.10 = (bf16[640,512]{1,0:T(8,128)(2,1)}, bf16[640,512]{1,0:T(8,128)(2,1)S(1)}, u32[]{:S(2)}, u32[]{:S(2)}) collective-permute-start(bf16[640,512]{1,0:T(8,128)(2,1)} %collective-permute-done.1.refs_1_), channel_id=1, source_target_pairs={{0,8},{8,0},{1,9},{9,1},{2,10},{10,2},{3,11},{11,3},{4,12},{12,4},... | collective-permute-start | bytes 1966088 | tf_op jit(solution)/shard_map/ppermute | solution.py:27
  42.0 18.8 %collective-permute-start.9 = (bf16[640,512]{1,0:T(8,128)(2,1)}, bf16[640,512]{1,0:T(8,128)(2,1)S(1)}, u32[]{:S(2)}, u32[]{:S(2)}) collective-permute-start(bf16[640,512]{1,0:T(8,128)(2,1)} %collective-permute-done.1.refs_1_), channel_id=1, source_target_pairs={{0,2},{2,4},{4,6},{6,0},{1,3},{3,5},{5,7},{7,1},{8,10},{10,12},{12... | collective-permute-start | bytes 1966088 | tf_op jit(solution)/shard_map/ppermute | solution.py:27
  43.6 16.2 %collective-permute-start.11 = (bf16[640,512]{1,0:T(8,128)(2,1)}, bf16[640,512]{1,0:T(8,128)(2,1)S(1)}, u32[]{:S(2)}, u32[]{:S(2)}) collective-permute-start(bf16[640,512]{1,0:T(8,128)(2,1)} %collective-permute-done.3.refs_3_), channel_id=1, source_target_pairs={{0,6},{2,0},{4,2},{6,4},{1,7},{3,1},{5,3},{7,5},{8,14},{10,8},{12,... | collective-permute-start | bytes 1966088 | tf_op jit(solution)/shard_map/ppermute | solution.py:27
  60.8 16.4 %collective-permute-start.13 = (bf16[224,512]{1,0:T(8,128)(2,1)S(1)}, bf16[224,512]{1,0:T(8,128)(2,1)S(1)}, u32[]{:S(2)}, u32[]{:S(2)}) collective-permute-start(bf16[224,512]{1,0:T(8,128)(2,1)S(1)} %slice.30), channel_id=1, source_target_pairs={{0,8},{8,0},{1,9},{9,1},{2,10},{10,2},{3,11},{11,3},{4,12},{12,4},... | collective-permute-start | bytes 688136 | tf_op jit(solution)/shard_map/ppermute | solution.py:27
  61.1 16.1 %collective-permute-start.14 = (bf16[208,512]{1,0:T(8,128)(2,1)S(1)}, bf16[208,512]{1,0:T(8,128)(2,1)S(1)}, u32[]{:S(2)}, u32[]{:S(2)}) collective-permute-start(bf16[208,512]{1,0:T(8,128)(2,1)S(1)} %slice.31), channel_id=1, source_target_pairs={{0,6},{2,0},{4,2},{6,4},{1,7},{3,1},{5,3},{7,5},{8,14},{10,8},{12,... | collective-permute-start | bytes 638984 | tf_op jit(solution)/shard_map/ppermute | solution.py:27
  63.5 13.7 %collective-permute-start.15 = (bf16[208,512]{1,0:T(8,128)(2,1)S(1)}, bf16[208,512]{1,0:T(8,128)(2,1)S(1)}, u32[]{:S(2)}, u32[]{:S(2)}) collective-permute-start(bf16[208,512]{1,0:T(8,128)(2,1)S(1)} %slice.32), channel_id=1, source_target_pairs={{0,2},{2,4},{4,6},{6,0},{1,3},{3,5},{5,7},{7,1},{8,10},{10,12},{12... | collective-permute-start | bytes 638984 | tf_op jit(solution)/shard_map/ppermute | solution.py:27
  97.8 11.1 %collective-permute-start.16 = (bf16[384,512]{1,0:T(8,128)(2,1)S(1)}, bf16[384,512]{1,0:T(8,128)(2,1)S(1)}, u32[]{:S(2)}, u32[]{:S(2)}) collective-permute-start(bf16[384,512]{1,0:T(8,128)(2,1)S(1)} %get-tuple-element.55), channel_id=1, source_target_pairs={{0,16},{16,32},{32,48},{48,0},{1,17},{17,33},{33,49},{49,1},{2,18}... | collective-permute-start | bytes 1179656 | tf_op jit(solution)/shard_map/ppermute | solution.py:27
  98.0 10.8 %collective-permute-start.18 = (bf16[384,512]{1,0:T(8,128)(2,1)S(1)}, bf16[384,512]{1,0:T(8,128)(2,1)S(1)}, u32[]{:S(2)}, u32[]{:S(2)}) collective-permute-start(bf16[384,512]{1,0:T(8,128)(2,1)S(1)} %get-tuple-element.57), channel_id=1, source_target_pairs={{0,48},{16,0},{32,16},{48,32},{1,49},{17,1},{33,17},{49,33},{2,50}... | collective-permute-start | bytes 1179656 | tf_op jit(solution)/shard_map/ppermute | solution.py:27
  100.5 14.9 %collective-permute-start.17 = (bf16[384,512]{1,0:T(8,128)(2,1)S(1)}, bf16[384,512]{1,0:T(8,128)(2,1)S(1)}, u32[]{:S(2)}, u32[]{:S(2)}) collective-permute-start(bf16[384,512]{1,0:T(8,128)(2,1)S(1)} %get-tuple-element.56), channel_id=1, source_target_pairs={{0,32},{16,48},{32,0},{48,16},{1,33},{17,49},{33,1},{49,17},{2,34}... | collective-permute-start | bytes 1179656 | tf_op jit(solution)/shard_map/ppermute | solution.py:27
  115.5 32.0 %collective-permute-start.22 = (bf16[1024,512]{1,0:T(8,128)(2,1)S(1)}, bf16[1024,512]{1,0:T(8,128)(2,1)S(1)}, u32[]{:S(2)}, u32[]{:S(2)}) collective-permute-start(bf16[1024,512]{1,0:T(8,128)(2,1)S(1)} %pad_maximum_fusion), channel_id=1, source_target_pairs={{0,1},{1,0},{2,3},{3,2},{4,5},{5,4},{6,7},{7,6},{8,9},{9,8},{10,11... | collective-permute-start | bytes 3145736 | tf_op jit(solution)/shard_map/ppermute | solution.py:27
  119.3 15.0 %collective-permute-start.20 = (bf16[512,512]{1,0:T(8,128)(2,1)S(1)}, bf16[512,512]{1,0:T(8,128)(2,1)S(1)}, u32[]{:S(2)}, u32[]{:S(2)}) collective-permute-start(bf16[512,512]{1,0:T(8,128)(2,1)S(1)} %pad_maximum_fusion.2), channel_id=1, source_target_pairs={{0,64},{64,0},{1,65},{65,1},{2,66},{66,2},{3,67},{67,3},{4,68},{68... | collective-permute-start | bytes 1572872 | tf_op jit(solution)/shard_map/ppermute | solution.py:27
  122.2 17.7 %collective-permute-start.19 = (bf16[256,512]{1,0:T(8,128)(2,1)S(1)}, bf16[256,512]{1,0:T(8,128)(2,1)S(1)}, u32[]{:S(2)}, u32[]{:S(2)}) collective-permute-start(bf16[256,512]{1,0:T(8,128)(2,1)S(1)} %get-tuple-element.53.refs_4_), channel_id=1, source_target_pairs={{0,64},{64,0},{1,65},{65,1},{2,66},{66,2},{3,67},{67,3},{4,68},{68... | collective-permute-start | bytes 786440 | tf_op jit(solution)/shard_map/ppermute | solution.py:27
  122.3 23.2 %collective-permute-start.21 = (bf16[256,512]{1,0:T(8,128)(2,1)S(1)}, bf16[256,512]{1,0:T(8,128)(2,1)S(1)}, u32[]{:S(2)}, u32[]{:S(2)}) collective-permute-start(bf16[256,512]{1,0:T(8,128)(2,1)S(1)} %slice.38), channel_id=1, source_target_pairs={{0,64},{64,0},{1,65},{65,1},{2,66},{66,2},{3,67},{67,3},{4,68},{68... | collective-permute-start | bytes 786440 | tf_op jit(solution)/shard_map/ppermute | solution.py:27
  134.3 13.3 %collective-permute-start.24 = (bf16[512,512]{1,0:T(8,128)(2,1)S(1)}, bf16[512,512]{1,0:T(8,128)(2,1)S(1)}, u32[]{:S(2)}, u32[]{:S(2)}) collective-permute-start(bf16[512,512]{1,0:T(8,128)(2,1)S(1)} %collective-permute-done.20.refs_10_), channel_id=1, source_target_pairs={{0,1},{1,0},{2,3},{3,2},{4,5},{5,4},{6,7},{7,6},{8,9},{9,8},{10,11... | collective-permute-start | bytes 1572872 | tf_op jit(solution)/shard_map/ppermute | solution.py:27
  163.2 7.2 %collective-permute-start.27 = (bf16[128,512]{1,0:T(8,128)(2,1)}, bf16[128,512]{1,0:T(8,128)(2,1)S(1)}, u32[]{:S(2)}, u32[]{:S(2)}) collective-permute-start(bf16[128,512]{1,0:T(8,128)(2,1)} %get-tuple-element.60), channel_id=1, source_target_pairs={{0,32},{16,48},{32,0},{48,16},{1,33},{17,49},{33,1},{49,17},{2,34}... | collective-permute-start | bytes 393224 | tf_op jit(solution)/shard_map/ppermute | solution.py:27
  163.3 10.0 %collective-permute-start.28 = (bf16[128,512]{1,0:T(8,128)(2,1)S(1)}, bf16[128,512]{1,0:T(8,128)(2,1)S(1)}, u32[]{:S(2)}, u32[]{:S(2)}) collective-permute-start(bf16[128,512]{1,0:T(8,128)(2,1)S(1)} %get-tuple-element.61), channel_id=1, source_target_pairs={{0,16},{16,32},{32,48},{48,0},{1,17},{17,33},{33,49},{49,1},{2,18}... | collective-permute-start | bytes 393224 | tf_op jit(solution)/shard_map/ppermute | solution.py:27
  178.1 18.5 %collective-permute-start.29 = (bf16[224,512]{1,0:T(8,128)(2,1)}, bf16[224,512]{1,0:T(8,128)(2,1)S(1)}, u32[]{:S(2)}, u32[]{:S(2)}) collective-permute-start(bf16[224,512]{1,0:T(8,128)(2,1)} %get-tuple-element.65), channel_id=1, source_target_pairs={{0,8},{8,0},{1,9},{9,1},{2,10},{10,2},{3,11},{11,3},{4,12},{12,4},... | collective-permute-start | bytes 688136 | tf_op jit(solution)/shard_map/ppermute | solution.py:27
  183.0 13.7 %collective-permute-start.30 = (bf16[208,512]{1,0:T(8,128)(2,1)}, bf16[208,512]{1,0:T(8,128)(2,1)S(1)}, u32[]{:S(2)}, u32[]{:S(2)}) collective-permute-start(bf16[208,512]{1,0:T(8,128)(2,1)} %copy-done.21), channel_id=1, source_target_pairs={{0,2},{2,4},{4,6},{6,0},{1,3},{3,5},{5,7},{7,1},{8,10},{10,12},{12... | collective-permute-start | bytes 638984 | tf_op jit(solution)/shard_map/ppermute | solution.py:27
  183.0 13.6 %collective-permute-start.31 = (bf16[208,512]{1,0:T(8,128)(2,1)}, bf16[208,512]{1,0:T(8,128)(2,1)S(1)}, u32[]{:S(2)}, u32[]{:S(2)}) collective-permute-start(bf16[208,512]{1,0:T(8,128)(2,1)} %copy-done.20), channel_id=1, source_target_pairs={{0,6},{2,0},{4,2},{6,4},{1,7},{3,1},{5,3},{7,5},{8,14},{10,8},{12,... | collective-permute-start | bytes 638984 | tf_op jit(solution)/shard_map/ppermute | solution.py:27
  196.9 14.4 %collective-permute-start.32 = (bf16[640,512]{1,0:T(8,128)(2,1)S(1)}, bf16[640,512]{1,0:T(8,128)(2,1)S(1)}, u32[]{:S(2)}, u32[]{:S(2)}) collective-permute-start(bf16[640,512]{1,0:T(8,128)(2,1)S(1)} %get-tuple-element.70), channel_id=1, source_target_pairs={{0,6},{2,0},{4,2},{6,4},{1,7},{3,1},{5,3},{7,5},{8,14},{10,8},{12,... | collective-permute-start | bytes 1966088 | tf_op jit(solution)/shard_map/ppermute | solution.py:27
  196.9 14.4 %collective-permute-start.33 = (bf16[640,512]{1,0:T(8,128)(2,1)S(1)}, bf16[640,512]{1,0:T(8,128)(2,1)S(1)}, u32[]{:S(2)}, u32[]{:S(2)}) collective-permute-start(bf16[640,512]{1,0:T(8,128)(2,1)S(1)} %get-tuple-element.71), channel_id=1, source_target_pairs={{0,8},{8,0},{1,9},{9,1},{2,10},{10,2},{3,11},{11,3},{4,12},{12,4},... | collective-permute-start | bytes 1966088 | tf_op jit(solution)/shard_map/ppermute | solution.py:27
  197.0 15.6 %collective-permute-start.34 = (bf16[640,512]{1,0:T(8,128)(2,1)S(1)}, bf16[640,512]{1,0:T(8,128)(2,1)S(1)}, u32[]{:S(2)}, u32[]{:S(2)}) collective-permute-start(bf16[640,512]{1,0:T(8,128)(2,1)S(1)} %get-tuple-element.73), channel_id=1, source_target_pairs={{0,2},{2,4},{4,6},{6,0},{1,3},{3,5},{5,7},{7,1},{8,10},{10,12},{12... | collective-permute-start | bytes 1966088 | tf_op jit(solution)/shard_map/ppermute | solution.py:27
  198.4 28.3 %collective-permute-start.36 = (bf16[640,512]{1,0:T(8,128)(2,1)}, bf16[640,512]{1,0:T(8,128)(2,1)S(1)}, u32[]{:S(2)}, u32[]{:S(2)}) collective-permute-start(bf16[640,512]{1,0:T(8,128)(2,1)} %get-tuple-element.75), channel_id=1, source_target_pairs={{0,2},{2,4},{4,6},{6,0},{1,3},{3,5},{5,7},{7,1},{8,10},{10,12},{12... | collective-permute-start | bytes 1966088 | tf_op jit(solution)/shard_map/ppermute | solution.py:27
  213.7 13.0 %collective-permute-start.35 = (bf16[640,512]{1,0:T(8,128)(2,1)}, bf16[640,512]{1,0:T(8,128)(2,1)S(1)}, u32[]{:S(2)}, u32[]{:S(2)}) collective-permute-start(bf16[640,512]{1,0:T(8,128)(2,1)} %get-tuple-element.74), channel_id=1, source_target_pairs={{0,6},{2,0},{4,2},{6,4},{1,7},{3,1},{5,3},{7,5},{8,14},{10,8},{12,... | collective-permute-start | bytes 1966088 | tf_op jit(solution)/shard_map/ppermute | solution.py:27
  213.8 12.8 %collective-permute-start.37 = (bf16[640,512]{1,0:T(8,128)(2,1)S(1)}, bf16[640,512]{1,0:T(8,128)(2,1)S(1)}, u32[]{:S(2)}, u32[]{:S(2)}) collective-permute-start(bf16[640,512]{1,0:T(8,128)(2,1)S(1)} %get-tuple-element.76), channel_id=1, source_target_pairs={{0,8},{8,0},{1,9},{9,1},{2,10},{10,2},{3,11},{11,3},{4,12},{12,4},... | collective-permute-start | bytes 1966088 | tf_op jit(solution)/shard_map/ppermute | solution.py:27
  (34 other events, 188.3 us)

commit v5 on v4

--- a/solution.py
+++ b/solution.py
@@ -50,7 +50,7 @@
         in_specs=[pl.BlockSpec((parts, deep, inner), lambda i: (0, i, 0))],
         out_specs=pl.BlockSpec((parts * inner, deep), lambda i: (0, i)),
         out_shape=jax.ShapeDtypeStruct((parts * inner, features), weight.dtype),
-        compiler_params=pltpu.CompilerParams(vmem_limit_bytes=16 * MIB),
+        compiler_params=pltpu.CompilerParams(vmem_limit_bytes=56 * MIB),
         cost_estimate=pl.CostEstimate(
             flops=0, bytes_accessed=4 * weight.size, transcendentals=0
         ),
@@ -58,9 +58,30 @@
     )(weight)
 
 
-def prepare_kernel(own, other, modulation, gain, bias, own_out, other_out):
-    own_out[...] = own[...].T
-    other_out[...] = other[...].T
+def stand_kernel(*refs):
+    half = len(refs) // 2
+    for weight, out in zip(refs[:half], refs[half:]):
+        out[...] = weight[...].T
+
+
+def stand(*weights):
+    inner, features = weights[0].shape
+    deep = 1024
+    return pl.pallas_call(
+        stand_kernel,
+        grid=(features // deep,),
+        in_specs=[pl.BlockSpec((inner, deep), lambda i: (0, i))] * len(weights),
+        out_specs=[pl.BlockSpec((deep, inner), lambda i: (i, 0))] * len(weights),
+        out_shape=[jax.ShapeDtypeStruct((features, inner), w.dtype) for w in weights],
+        compiler_params=pltpu.CompilerParams(vmem_limit_bytes=56 * MIB),
+        cost_estimate=pl.CostEstimate(
+            flops=0, bytes_accessed=4 * features * inner * len(weights), transcendentals=0
+        ),
+        name="stand",
+    )(*weights)
+
+
+def spread_kernel(modulation, gain, bias):
     for row, out, add in ((1, gain, 1.0), (0, bias, 0.0)):
         for part in range(out.shape[0] // BLK):
             rows = slice(part * BLK, (part + 1) * BLK)
@@ -68,35 +89,21 @@
             out[rows, :] = jnp.broadcast_to(line, (BLK, BLK)).T
 
 
-def prepare(own, other, modulation):
-    inner, features = own.shape
-    deep = 512
+def spread(modulation):
+    features = modulation.shape[1]
+    deep = 1024
     return pl.pallas_call(
-        prepare_kernel,
+        spread_kernel,
         grid=(features // deep,),
-        in_specs=[
-            pl.BlockSpec((inner, deep), lambda i: (0, i)),
-            pl.BlockSpec((inner, deep), lambda i: (0, i)),
-            pl.BlockSpec((3, deep), lambda i: (0, i)),
-        ],
-        out_specs=[
-            pl.BlockSpec((deep, BLK), lambda i: (i, 0)),
-            pl.BlockSpec((deep, BLK), lambda i: (i, 0)),
-            pl.BlockSpec((deep, inner), lambda i: (i, 0)),
-            pl.BlockSpec((deep, inner), lambda i: (i, 0)),
-        ],
-        out_shape=[
-            jax.ShapeDtypeStruct((features, BLK), jnp.float32),
-            jax.ShapeDtypeStruct((features, BLK), jnp.float32),
-            jax.ShapeDtypeStruct((features, inner), jnp.bfloat16),
-            jax.ShapeDtypeStruct((features, inner), jnp.bfloat16),
-        ],
-        compiler_params=pltpu.CompilerParams(vmem_limit_bytes=16 * MIB),
+        in_specs=[pl.BlockSpec((3, deep), lambda i: (0, i))],
+        out_specs=[pl.BlockSpec((deep, BLK), lambda i: (i, 0))] * 2,
+        out_shape=[jax.ShapeDtypeStruct((features, BLK), jnp.float32)] * 2,
+        compiler_params=pltpu.CompilerParams(vmem_limit_bytes=56 * MIB),
         cost_estimate=pl.CostEstimate(
-            flops=0, bytes_accessed=12 * features * inner, transcendentals=0
-        ),
-        name="prepare",
-    )(own, other, modulation)
+            flops=0, bytes_accessed=8 * features * BLK, transcendentals=0
+        ),
+        name="spread",
+    )(modulation)
 
 
 def together(arrays, others=()):
@@ -185,7 +192,7 @@
             kv[BLK : 2 * BLK, :] = total[pl.ds(base + 4 * BLK, BLK), :].astype(jnp.bfloat16)
 
 
-def project(chips, heads, xs, own, other, gain, bias, after):
+def project(chips, heads, xs, own, other, gain, bias):
     outs, features = own.shape
     deep, count = xs[0].shape
     whole = lambda shape: pl.BlockSpec(shape, lambda k, *_: (0, 0))
@@ -200,8 +207,7 @@
             num_scalar_prefetch=2,
             grid=(features // deep // 2,),
             in_specs=[whole(x.shape) for x in xs]
-            + [*blocks, *blocks, whole(gain.shape), whole(bias.shape)]
-            + [pl.BlockSpec(memory_space=pl.ANY)] * len(after),
+            + [*blocks, *blocks, whole(gain.shape), whole(bias.shape)],
             out_specs=[whole(s) for s in shapes],
             scratch_shapes=[
                 pltpu.VMEM((features // deep // 2, 2 * deep, count), jnp.bfloat16),
@@ -209,14 +215,14 @@
             ],
         ),
         out_shape=[jax.ShapeDtypeStruct(s, jnp.bfloat16) for s in shapes],
-        compiler_params=pltpu.CompilerParams(vmem_limit_bytes=50 * MIB),
+        compiler_params=pltpu.CompilerParams(vmem_limit_bytes=56 * MIB),
         cost_estimate=pl.CostEstimate(
             flops=4 * outs * features * count,
             bytes_accessed=2 * features * (count + 2 * outs),
             transcendentals=0,
         ),
         name="project",
-    )(chips, heads, *xs, own, own, other, other, gain, bias, *after)
+    )(chips, heads, *xs, own, own, other, other, gain, bias)
 
 
 def attend_kernel(factor, unroll, plan, places, counts, first, owner, *refs):
@@ -350,7 +356,7 @@
             pltpu.VMEM((rows, BLK, BLK), jnp.float32),
             pltpu.SemaphoreType.DMA((len(plan),)),
         ],
-        compiler_params=pltpu.CompilerParams(vmem_limit_bytes=32 * MIB),
+        compiler_params=pltpu.CompilerParams(vmem_limit_bytes=56 * MIB),
         cost_estimate=pl.CostEstimate(
             flops=rows * BLK * most * BLK * BLK,
             bytes_accessed=4 * most * BLK * BLK,
@@ -407,7 +413,7 @@
             scratch_shapes=[pltpu.VMEM((2 * inner, count), jnp.bfloat16)],
         ),
         out_shape=[jax.ShapeDtypeStruct(s, jnp.bfloat16) for s in shapes],
-        compiler_params=pltpu.CompilerParams(vmem_limit_bytes=32 * MIB),
+        compiler_params=pltpu.CompilerParams(vmem_limit_bytes=56 * MIB),
         cost_estimate=pl.CostEstimate(
             flops=4 * steps * high * inner * count,
             bytes_accessed=2 * steps * high * (2 * inner + count),
@@ -446,7 +452,7 @@
         in_specs=[pl.BlockSpec(memory_space=pltpu.VMEM)] * len(arrays),
         out_specs=[pl.BlockSpec(memory_space=pltpu.VMEM)] * len(plan),
         out_shape=[jax.ShapeDtypeStruct(share.shape, share.dtype) for share in shares],
-        compiler_params=pltpu.CompilerParams(vmem_limit_bytes=24 * MIB),
+        compiler_params=pltpu.CompilerParams(vmem_limit_bytes=56 * MIB),
         cost_estimate=pl.CostEstimate(
             flops=0, bytes_accessed=8 * shares[0].size, transcendentals=0
         ),
@@ -505,6 +511,30 @@
     )
     mask_mine, mask_given = mine_and_given(block_mask, 1)
     mask_other = swap(mask_given, "core")
+
+    raw, *_ = lax.optimization_barrier((qkv_weight, own, mask_other))
+    own_weight, other_weight = turn(raw), turn(swap(raw, "core"))
+    gain, bias = spread(modulation)
+    places, xs = gather_tokens(own, (own_weight, gain, bias), (other_weight,))
+
+    chips = jnp.stack([chip(*place) for place in places]).astype(jnp.int32)
+    slots = [head_slot(steps) for steps in range(4)]
+    bases = jnp.stack([side * 3 * heads_here + slot for side, slot in slots]).astype(jnp.int32)
+    kv, query, *packed = project(chips, bases, xs, own_weight, other_weight, gain, bias)
+    two, one, three = [shift(packed[i - 1], "x", i) for i in (2, 1, 3)]
+    away_kv = swap(kv, "yh")
+    out_own, _ = lax.optimization_barrier((out_weight, kv))
+    leaving = stand(out_weight, swap(out_own, "core"))
+    one, three = together((one, three), (away_kv, *leaving))
+    both = jnp.concatenate([one[: 2 * BLK], three[: 2 * BLK]], axis=0)
+    away_both = swap(both, "yh")
+    (two,) = together((two,), (away_both,))
+    last = two[: 2 * BLK]
+    away = [away_kv, away_both, swap(last, "yh")]
+    near = jnp.concatenate([kv, both, last], axis=0)
+    arrays = [kv, query, one, two, three, *away, swap(near, "core"), *[swap(a, "core") for a in away]]
+
+    mask_mine, mask_other, _ = lax.optimization_barrier((mask_mine, mask_other, one))
     mask_heads = jnp.stack([mask_mine, mask_other])
     mask_rows = []
     for steps in range(4):
@@ -513,18 +543,12 @@
             mask_heads, (side, slot, 0, 0), (1, 1, *mask_heads.shape[2:])
         )[0, 0]
         mask_rows.append(shift(part, "x", steps) if steps else part)
-    raw, _ = lax.optimization_barrier((qkv_weight, own))
-    other_raw = swap(raw, "core")
-    own_weight, other_weight = turn(raw), turn(other_raw)
-    places, xs = gather_tokens(own, (own_weight, *mask_rows[1:]), (other_weight,))
-    out_raw, _ = lax.optimization_barrier((out_weight, xs[1]))
-    gain, bias, *leaving = prepare(out_weight, swap(out_raw, "core"), modulation)
-
     keep = jnp.concatenate(mask_rows, axis=0) != 0
     blocks = jnp.arange(keep.shape[1], dtype=jnp.int32)
     per_core = half // BLK
     piece, inside = blocks // per_core, blocks % per_core
-    from_core, from_y, from_x = core ^ (piece // 8), frame_y ^ (piece // 4 % 2), (frame_x - piece % 4) % 4
+    from_core, from_y = core ^ (piece // 8), frame_y ^ (piece // 4 % 2)
+    from_x = (frame_x - piece % 4) % 4
     origin = (from_y * 4 + from_x) * (2 * per_core) + from_core * per_core + inside
     same = origin[:, None] == blocks[None, :]
     keep = jnp.sum(jnp.where(same[None] & keep[:, None, :], 1, 0), axis=2)
@@ -533,20 +557,8 @@
     rank = jnp.sum(jnp.where(earlier[None], keep[:, None, :], 0), axis=2)
     chosen = (keep[:, None, :] != 0) & (rank[:, None, :] == blocks[None, :, None])
     listed = jnp.sum(jnp.where(chosen, blocks[None, None, :], 0), axis=2)
-
-    chips = jnp.stack([chip(*place) for place in places]).astype(jnp.int32)
-    slots = [head_slot(steps) for steps in range(4)]
-    bases = jnp.stack([side * 3 * heads_here + slot for side, slot in slots]).astype(jnp.int32)
     lists = (listed, counts, *pair_lists(counts, listed.shape[1]))
-    kv, query, *packed = project(
-        chips, bases, xs, own_weight, other_weight, gain, bias, (*lists, *leaving)
-    )
-    two, one, three = [shift(packed[i - 1], "x", i) for i in (2, 1, 3)]
-    both = jnp.concatenate([one[: 2 * BLK], three[: 2 * BLK]], axis=0)
-    last = two[: 2 * BLK]
-    away = [swap(part, "yh") for part in (kv, both, last)]
-    near = jnp.concatenate([kv, both, last], axis=0)
-    arrays = [kv, query, one, two, three, *away, swap(near, "core"), *[swap(a, "core") for a in away]]
+
     step = 2 * BLK
     plan = [("kv", 0, 0, 0), ("q", 0, 1, 0)]
     for steps, array in ((1, 2), (2, 3), (3, 4)):

time: 234 us -> 231 us (0.987)
  waiting for transfers between devices: 84.6 us -> 48.3 us
  Pallas kernels: 63.7 us -> 89 us
  starting transfers between devices: 54.8 us -> 63.6 us
  local copies, waits for them, and re-layouts: 26.2 us -> 19.3 us
  other arithmetic: 4.31 us -> 8.33 us
    ppermute x39, waiting for transfers between devices: 84.6 us -> 48.3 us  [shift(): lax.ppermute(value, axis, [(i, (i + steps) % count) for i in range(count)])]
    unnamed x54 -> x60, local copies, waits for them, and re-layouts: 24 us -> 8.91 us
    pallas_call x2, Pallas kernels: 11.6 us -> 21.3 us  [turn(): pl.pallas_call(turn_kernel, grid=(features // deep,), in_specs=[pl.BlockS...]
    ppermute x39, starting transfers between devices: 54.8 us -> 63.6 us  [shift(): lax.ppermute(value, axis, [(i, (i + steps) % count) for i in range(count)])]
    pallas_call x3, Pallas kernels: 1.61 us -> 9.18 us  [arrive(): pl.pallas_call(kernel, in_specs=[pl.BlockSpec(memory_space=pltpu.VMEM)] *...]
    pallas_call x2, Pallas kernels: 7.26 us -> 13 us  [leave(): pl.pallas_call(kernel, grid_spec=pltpu.PrefetchScalarGridSpec(num_scalar_...]
    pallas_call x1 -> x2, Pallas kernels: 7.04 us -> 11 us  [the longest x1 6.72 us: stand(): pl.pallas_call(stand_kernel, grid=(features // deep,), in_specs=[pl.Block...]
    pallas_call x1, Pallas kernels: 15.5 us -> 12.3 us  [attend(): pl.pallas_call(kernel, in_specs=[pl.BlockSpec(memory_space=pltpu.SMEM)] *...]
  transfers between devices with their start and end apart: 39 -> 39, of which waited for: 20 -> 14; matrix products, arithmetic and copies ran while one was open for 1% -> 6% of each run, Pallas kernels for 11% -> 20%
where the time goes in v5:
time: 231 us; the launch traced here: 229 us
  Pallas kernels  89 us (39%)
  starting transfers between devices  63.6 us (28%)
  waiting for transfers between devices  48.3 us (21%)
  local copies, waits for them, and re-layouts  19.3 us (8%)
  other arithmetic  8.33 us (4%)
    ppermute x39, starting transfers between devices, shift(): lax.ppermute(value, axis, [(i, (i + steps) % count) for i in range(count)])  63.6 us
    ppermute x39, waiting for transfers between devices, shift(): lax.ppermute(value, axis, [(i, (i + steps) % count) for i in range(count)])  48.3 us
    pallas_call x1, Pallas kernels, project(): pl.pallas_call(project_kernel, grid_spec=pltpu.PrefetchScalarGridSpec(num...  22.3 us
    pallas_call x2, Pallas kernels, turn(): pl.pallas_call(turn_kernel, grid=(features // deep,), in_specs=[pl.BlockS...  21.3 us
    pallas_call x2, Pallas kernels, leave(): pl.pallas_call(kernel, grid_spec=pltpu.PrefetchScalarGridSpec(num_scalar_...  13 us
    pallas_call x1, Pallas kernels, attend(): pl.pallas_call(kernel, in_specs=[pl.BlockSpec(memory_space=pltpu.SMEM)] *...  12.3 us
    pallas_call x3, Pallas kernels, arrive(): pl.pallas_call(kernel, in_specs=[pl.BlockSpec(memory_space=pltpu.VMEM)] *...  9.18 us
    unnamed x60, local copies, waits for them, and re-layouts  8.91 us
  transfers between devices with their start and end apart: 39, of which 14 were waited for; matrix products, arithmetic and copies ran while one was open for 6% of the time, Pallas kernels for 20%

profile of v5, /device:TPU:1, one launch (start us, length us, event | category | flops | bytes accessed | tf_op | source)
XLA Modules:
  0.0 229.0 jit_solution(15876864194327712816)
XLA Ops:
  7.8 2.1 collective-permute-start.2
  11.2 4.3 %spread.1 = (f32[5120,128]{1,0:T(8,128)}, f32[5120,128]{1,0:T(8,128)}) custom-call(f32[3,5120]{1,0:T(4,128)} %modulation.1), custom_call_target="tpu_custom_call" | custom-call | bytes 5242880 | tf_op jit(solution)/shard_map/spread/pallas_call | solution.py:95
  15.5 10.7 %turn.2.refs_10_.refs_11_ = bf16[768,5120]{1,0:T(8,128)(2,1)} custom-call(bf16[3,5120,256]{2,1,0:T(8,128)(2,1)} %weight), custom_call_target="tpu_custom_call" | custom-call | bytes 15728640 | tf_op jit(solution)/shard_map/turn/pallas_call | solution.py:47
  27.4 2.7 %collective-permute-start.7 = (bf16[640,512]{1,0:T(8,128)(2,1)}, bf16[640,512]{1,0:T(8,128)(2,1)}, u32[]{:S(2)}, u32[]{:S(2)}) collective-permute-start(bf16[640,512]{1,0:T(8,128)(2,1)} %collective-permute-done.3.refs_3_), channel_id=1, source_target_pairs={{0,6},{2,0},{4,2},{6,4},{1,7},{3,1},{5,3},{7,5},{8,14},{10,8},{12,... | collective-permute-start | bytes 1966088 | tf_op jit(solution)/shard_map/ppermute | solution.py:27
  30.1 3.1 %copy-done = bf16[3,5120,256]{2,1,0:T(8,128)(2,1)} copy-done((bf16[3,5120,256]{2,1,0:T(8,128)(2,1)}, bf16[3,5120,256]{2,1,0:T(8,128)(2,1)S(1)}, u32[]{:S(2)}) %copy-start) | copy-done | bytes 7864344
  33.2 10.6 %turn.3.refs_12_.refs_13_ = bf16[768,5120]{1,0:T(8,128)(2,1)} custom-call(bf16[3,5120,256]{2,1,0:T(8,128)(2,1)} %copy-done), custom_call_target="tpu_custom_call" | custom-call | bytes 15728640 | tf_op jit(solution)/shard_map/turn/pallas_call | solution.py:47
  46.8 2.4 %collective-permute-start.10 = (bf16[208,512]{1,0:T(8,128)(2,1)}, bf16[208,512]{1,0:T(8,128)(2,1)S(1)}, u32[]{:S(2)}, u32[]{:S(2)}) collective-permute-start(bf16[208,512]{1,0:T(8,128)(2,1)} %slice.29), channel_id=1, source_target_pairs={{0,6},{2,0},{4,2},{6,4},{1,7},{3,1},{5,3},{7,5},{8,14},{10,8},{12,... | collective-permute-start | bytes 638984 | tf_op jit(solution)/shard_map/ppermute | solution.py:27
  52.4 4.6 %collective-permute-done.11.refs_9_ = bf16[208,512]{1,0:T(8,128)(2,1)S(1)} collective-permute-done((bf16[208,512]{1,0:T(8,128)(2,1)}, bf16[208,512]{1,0:T(8,128)(2,1)S(1)}, u32[]{:S(2)}, u32[]{:S(2)}) %collective-permute-start.11) | collective-permute-done | bytes 213024 | tf_op jit(solution)/shard_map/ppermute | solution.py:27
  58.4 22.3 %project.1 = (bf16[256,512]{1,0:T(8,128)(2,1)}, bf16[128,512]{1,0:T(8,128)(2,1)}, bf16[384,512]{1,0:T(8,128)(2,1)}, bf16[384,512]{1,0:T(8,128)(2,1)}, bf16[384,512]{1,0:T(8,128)(2,1)}) custom-call(s32[8]{0:T(128)} %stack.91.chips, s32[4]{0:T(128)} %pad_add_fusion.1.heads, bf16[640,512]{1,0:T(8,128)(2,1)} %pad_maximum_fusion.1.refs_0_, ...), custom_call_target="tpu_custom_call" | custom-call | flops 8053063680 | bytes 20971520 | tf_op jit(solution)/shard_map/project/pallas_call | solution.py:204
  80.7 4.4 %collective-permute-start.12 = (bf16[256,5120]{1,0:T(8,128)(2,1)S(1)}, bf16[256,5120]{1,0:T(8,128)(2,1)}, u32[]{:S(2)}, u32[]{:S(2)}) collective-permute-start(bf16[256,5120]{1,0:T(8,128)(2,1)S(1)} %copy-done.1), channel_id=1, source_target_pairs={{0,1},{1,0},{2,3},{3,2},{4,5},{5,4},{6,7},{7,6},{8,9},{9,8},{10,11... | collective-permute-start | bytes 7864328 | tf_op jit(solution)/shard_map/ppermute | solution.py:27
  87.7 2.7 %collective-permute-start.15 = (bf16[256,512]{1,0:T(8,128)(2,1)}, bf16[256,512]{1,0:T(8,128)(2,1)}, u32[]{:S(2)}, u32[]{:S(2)}) collective-permute-start(bf16[256,512]{1,0:T(8,128)(2,1)} %get-tuple-element.55.refs_4_), channel_id=1, source_target_pairs={{0,64},{64,0},{1,65},{65,1},{2,66},{66,2},{3,67},{67,3},{4,68},{68... | collective-permute-start | bytes 786440 | tf_op jit(solution)/shard_map/ppermute | solution.py:27
  92.1 6.7 %stand.1 = (bf16[5120,256]{1,0:T(8,128)(2,1)}, bf16[5120,256]{1,0:T(8,128)(2,1)}) custom-call(bf16[256,5120]{1,0:T(8,128)(2,1)} %refs_0_.1, bf16[256,5120]{1,0:T(8,128)(2,1)} %collective-permute-done.12.refs_1_), custom_call_target="tpu_custom_call" | custom-call | bytes 10485760 | tf_op jit(solution)/shard_map/stand/pallas_call | solution.py:70
  101.1 2.9 %collective-permute-start.17 = (s32[4,64]{1,0:T(4,128)S(1)}, s32[4,64]{1,0:T(4,128)S(1)}, u32[]{:S(2)}, u32[]{:S(2)}) collective-permute-start(s32[4,64]{1,0:T(4,128)S(1)} %get-tuple-element.95), channel_id=1, source_target_pairs={{0,32},{16,48},{32,0},{48,16},{1,33},{17,49},{33,1},{49,17},{2,34}... | collective-permute-start | bytes 3080 | tf_op jit(solution)/shard_map/ppermute | solution.py:27
  104.6 10.0 %collective-permute-start.23 = (bf16[256,512]{1,0:T(8,128)(2,1)}, bf16[256,512]{1,0:T(8,128)(2,1)S(1)}, u32[]{:S(2)}, u32[]{:S(2)}) collective-permute-start(bf16[256,512]{1,0:T(8,128)(2,1)} %collective-permute-done.15.refs_9_), channel_id=1, source_target_pairs={{0,1},{1,0},{2,3},{3,2},{4,5},{5,4},{6,7},{7,6},{8,9},{9,8},{10,11... | collective-permute-start | bytes 786440 | tf_op jit(solution)/shard_map/ppermute | solution.py:27
  115.9 3.4 %collective-permute-start.22 = (bf16[1024,512]{1,0:T(8,128)(2,1)S(1)}, bf16[1024,512]{1,0:T(8,128)(2,1)S(1)}, u32[]{:S(2)}, u32[]{:S(2)}) collective-permute-start(bf16[1024,512]{1,0:T(8,128)(2,1)S(1)} %pad_maximum_fusion), channel_id=1, source_target_pairs={{0,1},{1,0},{2,3},{3,2},{4,5},{5,4},{6,7},{7,6},{8,9},{9,8},{10,11... | collective-permute-start | bytes 3145736 | tf_op jit(solution)/shard_map/ppermute | solution.py:27
  121.2 8.2 %collective-permute-done.21.refs_11_ = bf16[256,512]{1,0:T(8,128)(2,1)S(1)} collective-permute-done((bf16[256,512]{1,0:T(8,128)(2,1)S(1)}, bf16[256,512]{1,0:T(8,128)(2,1)S(1)}, u32[]{:S(2)}, u32[]{:S(2)}) %collective-permute-start.21) | collective-permute-done | bytes 262176 | tf_op jit(solution)/shard_map/ppermute | solution.py:27
  133.5 12.3 %attend.1 = (bf16[128,512]{1,0:T(8,128)(2,1)}, bf16[128,512]{1,0:T(8,128)(2,1)}, bf16[128,512]{1,0:T(8,128)(2,1)}, bf16[128,512]{1,0:T(8,128)(2,1)}) custom-call(s32[16,64]{1,0:T(8,128)} %select_reduce_fusion.2.refs_0_, s32[16]{0:T(128)} %copy-done.21, s32[17]{0:T(128)} %copy-done.29, s32[512]{0:T(512)} %select_reduce_fusion.4.refs_3_, ...), custom_call_target="tpu_custom_call" | custom-call | flops 2147483648 | bytes 4194304 | tf_op jit(solution)/shard_map/attend/pallas_call | solution.py:343
  145.9 2.1 collective-permute-start.26
  148.0 2.5 %collective-permute-start.27 = (bf16[128,512]{1,0:T(8,128)(2,1)}, bf16[128,512]{1,0:T(8,128)(2,1)S(1)}, u32[]{:S(2)}, u32[]{:S(2)}) collective-permute-start(bf16[128,512]{1,0:T(8,128)(2,1)} %get-tuple-element.70), channel_id=1, source_target_pairs={{0,32},{16,48},{32,0},{48,16},{1,33},{17,49},{33,1},{49,17},{2,34}... | collective-permute-start | bytes 393224 | tf_op jit(solution)/shard_map/ppermute | solution.py:27
  152.8 1.7 collective-permute-done.27.refs_6_
  154.5 3.1 %collective-permute-done.28.refs_7_ = bf16[128,512]{1,0:T(8,128)(2,1)S(1)} collective-permute-done((bf16[128,512]{1,0:T(8,128)(2,1)}, bf16[128,512]{1,0:T(8,128)(2,1)S(1)}, u32[]{:S(2)}, u32[]{:S(2)}) %collective-permute-start.28) | collective-permute-done | bytes 131104 | tf_op jit(solution)/shard_map/ppermute | solution.py:27
  158.2 3.2 %leave.3 = (bf16[224,512]{1,0:T(8,128)(2,1)}, bf16[208,512]{1,0:T(8,128)(2,1)}, bf16[208,512]{1,0:T(8,128)(2,1)}) custom-call(s32[1]{0:T(128)} %bitcast.12.refs_0_, s32[4]{0:T(128)} %pad_add_fusion.refs_1_, bf16[5120,256]{1,0:T(8,128)(2,1)} %get-tuple-element.57.refs_2_, bf16[5120,256]{1,0:T(8,128)(2,1)} %get-tuple-element.58.refs_3_, ...), custom_call_target="tpu_custom_call" | custom-call | flops 335544320 | bytes 1310720 | tf_op jit(solution)/shard_map/leave/pallas_call | solution.py:405
  161.4 2.8 %collective-permute-start.29 = (bf16[224,512]{1,0:T(8,128)(2,1)}, bf16[224,512]{1,0:T(8,128)(2,1)S(1)}, u32[]{:S(2)}, u32[]{:S(2)}) collective-permute-start(bf16[224,512]{1,0:T(8,128)(2,1)} %get-tuple-element.75), channel_id=1, source_target_pairs={{0,8},{8,0},{1,9},{9,1},{2,10},{10,2},{3,11},{11,3},{4,12},{12,4},... | collective-permute-start | bytes 688136 | tf_op jit(solution)/shard_map/ppermute | solution.py:27
  164.9 2.7 %collective-permute-start.31 = (bf16[208,512]{1,0:T(8,128)(2,1)}, bf16[208,512]{1,0:T(8,128)(2,1)S(1)}, u32[]{:S(2)}, u32[]{:S(2)}) collective-permute-start(bf16[208,512]{1,0:T(8,128)(2,1)} %get-tuple-element.79), channel_id=1, source_target_pairs={{0,6},{2,0},{4,2},{6,4},{1,7},{3,1},{5,3},{7,5},{8,14},{10,8},{12,... | collective-permute-start | bytes 638984 | tf_op jit(solution)/shard_map/ppermute | solution.py:27
  167.6 9.8 %leave.2 = (bf16[640,512]{1,0:T(8,128)(2,1)}, bf16[640,512]{1,0:T(8,128)(2,1)}, bf16[640,512]{1,0:T(8,128)(2,1)}, bf16[640,512]{1,0:T(8,128)(2,1)}, bf16[640,512...) custom-call(s32[7]{0:T(128)} %stack.84.refs_0_, s32[4]{0:T(128)} %pad_add_fusion.refs_1_, ...), custom_call_target="tpu_custom_call" | custom-call | flops 2348810240 | bytes 9175040 | tf_op jit(solution)/shard_map/leave/pallas_call | solution.py:405
  178.2 3.1 %arrive.3 = (bf16[640,512]{1,0:T(8,128)(2,1)}, bf16[640,512]{1,0:T(8,128)(2,1)}, bf16[640,512]{1,0:T(8,128)(2,1)}) custom-call(bf16[640,512]{1,0:T(8,128)(2,1)} %get-tuple-element.74.refs_0_, bf16[224,512]{1,0:T(8,128)(2,1)} %copy-done.10, bf16[640,512]{1,0:T(8,128)(2,1)} %get-tuple-element.76.refs_2_, bf16[208,512]{1,0:T(8,128)(2,1)} %copy-done.14, ...), custom_call_target="tpu_custom_call" | custom-call | bytes 2621440 | tf_op jit(solution)/shard_map/arrive/pallas_call | solution.py:450
  182.9 13.5 %collective-permute-done.32.refs_1_ = bf16[640,512]{1,0:T(8,128)(2,1)S(1)} collective-permute-done((bf16[640,512]{1,0:T(8,128)(2,1)}, bf16[640,512]{1,0:T(8,128)(2,1)S(1)}, u32[]{:S(2)}, u32[]{:S(2)}) %collective-permute-start.32) | collective-permute-done | bytes 655392 | tf_op jit(solution)/shard_map/ppermute | solution.py:27
  199.5 3.2 %arrive.4 = (bf16[640,512]{1,0:T(8,128)(2,1)}, bf16[640,512]{1,0:T(8,128)(2,1)}) custom-call(bf16[640,512]{1,0:T(8,128)(2,1)} %get-tuple-element.73.refs_0_, bf16[640,512]{1,0:T(8,128)(2,1)} %copy-done.4, bf16[640,512]{1,0:T(8,128)(2,1)} %copy-done.6, bf16[640,512]{1,0:T(8,128)(2,1)} %get-tuple-element.82.refs_3_, bf16[640,512]{1,0:T(8,128)(2,1)} %copy-done.8), custom_call_target="tpu_custom_call" | custom-call | bytes 2621440 | tf_op jit(solution)/shard_map/arrive/pallas_call | solution.py:450
  203.9 8.8 %collective-permute-done.36.refs_2_ = bf16[640,512]{1,0:T(8,128)(2,1)S(1)} collective-permute-done((bf16[640,512]{1,0:T(8,128)(2,1)S(1)}, bf16[640,512]{1,0:T(8,128)(2,1)S(1)}, u32[]{:S(2)}, u32[]{:S(2)}) %collective-permute-start.36) | collective-permute-done | bytes 655392 | tf_op jit(solution)/shard_map/ppermute | solution.py:27
  212.7 2.0 collective-permute-done.35.refs_1_
  217.0 2.9 %arrive.5 = bf16[640,512]{1,0:T(8,128)(2,1)} custom-call(bf16[640,512]{1,0:T(8,128)(2,1)} %get-tuple-element.72.refs_0_, bf16[640,512]{1,0:T(8,128)(2,1)} %copy-done.5, bf16[640,512]{1,0:T(8,128)(2,1)} %copy-done.3, bf16[640,512]{1,0:T(8,128)(2,1)} %copy-done.7), custom_call_target="tpu_custom_call" | custom-call | bytes 2621440 | tf_op jit(solution)/shard_map/arrive/pallas_call | solution.py:450
  220.8 4.7 %collective-permute-start.38 = (bf16[320,512]{1,0:T(8,128)(2,1)S(1)}, bf16[320,512]{1,0:T(8,128)(2,1)S(1)}, u32[]{:S(2)}, u32[]{:S(2)}) collective-permute-start(bf16[320,512]{1,0:T(8,128)(2,1)S(1)} %constant_dynamic-slice_fusion), channel_id=1, source_target_pairs={{0,1},{1,0},{2,3},{3,2},{4,5},{5,4},{6,7},{7,6},{8,9},{9,8},{10,11... | collective-permute-start | bytes 983048 | tf_op jit(solution)/shard_map/ppermute | solution.py:27
  (151 shorter events, 49.1 us)
Async XLA Ops:
  5.7 24.4 %collective-permute-start.8 = (bf16[3,5120,256]{2,1,0:T(8,128)(2,1)}, bf16[3,5120,256]{2,1,0:T(8,128)(2,1)S(1)}, u32[]{:S(2)}, u32[]{:S(2)}) collective-permute-start(bf16[3,5120,256]{2,1,0:T(8,128)(2,1)} %weight), channel_id=1, source_target_pairs={{0,1},{1,0},{2,3},{3,2},{4,5},{5,4},{6,7},{7,6},{8,9},{9,8},{10,11... | collective-permute-start | bytes 23592968 | tf_op jit(solution)/shard_map/ppermute | solution.py:27
  6.1 20.1 %collective-permute-start.1 = (bf16[640,512]{1,0:T(8,128)(2,1)}, bf16[640,512]{1,0:T(8,128)(2,1)}, u32[]{:S(2)}, u32[]{:S(2)}) collective-permute-start(bf16[640,512]{1,0:T(8,128)(2,1)} %pad_maximum_fusion.1.refs_0_), channel_id=1, source_target_pairs={{0,2},{2,4},{4,6},{6,0},{1,3},{3,5},{5,7},{7,1},{8,10},{10,12},{12... | collective-permute-start | bytes 1966088 | tf_op jit(solution)/shard_map/ppermute | solution.py:27
  7.8 18.4 %collective-permute-start.2 = (bf16[640,512]{1,0:T(8,128)(2,1)}, bf16[640,512]{1,0:T(8,128)(2,1)}, u32[]{:S(2)}, u32[]{:S(2)}) collective-permute-start(bf16[640,512]{1,0:T(8,128)(2,1)} %pad_maximum_fusion.1.refs_0_), channel_id=1, source_target_pairs={{0,6},{2,0},{4,2},{6,4},{1,7},{3,1},{5,3},{7,5},{8,14},{10,8},{12,... | collective-permute-start | bytes 1966088 | tf_op jit(solution)/shard_map/ppermute | solution.py:27
  9.9 16.3 %collective-permute-start.3 = (bf16[640,512]{1,0:T(8,128)(2,1)}, bf16[640,512]{1,0:T(8,128)(2,1)}, u32[]{:S(2)}, u32[]{:S(2)}) collective-permute-start(bf16[640,512]{1,0:T(8,128)(2,1)} %pad_maximum_fusion.1.refs_0_), channel_id=1, source_target_pairs={{0,8},{8,0},{1,9},{9,1},{2,10},{10,2},{3,11},{11,3},{4,12},{12,4},... | collective-permute-start | bytes 1966088 | tf_op jit(solution)/shard_map/ppermute | solution.py:27
  26.3 17.5 %collective-permute-start.5 = (bf16[640,512]{1,0:T(8,128)(2,1)}, bf16[640,512]{1,0:T(8,128)(2,1)}, u32[]{:S(2)}, u32[]{:S(2)}) collective-permute-start(bf16[640,512]{1,0:T(8,128)(2,1)} %collective-permute-done.1.refs_1_), channel_id=1, source_target_pairs={{0,2},{2,4},{4,6},{6,0},{1,3},{3,5},{5,7},{7,1},{8,10},{10,12},{12... | collective-permute-start | bytes 1966088 | tf_op jit(solution)/shard_map/ppermute | solution.py:27
  26.3 17.4 %collective-permute-start.6 = (bf16[640,512]{1,0:T(8,128)(2,1)}, bf16[640,512]{1,0:T(8,128)(2,1)}, u32[]{:S(2)}, u32[]{:S(2)}) collective-permute-start(bf16[640,512]{1,0:T(8,128)(2,1)} %collective-permute-done.1.refs_1_), channel_id=1, source_target_pairs={{0,8},{8,0},{1,9},{9,1},{2,10},{10,2},{3,11},{11,3},{4,12},{12,4},... | collective-permute-start | bytes 1966088 | tf_op jit(solution)/shard_map/ppermute | solution.py:27
  27.4 16.3 %collective-permute-start.7 = (bf16[640,512]{1,0:T(8,128)(2,1)}, bf16[640,512]{1,0:T(8,128)(2,1)}, u32[]{:S(2)}, u32[]{:S(2)}) collective-permute-start(bf16[640,512]{1,0:T(8,128)(2,1)} %collective-permute-done.3.refs_3_), channel_id=1, source_target_pairs={{0,6},{2,0},{4,2},{6,4},{1,7},{3,1},{5,3},{7,5},{8,14},{10,8},{12,... | collective-permute-start | bytes 1966088 | tf_op jit(solution)/shard_map/ppermute | solution.py:27
  44.7 12.3 %collective-permute-start.9 = (bf16[224,512]{1,0:T(8,128)(2,1)S(1)}, bf16[224,512]{1,0:T(8,128)(2,1)S(1)}, u32[]{:S(2)}, u32[]{:S(2)}) collective-permute-start(bf16[224,512]{1,0:T(8,128)(2,1)S(1)} %slice.28), channel_id=1, source_target_pairs={{0,8},{8,0},{1,9},{9,1},{2,10},{10,2},{3,11},{11,3},{4,12},{12,4},... | collective-permute-start | bytes 688136 | tf_op jit(solution)/shard_map/ppermute | solution.py:27
  80.7 11.4 %collective-permute-start.12 = (bf16[256,5120]{1,0:T(8,128)(2,1)S(1)}, bf16[256,5120]{1,0:T(8,128)(2,1)}, u32[]{:S(2)}, u32[]{:S(2)}) collective-permute-start(bf16[256,5120]{1,0:T(8,128)(2,1)S(1)} %copy-done.1), channel_id=1, source_target_pairs={{0,1},{1,0},{2,3},{3,2},{4,5},{5,4},{6,7},{7,6},{8,9},{9,8},{10,11... | collective-permute-start | bytes 7864328 | tf_op jit(solution)/shard_map/ppermute | solution.py:27
  85.0 13.8 %collective-permute-start.13 = (bf16[384,512]{1,0:T(8,128)(2,1)}, bf16[384,512]{1,0:T(8,128)(2,1)S(1)}, u32[]{:S(2)}, u32[]{:S(2)}) collective-permute-start(bf16[384,512]{1,0:T(8,128)(2,1)} %get-tuple-element.59), channel_id=1, source_target_pairs={{0,16},{16,32},{32,48},{48,0},{1,17},{17,33},{33,49},{49,1},{2,18}... | collective-permute-start | bytes 1179656 | tf_op jit(solution)/shard_map/ppermute | solution.py:27
  86.2 12.6 %collective-permute-start.14 = (bf16[384,512]{1,0:T(8,128)(2,1)}, bf16[384,512]{1,0:T(8,128)(2,1)S(1)}, u32[]{:S(2)}, u32[]{:S(2)}) collective-permute-start(bf16[384,512]{1,0:T(8,128)(2,1)} %get-tuple-element.60), channel_id=1, source_target_pairs={{0,48},{16,0},{32,16},{48,32},{1,49},{17,1},{33,17},{49,33},{2,50}... | collective-permute-start | bytes 1179656 | tf_op jit(solution)/shard_map/ppermute | solution.py:27
  87.7 11.1 %collective-permute-start.15 = (bf16[256,512]{1,0:T(8,128)(2,1)}, bf16[256,512]{1,0:T(8,128)(2,1)}, u32[]{:S(2)}, u32[]{:S(2)}) collective-permute-start(bf16[256,512]{1,0:T(8,128)(2,1)} %get-tuple-element.55.refs_4_), channel_id=1, source_target_pairs={{0,64},{64,0},{1,65},{65,1},{2,66},{66,2},{3,67},{67,3},{4,68},{68... | collective-permute-start | bytes 786440 | tf_op jit(solution)/shard_map/ppermute | solution.py:27
  90.4 24.1 %collective-permute-start.19 = (bf16[384,512]{1,0:T(8,128)(2,1)}, bf16[384,512]{1,0:T(8,128)(2,1)}, u32[]{:S(2)}, u32[]{:S(2)}) collective-permute-start(bf16[384,512]{1,0:T(8,128)(2,1)} %get-tuple-element.65), channel_id=1, source_target_pairs={{0,32},{16,48},{32,0},{48,16},{1,33},{17,49},{33,1},{49,17},{2,34}... | collective-permute-start | bytes 1179656 | tf_op jit(solution)/shard_map/ppermute | solution.py:27
  98.9 15.6 %collective-permute-start.20 = (bf16[512,512]{1,0:T(8,128)(2,1)S(1)}, bf16[512,512]{1,0:T(8,128)(2,1)S(1)}, u32[]{:S(2)}, u32[]{:S(2)}) collective-permute-start(bf16[512,512]{1,0:T(8,128)(2,1)S(1)} %pad_maximum_fusion.2), channel_id=1, source_target_pairs={{0,64},{64,0},{1,65},{65,1},{2,66},{66,2},{3,67},{67,3},{4,68},{68... | collective-permute-start | bytes 1572872 | tf_op jit(solution)/shard_map/ppermute | solution.py:27
  101.1 13.4 %collective-permute-start.17 = (s32[4,64]{1,0:T(4,128)S(1)}, s32[4,64]{1,0:T(4,128)S(1)}, u32[]{:S(2)}, u32[]{:S(2)}) collective-permute-start(s32[4,64]{1,0:T(4,128)S(1)} %get-tuple-element.95), channel_id=1, source_target_pairs={{0,32},{16,48},{32,0},{48,16},{1,33},{17,49},{33,1},{49,17},{2,34}... | collective-permute-start | bytes 3080 | tf_op jit(solution)/shard_map/ppermute | solution.py:27
  104.0 10.5 %collective-permute-start.18 = (s32[4,64]{1,0:T(4,128)S(1)}, s32[4,64]{1,0:T(4,128)S(1)}, u32[]{:S(2)}, u32[]{:S(2)}) collective-permute-start(s32[4,64]{1,0:T(4,128)S(1)} %get-tuple-element.96), channel_id=1, source_target_pairs={{0,48},{16,0},{32,16},{48,32},{1,49},{17,1},{33,17},{49,33},{2,50}... | collective-permute-start | bytes 3080 | tf_op jit(solution)/shard_map/ppermute | solution.py:27
  104.6 27.7 %collective-permute-start.23 = (bf16[256,512]{1,0:T(8,128)(2,1)}, bf16[256,512]{1,0:T(8,128)(2,1)S(1)}, u32[]{:S(2)}, u32[]{:S(2)}) collective-permute-start(bf16[256,512]{1,0:T(8,128)(2,1)} %collective-permute-done.15.refs_9_), channel_id=1, source_target_pairs={{0,1},{1,0},{2,3},{3,2},{4,5},{5,4},{6,7},{7,6},{8,9},{9,8},{10,11... | collective-permute-start | bytes 786440 | tf_op jit(solution)/shard_map/ppermute | solution.py:27
  115.9 16.4 %collective-permute-start.22 = (bf16[1024,512]{1,0:T(8,128)(2,1)S(1)}, bf16[1024,512]{1,0:T(8,128)(2,1)S(1)}, u32[]{:S(2)}, u32[]{:S(2)}) collective-permute-start(bf16[1024,512]{1,0:T(8,128)(2,1)S(1)} %pad_maximum_fusion), channel_id=1, source_target_pairs={{0,1},{1,0},{2,3},{3,2},{4,5},{5,4},{6,7},{7,6},{8,9},{9,8},{10,11... | collective-permute-start | bytes 3145736 | tf_op jit(solution)/shard_map/ppermute | solution.py:27
  119.9 9.5 %collective-permute-start.21 = (bf16[256,512]{1,0:T(8,128)(2,1)S(1)}, bf16[256,512]{1,0:T(8,128)(2,1)S(1)}, u32[]{:S(2)}, u32[]{:S(2)}) collective-permute-start(bf16[256,512]{1,0:T(8,128)(2,1)S(1)} %slice.35), channel_id=1, source_target_pairs={{0,64},{64,0},{1,65},{65,1},{2,66},{66,2},{3,67},{67,3},{4,68},{68... | collective-permute-start | bytes 786440 | tf_op jit(solution)/shard_map/ppermute | solution.py:27
  120.9 11.3 %collective-permute-start.24 = (bf16[512,512]{1,0:T(8,128)(2,1)}, bf16[512,512]{1,0:T(8,128)(2,1)S(1)}, u32[]{:S(2)}, u32[]{:S(2)}) collective-permute-start(bf16[512,512]{1,0:T(8,128)(2,1)} %copy-done.24), channel_id=1, source_target_pairs={{0,1},{1,0},{2,3},{3,2},{4,5},{5,4},{6,7},{7,6},{8,9},{9,8},{10,11... | collective-permute-start | bytes 1572872 | tf_op jit(solution)/shard_map/ppermute | solution.py:27
  145.9 6.9 %collective-permute-start.26 = (bf16[128,512]{1,0:T(8,128)(2,1)}, bf16[128,512]{1,0:T(8,128)(2,1)S(1)}, u32[]{:S(2)}, u32[]{:S(2)}) collective-permute-start(bf16[128,512]{1,0:T(8,128)(2,1)} %get-tuple-element.69), channel_id=1, source_target_pairs={{0,48},{16,0},{32,16},{48,32},{1,49},{17,1},{33,17},{49,33},{2,50}... | collective-permute-start | bytes 393224 | tf_op jit(solution)/shard_map/ppermute | solution.py:27
  148.0 6.5 %collective-permute-start.27 = (bf16[128,512]{1,0:T(8,128)(2,1)}, bf16[128,512]{1,0:T(8,128)(2,1)S(1)}, u32[]{:S(2)}, u32[]{:S(2)}) collective-permute-start(bf16[128,512]{1,0:T(8,128)(2,1)} %get-tuple-element.70), channel_id=1, source_target_pairs={{0,32},{16,48},{32,0},{48,16},{1,33},{17,49},{33,1},{49,17},{2,34}... | collective-permute-start | bytes 393224 | tf_op jit(solution)/shard_map/ppermute | solution.py:27
  150.5 7.1 %collective-permute-start.28 = (bf16[128,512]{1,0:T(8,128)(2,1)}, bf16[128,512]{1,0:T(8,128)(2,1)S(1)}, u32[]{:S(2)}, u32[]{:S(2)}) collective-permute-start(bf16[128,512]{1,0:T(8,128)(2,1)} %get-tuple-element.71), channel_id=1, source_target_pairs={{0,16},{16,32},{32,48},{48,0},{1,17},{17,33},{33,49},{49,1},{2,18}... | collective-permute-start | bytes 393224 | tf_op jit(solution)/shard_map/ppermute | solution.py:27
  161.4 16.0 %collective-permute-start.29 = (bf16[224,512]{1,0:T(8,128)(2,1)}, bf16[224,512]{1,0:T(8,128)(2,1)S(1)}, u32[]{:S(2)}, u32[]{:S(2)}) collective-permute-start(bf16[224,512]{1,0:T(8,128)(2,1)} %get-tuple-element.75), channel_id=1, source_target_pairs={{0,8},{8,0},{1,9},{9,1},{2,10},{10,2},{3,11},{11,3},{4,12},{12,4},... | collective-permute-start | bytes 688136 | tf_op jit(solution)/shard_map/ppermute | solution.py:27
  164.9 12.5 %collective-permute-start.30 = (bf16[208,512]{1,0:T(8,128)(2,1)}, bf16[208,512]{1,0:T(8,128)(2,1)S(1)}, u32[]{:S(2)}, u32[]{:S(2)}) collective-permute-start(bf16[208,512]{1,0:T(8,128)(2,1)} %get-tuple-element.77), channel_id=1, source_target_pairs={{0,2},{2,4},{4,6},{6,0},{1,3},{3,5},{5,7},{7,1},{8,10},{10,12},{12... | collective-permute-start | bytes 638984 | tf_op jit(solution)/shard_map/ppermute | solution.py:27
  164.9 12.5 %collective-permute-start.31 = (bf16[208,512]{1,0:T(8,128)(2,1)}, bf16[208,512]{1,0:T(8,128)(2,1)S(1)}, u32[]{:S(2)}, u32[]{:S(2)}) collective-permute-start(bf16[208,512]{1,0:T(8,128)(2,1)} %get-tuple-element.79), channel_id=1, source_target_pairs={{0,6},{2,0},{4,2},{6,4},{1,7},{3,1},{5,3},{7,5},{8,14},{10,8},{12,... | collective-permute-start | bytes 638984 | tf_op jit(solution)/shard_map/ppermute | solution.py:27
  181.4 15.1 %collective-permute-start.32 = (bf16[640,512]{1,0:T(8,128)(2,1)}, bf16[640,512]{1,0:T(8,128)(2,1)S(1)}, u32[]{:S(2)}, u32[]{:S(2)}) collective-permute-start(bf16[640,512]{1,0:T(8,128)(2,1)} %get-tuple-element.80), channel_id=1, source_target_pairs={{0,6},{2,0},{4,2},{6,4},{1,7},{3,1},{5,3},{7,5},{8,14},{10,8},{12,... | collective-permute-start | bytes 1966088 | tf_op jit(solution)/shard_map/ppermute | solution.py:27
  182.5 14.9 %collective-permute-start.33 = (bf16[640,512]{1,0:T(8,128)(2,1)}, bf16[640,512]{1,0:T(8,128)(2,1)S(1)}, u32[]{:S(2)}, u32[]{:S(2)}) collective-permute-start(bf16[640,512]{1,0:T(8,128)(2,1)} %get-tuple-element.81), channel_id=1, source_target_pairs={{0,8},{8,0},{1,9},{9,1},{2,10},{10,2},{3,11},{11,3},{4,12},{12,4},... | collective-permute-start | bytes 1966088 | tf_op jit(solution)/shard_map/ppermute | solution.py:27
  182.5 16.2 %collective-permute-start.34 = (bf16[640,512]{1,0:T(8,128)(2,1)}, bf16[640,512]{1,0:T(8,128)(2,1)S(1)}, u32[]{:S(2)}, u32[]{:S(2)}) collective-permute-start(bf16[640,512]{1,0:T(8,128)(2,1)} %get-tuple-element.83), channel_id=1, source_target_pairs={{0,2},{2,4},{4,6},{6,0},{1,3},{3,5},{5,7},{7,1},{8,10},{10,12},{12... | collective-permute-start | bytes 1966088 | tf_op jit(solution)/shard_map/ppermute | solution.py:27
  182.8 29.9 %collective-permute-start.36 = (bf16[640,512]{1,0:T(8,128)(2,1)S(1)}, bf16[640,512]{1,0:T(8,128)(2,1)S(1)}, u32[]{:S(2)}, u32[]{:S(2)}) collective-permute-start(bf16[640,512]{1,0:T(8,128)(2,1)S(1)} %copy-done.23), channel_id=1, source_target_pairs={{0,2},{2,4},{4,6},{6,0},{1,3},{3,5},{5,7},{7,1},{8,10},{10,12},{12... | collective-permute-start | bytes 1966088 | tf_op jit(solution)/shard_map/ppermute | solution.py:27
  202.7 12.0 %collective-permute-start.35 = (bf16[640,512]{1,0:T(8,128)(2,1)}, bf16[640,512]{1,0:T(8,128)(2,1)S(1)}, u32[]{:S(2)}, u32[]{:S(2)}) collective-permute-start(bf16[640,512]{1,0:T(8,128)(2,1)} %get-tuple-element.84), channel_id=1, source_target_pairs={{0,6},{2,0},{4,2},{6,4},{1,7},{3,1},{5,3},{7,5},{8,14},{10,8},{12,... | collective-permute-start | bytes 1966088 | tf_op jit(solution)/shard_map/ppermute | solution.py:27
  203.4 12.7 %collective-permute-start.37 = (bf16[640,512]{1,0:T(8,128)(2,1)}, bf16[640,512]{1,0:T(8,128)(2,1)S(1)}, u32[]{:S(2)}, u32[]{:S(2)}) collective-permute-start(bf16[640,512]{1,0:T(8,128)(2,1)} %get-tuple-element.86), channel_id=1, source_target_pairs={{0,8},{8,0},{1,9},{9,1},{2,10},{10,2},{3,11},{11,3},{4,12},{12,4},... | collective-permute-start | bytes 1966088 | tf_op jit(solution)/shard_map/ppermute | solution.py:27
  (37 other events, 187.3 us)

commit v6 on v5

--- a/solution.py
+++ b/solution.py
@@ -16,7 +16,7 @@
 HEAD = ("yl", "z", "core")
 MIB = 1 << 20
 PAIRS = 8
-CUTS = ((0, 224), (224, 432), (432, 640))
+CUTS = ((0, 256), (256, 512), (512, 640))
 
 
 DEEP = CUTS[-1][1]
@@ -31,150 +31,87 @@
     return shift(value, axis, 1)
 
 
-def tile_of(rows):
-    return {640: 128, 224: 112}.get(rows, rows)
-
-
-def turn_kernel(weight, out):
-    inner = weight.shape[2]
-    for part in range(weight.shape[0]):
-        out[part * inner : (part + 1) * inner, :] = weight[part].T
-
-
-def turn(weight):
-    parts, features, inner = weight.shape
-    deep = 512
+def lay_kernel(core, mine, other, out):
+    first = core[0] == 0
+    mine, other = mine[...].astype(jnp.float32), other[...].astype(jnp.float32)
+    half = mine.shape[0]
+    upper = jnp.where(first, mine, other)
+    lower = jnp.where(first, other, mine)
+    out[...] = jnp.concatenate([upper, lower], axis=0).T.astype(out.dtype)
+
+
+def lay(core, mine, other):
+    half, count = mine.shape
     return pl.pallas_call(
-        turn_kernel,
-        grid=(features // deep,),
-        in_specs=[pl.BlockSpec((parts, deep, inner), lambda i: (0, i, 0))],
-        out_specs=pl.BlockSpec((parts * inner, deep), lambda i: (0, i)),
-        out_shape=jax.ShapeDtypeStruct((parts * inner, features), weight.dtype),
-        compiler_params=pltpu.CompilerParams(vmem_limit_bytes=56 * MIB),
+        lay_kernel,
+        in_specs=[pl.BlockSpec(memory_space=pltpu.SMEM)]
+        + [pl.BlockSpec(memory_space=pltpu.VMEM)] * 2,
+        out_specs=pl.BlockSpec(memory_space=pltpu.VMEM),
+        out_shape=jax.ShapeDtypeStruct((count, 2 * half), mine.dtype),
+        compiler_params=pltpu.CompilerParams(vmem_limit_bytes=12 * MIB),
         cost_estimate=pl.CostEstimate(
-            flops=0, bytes_accessed=4 * weight.size, transcendentals=0
-        ),
-        name="turn",
-    )(weight)
-
-
-def stand_kernel(*refs):
-    half = len(refs) // 2
-    for weight, out in zip(refs[:half], refs[half:]):
-        out[...] = weight[...].T
-
-
-def stand(*weights):
-    inner, features = weights[0].shape
-    deep = 1024
-    return pl.pallas_call(
-        stand_kernel,
-        grid=(features // deep,),
-        in_specs=[pl.BlockSpec((inner, deep), lambda i: (0, i))] * len(weights),
-        out_specs=[pl.BlockSpec((deep, inner), lambda i: (i, 0))] * len(weights),
-        out_shape=[jax.ShapeDtypeStruct((features, inner), w.dtype) for w in weights],
-        compiler_params=pltpu.CompilerParams(vmem_limit_bytes=56 * MIB),
-        cost_estimate=pl.CostEstimate(
-            flops=0, bytes_accessed=4 * features * inner * len(weights), transcendentals=0
-        ),
-        name="stand",
-    )(*weights)
-
-
-def spread_kernel(modulation, gain, bias):
-    for row, out, add in ((1, gain, 1.0), (0, bias, 0.0)):
-        for part in range(out.shape[0] // BLK):
-            rows = slice(part * BLK, (part + 1) * BLK)
-            line = modulation[row : row + 1, rows] + add
-            out[rows, :] = jnp.broadcast_to(line, (BLK, BLK)).T
-
-
-def spread(modulation):
-    features = modulation.shape[1]
-    deep = 1024
-    return pl.pallas_call(
-        spread_kernel,
-        grid=(features // deep,),
-        in_specs=[pl.BlockSpec((3, deep), lambda i: (0, i))],
-        out_specs=[pl.BlockSpec((deep, BLK), lambda i: (i, 0))] * 2,
-        out_shape=[jax.ShapeDtypeStruct((features, BLK), jnp.float32)] * 2,
-        compiler_params=pltpu.CompilerParams(vmem_limit_bytes=56 * MIB),
-        cost_estimate=pl.CostEstimate(
-            flops=0, bytes_accessed=8 * features * BLK, transcendentals=0
-        ),
-        name="spread",
-    )(modulation)
+            flops=0, bytes_accessed=8 * half * count, transcendentals=0
+        ),
+        name="lay",
+    )(jnp.reshape(core, (1,)).astype(jnp.int32), mine, other)
 
 
 def together(arrays, others=()):
     return lax.optimization_barrier((*arrays, *others))[: len(arrays)]
 
 
-def project_kernel(
-    chips, heads, *refs
-):
-    xs, weights, (gain, bias), rest = refs[:10], refs[10:14], refs[14:16], refs[16:]
-    (kv0, q0, *packed), (normed, total) = rest[-7:-2], rest[-2:]
+ROWS = 32
+
+
+def project_kernel(chips, heads, *refs):
+    xs, weights, modulation, rest = refs[:10], refs[10:14], refs[14], refs[15:]
+    (kv0, q0, *packed), (normed, total) = rest[:-2], rest[-2:]
     step = pl.program_id(0)
     features = 8 * DEEP
-    count = normed.shape[2]
+    count = normed.shape[1]
     lay = [(piece, 0, x) for piece, x in enumerate(xs[:7])]
     lay += [(7, cut[0], x) for cut, x in zip(CUTS, xs[7:])]
-
-    def fold(values):
-        return jnp.sum(values.reshape(values.shape[0] // 8, 8, count), axis=0)
+    tiles = [
+        (piece, first + at, x, at) for piece, first, x in lay for at in range(0, x.shape[1], BLK)
+    ]
 
     @pl.when(step == 0)
     def _():
         total[...] = jnp.zeros_like(total)
-        summed = jnp.zeros((8, count), jnp.float32)
-        for _, _, x in lay:
-            tile = tile_of(x.shape[0])
-
-            def add(i, state, x=x, tile=tile):
-                wide = x[pl.ds(pl.multiple_of(i * tile, 16), tile), :].astype(jnp.float32)
-                return state + fold(wide)
-
-            summed = lax.fori_loop(0, x.shape[0] // tile, add, summed)
-        center = jnp.sum(summed, axis=0, keepdims=True) / features
-        summed = jnp.zeros((8, count), jnp.float32)
-        for _, _, x in lay:
-            tile = tile_of(x.shape[0])
-
-            def square(i, state, x=x, tile=tile):
-                wide = x[pl.ds(pl.multiple_of(i * tile, 16), tile), :].astype(jnp.float32)
-                return state + fold(jnp.square(wide - center))
-
-            summed = lax.fori_loop(0, x.shape[0] // tile, square, summed)
-        rate = lax.rsqrt(jnp.sum(summed, axis=0, keepdims=True) / features + EPSILON)
-        for piece, first, x in lay:
-            tile = tile_of(x.shape[0])
-
-            def norm(i, _, x=x, tile=tile, piece=piece, first=first):
-                start = pl.multiple_of(i * tile, 16)
-                row = pl.multiple_of(chips[piece] * DEEP + first + start, 16)
-                part_gain = gain[pl.ds(row, tile), :]
-                part_bias = bias[pl.ds(row, tile), :]
-                for part in range(count // BLK):
-                    columns = slice(part * BLK, (part + 1) * BLK)
-                    wide = x[pl.ds(start, tile), columns].astype(jnp.float32)
-                    value = (wide - center[:, columns]) * rate[:, columns] * part_gain + part_bias
-                    normed[
-                        piece // 2,
-                        pl.ds(pl.multiple_of(piece % 2 * DEEP + first + start, 16), tile),
-                        columns,
-                    ] = value.astype(jnp.bfloat16)
-                return 0
-
-            lax.fori_loop(0, x.shape[0] // tile, norm, 0)
+
+        def norm(i, _):
+            rows = pl.ds(pl.multiple_of(i * ROWS, ROWS), ROWS)
+
+            def load(x, at):
+                return x[rows, at : at + BLK].astype(jnp.float32)
+
+            summed = jnp.zeros((ROWS, BLK), jnp.float32)
+            for _, _, x, at in tiles:
+                summed = summed + load(x, at)
+            center = jnp.sum(summed, axis=1, keepdims=True) / features
+            center = jnp.broadcast_to(center, (ROWS, BLK))
+            summed = jnp.zeros((ROWS, BLK), jnp.float32)
+            for _, _, x, at in tiles:
+                summed = summed + jnp.square(load(x, at) - center)
+            spread = jnp.sum(summed, axis=1, keepdims=True) / features
+            rate = jnp.broadcast_to(lax.rsqrt(spread + EPSILON), (ROWS, BLK))
+            for piece, first, x, at in tiles:
+                place = pl.ds(pl.multiple_of(chips[piece] * DEEP + first, BLK), BLK)
+                gain = 1.0 + modulation[1:2, place]
+                value = (load(x, at) - center) * rate * gain + modulation[0:1, place]
+                column = piece % 2 * DEEP + first
+                normed[piece // 2, rows, column : column + BLK] = value.astype(jnp.bfloat16)
+            return 0
+
+        lax.fori_loop(0, count // ROWS, norm, 0)
 
     held = normed[step]
-    outs = total.shape[0] // 2
     for side in range(2):
-        weight = jnp.concatenate([w[...] for w in weights[2 * side : 2 * side + 2]], axis=1)
-        total[side * outs : (side + 1) * outs] += jnp.dot(
-            weight, held, preferred_element_type=jnp.float32
-        )
+        for part in range(3):
+            weight = jnp.concatenate([w[part] for w in weights[2 * side : 2 * side + 2]], axis=0)
+            made = jnp.dot(held, weight, preferred_element_type=jnp.float32)
+            for slot in range(2):
+                total[side * 6 + part * 2 + slot] += made[:, slot * BLK : (slot + 1) * BLK]
 
     @pl.when(step == pl.num_programs(0) - 1)
     def _():
@@ -183,21 +120,21 @@
                 kv, q = packed[index - 1], packed[index - 1].at[2 * BLK :]
             else:
                 kv, q = kv0, q0
-            base = pl.multiple_of(heads[index] * BLK, BLK)
-            q[...] = total[pl.ds(base, BLK), :].astype(jnp.bfloat16)
-            keys = total[pl.ds(base + 2 * BLK, BLK), :]
+            base = heads[index]
+            q[...] = total[base].T.astype(jnp.bfloat16)
+            keys = total[base + 2]
             for part in range(count // BLK):
-                columns = slice(part * BLK, (part + 1) * BLK)
-                kv[:BLK, columns] = keys[:, columns].T.astype(jnp.bfloat16)
-            kv[BLK : 2 * BLK, :] = total[pl.ds(base + 4 * BLK, BLK), :].astype(jnp.bfloat16)
-
-
-def project(chips, heads, xs, own, other, gain, bias):
-    outs, features = own.shape
-    deep, count = xs[0].shape
+                rows = slice(part * BLK, (part + 1) * BLK)
+                kv[:BLK, rows] = keys[rows].astype(jnp.bfloat16)
+            kv[BLK : 2 * BLK, :] = total[base + 4].T.astype(jnp.bfloat16)
+
+
+def project(chips, heads, xs, own, other, modulation):
+    parts, features, inner = own.shape
+    count, deep = xs[0].shape
     whole = lambda shape: pl.BlockSpec(shape, lambda k, *_: (0, 0))
     blocks = [
-        pl.BlockSpec((outs, deep), lambda k, chips, heads, i=i: (0, chips[2 * k + i]))
+        pl.BlockSpec((parts, deep, inner), lambda k, chips, heads, i=i: (0, chips[2 * k + i], 0))
         for i in range(2)
     ]
     shapes = [(2 * BLK, count), (BLK, count)] + [(3 * BLK, count)] * 3
@@ -207,22 +144,22 @@
             num_scalar_prefetch=2,
             grid=(features // deep // 2,),
             in_specs=[whole(x.shape) for x in xs]
-            + [*blocks, *blocks, whole(gain.shape), whole(bias.shape)],
+            + [*blocks, *blocks, whole(modulation.shape)],
             out_specs=[whole(s) for s in shapes],
             scratch_shapes=[
-                pltpu.VMEM((features // deep // 2, 2 * deep, count), jnp.bfloat16),
-                pltpu.VMEM((2 * outs, count), jnp.float32),
+                pltpu.VMEM((features // deep // 2, count, 2 * deep), jnp.bfloat16),
+                pltpu.VMEM((2 * parts * inner // BLK, count, BLK), jnp.float32),
             ],
         ),
         out_shape=[jax.ShapeDtypeStruct(s, jnp.bfloat16) for s in shapes],
-        compiler_params=pltpu.CompilerParams(vmem_limit_bytes=56 * MIB),
+        compiler_params=pltpu.CompilerParams(vmem_limit_bytes=44 * MIB),
         cost_estimate=pl.CostEstimate(
-            flops=4 * outs * features * count,
-            bytes_accessed=2 * features * (count + 2 * outs),
+            flops=4 * parts * inner * features * count,
+            bytes_accessed=2 * features * (count + 2 * parts * inner),
             transcendentals=0,
         ),
         name="project",
-    )(chips, heads, *xs, own, own, other, other, gain, bias)
+    )(chips, heads, *xs, own, own, other, other, modulation)
 
 
 def attend_kernel(factor, unroll, plan, places, counts, first, owner, *refs):
@@ -319,7 +256,8 @@
         for part in range(per_piece):
             row = index * per_piece + part
             total = jnp.sum(totals[row], axis=0, keepdims=True)
-            out[:, part * BLK : (part + 1) * BLK] = (sums[row] / total).astype(jnp.bfloat16)
+            value = (sums[row] / total).T.astype(jnp.bfloat16)
+            out[part * BLK : (part + 1) * BLK, :] = value
 
 
 def pair_lists(counts, most):
@@ -345,7 +283,7 @@
         in_specs=[pl.BlockSpec(memory_space=pltpu.SMEM)] * len(lists)
         + [pl.BlockSpec(memory_space=pl.ANY)] * len(arrays),
         out_specs=[pl.BlockSpec(memory_space=pltpu.VMEM)] * asking,
-        out_shape=[jax.ShapeDtypeStruct(shape, jnp.bfloat16)] * asking,
+        out_shape=[jax.ShapeDtypeStruct((count, BLK), jnp.bfloat16)] * asking,
         scratch_shapes=[
             pltpu.VMEM((pieces, 2 * BLK, count), jnp.bfloat16),
             pltpu.VMEM((asking, *shape), jnp.bfloat16),
@@ -356,7 +294,7 @@
             pltpu.VMEM((rows, BLK, BLK), jnp.float32),
             pltpu.SemaphoreType.DMA((len(plan),)),
         ],
-        compiler_params=pltpu.CompilerParams(vmem_limit_bytes=56 * MIB),
+        compiler_params=pltpu.CompilerParams(vmem_limit_bytes=32 * MIB),
         cost_estimate=pl.CostEstimate(
             flops=rows * BLK * most * BLK * BLK,
             bytes_accessed=4 * most * BLK * BLK,
@@ -366,38 +304,36 @@
     )(*lists, *arrays)
 
 
-def leave_kernel(plan, chips, columns, *refs):
-    weights, heads, rest, ordered = refs[:2], refs[2:6], refs[6:-1], refs[-1]
+def leave_kernel(plan, chips, columns, own, other, *refs):
+    heads, outs, ordered = refs[:4], list(refs[4:-1]), refs[-1]
     step = pl.program_id(0)
 
     @pl.when(step == 0)
     def _():
         for index, head in enumerate(heads):
-            ordered[pl.ds(pl.multiple_of(columns[index] * BLK, BLK), BLK), :] = head[...]
+            ordered[columns[index]] = head[...]
 
     summed = jnp.dot(
-        jnp.concatenate([weight[...] for weight in weights], axis=1),
-        ordered[...],
+        jnp.concatenate([ordered[index] for index in range(4)], axis=1),
+        jnp.concatenate([own[...], other[...]], axis=0),
         preferred_element_type=jnp.float32,
     )
-    outs = list(rest)
     for index, cuts in enumerate(plan):
         mine = [outs.pop(0) for _ in cuts]
 
         @pl.when(step == index)
         def _():
             for cut, out in zip(cuts, mine):
-                out[...] = summed[cut[0] : cut[1]].astype(out.dtype)
+                out[...] = summed[:, cut[0] : cut[1]].astype(out.dtype)
 
 
 def leave(chips, columns, weights, heads, plan):
-    high = CUTS[-1][1]
-    count = heads[0].shape[1]
+    count = heads[0].shape[0]
     steps = len(plan)
-    inner = weights[0].shape[1]
-    block = pl.BlockSpec((high, inner), lambda i, chips, columns: (chips[i], 0))
+    inner = weights[0].shape[0]
+    block = pl.BlockSpec((inner, DEEP), lambda i, chips, columns: (0, chips[i]))
     whole = lambda shape: pl.BlockSpec(shape, lambda i, *_: (0, 0))
-    shapes = [(cut[1] - cut[0], count) for cuts in plan for cut in cuts]
+    shapes = [(count, cut[1] - cut[0]) for cuts in plan for cut in cuts]
 
     def kernel(*refs):
         leave_kernel(plan, *refs)
@@ -407,73 +343,75 @@
         grid_spec=pltpu.PrefetchScalarGridSpec(
             num_scalar_prefetch=2,
             grid=(steps,),
-            in_specs=[block] * 2
-            + [whole(h.shape) for h in heads],
+            in_specs=[block] * 2 + [whole(h.shape) for h in heads],
             out_specs=[whole(s) for s in shapes],
-            scratch_shapes=[pltpu.VMEM((2 * inner, count), jnp.bfloat16)],
+            scratch_shapes=[pltpu.VMEM((4, count, BLK), jnp.bfloat16)],
         ),
         out_shape=[jax.ShapeDtypeStruct(s, jnp.bfloat16) for s in shapes],
-        compiler_params=pltpu.CompilerParams(vmem_limit_bytes=56 * MIB),
+        compiler_params=pltpu.CompilerParams(vmem_limit_bytes=28 * MIB),
         cost_estimate=pl.CostEstimate(
-            flops=4 * steps * high * inner * count,
-            bytes_accessed=2 * steps * high * (2 * inner + count),
+            flops=4 * steps * DEEP * inner * count,
+            bytes_accessed=2 * steps * DEEP * (2 * inner + count),
             transcendentals=0,
         ),
         name="leave",
     )(chips, columns, *weights, *heads)
 
 
-def arrive_kernel(plan, *refs):
+def arrive_kernel(plan, turned, *refs):
     outs = refs[-len(plan) :]
     at = 0
     for cuts, out in zip(plan, outs):
         share, arrived = refs[at], refs[at + 1 : at + 1 + len(cuts)]
         at += 1 + len(cuts)
-        rows = sorted({0, out.shape[0], *[edge for cut in cuts for edge in cut]})
-        for low, high in zip(rows, rows[1:]):
-            value = share[low:high].astype(jnp.float32)
+        edges = sorted({0, share.shape[1], *[edge for cut in cuts for edge in cut]})
+        for low, high in zip(edges, edges[1:]):
+            value = share[:, low:high].astype(jnp.float32)
             for (first, last), ref in zip(cuts, arrived):
                 if first <= low and high <= last:
-                    value += ref[low - first : high - first].astype(jnp.float32)
-            out[low:high] = value.astype(out.dtype)
-
-
-def arrive(plan, *arrays):
-    shares, at = [], 0
+                    value += ref[:, low - first : high - first].astype(jnp.float32)
+            if turned:
+                out[low:high, :] = value.T.astype(out.dtype)
+            else:
+                out[:, low:high] = value.astype(out.dtype)
+
+
+def arrive(plan, *arrays, turned=False):
+    shapes, at = [], 0
     for cuts in plan:
-        shares.append(arrays[at])
+        shapes.append(arrays[at].shape[::-1] if turned else arrays[at].shape)
         at += 1 + len(cuts)
 
     def kernel(*refs):
-        arrive_kernel(plan, *refs)
+        arrive_kernel(plan, turned, *refs)
 
     return pl.pallas_call(
         kernel,
         in_specs=[pl.BlockSpec(memory_space=pltpu.VMEM)] * len(arrays),
         out_specs=[pl.BlockSpec(memory_space=pltpu.VMEM)] * len(plan),
-        out_shape=[jax.ShapeDtypeStruct(share.shape, share.dtype) for share in shares],
-        compiler_params=pltpu.CompilerParams(vmem_limit_bytes=56 * MIB),
+        out_shape=[jax.ShapeDtypeStruct(shape, arrays[0].dtype) for shape in shapes],
+        compiler_params=pltpu.CompilerParams(vmem_limit_bytes=16 * MIB),
         cost_estimate=pl.CostEstimate(
-            flops=0, bytes_accessed=8 * shares[0].size, transcendentals=0
+            flops=0, bytes_accessed=8 * arrays[0].size, transcendentals=0
         ),
         name="arrive",
     )(*arrays)
 
 
-def gather_tokens(own, first_others, second_others):
+def gather_tokens(own):
     below = shift(own, "z", 1)
     above = shift(own, "z", -1)
     beside = swap(own, "yl")
-    below, above, beside = together((below, above, beside), first_others)
+    below, above, beside = together((below, above, beside))
     far = shift(below, "z", 1)
     beside_below = swap(below, "yl")
     beside_above = shift(beside, "z", -1)
-    far, beside_below, beside_above = together((far, beside_below, beside_above), second_others)
+    far, beside_below, beside_above = together((far, beside_below, beside_above))
     first, second, third = [slice(*cut) for cut in CUTS]
     parts = [
-        swap(far[first], "yl"),
-        shift(beside_above[second], "z", -1),
-        shift(beside_below[third], "z", 1),
+        swap(far[:, first], "yl"),
+        shift(beside_above[:, second], "z", -1),
+        shift(beside_below[:, third], "z", 1),
     ]
     places = [(0, 0), (0, -1), (0, 1), (1, 0), (0, 2), (1, -1), (1, 1), (1, 2)]
     return places, [own, below, above, beside, far, beside_below, beside_above, *parts]
@@ -506,26 +444,23 @@
 
     mine, given = mine_and_given(across, 1)
     other = swap(given, "core")
-    own = jnp.concatenate(
-        [jnp.where(core == 0, mine, other), jnp.where(core == 0, other, mine)], axis=0
-    )
+    own = lay(core, mine, other)
     mask_mine, mask_given = mine_and_given(block_mask, 1)
     mask_other = swap(mask_given, "core")
 
     raw, *_ = lax.optimization_barrier((qkv_weight, own, mask_other))
-    own_weight, other_weight = turn(raw), turn(swap(raw, "core"))
-    gain, bias = spread(modulation)
-    places, xs = gather_tokens(own, (own_weight, gain, bias), (other_weight,))
+    other_weight = swap(raw, "core")
+    places, xs = gather_tokens(own)
 
     chips = jnp.stack([chip(*place) for place in places]).astype(jnp.int32)
     slots = [head_slot(steps) for steps in range(4)]
     bases = jnp.stack([side * 3 * heads_here + slot for side, slot in slots]).astype(jnp.int32)
-    kv, query, *packed = project(chips, bases, xs, own_weight, other_weight, gain, bias)
+    kv, query, *packed = project(chips, bases, xs, qkv_weight, other_weight, modulation)
     two, one, three = [shift(packed[i - 1], "x", i) for i in (2, 1, 3)]
     away_kv = swap(kv, "yh")
     out_own, _ = lax.optimization_barrier((out_weight, kv))
-    leaving = stand(out_weight, swap(out_own, "core"))
-    one, three = together((one, three), (away_kv, *leaving))
+    leaving = out_weight, swap(out_own, "core")
+    one, three = together((one, three), (away_kv,))
     both = jnp.concatenate([one[: 2 * BLK], three[: 2 * BLK]], axis=0)
     away_both = swap(both, "yh")
     (two,) = together((two,), (away_both,))
@@ -592,7 +527,7 @@
         [(whole, whole), (whole,)], share[0, -1], down, side, share[1, 0], up
     )
     down, up, side = shift(down, "z", -1), shift(share[0, 1], "z", 1), swap(side, "yl")
-    (summed,) = arrive([(whole, whole, whole)], share[0, 0], down, up, side)
+    (summed,) = arrive([(whole, whole, whole)], share[0, 0], down, up, side, turned=True)
 
     kept, given = mine_and_given(summed, 0)
     other = swap(given, "core")

time: 231 us -> 222 us (0.961); the launches traced: 229 us -> 223 us
  Pallas kernels: 89 us -> 50.7 us
  waiting for transfers between devices: 48.3 us -> 82.1 us
  other arithmetic: 8.33 us -> 4.13 us
  local copies, waits for them, and re-layouts: 19.3 us -> 21.9 us
    ppermute x39, waiting for transfers between devices: 48.3 us -> 82.1 us  [shift(): lax.ppermute(value, axis, [(i, (i + steps) % count) for i in range(count)])]
    pallas_call x4 -> x1, Pallas kernels: 32.3 us -> 0.26 us  [lay(): pl.pallas_call(lay_kernel, in_specs=[pl.BlockSpec(memory_space=pltpu.SMEM...]
    unnamed x60 -> x52, local copies, waits for them, and re-layouts: 8.91 us -> 16.8 us
    pallas_call x3, Pallas kernels: 9.18 us -> 2.81 us  [arrive(): pl.pallas_call(kernel, in_specs=[pl.BlockSpec(memory_space=pltpu.VMEM)] *...]
    pallas_call x1, Pallas kernels: 12.3 us -> 16.9 us  [attend(): pl.pallas_call(kernel, in_specs=[pl.BlockSpec(memory_space=pltpu.SMEM)] *...]
    pallas_call x1, Pallas kernels: 22.3 us -> 19.5 us  [project(): pl.pallas_call(project_kernel, grid_spec=pltpu.PrefetchScalarGridSpec(num...]
  transfers between devices with their start and end apart: 39 -> 39, of which waited for: 14 -> 20; matrix products, arithmetic and copies ran while one was open for 6% -> 3% of each run, Pallas kernels for 20% -> 12%
where the time goes in v6:
time: 222 us; the launch traced here: 223 us
  waiting for transfers between devices  82.1 us (37%)
  starting transfers between devices  63.5 us (29%)
  Pallas kernels  50.7 us (23%)
  local copies, waits for them, and re-layouts  21.9 us (10%)
  other arithmetic  4.13 us (2%)
    ppermute x39, waiting for transfers between devices, shift(): lax.ppermute(value, axis, [(i, (i + steps) % count) for i in range(count)])  82.1 us
    ppermute x39, starting transfers between devices, shift(): lax.ppermute(value, axis, [(i, (i + steps) % count) for i in range(count)])  63.5 us
    pallas_call x1, Pallas kernels, project(): pl.pallas_call(project_kernel, grid_spec=pltpu.PrefetchScalarGridSpec(num...  19.5 us
    pallas_call x1, Pallas kernels, attend(): pl.pallas_call(kernel, in_specs=[pl.BlockSpec(memory_space=pltpu.SMEM)] *...  16.9 us
    unnamed x52, local copies, waits for them, and re-layouts  16.8 us
    pallas_call x2, Pallas kernels, leave(): pl.pallas_call(kernel, grid_spec=pltpu.PrefetchScalarGridSpec(num_scalar_...  11.1 us
  transfers between devices with their start and end apart: 39, of which 20 were waited for; matrix products, arithmetic and copies ran while one was open for 3% of the time, Pallas kernels for 12%

profile of v6, /device:TPU:1, one launch (start us, length us, event | category | flops | bytes accessed | tf_op | source)
XLA Modules:
  0.0 222.6 jit_solution(6190354766952135503)
XLA Ops:
  1.1 1.5 collective-permute-start
  4.7 1.7 collective-permute-start.1
  6.5 2.1 collective-permute-start.2
  9.9 13.5 %collective-permute-done.1.refs_1_ = bf16[512,640]{1,0:T(8,128)(2,1)S(1)} collective-permute-done((bf16[512,640]{1,0:T(8,128)(2,1)S(1)}, bf16[512,640]{1,0:T(8,128)(2,1)S(1)}, u32[]{:S(2)}, u32[]{:S(2)}) %collective-permute-start.1) | collective-permute-done | bytes 655392 | tf_op jit(solution)/shard_map/ppermute | solution.py:27
  26.8 2.3 %collective-permute-start.6 = (bf16[512,640]{1,0:T(8,128)(2,1)S(1)}, bf16[512,640]{1,0:T(8,128)(2,1)S(1)}, u32[]{:S(2)}, u32[]{:S(2)}) collective-permute-start(bf16[512,640]{1,0:T(8,128)(2,1)S(1)} %collective-permute-done.3.refs_3_), channel_id=1, source_target_pairs={{0,6},{2,0},{4,2},{6,4},{1,7},{3,1},{5,3},{7,5},{8,14},{10,8},{12,... | collective-permute-start | bytes 1966088 | tf_op jit(solution)/shard_map/ppermute | solution.py:27
  30.0 10.4 %collective-permute-done.4.refs_4_ = bf16[512,640]{1,0:T(8,128)(2,1)S(1)} collective-permute-done((bf16[512,640]{1,0:T(8,128)(2,1)S(1)}, bf16[512,640]{1,0:T(8,128)(2,1)S(1)}, u32[]{:S(2)}, u32[]{:S(2)}) %collective-permute-start.4) | collective-permute-done | bytes 655392 | tf_op jit(solution)/shard_map/ppermute | solution.py:27
  44.8 3.1 %collective-permute-start.8 = (bf16[512,256]{1,0:T(8,128)(2,1)}, bf16[512,256]{1,0:T(8,128)(2,1)}, u32[]{:S(2)}, u32[]{:S(2)}) collective-permute-start(bf16[512,256]{1,0:T(8,128)(2,1)} %slice.29), channel_id=1, source_target_pairs={{0,6},{2,0},{4,2},{6,4},{1,7},{3,1},{5,3},{7,5},{8,14},{10,8},{12,... | collective-permute-start | bytes 786440 | tf_op jit(solution)/shard_map/ppermute | solution.py:27
  49.6 5.2 %collective-permute-done.9.refs_9_ = bf16[512,128]{1,0:T(8,128)(2,1)} collective-permute-done((bf16[512,128]{1,0:T(8,128)(2,1)}, bf16[512,128]{1,0:T(8,128)(2,1)}, u32[]{:S(2)}, u32[]{:S(2)}) %collective-permute-start.9) | collective-permute-done | bytes 131104 | tf_op jit(solution)/shard_map/ppermute | solution.py:27
  62.2 19.5 %project.1 = (bf16[256,512]{1,0:T(8,128)(2,1)}, bf16[128,512]{1,0:T(8,128)(2,1)S(1)}, bf16[384,512]{1,0:T(8,128)(2,1)}, bf16[384,512]{1,0:T(8,128)(2,1)S(1)}, bf16[384,512]{1,0:T(8,128)(2,1)}) custom-call(s32[8]{0:T(128)S(1)} %stack.91.chips, s32[4]{0:T(128)S(1)} %pad_add_fusion.1.heads, bf16[512,640]{1,0:T(8,128)(2,1)S(1)} %lay.1.refs_0_, ...), custom_call_target="tpu_custom_call" | custom-call | flops 8053063680 | bytes 20971520 | tf_op jit(solution)/shard_map/project/pallas_call | solution.py:141
  82.4 4.6 %collective-permute-start.12 = (bf16[256,5120]{1,0:T(8,128)(2,1)S(1)}, bf16[256,5120]{1,0:T(8,128)(2,1)}, u32[]{:S(2)}, u32[]{:S(2)}) collective-permute-start(bf16[256,5120]{1,0:T(8,128)(2,1)S(1)} %copy-done), channel_id=1, source_target_pairs={{0,1},{1,0},{2,3},{3,2},{4,5},{5,4},{6,7},{7,6},{8,9},{9,8},{10,11... | collective-permute-start | bytes 7864328 | tf_op jit(solution)/shard_map/ppermute | solution.py:27
  88.2 1.5 collective-permute-start.14
  89.7 2.9 %collective-permute-start.15 = (bf16[256,512]{1,0:T(8,128)(2,1)}, bf16[256,512]{1,0:T(8,128)(2,1)}, u32[]{:S(2)}, u32[]{:S(2)}) collective-permute-start(bf16[256,512]{1,0:T(8,128)(2,1)} %get-tuple-element.49.refs_4_), channel_id=1, source_target_pairs={{0,64},{64,0},{1,65},{65,1},{2,66},{66,2},{3,67},{67,3},{4,68},{68... | collective-permute-start | bytes 786440 | tf_op jit(solution)/shard_map/ppermute | solution.py:27
  92.6 1.6 collective-permute-start.19
  94.2 4.3 %collective-permute-done.15.refs_9_ = bf16[256,512]{1,0:T(8,128)(2,1)} collective-permute-done((bf16[256,512]{1,0:T(8,128)(2,1)}, bf16[256,512]{1,0:T(8,128)(2,1)}, u32[]{:S(2)}, u32[]{:S(2)}) %collective-permute-start.15) | collective-permute-done | bytes 262176 | tf_op jit(solution)/shard_map/ppermute | solution.py:27
  99.3 2.9 %collective-permute-start.20 = (bf16[512,512]{1,0:T(8,128)(2,1)S(1)}, bf16[512,512]{1,0:T(8,128)(2,1)S(1)}, u32[]{:S(2)}, u32[]{:S(2)}) collective-permute-start(bf16[512,512]{1,0:T(8,128)(2,1)S(1)} %pad_maximum_fusion.1), channel_id=1, source_target_pairs={{0,64},{64,0},{1,65},{65,1},{2,66},{66,2},{3,67},{67,3},{4,68},{68... | collective-permute-start | bytes 1572872 | tf_op jit(solution)/shard_map/ppermute | solution.py:27
  102.2 2.3 %collective-permute-start.18 = (s32[4,64]{1,0:T(4,128)S(1)}, s32[4,64]{1,0:T(4,128)S(1)}, u32[]{:S(2)}, u32[]{:S(2)}) collective-permute-start(s32[4,64]{1,0:T(4,128)S(1)} %get-tuple-element.88), channel_id=1, source_target_pairs={{0,48},{16,0},{32,16},{48,32},{1,49},{17,1},{33,17},{49,33},{2,50}... | collective-permute-start | bytes 3080 | tf_op jit(solution)/shard_map/ppermute | solution.py:27
  105.1 2.2 collective-permute-done.18
  107.3 1.7 collective-permute-done.17
  109.0 11.1 %collective-permute-start.23 = (bf16[256,512]{1,0:T(8,128)(2,1)}, bf16[256,512]{1,0:T(8,128)(2,1)S(1)}, u32[]{:S(2)}, u32[]{:S(2)}) collective-permute-start(bf16[256,512]{1,0:T(8,128)(2,1)} %collective-permute-done.15.refs_9_), channel_id=1, source_target_pairs={{0,1},{1,0},{2,3},{3,2},{4,5},{5,4},{6,7},{7,6},{8,9},{9,8},{10,11... | collective-permute-start | bytes 786440 | tf_op jit(solution)/shard_map/ppermute | solution.py:27
  123.8 8.7 %collective-permute-done.21.refs_11_ = bf16[256,512]{1,0:T(8,128)(2,1)S(1)} collective-permute-done((bf16[256,512]{1,0:T(8,128)(2,1)S(1)}, bf16[256,512]{1,0:T(8,128)(2,1)S(1)}, u32[]{:S(2)}, u32[]{:S(2)}) %collective-permute-start.21) | collective-permute-done | bytes 262176 | tf_op jit(solution)/shard_map/ppermute | solution.py:27
  134.5 16.9 %attend.1 = (bf16[512,128]{1,0:T(8,128)(2,1)S(1)}, bf16[512,128]{1,0:T(8,128)(2,1)}, bf16[512,128]{1,0:T(8,128)(2,1)}, bf16[512,128]{1,0:T(8,128)(2,1)}) custom-call(s32[16,64]{1,0:T(8,128)S(1)} %select_reduce_fusion.2.refs_0_, s32[16]{0:T(128)S(1)} %get-tuple-element.79.refs_1_, s32[17]{0:T(128)S(1)} %select_reduce_fusion.5.refs_2_, ...), custom_call_target="tpu_custom_call" | custom-call | flops 2147483648 | bytes 4194304 | tf_op jit(solution)/shard_map/attend/pallas_call | solution.py:281
  153.1 2.5 %collective-permute-done.26.refs_5_ = bf16[512,128]{1,0:T(8,128)(2,1)S(1)} collective-permute-done((bf16[512,128]{1,0:T(8,128)(2,1)}, bf16[512,128]{1,0:T(8,128)(2,1)S(1)}, u32[]{:S(2)}, u32[]{:S(2)}) %collective-permute-start.26) | collective-permute-done | bytes 131104 | tf_op jit(solution)/shard_map/ppermute | solution.py:27
  155.6 1.7 collective-permute-done.27.refs_6_
  157.2 2.2 %collective-permute-done.28.refs_7_ = bf16[512,128]{1,0:T(8,128)(2,1)S(1)} collective-permute-done((bf16[512,128]{1,0:T(8,128)(2,1)}, bf16[512,128]{1,0:T(8,128)(2,1)S(1)}, u32[]{:S(2)}, u32[]{:S(2)}) %collective-permute-start.28) | collective-permute-done | bytes 131104 | tf_op jit(solution)/shard_map/ppermute | solution.py:27
  159.5 2.9 %leave.3 = (bf16[512,256]{1,0:T(8,128)(2,1)}, bf16[512,256]{1,0:T(8,128)(2,1)}, bf16[512,128]{1,0:T(8,128)(2,1)}) custom-call(s32[1]{0:T(128)} %bitcast.12.refs_0_, s32[4]{0:T(128)S(1)} %pad_add_fusion.refs_1_, bf16[256,5120]{1,0:T(8,128)(2,1)S(1)} %copy-done, bf16[256,5120]{1,0:T(8,128)(2,1)} %collective-permute-done.12.refs_3_, ...), custom_call_target="tpu_custom_call" | custom-call | flops 335544320 | bytes 1310720 | tf_op jit(solution)/shard_map/leave/pallas_call | solution.py:341
  162.4 6.3 %collective-permute-start.29 = (bf16[512,256]{1,0:T(8,128)(2,1)}, bf16[512,256]{1,0:T(8,128)(2,1)S(1)}, u32[]{:S(2)}, u32[]{:S(2)}) collective-permute-start(bf16[512,256]{1,0:T(8,128)(2,1)} %get-tuple-element.67), channel_id=1, source_target_pairs={{0,8},{8,0},{1,9},{9,1},{2,10},{10,2},{3,11},{11,3},{4,12},{12,4},... | collective-permute-start | bytes 786440 | tf_op jit(solution)/shard_map/ppermute | solution.py:27
  168.8 2.7 %collective-permute-start.31 = (bf16[512,128]{1,0:T(8,128)(2,1)}, bf16[512,128]{1,0:T(8,128)(2,1)S(1)}, u32[]{:S(2)}, u32[]{:S(2)}) collective-permute-start(bf16[512,128]{1,0:T(8,128)(2,1)} %get-tuple-element.71), channel_id=1, source_target_pairs={{0,6},{2,0},{4,2},{6,4},{1,7},{3,1},{5,3},{7,5},{8,14},{10,8},{12,... | collective-permute-start | bytes 393224 | tf_op jit(solution)/shard_map/ppermute | solution.py:27
  175.1 8.2 %leave.2 = (bf16[512,640]{1,0:T(8,128)(2,1)S(1)}, bf16[512,640]{1,0:T(8,128)(2,1)S(1)}, bf16[512,640]{1,0:T(8,128)(2,1)S(1)}, bf16[512,640]{1,0:T(8,128)(2,1)S(1...) custom-call(s32[7]{0:T(128)S(1)} %stack.84.refs_0_, ...), custom_call_target="tpu_custom_call" | custom-call | flops 2348810240 | bytes 9175040 | tf_op jit(solution)/shard_map/leave/pallas_call | solution.py:341
  184.7 1.4 collective-permute-start.34
  186.1 13.4 %collective-permute-done.32.refs_1_ = bf16[512,640]{1,0:T(8,128)(2,1)S(1)} collective-permute-done((bf16[512,640]{1,0:T(8,128)(2,1)S(1)}, bf16[512,640]{1,0:T(8,128)(2,1)S(1)}, u32[]{:S(2)}, u32[]{:S(2)}) %collective-permute-start.32) | collective-permute-done | bytes 655392 | tf_op jit(solution)/shard_map/ppermute | solution.py:27
  203.2 11.7 %collective-permute-done.36.refs_2_ = bf16[512,640]{1,0:T(8,128)(2,1)S(1)} collective-permute-done((bf16[512,640]{1,0:T(8,128)(2,1)}, bf16[512,640]{1,0:T(8,128)(2,1)S(1)}, u32[]{:S(2)}, u32[]{:S(2)}) %collective-permute-start.36) | collective-permute-done | bytes 655392 | tf_op jit(solution)/shard_map/ppermute | solution.py:27
  215.5 4.6 %collective-permute-start.38 = (bf16[320,512]{1,0:T(8,128)(2,1)S(1)}, bf16[320,512]{1,0:T(8,128)(2,1)S(1)}, u32[]{:S(2)}, u32[]{:S(2)}) collective-permute-start(bf16[320,512]{1,0:T(8,128)(2,1)S(1)} %constant_dynamic-slice_fusion), channel_id=1, source_target_pairs={{0,1},{1,0},{2,3},{3,2},{4,5},{5,4},{6,7},{7,6},{8,9},{9,8},{10,11... | collective-permute-start | bytes 983048 | tf_op jit(solution)/shard_map/ppermute | solution.py:27
  (138 shorter events, 44.6 us)
Async XLA Ops:
  4.6 50.2 %collective-permute-start.11 = (bf16[3,5120,256]{2,1,0:T(8,128)(2,1)}, bf16[3,5120,256]{2,1,0:T(8,128)(2,1)}, u32[]{:S(2)}, u32[]{:S(2)}) collective-permute-start(bf16[3,5120,256]{2,1,0:T(8,128)(2,1)} %refs_11_.1), channel_id=1, source_target_pairs={{0,1},{1,0},{2,3},{3,2},{4,5},{5,4},{6,7},{7,6},{8,9},{9,8},{10,11... | collective-permute-start | bytes 23592968 | tf_op jit(solution)/shard_map/ppermute | solution.py:27
  4.7 18.7 %collective-permute-start.1 = (bf16[512,640]{1,0:T(8,128)(2,1)S(1)}, bf16[512,640]{1,0:T(8,128)(2,1)S(1)}, u32[]{:S(2)}, u32[]{:S(2)}) collective-permute-start(bf16[512,640]{1,0:T(8,128)(2,1)S(1)} %lay.1.refs_0_), channel_id=1, source_target_pairs={{0,2},{2,4},{4,6},{6,0},{1,3},{3,5},{5,7},{7,1},{8,10},{10,12},{12... | collective-permute-start | bytes 1966088 | tf_op jit(solution)/shard_map/ppermute | solution.py:27
  6.5 17.0 %collective-permute-start.2 = (bf16[512,640]{1,0:T(8,128)(2,1)S(1)}, bf16[512,640]{1,0:T(8,128)(2,1)S(1)}, u32[]{:S(2)}, u32[]{:S(2)}) collective-permute-start(bf16[512,640]{1,0:T(8,128)(2,1)S(1)} %lay.1.refs_0_), channel_id=1, source_target_pairs={{0,6},{2,0},{4,2},{6,4},{1,7},{3,1},{5,3},{7,5},{8,14},{10,8},{12,... | collective-permute-start | bytes 1966088 | tf_op jit(solution)/shard_map/ppermute | solution.py:27
  8.6 15.8 %collective-permute-start.3 = (bf16[512,640]{1,0:T(8,128)(2,1)S(1)}, bf16[512,640]{1,0:T(8,128)(2,1)S(1)}, u32[]{:S(2)}, u32[]{:S(2)}) collective-permute-start(bf16[512,640]{1,0:T(8,128)(2,1)S(1)} %lay.1.refs_0_), channel_id=1, source_target_pairs={{0,8},{8,0},{1,9},{9,1},{2,10},{10,2},{3,11},{11,3},{4,12},{12,4},... | collective-permute-start | bytes 1966088 | tf_op jit(solution)/shard_map/ppermute | solution.py:27
  24.3 16.0 %collective-permute-start.4 = (bf16[512,640]{1,0:T(8,128)(2,1)S(1)}, bf16[512,640]{1,0:T(8,128)(2,1)S(1)}, u32[]{:S(2)}, u32[]{:S(2)}) collective-permute-start(bf16[512,640]{1,0:T(8,128)(2,1)S(1)} %collective-permute-done.1.refs_1_), channel_id=1, source_target_pairs={{0,2},{2,4},{4,6},{6,0},{1,3},{3,5},{5,7},{7,1},{8,10},{10,12},{12... | collective-permute-start | bytes 1966088 | tf_op jit(solution)/shard_map/ppermute | solution.py:27
  24.7 15.7 %collective-permute-start.5 = (bf16[512,640]{1,0:T(8,128)(2,1)S(1)}, bf16[512,640]{1,0:T(8,128)(2,1)S(1)}, u32[]{:S(2)}, u32[]{:S(2)}) collective-permute-start(bf16[512,640]{1,0:T(8,128)(2,1)S(1)} %collective-permute-done.1.refs_1_), channel_id=1, source_target_pairs={{0,8},{8,0},{1,9},{9,1},{2,10},{10,2},{3,11},{11,3},{4,12},{12,4},... | collective-permute-start | bytes 1966088 | tf_op jit(solution)/shard_map/ppermute | solution.py:27
  26.8 14.4 %collective-permute-start.6 = (bf16[512,640]{1,0:T(8,128)(2,1)S(1)}, bf16[512,640]{1,0:T(8,128)(2,1)S(1)}, u32[]{:S(2)}, u32[]{:S(2)}) collective-permute-start(bf16[512,640]{1,0:T(8,128)(2,1)S(1)} %collective-permute-done.3.refs_3_), channel_id=1, source_target_pairs={{0,6},{2,0},{4,2},{6,4},{1,7},{3,1},{5,3},{7,5},{8,14},{10,8},{12,... | collective-permute-start | bytes 1966088 | tf_op jit(solution)/shard_map/ppermute | solution.py:27
  42.8 12.0 %collective-permute-start.7 = (bf16[512,256]{1,0:T(8,128)(2,1)}, bf16[512,256]{1,0:T(8,128)(2,1)S(1)}, u32[]{:S(2)}, u32[]{:S(2)}) collective-permute-start(bf16[512,256]{1,0:T(8,128)(2,1)} %slice.28), channel_id=1, source_target_pairs={{0,8},{8,0},{1,9},{9,1},{2,10},{10,2},{3,11},{11,3},{4,12},{12,4},... | collective-permute-start | bytes 786440 | tf_op jit(solution)/shard_map/ppermute | solution.py:27
  44.8 10.0 %collective-permute-start.8 = (bf16[512,256]{1,0:T(8,128)(2,1)}, bf16[512,256]{1,0:T(8,128)(2,1)}, u32[]{:S(2)}, u32[]{:S(2)}) collective-permute-start(bf16[512,256]{1,0:T(8,128)(2,1)} %slice.29), channel_id=1, source_target_pairs={{0,6},{2,0},{4,2},{6,4},{1,7},{3,1},{5,3},{7,5},{8,14},{10,8},{12,... | collective-permute-start | bytes 786440 | tf_op jit(solution)/shard_map/ppermute | solution.py:27
  82.4 77.1 %collective-permute-start.12 = (bf16[256,5120]{1,0:T(8,128)(2,1)S(1)}, bf16[256,5120]{1,0:T(8,128)(2,1)}, u32[]{:S(2)}, u32[]{:S(2)}) collective-permute-start(bf16[256,5120]{1,0:T(8,128)(2,1)S(1)} %copy-done), channel_id=1, source_target_pairs={{0,1},{1,0},{2,3},{3,2},{4,5},{5,4},{6,7},{7,6},{8,9},{9,8},{10,11... | collective-permute-start | bytes 7864328 | tf_op jit(solution)/shard_map/ppermute | solution.py:27
  87.0 12.2 %collective-permute-start.13 = (bf16[384,512]{1,0:T(8,128)(2,1)}, bf16[384,512]{1,0:T(8,128)(2,1)S(1)}, u32[]{:S(2)}, u32[]{:S(2)}) collective-permute-start(bf16[384,512]{1,0:T(8,128)(2,1)} %get-tuple-element.51), channel_id=1, source_target_pairs={{0,16},{16,32},{32,48},{48,0},{1,17},{17,33},{33,49},{49,1},{2,18}... | collective-permute-start | bytes 1179656 | tf_op jit(solution)/shard_map/ppermute | solution.py:27
  88.2 11.0 %collective-permute-start.14 = (bf16[384,512]{1,0:T(8,128)(2,1)}, bf16[384,512]{1,0:T(8,128)(2,1)S(1)}, u32[]{:S(2)}, u32[]{:S(2)}) collective-permute-start(bf16[384,512]{1,0:T(8,128)(2,1)} %get-tuple-element.52), channel_id=1, source_target_pairs={{0,48},{16,0},{32,16},{48,32},{1,49},{17,1},{33,17},{49,33},{2,50}... | collective-permute-start | bytes 1179656 | tf_op jit(solution)/shard_map/ppermute | solution.py:27
  89.7 8.8 %collective-permute-start.15 = (bf16[256,512]{1,0:T(8,128)(2,1)}, bf16[256,512]{1,0:T(8,128)(2,1)}, u32[]{:S(2)}, u32[]{:S(2)}) collective-permute-start(bf16[256,512]{1,0:T(8,128)(2,1)} %get-tuple-element.49.refs_4_), channel_id=1, source_target_pairs={{0,64},{64,0},{1,65},{65,1},{2,66},{66,2},{3,67},{67,3},{4,68},{68... | collective-permute-start | bytes 786440 | tf_op jit(solution)/shard_map/ppermute | solution.py:27
  92.6 27.5 %collective-permute-start.19 = (bf16[384,512]{1,0:T(8,128)(2,1)}, bf16[384,512]{1,0:T(8,128)(2,1)S(1)}, u32[]{:S(2)}, u32[]{:S(2)}) collective-permute-start(bf16[384,512]{1,0:T(8,128)(2,1)} %copy-done.22), channel_id=1, source_target_pairs={{0,32},{16,48},{32,0},{48,16},{1,33},{17,49},{33,1},{49,17},{2,34}... | collective-permute-start | bytes 1179656 | tf_op jit(solution)/shard_map/ppermute | solution.py:27
  99.3 20.8 %collective-permute-start.20 = (bf16[512,512]{1,0:T(8,128)(2,1)S(1)}, bf16[512,512]{1,0:T(8,128)(2,1)S(1)}, u32[]{:S(2)}, u32[]{:S(2)}) collective-permute-start(bf16[512,512]{1,0:T(8,128)(2,1)S(1)} %pad_maximum_fusion.1), channel_id=1, source_target_pairs={{0,64},{64,0},{1,65},{65,1},{2,66},{66,2},{3,67},{67,3},{4,68},{68... | collective-permute-start | bytes 1572872 | tf_op jit(solution)/shard_map/ppermute | solution.py:27
  107.3 12.8 %collective-permute-start.16 = (s32[4,64]{1,0:T(4,128)S(1)}, s32[4,64]{1,0:T(4,128)S(1)}, u32[]{:S(2)}, u32[]{:S(2)}) collective-permute-start(s32[4,64]{1,0:T(4,128)S(1)} %get-tuple-element.86), channel_id=1, source_target_pairs={{0,16},{16,32},{32,48},{48,0},{1,17},{17,33},{33,49},{49,1},{2,18}... | collective-permute-start | bytes 3080 | tf_op jit(solution)/shard_map/ppermute | solution.py:27
  109.0 25.2 %collective-permute-start.23 = (bf16[256,512]{1,0:T(8,128)(2,1)}, bf16[256,512]{1,0:T(8,128)(2,1)S(1)}, u32[]{:S(2)}, u32[]{:S(2)}) collective-permute-start(bf16[256,512]{1,0:T(8,128)(2,1)} %collective-permute-done.15.refs_9_), channel_id=1, source_target_pairs={{0,1},{1,0},{2,3},{3,2},{4,5},{5,4},{6,7},{7,6},{8,9},{9,8},{10,11... | collective-permute-start | bytes 786440 | tf_op jit(solution)/shard_map/ppermute | solution.py:27
  121.2 13.3 %collective-permute-start.22 = (bf16[1024,512]{1,0:T(8,128)(2,1)S(1)}, bf16[1024,512]{1,0:T(8,128)(2,1)S(1)}, u32[]{:S(2)}, u32[]{:S(2)}) collective-permute-start(bf16[1024,512]{1,0:T(8,128)(2,1)S(1)} %pad_maximum_fusion), channel_id=1, source_target_pairs={{0,1},{1,0},{2,3},{3,2},{4,5},{5,4},{6,7},{7,6},{8,9},{9,8},{10,11... | collective-permute-start | bytes 3145736 | tf_op jit(solution)/shard_map/ppermute | solution.py:27
  123.0 9.5 %collective-permute-start.21 = (bf16[256,512]{1,0:T(8,128)(2,1)S(1)}, bf16[256,512]{1,0:T(8,128)(2,1)S(1)}, u32[]{:S(2)}, u32[]{:S(2)}) collective-permute-start(bf16[256,512]{1,0:T(8,128)(2,1)S(1)} %slice.35), channel_id=1, source_target_pairs={{0,64},{64,0},{1,65},{65,1},{2,66},{66,2},{3,67},{67,3},{4,68},{68... | collective-permute-start | bytes 786440 | tf_op jit(solution)/shard_map/ppermute | solution.py:27
  123.4 10.8 %collective-permute-start.24 = (bf16[512,512]{1,0:T(8,128)(2,1)S(1)}, bf16[512,512]{1,0:T(8,128)(2,1)S(1)}, u32[]{:S(2)}, u32[]{:S(2)}) collective-permute-start(bf16[512,512]{1,0:T(8,128)(2,1)S(1)} %collective-permute-done.20.refs_10_), channel_id=1, source_target_pairs={{0,1},{1,0},{2,3},{3,2},{4,5},{5,4},{6,7},{7,6},{8,9},{9,8},{10,11... | collective-permute-start | bytes 1572872 | tf_op jit(solution)/shard_map/ppermute | solution.py:27
  151.6 5.7 %collective-permute-start.27 = (bf16[512,128]{1,0:T(8,128)(2,1)}, bf16[512,128]{1,0:T(8,128)(2,1)S(1)}, u32[]{:S(2)}, u32[]{:S(2)}) collective-permute-start(bf16[512,128]{1,0:T(8,128)(2,1)} %get-tuple-element.62), channel_id=1, source_target_pairs={{0,32},{16,48},{32,0},{48,16},{1,33},{17,49},{33,1},{49,17},{2,34}... | collective-permute-start | bytes 393224 | tf_op jit(solution)/shard_map/ppermute | solution.py:27
  151.7 7.8 %collective-permute-start.28 = (bf16[512,128]{1,0:T(8,128)(2,1)}, bf16[512,128]{1,0:T(8,128)(2,1)S(1)}, u32[]{:S(2)}, u32[]{:S(2)}) collective-permute-start(bf16[512,128]{1,0:T(8,128)(2,1)} %get-tuple-element.63), channel_id=1, source_target_pairs={{0,16},{16,32},{32,48},{48,0},{1,17},{17,33},{33,49},{49,1},{2,18}... | collective-permute-start | bytes 393224 | tf_op jit(solution)/shard_map/ppermute | solution.py:27
  162.4 20.9 %collective-permute-start.29 = (bf16[512,256]{1,0:T(8,128)(2,1)}, bf16[512,256]{1,0:T(8,128)(2,1)S(1)}, u32[]{:S(2)}, u32[]{:S(2)}) collective-permute-start(bf16[512,256]{1,0:T(8,128)(2,1)} %get-tuple-element.67), channel_id=1, source_target_pairs={{0,8},{8,0},{1,9},{9,1},{2,10},{10,2},{3,11},{11,3},{4,12},{12,4},... | collective-permute-start | bytes 786440 | tf_op jit(solution)/shard_map/ppermute | solution.py:27
  168.7 14.6 %collective-permute-start.30 = (bf16[512,256]{1,0:T(8,128)(2,1)}, bf16[512,256]{1,0:T(8,128)(2,1)}, u32[]{:S(2)}, u32[]{:S(2)}) collective-permute-start(bf16[512,256]{1,0:T(8,128)(2,1)} %get-tuple-element.69), channel_id=1, source_target_pairs={{0,2},{2,4},{4,6},{6,0},{1,3},{3,5},{5,7},{7,1},{8,10},{10,12},{12... | collective-permute-start | bytes 786440 | tf_op jit(solution)/shard_map/ppermute | solution.py:27
  168.8 14.5 %collective-permute-start.31 = (bf16[512,128]{1,0:T(8,128)(2,1)}, bf16[512,128]{1,0:T(8,128)(2,1)S(1)}, u32[]{:S(2)}, u32[]{:S(2)}) collective-permute-start(bf16[512,128]{1,0:T(8,128)(2,1)} %get-tuple-element.71), channel_id=1, source_target_pairs={{0,6},{2,0},{4,2},{6,4},{1,7},{3,1},{5,3},{7,5},{8,14},{10,8},{12,... | collective-permute-start | bytes 393224 | tf_op jit(solution)/shard_map/ppermute | solution.py:27
  184.5 15.1 %collective-permute-start.32 = (bf16[512,640]{1,0:T(8,128)(2,1)S(1)}, bf16[512,640]{1,0:T(8,128)(2,1)S(1)}, u32[]{:S(2)}, u32[]{:S(2)}) collective-permute-start(bf16[512,640]{1,0:T(8,128)(2,1)S(1)} %get-tuple-element.72), channel_id=1, source_target_pairs={{0,6},{2,0},{4,2},{6,4},{1,7},{3,1},{5,3},{7,5},{8,14},{10,8},{12,... | collective-permute-start | bytes 1966088 | tf_op jit(solution)/shard_map/ppermute | solution.py:27
  184.6 15.1 %collective-permute-start.33 = (bf16[512,640]{1,0:T(8,128)(2,1)S(1)}, bf16[512,640]{1,0:T(8,128)(2,1)S(1)}, u32[]{:S(2)}, u32[]{:S(2)}) collective-permute-start(bf16[512,640]{1,0:T(8,128)(2,1)S(1)} %get-tuple-element.73), channel_id=1, source_target_pairs={{0,8},{8,0},{1,9},{9,1},{2,10},{10,2},{3,11},{11,3},{4,12},{12,4},... | collective-permute-start | bytes 1966088 | tf_op jit(solution)/shard_map/ppermute | solution.py:27
  184.7 16.2 %collective-permute-start.34 = (bf16[512,640]{1,0:T(8,128)(2,1)S(1)}, bf16[512,640]{1,0:T(8,128)(2,1)S(1)}, u32[]{:S(2)}, u32[]{:S(2)}) collective-permute-start(bf16[512,640]{1,0:T(8,128)(2,1)S(1)} %get-tuple-element.75), channel_id=1, source_target_pairs={{0,2},{2,4},{4,6},{6,0},{1,3},{3,5},{5,7},{7,1},{8,10},{10,12},{12... | collective-permute-start | bytes 1966088 | tf_op jit(solution)/shard_map/ppermute | solution.py:27
  186.1 28.9 %collective-permute-start.36 = (bf16[512,640]{1,0:T(8,128)(2,1)}, bf16[512,640]{1,0:T(8,128)(2,1)S(1)}, u32[]{:S(2)}, u32[]{:S(2)}) collective-permute-start(bf16[512,640]{1,0:T(8,128)(2,1)} %get-tuple-element.77), channel_id=1, source_target_pairs={{0,2},{2,4},{4,6},{6,0},{1,3},{3,5},{5,7},{7,1},{8,10},{10,12},{12... | collective-permute-start | bytes 1966088 | tf_op jit(solution)/shard_map/ppermute | solution.py:27
  202.1 12.8 %collective-permute-start.35 = (bf16[512,640]{1,0:T(8,128)(2,1)}, bf16[512,640]{1,0:T(8,128)(2,1)S(1)}, u32[]{:S(2)}, u32[]{:S(2)}) collective-permute-start(bf16[512,640]{1,0:T(8,128)(2,1)} %get-tuple-element.76), channel_id=1, source_target_pairs={{0,6},{2,0},{4,2},{6,4},{1,7},{3,1},{5,3},{7,5},{8,14},{10,8},{12,... | collective-permute-start | bytes 1966088 | tf_op jit(solution)/shard_map/ppermute | solution.py:27
  202.3 12.7 %collective-permute-start.37 = (bf16[512,640]{1,0:T(8,128)(2,1)S(1)}, bf16[512,640]{1,0:T(8,128)(2,1)S(1)}, u32[]{:S(2)}, u32[]{:S(2)}) collective-permute-start(bf16[512,640]{1,0:T(8,128)(2,1)S(1)} %get-tuple-element.78), channel_id=1, source_target_pairs={{0,8},{8,0},{1,9},{9,1},{2,10},{10,2},{3,11},{11,3},{4,12},{12,4},... | collective-permute-start | bytes 1966088 | tf_op jit(solution)/shard_map/ppermute | solution.py:27
  215.5 5.8 %collective-permute-start.38 = (bf16[320,512]{1,0:T(8,128)(2,1)S(1)}, bf16[320,512]{1,0:T(8,128)(2,1)S(1)}, u32[]{:S(2)}, u32[]{:S(2)}) collective-permute-start(bf16[320,512]{1,0:T(8,128)(2,1)S(1)} %constant_dynamic-slice_fusion), channel_id=1, source_target_pairs={{0,1},{1,0},{2,3},{3,2},{4,5},{5,4},{6,7},{7,6},{8,9},{9,8},{10,11... | collective-permute-start | bytes 983048 | tf_op jit(solution)/shard_map/ppermute | solution.py:27
  (33 other events, 147.2 us)

commit v7 on v6

--- a/solution.py
+++ b/solution.py
@@ -65,41 +65,47 @@
 
 def project_kernel(chips, heads, *refs):
     xs, weights, modulation, rest = refs[:10], refs[10:14], refs[14], refs[15:]
-    (kv0, q0, *packed), (normed, total) = rest[:-2], rest[-2:]
+    outs, (held_x, normed, total, arrived) = rest[:-4], rest[-4:]
     step = pl.program_id(0)
     features = 8 * DEEP
     count = normed.shape[1]
-    lay = [(piece, 0, x) for piece, x in enumerate(xs[:7])]
-    lay += [(7, cut[0], x) for cut, x in zip(CUTS, xs[7:])]
-    tiles = [
-        (piece, first + at, x, at) for piece, first, x in lay for at in range(0, x.shape[1], BLK)
-    ]
+    tiles = [(piece, at) for piece in range(8) for at in range(0, DEEP, BLK)]
 
     @pl.when(step == 0)
     def _():
+        places = [held_x.at[piece] for piece in range(7)]
+        places += [held_x.at[7, :, cut[0] : cut[1]] for cut in CUTS]
+        copies = [
+            pltpu.make_async_copy(x, place, arrived.at[index])
+            for index, (x, place) in enumerate(zip(xs, places))
+        ]
+        for copy in copies:
+            copy.start()
+        for copy in copies:
+            copy.wait()
         total[...] = jnp.zeros_like(total)
 
         def norm(i, _):
             rows = pl.ds(pl.multiple_of(i * ROWS, ROWS), ROWS)
 
-            def load(x, at):
-                return x[rows, at : at + BLK].astype(jnp.float32)
+            def load(piece, at):
+                return held_x[piece, rows, at : at + BLK].astype(jnp.float32)
 
             summed = jnp.zeros((ROWS, BLK), jnp.float32)
-            for _, _, x, at in tiles:
-                summed = summed + load(x, at)
+            for tile in tiles:
+                summed = summed + load(*tile)
             center = jnp.sum(summed, axis=1, keepdims=True) / features
             center = jnp.broadcast_to(center, (ROWS, BLK))
             summed = jnp.zeros((ROWS, BLK), jnp.float32)
-            for _, _, x, at in tiles:
-                summed = summed + jnp.square(load(x, at) - center)
+            for tile in tiles:
+                summed = summed + jnp.square(load(*tile) - center)
             spread = jnp.sum(summed, axis=1, keepdims=True) / features
             rate = jnp.broadcast_to(lax.rsqrt(spread + EPSILON), (ROWS, BLK))
-            for piece, first, x, at in tiles:
-                place = pl.ds(pl.multiple_of(chips[piece] * DEEP + first, BLK), BLK)
+            for piece, at in tiles:
+                place = pl.ds(pl.multiple_of(chips[piece] * DEEP + at, BLK), BLK)
                 gain = 1.0 + modulation[1:2, place]
-                value = (load(x, at) - center) * rate * gain + modulation[0:1, place]
-                column = piece % 2 * DEEP + first
+                value = (load(piece, at) - center) * rate * gain + modulation[0:1, place]
+                column = piece % 2 * DEEP + at
                 normed[piece // 2, rows, column : column + BLK] = value.astype(jnp.bfloat16)
             return 0
 
@@ -116,10 +122,7 @@
     @pl.when(step == pl.num_programs(0) - 1)
     def _():
         for index in range(4):
-            if index:
-                kv, q = packed[index - 1], packed[index - 1].at[2 * BLK :]
-            else:
-                kv, q = kv0, q0
+            kv, q = outs[2 * index], outs[2 * index + 1]
             base = heads[index]
             q[...] = total[base].T.astype(jnp.bfloat16)
             keys = total[base + 2]
@@ -137,22 +140,24 @@
         pl.BlockSpec((parts, deep, inner), lambda k, chips, heads, i=i: (0, chips[2 * k + i], 0))
         for i in range(2)
     ]
-    shapes = [(2 * BLK, count), (BLK, count)] + [(3 * BLK, count)] * 3
+    shapes = [(2 * BLK, count), (BLK, count)] * 4
     return pl.pallas_call(
         project_kernel,
         grid_spec=pltpu.PrefetchScalarGridSpec(
             num_scalar_prefetch=2,
             grid=(features // deep // 2,),
-            in_specs=[whole(x.shape) for x in xs]
+            in_specs=[pl.BlockSpec(memory_space=pl.ANY)] * len(xs)
             + [*blocks, *blocks, whole(modulation.shape)],
             out_specs=[whole(s) for s in shapes],
             scratch_shapes=[
+                pltpu.VMEM((features // deep, count, deep), jnp.bfloat16),
                 pltpu.VMEM((features // deep // 2, count, 2 * deep), jnp.bfloat16),
                 pltpu.VMEM((2 * parts * inner // BLK, count, BLK), jnp.float32),
+                pltpu.SemaphoreType.DMA((len(xs),)),
             ],
         ),
         out_shape=[jax.ShapeDtypeStruct(s, jnp.bfloat16) for s in shapes],
-        compiler_params=pltpu.CompilerParams(vmem_limit_bytes=44 * MIB),
+        compiler_params=pltpu.CompilerParams(vmem_limit_bytes=56 * MIB),
         cost_estimate=pl.CostEstimate(
             flops=4 * parts * inner * features * count,
             bytes_accessed=2 * features * (count + 2 * parts * inner),
@@ -305,13 +310,19 @@
 
 
 def leave_kernel(plan, chips, columns, own, other, *refs):
-    heads, outs, ordered = refs[:4], list(refs[4:-1]), refs[-1]
+    heads, outs, ordered, arrived = refs[:4], list(refs[4:-2]), *refs[-2:]
     step = pl.program_id(0)
 
     @pl.when(step == 0)
     def _():
-        for index, head in enumerate(heads):
-            ordered[columns[index]] = head[...]
+        copies = [
+            pltpu.make_async_copy(head, ordered.at[columns[index]], arrived.at[index])
+            for index, head in enumerate(heads)
+        ]
+        for copy in copies:
+            copy.start()
+        for copy in copies:
+            copy.wait()
 
     summed = jnp.dot(
         jnp.concatenate([ordered[index] for index in range(4)], axis=1),
@@ -343,9 +354,12 @@
         grid_spec=pltpu.PrefetchScalarGridSpec(
             num_scalar_prefetch=2,
             grid=(steps,),
-            in_specs=[block] * 2 + [whole(h.shape) for h in heads],
+            in_specs=[block] * 2 + [pl.BlockSpec(memory_space=pl.ANY)] * 4,
             out_specs=[whole(s) for s in shapes],
-            scratch_shapes=[pltpu.VMEM((4, count, BLK), jnp.bfloat16)],
+            scratch_shapes=[
+                pltpu.VMEM((4, count, BLK), jnp.bfloat16),
+                pltpu.SemaphoreType.DMA((4,)),
+            ],
         ),
         out_shape=[jax.ShapeDtypeStruct(s, jnp.bfloat16) for s in shapes],
         compiler_params=pltpu.CompilerParams(vmem_limit_bytes=28 * MIB),
@@ -398,15 +412,15 @@
     )(*arrays)
 
 
-def gather_tokens(own):
+def gather_tokens(own, first_others, second_others):
     below = shift(own, "z", 1)
     above = shift(own, "z", -1)
     beside = swap(own, "yl")
-    below, above, beside = together((below, above, beside))
+    below, above, beside = together((below, above, beside), first_others)
     far = shift(below, "z", 1)
     beside_below = swap(below, "yl")
     beside_above = shift(beside, "z", -1)
-    far, beside_below, beside_above = together((far, beside_below, beside_above))
+    far, beside_below, beside_above = together((far, beside_below, beside_above), second_others)
     first, second, third = [slice(*cut) for cut in CUTS]
     parts = [
         swap(far[:, first], "yl"),
@@ -450,26 +464,6 @@
 
     raw, *_ = lax.optimization_barrier((qkv_weight, own, mask_other))
     other_weight = swap(raw, "core")
-    places, xs = gather_tokens(own)
-
-    chips = jnp.stack([chip(*place) for place in places]).astype(jnp.int32)
-    slots = [head_slot(steps) for steps in range(4)]
-    bases = jnp.stack([side * 3 * heads_here + slot for side, slot in slots]).astype(jnp.int32)
-    kv, query, *packed = project(chips, bases, xs, qkv_weight, other_weight, modulation)
-    two, one, three = [shift(packed[i - 1], "x", i) for i in (2, 1, 3)]
-    away_kv = swap(kv, "yh")
-    out_own, _ = lax.optimization_barrier((out_weight, kv))
-    leaving = out_weight, swap(out_own, "core")
-    one, three = together((one, three), (away_kv,))
-    both = jnp.concatenate([one[: 2 * BLK], three[: 2 * BLK]], axis=0)
-    away_both = swap(both, "yh")
-    (two,) = together((two,), (away_both,))
-    last = two[: 2 * BLK]
-    away = [away_kv, away_both, swap(last, "yh")]
-    near = jnp.concatenate([kv, both, last], axis=0)
-    arrays = [kv, query, one, two, three, *away, swap(near, "core"), *[swap(a, "core") for a in away]]
-
-    mask_mine, mask_other, _ = lax.optimization_barrier((mask_mine, mask_other, one))
     mask_heads = jnp.stack([mask_mine, mask_other])
     mask_rows = []
     for steps in range(4):
@@ -493,31 +487,56 @@
     chosen = (keep[:, None, :] != 0) & (rank[:, None, :] == blocks[None, :, None])
     listed = jnp.sum(jnp.where(chosen, blocks[None, None, :], 0), axis=2)
     lists = (listed, counts, *pair_lists(counts, listed.shape[1]))
-
+    places, xs = gather_tokens(own, (), mask_rows[1:])
+
+    chips = jnp.stack([chip(*place) for place in places]).astype(jnp.int32)
+    slots = [head_slot(steps) for steps in range(4)]
+    bases = jnp.stack([side * 3 * heads_here + slot for side, slot in slots]).astype(jnp.int32)
+    made = project(chips, bases, xs, qkv_weight, other_weight, modulation)
+    kv, queries = made[::2], made[1::2]
+    one, three = shift(kv[1], "x", 1), shift(kv[3], "x", 3)
+    away_kv = swap(kv[0], "yh")
+    one, three = together((one, three), (away_kv,))
+    both = jnp.concatenate([one, three], axis=0)
+    away_both = swap(both, "yh")
+    kv_two, *asked = together((kv[2], *queries[1:]), (one,))
+    two = shift(kv_two, "x", 2)
+    queries = [queries[0]] + [shift(asked[i - 1], "x", i) for i in (1, 2, 3)]
+    near = swap(jnp.concatenate([kv[0], both], axis=0), "core")
+    away_kv_other = swap(away_kv, "core")
+    two, out_own = together(
+        (two, out_weight), (away_both, *queries[1:], *lists, near, away_kv_other)
+    )
+    away_two = swap(two, "yh")
+    arrays = [kv[0], both, two, away_kv, away_both, away_two, near, swap(two, "core")]
+    arrays += [away_kv_other, swap(away_both, "core"), swap(away_two, "core")] + queries
+    leaving = out_weight, swap(out_own, "core")
     step = 2 * BLK
-    plan = [("kv", 0, 0, 0), ("q", 0, 1, 0)]
-    for steps, array in ((1, 2), (2, 3), (3, 4)):
-        plan += [("kv", steps, array, 0), ("q", steps, array, step)]
-    for index, array in ((4, 5), (12, 9)):
+    plan = []
+    for index, array in ((0, 0), (4, 3), (12, 8)):
         plan += [("kv", index, array, 0), ("kv", index + 1, array + 1, 0)]
         plan += [("kv", index + 3, array + 1, step), ("kv", index + 2, array + 2, 0)]
-    plan += [("kv", 8 + steps, 8, at * step) for at, steps in enumerate((0, 1, 3, 2))]
+    plan += [("kv", 8, 6, 0), ("kv", 9, 6, step), ("kv", 11, 6, 2 * step), ("kv", 10, 7, 0)]
+    plan += [("q", index, 11 + index, 0) for index in range(4)]
     heads = attend(factor, lists, plan, arrays, half)
     heads = [heads[0]] + [shift(heads[steps], "x", -steps) for steps in (1, 2, 3)]
 
     columns = jnp.stack([side * heads_here + slot for side, slot in slots]).astype(jnp.int32)
     whole = CUTS[0][0], CUTS[-1][1]
 
-    def shares(targets, cuts):
+    def shares(targets, cuts, heads):
         chips = jnp.stack([chip(*target) for target in targets]).astype(jnp.int32)
         return leave(chips, columns, leaving, heads, [cuts] * len(targets))
 
-    parts = shares([(1, 2)], CUTS)
-    near = [(0, 2), (1, 1), (1, -1), (0, -1), (0, 1), (1, 0), (0, 0)]
-    share = dict(zip(near, shares(near, (whole,))))
+    parts = shares([(1, 2)], CUTS, heads)
+    middle = [(0, 2), (1, 1), (1, -1)]
+    share = dict(zip(middle, shares(middle, (whole,), heads)))
     first = swap(parts[0], "yl")
     second = shift(parts[1], "z", 1)
     third = shift(parts[2], "z", -1)
+    heads = together(heads, (first, second, third))
+    near = [(0, -1), (0, 1), (1, 0), (0, 0)]
+    share |= dict(zip(near, shares(near, (whole,), heads)))
     down, up, side = arrive(
         [(CUTS[0],), (CUTS[1],), (CUTS[2],)],
         *[share[0, 2], first, share[1, 1], second, share[1, -1], third],

time: 222 us -> 206 us (0.928)
  local copies, waits for them, and re-layouts: 21.9 us -> 10.3 us
  waiting for transfers between devices: 82.1 us -> 75.1 us
  starting transfers between devices: 63.5 us -> 68.2 us
  Pallas kernels: 50.7 us -> 47.5 us
    unnamed x52 -> x33, local copies, waits for them, and re-layouts: 16.8 us -> 4.52 us
    ppermute x39 -> x43, waiting for transfers between devices: 82.1 us -> 75.1 us  [shift(): lax.ppermute(value, axis, [(i, (i + steps) % count) for i in range(count)])]
    pallas_call x1, Pallas kernels: 16.9 us -> 10.3 us  [attend(): pl.pallas_call(kernel, in_specs=[pl.BlockSpec(memory_space=pltpu.SMEM)] *...]
    ppermute x39 -> x43, starting transfers between devices: 63.5 us -> 68.2 us  [shift(): lax.ppermute(value, axis, [(i, (i + steps) % count) for i in range(count)])]
    pallas_call x1, Pallas kernels: 19.5 us -> 22.4 us  [project(): pl.pallas_call(project_kernel, grid_spec=pltpu.PrefetchScalarGridSpec(num...]
    pallas_call x2 -> x3, Pallas kernels: 11.1 us -> 13.5 us  [leave(): pl.pallas_call(kernel, grid_spec=pltpu.PrefetchScalarGridSpec(num_scalar_...]
  transfers between devices with their start and end apart: 39 -> 43, of which waited for: 20 -> 24; matrix products, arithmetic and copies ran while one was open for 3% -> 4% of each run, Pallas kernels for 12% -> 10%
where the time goes in v7:
time: 206 us; the launch traced here: 208 us
  waiting for transfers between devices  75.1 us (36%)
  starting transfers between devices  68.2 us (33%)
  Pallas kernels  47.5 us (23%)
  local copies, waits for them, and re-layouts  10.3 us (5%)
  other arithmetic  6.04 us (3%)
    ppermute x43, waiting for transfers between devices, shift(): lax.ppermute(value, axis, [(i, (i + steps) % count) for i in range(count)])  75.1 us
    ppermute x43, starting transfers between devices, shift(): lax.ppermute(value, axis, [(i, (i + steps) % count) for i in range(count)])  68.2 us
    pallas_call x1, Pallas kernels, project(): pl.pallas_call(project_kernel, grid_spec=pltpu.PrefetchScalarGridSpec(num...  22.4 us
    pallas_call x3, Pallas kernels, leave(): pl.pallas_call(kernel, grid_spec=pltpu.PrefetchScalarGridSpec(num_scalar_...  13.5 us
    pallas_call x1, Pallas kernels, attend(): pl.pallas_call(kernel, in_specs=[pl.BlockSpec(memory_space=pltpu.SMEM)] *...  10.3 us
    unnamed x33, local copies, waits for them, and re-layouts  4.52 us
  transfers between devices with their start and end apart: 43, of which 24 were waited for; matrix products, arithmetic and copies ran while one was open for 4% of the time, Pallas kernels for 10%

profile of v7, /device:TPU:1, one launch (start us, length us, event | category | flops | bytes accessed | tf_op | source)
XLA Modules:
  0.0 207.6 jit_solution(13395633298982389888)
XLA Ops:
  1.1 1.5 collective-permute-start
  4.7 1.7 collective-permute-start.1
  6.5 2.1 %collective-permute-start.2 = (bf16[512,640]{1,0:T(8,128)(2,1)S(1)}, bf16[512,640]{1,0:T(8,128)(2,1)S(1)}, u32[]{:S(2)}, u32[]{:S(2)}) collective-permute-start(bf16[512,640]{1,0:T(8,128)(2,1)S(1)} %lay.1.refs_0_), channel_id=1, source_target_pairs={{0,6},{2,0},{4,2},{6,4},{1,7},{3,1},{5,3},{7,5},{8,14},{10,8},{12,... | collective-permute-start | bytes 1966088 | tf_op jit(solution)/shard_map/ppermute | solution.py:27
  9.9 13.5 %collective-permute-done.1.refs_1_ = bf16[512,640]{1,0:T(8,128)(2,1)S(1)} collective-permute-done((bf16[512,640]{1,0:T(8,128)(2,1)S(1)}, bf16[512,640]{1,0:T(8,128)(2,1)S(1)}, u32[]{:S(2)}, u32[]{:S(2)}) %collective-permute-start.1) | collective-permute-done | bytes 655392 | tf_op jit(solution)/shard_map/ppermute | solution.py:27
  26.0 2.3 %collective-permute-start.6 = (bf16[512,640]{1,0:T(8,128)(2,1)}, bf16[512,640]{1,0:T(8,128)(2,1)S(1)}, u32[]{:S(2)}, u32[]{:S(2)}) collective-permute-start(bf16[512,640]{1,0:T(8,128)(2,1)} %collective-permute-done.3.refs_3_), channel_id=1, source_target_pairs={{0,6},{2,0},{4,2},{6,4},{1,7},{3,1},{5,3},{7,5},{8,14},{10,8},{12,... | collective-permute-start | bytes 1966088 | tf_op jit(solution)/shard_map/ppermute | solution.py:27
  30.1 2.7 %collective-permute-done.8 = s32[4,64]{1,0:T(4,128)S(1)} collective-permute-done((s32[4,64]{1,0:T(4,128)S(1)}, s32[4,64]{1,0:T(4,128)S(1)}, u32[]{:S(2)}, u32[]{:S(2)}) %collective-permute-start.8) | collective-permute-done | bytes 1056 | tf_op jit(solution)/shard_map/ppermute | solution.py:27
  32.8 1.5 collective-permute-start.9
  34.4 2.4 %collective-permute-done.9 = s32[4,64]{1,0:T(4,128)S(1)} collective-permute-done((s32[4,64]{1,0:T(4,128)S(1)}, s32[4,64]{1,0:T(4,128)S(1)}, u32[]{:S(2)}, u32[]{:S(2)}) %collective-permute-start.9) | collective-permute-done | bytes 1056 | tf_op jit(solution)/shard_map/ppermute | solution.py:27
  43.1 2.5 %collective-permute-start.12 = (bf16[512,256]{1,0:T(8,128)(2,1)}, bf16[512,256]{1,0:T(8,128)(2,1)}, u32[]{:S(2)}, u32[]{:S(2)}) collective-permute-start(bf16[512,256]{1,0:T(8,128)(2,1)} %slice.20), channel_id=1, source_target_pairs={{0,6},{2,0},{4,2},{6,4},{1,7},{3,1},{5,3},{7,5},{8,14},{10,8},{12,... | collective-permute-start | bytes 786440 | tf_op jit(solution)/shard_map/ppermute | solution.py:27
  48.4 3.3 %collective-permute-done.13.refs_9_ = bf16[512,128]{1,0:T(8,128)(2,1)} collective-permute-done((bf16[512,128]{1,0:T(8,128)(2,1)}, bf16[512,128]{1,0:T(8,128)(2,1)}, u32[]{:S(2)}, u32[]{:S(2)}) %collective-permute-start.13) | collective-permute-done | bytes 131104 | tf_op jit(solution)/shard_map/ppermute | solution.py:27
  52.4 22.4 %project.1 = (bf16[256,512]{1,0:T(8,128)(2,1)}, bf16[128,512]{1,0:T(8,128)(2,1)}, bf16[256,512]{1,0:T(8,128)(2,1)}, bf16[128,512]{1,0:T(8,128)(2,1)}, bf16[256,5...) custom-call(s32[8]{0:T(128)} %stack.94.chips, ...), custom_call_target="tpu_custom_call" | custom-call | flops 8053063680 | bytes 20971520 | tf_op jit(solution)/shard_map/project/pallas_call | solution.py:144
  76.1 1.5 collective-permute-start.16
  77.6 2.9 %collective-permute-start.17 = (bf16[256,512]{1,0:T(8,128)(2,1)}, bf16[256,512]{1,0:T(8,128)(2,1)S(1)}, u32[]{:S(2)}, u32[]{:S(2)}) collective-permute-start(bf16[256,512]{1,0:T(8,128)(2,1)} %get-tuple-element.64.refs_4_), channel_id=1, source_target_pairs={{0,64},{64,0},{1,65},{65,1},{2,66},{66,2},{3,67},{67,3},{4,68},{68... | collective-permute-start | bytes 786440 | tf_op jit(solution)/shard_map/ppermute | solution.py:27
  81.5 3.0 %collective-permute-done.17.refs_7_ = bf16[256,512]{1,0:T(8,128)(2,1)S(1)} collective-permute-done((bf16[256,512]{1,0:T(8,128)(2,1)}, bf16[256,512]{1,0:T(8,128)(2,1)S(1)}, u32[]{:S(2)}, u32[]{:S(2)}) %collective-permute-start.17) | collective-permute-done | bytes 262176 | tf_op jit(solution)/shard_map/ppermute | solution.py:27
  85.5 6.5 %collective-permute-start.23 = (bf16[768,512]{1,0:T(8,128)(2,1)S(1)}, bf16[768,512]{1,0:T(8,128)(2,1)S(1)}, u32[]{:S(2)}, u32[]{:S(2)}) collective-permute-start(bf16[768,512]{1,0:T(8,128)(2,1)S(1)} %pad_maximum_fusion), channel_id=1, source_target_pairs={{0,1},{1,0},{2,3},{3,2},{4,5},{5,4},{6,7},{7,6},{8,9},{9,8},{10,11... | collective-permute-start | bytes 2359304 | tf_op jit(solution)/shard_map/ppermute | solution.py:27
  92.0 3.0 %collective-permute-start.19 = (bf16[512,512]{1,0:T(8,128)(2,1)S(1)}, bf16[512,512]{1,0:T(8,128)(2,1)S(1)}, u32[]{:S(2)}, u32[]{:S(2)}) collective-permute-start(bf16[512,512]{1,0:T(8,128)(2,1)S(1)} %constant_dynamic-update-slice_fusion.refs_5_), channel_id=1, source_target_pairs={{0,64},{64,0},{1,65},{65,1},{2,66},{66,2},{3,67},{67,3},{4,68},{68... | collective-permute-start | bytes 1572872 | tf_op jit(solution)/shard_map/ppermute | solution.py:27
  95.0 2.5 %collective-permute-start.21 = (bf16[128,512]{1,0:T(8,128)(2,1)}, bf16[128,512]{1,0:T(8,128)(2,1)S(1)}, u32[]{:S(2)}, u32[]{:S(2)}) collective-permute-start(bf16[128,512]{1,0:T(8,128)(2,1)} %get-tuple-element.69), channel_id=1, source_target_pairs={{0,32},{16,48},{32,0},{48,16},{1,33},{17,49},{33,1},{49,17},{2,34}... | collective-permute-start | bytes 393224 | tf_op jit(solution)/shard_map/ppermute | solution.py:27
  98.5 2.9 %collective-permute-done.20.refs_16_ = bf16[128,512]{1,0:T(8,128)(2,1)S(1)} collective-permute-done((bf16[128,512]{1,0:T(8,128)(2,1)}, bf16[128,512]{1,0:T(8,128)(2,1)S(1)}, u32[]{:S(2)}, u32[]{:S(2)}) %collective-permute-start.20) | collective-permute-done | bytes 131104 | tf_op jit(solution)/shard_map/ppermute | solution.py:27
  101.4 9.3 %collective-permute-start.24 = (bf16[256,512]{1,0:T(8,128)(2,1)S(1)}, bf16[256,512]{1,0:T(8,128)(2,1)S(1)}, u32[]{:S(2)}, u32[]{:S(2)}) collective-permute-start(bf16[256,512]{1,0:T(8,128)(2,1)S(1)} %collective-permute-done.17.refs_7_), channel_id=1, source_target_pairs={{0,1},{1,0},{2,3},{3,2},{4,5},{5,4},{6,7},{7,6},{8,9},{9,8},{10,11... | collective-permute-start | bytes 786440 | tf_op jit(solution)/shard_map/ppermute | solution.py:27
  111.4 4.9 %collective-permute-done.22.refs_18_ = bf16[128,512]{1,0:T(8,128)(2,1)S(1)} collective-permute-done((bf16[128,512]{1,0:T(8,128)(2,1)}, bf16[128,512]{1,0:T(8,128)(2,1)S(1)}, u32[]{:S(2)}, u32[]{:S(2)}) %collective-permute-start.22) | collective-permute-done | bytes 131104 | tf_op jit(solution)/shard_map/ppermute | solution.py:27
  118.1 8.2 %collective-permute-done.26.refs_9_ = bf16[256,512]{1,0:T(8,128)(2,1)S(1)} collective-permute-done((bf16[256,512]{1,0:T(8,128)(2,1)S(1)}, bf16[256,512]{1,0:T(8,128)(2,1)S(1)}, u32[]{:S(2)}, u32[]{:S(2)}) %collective-permute-start.26) | collective-permute-done | bytes 262176 | tf_op jit(solution)/shard_map/ppermute | solution.py:27
  130.5 10.3 %attend.1 = (bf16[512,128]{1,0:T(8,128)(2,1)S(1)}, bf16[512,128]{1,0:T(8,128)(2,1)S(1)}, bf16[512,128]{1,0:T(8,128)(2,1)S(1)}, bf16[512,128]{1,0:T(8,128)(2,1)S(1)}) custom-call(s32[16,64]{1,0:T(8,128)S(1)} %select_reduce_fusion.2.refs_0_, s32[16]{0:T(128)S(1)} %get-tuple-element.97.refs_1_, s32[17]{0:T(128)S(1)} %select_reduce_fusion.5.refs_2_, ...), custom_call_target="tpu_custom_call" | custom-call | flops 2147483648 | bytes 4194304 | tf_op jit(solution)/shard_map/attend/pallas_call | solution.py:286
  140.9 8.0 %collective-permute-start.30 = (bf16[512,128]{1,0:T(8,128)(2,1)S(1)}, bf16[512,128]{1,0:T(8,128)(2,1)S(1)}, u32[]{:S(2)}, u32[]{:S(2)}) collective-permute-start(bf16[512,128]{1,0:T(8,128)(2,1)S(1)} %get-tuple-element.75), channel_id=1, source_target_pairs={{0,48},{16,0},{32,16},{48,32},{1,49},{17,1},{33,17},{49,33},{2,50}... | collective-permute-start | bytes 393224 | tf_op jit(solution)/shard_map/ppermute | solution.py:27
  149.6 4.9 %collective-permute-done.30.refs_5_ = bf16[512,128]{1,0:T(8,128)(2,1)S(1)} collective-permute-done((bf16[512,128]{1,0:T(8,128)(2,1)S(1)}, bf16[512,128]{1,0:T(8,128)(2,1)S(1)}, u32[]{:S(2)}, u32[]{:S(2)}) %collective-permute-start.30) | collective-permute-done | bytes 131104 | tf_op jit(solution)/shard_map/ppermute | solution.py:27
  154.8 3.2 %collective-permute-done.32.refs_7_ = bf16[512,128]{1,0:T(8,128)(2,1)S(1)} collective-permute-done((bf16[512,128]{1,0:T(8,128)(2,1)S(1)}, bf16[512,128]{1,0:T(8,128)(2,1)S(1)}, u32[]{:S(2)}, u32[]{:S(2)}) %collective-permute-start.32) | collective-permute-done | bytes 131104 | tf_op jit(solution)/shard_map/ppermute | solution.py:27
  157.9 2.8 %leave.3 = (bf16[512,256]{1,0:T(8,128)(2,1)S(1)}, bf16[512,256]{1,0:T(8,128)(2,1)S(1)}, bf16[512,128]{1,0:T(8,128)(2,1)S(1)}) custom-call(s32[1]{0:T(128)} %bitcast.12.refs_0_, s32[4]{0:T(128)S(1)} %pad_add_fusion.1.refs_1_, bf16[256,5120]{1,0:T(8,128)(2,1)S(1)} %copy-done, bf16[256,5120]{1,0:T(8,128)(2,1)} %collective-permute-done.25.refs_3_, ...), custom_call_target="tpu_custom_call" | custom-call | flops 335544320 | bytes 1310720 | tf_op jit(solution)/shard_map/leave/pallas_call | solution.py:352
  160.9 2.7 %collective-permute-start.35 = (bf16[512,128]{1,0:T(8,128)(2,1)S(1)}, bf16[512,128]{1,0:T(8,128)(2,1)S(1)}, u32[]{:S(2)}, u32[]{:S(2)}) collective-permute-start(bf16[512,128]{1,0:T(8,128)(2,1)S(1)} %get-tuple-element.80), channel_id=1, source_target_pairs={{0,6},{2,0},{4,2},{6,4},{1,7},{3,1},{5,3},{7,5},{8,14},{10,8},{12,... | collective-permute-start | bytes 393224 | tf_op jit(solution)/shard_map/ppermute | solution.py:27
  163.7 4.6 %leave.5 = (bf16[512,640]{1,0:T(8,128)(2,1)S(1)}, bf16[512,640]{1,0:T(8,128)(2,1)S(1)}, bf16[512,640]{1,0:T(8,128)(2,1)S(1)}) custom-call(s32[3]{0:T(128)S(1)} %pad_add_fusion.3.refs_0_, s32[4]{0:T(128)S(1)} %pad_add_fusion.1.refs_1_, bf16[256,5120]{1,0:T(8,128)(2,1)S(1)} %copy-done, bf16[256,5120]{1,0:T(8,128)(2,1)} %collective-permute-done.25.refs_3_, ...), custom_call_target="tpu_custom_call" | custom-call | flops 1006632960 | bytes 3932160 | tf_op jit(solution)/shard_map/leave/pallas_call | solution.py:352
  172.1 6.2 %leave.4 = (bf16[512,640]{1,0:T(8,128)(2,1)S(1)}, bf16[512,640]{1,0:T(8,128)(2,1)}, bf16[512,640]{1,0:T(8,128)(2,1)S(1)}, bf16[512,640]{1,0:T(8,128)(2,1)S(1)}) custom-call(s32[4]{0:T(128)S(1)} %pad_add_fusion.refs_0_, s32[4]{0:T(128)S(1)} %pad_add_fusion.1.refs_1_, bf16[256,5120]{1,0:T(8,128)(2,1)S(1)} %copy-done, ...), custom_call_target="tpu_custom_call" | custom-call | flops 1342177280 | bytes 5242880 | tf_op jit(solution)/shard_map/leave/pallas_call | solution.py:352
  178.3 5.7 %collective-permute-done.36.refs_1_ = bf16[512,640]{1,0:T(8,128)(2,1)S(1)} collective-permute-done((bf16[512,640]{1,0:T(8,128)(2,1)S(1)}, bf16[512,640]{1,0:T(8,128)(2,1)S(1)}, u32[]{:S(2)}, u32[]{:S(2)}) %collective-permute-start.36) | collective-permute-done | bytes 655392 | tf_op jit(solution)/shard_map/ppermute | solution.py:27
  186.8 12.5 %collective-permute-done.40.refs_2_ = bf16[512,640]{1,0:T(8,128)(2,1)S(1)} collective-permute-done((bf16[512,640]{1,0:T(8,128)(2,1)}, bf16[512,640]{1,0:T(8,128)(2,1)S(1)}, u32[]{:S(2)}, u32[]{:S(2)}) %collective-permute-start.40) | collective-permute-done | bytes 655392 | tf_op jit(solution)/shard_map/ppermute | solution.py:27
  200.9 4.2 %collective-permute-start.42 = (bf16[320,512]{1,0:T(8,128)(2,1)S(1)}, bf16[320,512]{1,0:T(8,128)(2,1)S(1)}, u32[]{:S(2)}, u32[]{:S(2)}) collective-permute-start(bf16[320,512]{1,0:T(8,128)(2,1)S(1)} %constant_dynamic-slice_fusion), channel_id=1, source_target_pairs={{0,1},{1,0},{2,3},{3,2},{4,5},{5,4},{6,7},{7,6},{8,9},{9,8},{10,11... | collective-permute-start | bytes 983048 | tf_op jit(solution)/shard_map/ppermute | solution.py:27
  (126 shorter events, 41.6 us)
Async XLA Ops:
  4.6 47.1 %collective-permute-start.14 = (bf16[3,5120,256]{2,1,0:T(8,128)(2,1)}, bf16[3,5120,256]{2,1,0:T(8,128)(2,1)}, u32[]{:S(2)}, u32[]{:S(2)}) collective-permute-start(bf16[3,5120,256]{2,1,0:T(8,128)(2,1)} %refs_11_.1), channel_id=1, source_target_pairs={{0,1},{1,0},{2,3},{3,2},{4,5},{5,4},{6,7},{7,6},{8,9},{9,8},{10,11... | collective-permute-start | bytes 23592968 | tf_op jit(solution)/shard_map/ppermute | solution.py:27
  4.7 18.7 %collective-permute-start.1 = (bf16[512,640]{1,0:T(8,128)(2,1)S(1)}, bf16[512,640]{1,0:T(8,128)(2,1)S(1)}, u32[]{:S(2)}, u32[]{:S(2)}) collective-permute-start(bf16[512,640]{1,0:T(8,128)(2,1)S(1)} %lay.1.refs_0_), channel_id=1, source_target_pairs={{0,2},{2,4},{4,6},{6,0},{1,3},{3,5},{5,7},{7,1},{8,10},{10,12},{12... | collective-permute-start | bytes 1966088 | tf_op jit(solution)/shard_map/ppermute | solution.py:27
  6.5 17.0 %collective-permute-start.2 = (bf16[512,640]{1,0:T(8,128)(2,1)S(1)}, bf16[512,640]{1,0:T(8,128)(2,1)S(1)}, u32[]{:S(2)}, u32[]{:S(2)}) collective-permute-start(bf16[512,640]{1,0:T(8,128)(2,1)S(1)} %lay.1.refs_0_), channel_id=1, source_target_pairs={{0,6},{2,0},{4,2},{6,4},{1,7},{3,1},{5,3},{7,5},{8,14},{10,8},{12,... | collective-permute-start | bytes 1966088 | tf_op jit(solution)/shard_map/ppermute | solution.py:27
  8.6 15.8 %collective-permute-start.3 = (bf16[512,640]{1,0:T(8,128)(2,1)S(1)}, bf16[512,640]{1,0:T(8,128)(2,1)}, u32[]{:S(2)}, u32[]{:S(2)}) collective-permute-start(bf16[512,640]{1,0:T(8,128)(2,1)S(1)} %lay.1.refs_0_), channel_id=1, source_target_pairs={{0,8},{8,0},{1,9},{9,1},{2,10},{10,2},{3,11},{11,3},{4,12},{12,4},... | collective-permute-start | bytes 1966088 | tf_op jit(solution)/shard_map/ppermute | solution.py:27
  24.3 15.9 %collective-permute-start.4 = (bf16[512,640]{1,0:T(8,128)(2,1)S(1)}, bf16[512,640]{1,0:T(8,128)(2,1)S(1)}, u32[]{:S(2)}, u32[]{:S(2)}) collective-permute-start(bf16[512,640]{1,0:T(8,128)(2,1)S(1)} %collective-permute-done.1.refs_1_), channel_id=1, source_target_pairs={{0,2},{2,4},{4,6},{6,0},{1,3},{3,5},{5,7},{7,1},{8,10},{10,12},{12... | collective-permute-start | bytes 1966088 | tf_op jit(solution)/shard_map/ppermute | solution.py:27
  24.7 15.6 %collective-permute-start.5 = (bf16[512,640]{1,0:T(8,128)(2,1)S(1)}, bf16[512,640]{1,0:T(8,128)(2,1)S(1)}, u32[]{:S(2)}, u32[]{:S(2)}) collective-permute-start(bf16[512,640]{1,0:T(8,128)(2,1)S(1)} %collective-permute-done.1.refs_1_), channel_id=1, source_target_pairs={{0,8},{8,0},{1,9},{9,1},{2,10},{10,2},{3,11},{11,3},{4,12},{12,4},... | collective-permute-start | bytes 1966088 | tf_op jit(solution)/shard_map/ppermute | solution.py:27
  26.0 14.6 %collective-permute-start.6 = (bf16[512,640]{1,0:T(8,128)(2,1)}, bf16[512,640]{1,0:T(8,128)(2,1)S(1)}, u32[]{:S(2)}, u32[]{:S(2)}) collective-permute-start(bf16[512,640]{1,0:T(8,128)(2,1)} %collective-permute-done.3.refs_3_), channel_id=1, source_target_pairs={{0,6},{2,0},{4,2},{6,4},{1,7},{3,1},{5,3},{7,5},{8,14},{10,8},{12,... | collective-permute-start | bytes 1966088 | tf_op jit(solution)/shard_map/ppermute | solution.py:27
  41.5 10.2 %collective-permute-start.11 = (bf16[512,256]{1,0:T(8,128)(2,1)}, bf16[512,256]{1,0:T(8,128)(2,1)S(1)}, u32[]{:S(2)}, u32[]{:S(2)}) collective-permute-start(bf16[512,256]{1,0:T(8,128)(2,1)} %slice.19), channel_id=1, source_target_pairs={{0,8},{8,0},{1,9},{9,1},{2,10},{10,2},{3,11},{11,3},{4,12},{12,4},... | collective-permute-start | bytes 786440 | tf_op jit(solution)/shard_map/ppermute | solution.py:27
  43.1 8.5 %collective-permute-start.12 = (bf16[512,256]{1,0:T(8,128)(2,1)}, bf16[512,256]{1,0:T(8,128)(2,1)}, u32[]{:S(2)}, u32[]{:S(2)}) collective-permute-start(bf16[512,256]{1,0:T(8,128)(2,1)} %slice.20), channel_id=1, source_target_pairs={{0,6},{2,0},{4,2},{6,4},{1,7},{3,1},{5,3},{7,5},{8,14},{10,8},{12,... | collective-permute-start | bytes 786440 | tf_op jit(solution)/shard_map/ppermute | solution.py:27
  74.8 6.7 %collective-permute-start.15 = (bf16[256,512]{1,0:T(8,128)(2,1)}, bf16[256,512]{1,0:T(8,128)(2,1)S(1)}, u32[]{:S(2)}, u32[]{:S(2)}) collective-permute-start(bf16[256,512]{1,0:T(8,128)(2,1)} %get-tuple-element.62), channel_id=1, source_target_pairs={{0,16},{16,32},{32,48},{48,0},{1,17},{17,33},{33,49},{49,1},{2,18}... | collective-permute-start | bytes 786440 | tf_op jit(solution)/shard_map/ppermute | solution.py:27
  77.6 6.9 %collective-permute-start.17 = (bf16[256,512]{1,0:T(8,128)(2,1)}, bf16[256,512]{1,0:T(8,128)(2,1)S(1)}, u32[]{:S(2)}, u32[]{:S(2)}) collective-permute-start(bf16[256,512]{1,0:T(8,128)(2,1)} %get-tuple-element.64.refs_4_), channel_id=1, source_target_pairs={{0,64},{64,0},{1,65},{65,1},{2,66},{66,2},{3,67},{67,3},{4,68},{68... | collective-permute-start | bytes 786440 | tf_op jit(solution)/shard_map/ppermute | solution.py:27
  85.5 30.8 %collective-permute-start.23 = (bf16[768,512]{1,0:T(8,128)(2,1)S(1)}, bf16[768,512]{1,0:T(8,128)(2,1)S(1)}, u32[]{:S(2)}, u32[]{:S(2)}) collective-permute-start(bf16[768,512]{1,0:T(8,128)(2,1)S(1)} %pad_maximum_fusion), channel_id=1, source_target_pairs={{0,1},{1,0},{2,3},{3,2},{4,5},{5,4},{6,7},{7,6},{8,9},{9,8},{10,11... | collective-permute-start | bytes 2359304 | tf_op jit(solution)/shard_map/ppermute | solution.py:27
  92.0 24.3 %collective-permute-start.19 = (bf16[512,512]{1,0:T(8,128)(2,1)S(1)}, bf16[512,512]{1,0:T(8,128)(2,1)S(1)}, u32[]{:S(2)}, u32[]{:S(2)}) collective-permute-start(bf16[512,512]{1,0:T(8,128)(2,1)S(1)} %constant_dynamic-update-slice_fusion.refs_5_), channel_id=1, source_target_pairs={{0,64},{64,0},{1,65},{65,1},{2,66},{66,2},{3,67},{67,3},{4,68},{68... | collective-permute-start | bytes 1572872 | tf_op jit(solution)/shard_map/ppermute | solution.py:27
  95.0 6.4 %collective-permute-start.20 = (bf16[128,512]{1,0:T(8,128)(2,1)}, bf16[128,512]{1,0:T(8,128)(2,1)S(1)}, u32[]{:S(2)}, u32[]{:S(2)}) collective-permute-start(bf16[128,512]{1,0:T(8,128)(2,1)} %get-tuple-element.68), channel_id=1, source_target_pairs={{0,16},{16,32},{32,48},{48,0},{1,17},{17,33},{33,49},{49,1},{2,18}... | collective-permute-start | bytes 393224 | tf_op jit(solution)/shard_map/ppermute | solution.py:27
  95.0 15.9 %collective-permute-start.21 = (bf16[128,512]{1,0:T(8,128)(2,1)}, bf16[128,512]{1,0:T(8,128)(2,1)S(1)}, u32[]{:S(2)}, u32[]{:S(2)}) collective-permute-start(bf16[128,512]{1,0:T(8,128)(2,1)} %get-tuple-element.69), channel_id=1, source_target_pairs={{0,32},{16,48},{32,0},{48,16},{1,33},{17,49},{33,1},{49,17},{2,34}... | collective-permute-start | bytes 393224 | tf_op jit(solution)/shard_map/ppermute | solution.py:27
  97.9 18.4 %collective-permute-start.18 = (bf16[256,512]{1,0:T(8,128)(2,1)}, bf16[256,512]{1,0:T(8,128)(2,1)S(1)}, u32[]{:S(2)}, u32[]{:S(2)}) collective-permute-start(bf16[256,512]{1,0:T(8,128)(2,1)} %get-tuple-element.66), channel_id=1, source_target_pairs={{0,32},{16,48},{32,0},{48,16},{1,33},{17,49},{33,1},{49,17},{2,34}... | collective-permute-start | bytes 786440 | tf_op jit(solution)/shard_map/ppermute | solution.py:27
  101.4 14.9 %collective-permute-start.24 = (bf16[256,512]{1,0:T(8,128)(2,1)S(1)}, bf16[256,512]{1,0:T(8,128)(2,1)S(1)}, u32[]{:S(2)}, u32[]{:S(2)}) collective-permute-start(bf16[256,512]{1,0:T(8,128)(2,1)S(1)} %collective-permute-done.17.refs_7_), channel_id=1, source_target_pairs={{0,1},{1,0},{2,3},{3,2},{4,5},{5,4},{6,7},{7,6},{8,9},{9,8},{10,11... | collective-permute-start | bytes 786440 | tf_op jit(solution)/shard_map/ppermute | solution.py:27
  116.3 41.6 %collective-permute-start.25 = (bf16[256,5120]{1,0:T(8,128)(2,1)S(1)}, bf16[256,5120]{1,0:T(8,128)(2,1)}, u32[]{:S(2)}, u32[]{:S(2)}) collective-permute-start(bf16[256,5120]{1,0:T(8,128)(2,1)S(1)} %copy-done), channel_id=1, source_target_pairs={{0,1},{1,0},{2,3},{3,2},{4,5},{5,4},{6,7},{7,6},{8,9},{9,8},{10,11... | collective-permute-start | bytes 7864328 | tf_op jit(solution)/shard_map/ppermute | solution.py:27
  117.2 10.3 %collective-permute-start.28 = (bf16[512,512]{1,0:T(8,128)(2,1)S(1)}, bf16[512,512]{1,0:T(8,128)(2,1)S(1)}, u32[]{:S(2)}, u32[]{:S(2)}) collective-permute-start(bf16[512,512]{1,0:T(8,128)(2,1)S(1)} %collective-permute-done.19.refs_8_), channel_id=1, source_target_pairs={{0,1},{1,0},{2,3},{3,2},{4,5},{5,4},{6,7},{7,6},{8,9},{9,8},{10,11... | collective-permute-start | bytes 1572872 | tf_op jit(solution)/shard_map/ppermute | solution.py:27
  117.3 9.0 %collective-permute-start.26 = (bf16[256,512]{1,0:T(8,128)(2,1)S(1)}, bf16[256,512]{1,0:T(8,128)(2,1)S(1)}, u32[]{:S(2)}, u32[]{:S(2)}) collective-permute-start(bf16[256,512]{1,0:T(8,128)(2,1)S(1)} %collective-permute-done.18.refs_6_), channel_id=1, source_target_pairs={{0,64},{64,0},{1,65},{65,1},{2,66},{66,2},{3,67},{67,3},{4,68},{68... | collective-permute-start | bytes 786440 | tf_op jit(solution)/shard_map/ppermute | solution.py:27
  117.4 10.1 %collective-permute-start.27 = (bf16[256,512]{1,0:T(8,128)(2,1)S(1)}, bf16[256,512]{1,0:T(8,128)(2,1)S(1)}, u32[]{:S(2)}, u32[]{:S(2)}) collective-permute-start(bf16[256,512]{1,0:T(8,128)(2,1)S(1)} %collective-permute-done.18.refs_6_), channel_id=1, source_target_pairs={{0,1},{1,0},{2,3},{3,2},{4,5},{5,4},{6,7},{7,6},{8,9},{9,8},{10,11... | collective-permute-start | bytes 786440 | tf_op jit(solution)/shard_map/ppermute | solution.py:27
  140.9 13.6 %collective-permute-start.30 = (bf16[512,128]{1,0:T(8,128)(2,1)S(1)}, bf16[512,128]{1,0:T(8,128)(2,1)S(1)}, u32[]{:S(2)}, u32[]{:S(2)}) collective-permute-start(bf16[512,128]{1,0:T(8,128)(2,1)S(1)} %get-tuple-element.75), channel_id=1, source_target_pairs={{0,48},{16,0},{32,16},{48,32},{1,49},{17,1},{33,17},{49,33},{2,50}... | collective-permute-start | bytes 393224 | tf_op jit(solution)/shard_map/ppermute | solution.py:27
  148.8 9.1 %collective-permute-start.32 = (bf16[512,128]{1,0:T(8,128)(2,1)S(1)}, bf16[512,128]{1,0:T(8,128)(2,1)S(1)}, u32[]{:S(2)}, u32[]{:S(2)}) collective-permute-start(bf16[512,128]{1,0:T(8,128)(2,1)S(1)} %get-tuple-element.77), channel_id=1, source_target_pairs={{0,16},{16,32},{32,48},{48,0},{1,17},{17,33},{33,49},{49,1},{2,18}... | collective-permute-start | bytes 393224 | tf_op jit(solution)/shard_map/ppermute | solution.py:27
  160.8 7.5 %collective-permute-start.33 = (bf16[512,256]{1,0:T(8,128)(2,1)S(1)}, bf16[512,256]{1,0:T(8,128)(2,1)S(1)}, u32[]{:S(2)}, u32[]{:S(2)}) collective-permute-start(bf16[512,256]{1,0:T(8,128)(2,1)S(1)} %get-tuple-element.78), channel_id=1, source_target_pairs={{0,8},{8,0},{1,9},{9,1},{2,10},{10,2},{3,11},{11,3},{4,12},{12,4},... | collective-permute-start | bytes 786440 | tf_op jit(solution)/shard_map/ppermute | solution.py:27
  160.8 8.3 %collective-permute-start.34 = (bf16[512,256]{1,0:T(8,128)(2,1)S(1)}, bf16[512,256]{1,0:T(8,128)(2,1)S(1)}, u32[]{:S(2)}, u32[]{:S(2)}) collective-permute-start(bf16[512,256]{1,0:T(8,128)(2,1)S(1)} %get-tuple-element.79), channel_id=1, source_target_pairs={{0,2},{2,4},{4,6},{6,0},{1,3},{3,5},{5,7},{7,1},{8,10},{10,12},{12... | collective-permute-start | bytes 786440 | tf_op jit(solution)/shard_map/ppermute | solution.py:27
  160.9 7.3 %collective-permute-start.35 = (bf16[512,128]{1,0:T(8,128)(2,1)S(1)}, bf16[512,128]{1,0:T(8,128)(2,1)S(1)}, u32[]{:S(2)}, u32[]{:S(2)}) collective-permute-start(bf16[512,128]{1,0:T(8,128)(2,1)S(1)} %get-tuple-element.80), channel_id=1, source_target_pairs={{0,6},{2,0},{4,2},{6,4},{1,7},{3,1},{5,3},{7,5},{8,14},{10,8},{12,... | collective-permute-start | bytes 393224 | tf_op jit(solution)/shard_map/ppermute | solution.py:27
  169.4 14.6 %collective-permute-start.36 = (bf16[512,640]{1,0:T(8,128)(2,1)S(1)}, bf16[512,640]{1,0:T(8,128)(2,1)S(1)}, u32[]{:S(2)}, u32[]{:S(2)}) collective-permute-start(bf16[512,640]{1,0:T(8,128)(2,1)S(1)} %get-tuple-element.90), channel_id=1, source_target_pairs={{0,6},{2,0},{4,2},{6,4},{1,7},{3,1},{5,3},{7,5},{8,14},{10,8},{12,... | collective-permute-start | bytes 1966088 | tf_op jit(solution)/shard_map/ppermute | solution.py:27
  169.4 14.5 %collective-permute-start.37 = (bf16[512,640]{1,0:T(8,128)(2,1)S(1)}, bf16[512,640]{1,0:T(8,128)(2,1)S(1)}, u32[]{:S(2)}, u32[]{:S(2)}) collective-permute-start(bf16[512,640]{1,0:T(8,128)(2,1)S(1)} %get-tuple-element.91), channel_id=1, source_target_pairs={{0,8},{8,0},{1,9},{9,1},{2,10},{10,2},{3,11},{11,3},{4,12},{12,4},... | collective-permute-start | bytes 1966088 | tf_op jit(solution)/shard_map/ppermute | solution.py:27
  170.6 14.7 %collective-permute-start.38 = (bf16[512,640]{1,0:T(8,128)(2,1)S(1)}, bf16[512,640]{1,0:T(8,128)(2,1)S(1)}, u32[]{:S(2)}, u32[]{:S(2)}) collective-permute-start(bf16[512,640]{1,0:T(8,128)(2,1)S(1)} %get-tuple-element.93), channel_id=1, source_target_pairs={{0,2},{2,4},{4,6},{6,0},{1,3},{3,5},{5,7},{7,1},{8,10},{10,12},{12... | collective-permute-start | bytes 1966088 | tf_op jit(solution)/shard_map/ppermute | solution.py:27
  178.2 21.1 %collective-permute-start.40 = (bf16[512,640]{1,0:T(8,128)(2,1)}, bf16[512,640]{1,0:T(8,128)(2,1)S(1)}, u32[]{:S(2)}, u32[]{:S(2)}) collective-permute-start(bf16[512,640]{1,0:T(8,128)(2,1)} %get-tuple-element.95), channel_id=1, source_target_pairs={{0,2},{2,4},{4,6},{6,0},{1,3},{3,5},{5,7},{7,1},{8,10},{10,12},{12... | collective-permute-start | bytes 1966088 | tf_op jit(solution)/shard_map/ppermute | solution.py:27
  185.7 13.6 %collective-permute-start.39 = (bf16[512,640]{1,0:T(8,128)(2,1)S(1)}, bf16[512,640]{1,0:T(8,128)(2,1)S(1)}, u32[]{:S(2)}, u32[]{:S(2)}) collective-permute-start(bf16[512,640]{1,0:T(8,128)(2,1)S(1)} %get-tuple-element.94), channel_id=1, source_target_pairs={{0,6},{2,0},{4,2},{6,4},{1,7},{3,1},{5,3},{7,5},{8,14},{10,8},{12,... | collective-permute-start | bytes 1966088 | tf_op jit(solution)/shard_map/ppermute | solution.py:27
  185.8 13.6 %collective-permute-start.41 = (bf16[512,640]{1,0:T(8,128)(2,1)S(1)}, bf16[512,640]{1,0:T(8,128)(2,1)S(1)}, u32[]{:S(2)}, u32[]{:S(2)}) collective-permute-start(bf16[512,640]{1,0:T(8,128)(2,1)S(1)} %get-tuple-element.96), channel_id=1, source_target_pairs={{0,8},{8,0},{1,9},{9,1},{2,10},{10,2},{3,11},{11,3},{4,12},{12,4},... | collective-permute-start | bytes 1966088 | tf_op jit(solution)/shard_map/ppermute | solution.py:27
  (27 other events, 236.2 us)

commit v8 on v7

--- a/solution.py
+++ b/solution.py
@@ -60,7 +60,7 @@
     return lax.optimization_barrier((*arrays, *others))[: len(arrays)]
 
 
-ROWS = 32
+ROWS = 64
 
 
 def project_kernel(chips, heads, *refs):
@@ -496,21 +496,21 @@
     kv, queries = made[::2], made[1::2]
     one, three = shift(kv[1], "x", 1), shift(kv[3], "x", 3)
     away_kv = swap(kv[0], "yh")
-    one, three = together((one, three), (away_kv,))
+    q_one, q_three = shift(queries[1], "x", 1), shift(queries[3], "x", 3)
+    one, three = together((one, three), (away_kv, q_one, q_three))
     both = jnp.concatenate([one, three], axis=0)
     away_both = swap(both, "yh")
-    kv_two, *asked = together((kv[2], *queries[1:]), (one,))
-    two = shift(kv_two, "x", 2)
-    queries = [queries[0]] + [shift(asked[i - 1], "x", i) for i in (1, 2, 3)]
+    kv_two, q_two = together((kv[2], queries[2]), (one,))
+    two, q_two = shift(kv_two, "x", 2), shift(q_two, "x", 2)
     near = swap(jnp.concatenate([kv[0], both], axis=0), "core")
     away_kv_other = swap(away_kv, "core")
-    two, out_own = together(
-        (two, out_weight), (away_both, *queries[1:], *lists, near, away_kv_other)
-    )
+    (two,) = together((two,), (away_both, q_two, *lists, near, away_kv_other))
     away_two = swap(two, "yh")
+    (out_own,) = together((out_weight,), (away_two,))
+    leaving = out_weight, swap(out_own, "core")
     arrays = [kv[0], both, two, away_kv, away_both, away_two, near, swap(two, "core")]
-    arrays += [away_kv_other, swap(away_both, "core"), swap(away_two, "core")] + queries
-    leaving = out_weight, swap(out_own, "core")
+    arrays += [away_kv_other, swap(away_both, "core"), swap(away_two, "core")]
+    arrays += [queries[0], q_one, q_two, q_three]
     step = 2 * BLK
     plan = []
     for index, array in ((0, 0), (4, 3), (12, 8)):

time: 206 us -> 204 us (level); the launches traced: 208 us -> 202 us
  starting transfers between devices: 68.2 us -> 52.5 us
  waiting for transfers between devices: 75.1 us -> 82.4 us
  Pallas kernels: 47.5 us -> 50.4 us
    ppermute x43, starting transfers between devices: 68.2 us -> 52.5 us  [shift(): lax.ppermute(value, axis, [(i, (i + steps) % count) for i in range(count)])]
    ppermute x43, waiting for transfers between devices: 75.1 us -> 82.4 us  [shift(): lax.ppermute(value, axis, [(i, (i + steps) % count) for i in range(count)])]
    pallas_call x1, Pallas kernels: 10.3 us -> 14.3 us  [attend(): pl.pallas_call(kernel, in_specs=[pl.BlockSpec(memory_space=pltpu.SMEM)] *...]
  transfers between devices with their start and end apart: 43 -> 43, of which waited for: 24 -> 24; matrix products, arithmetic and copies ran while one was open for 4% -> 4% of each run, Pallas kernels for 10% -> 13%
where the time goes in v8:
time: 204 us; the launch traced here: 202 us
  waiting for transfers between devices  82.4 us (40%)
  starting transfers between devices  52.5 us (26%)
  Pallas kernels  50.4 us (25%)
  local copies, waits for them, and re-layouts  10.3 us (5%)
  other arithmetic  6.04 us (3%)
    ppermute x43, waiting for transfers between devices, shift(): lax.ppermute(value, axis, [(i, (i + steps) % count) for i in range(count)])  82.4 us
    ppermute x43, starting transfers between devices, shift(): lax.ppermute(value, axis, [(i, (i + steps) % count) for i in range(count)])  52.5 us
    pallas_call x1, Pallas kernels, project(): pl.pallas_call(project_kernel, grid_spec=pltpu.PrefetchScalarGridSpec(num...  21.3 us
    pallas_call x1, Pallas kernels, attend(): pl.pallas_call(kernel, in_specs=[pl.BlockSpec(memory_space=pltpu.SMEM)] *...  14.3 us
    pallas_call x3, Pallas kernels, leave(): pl.pallas_call(kernel, grid_spec=pltpu.PrefetchScalarGridSpec(num_scalar_...  13.5 us
    unnamed x33, local copies, waits for them, and re-layouts  4.53 us
  transfers between devices with their start and end apart: 43, of which 24 were waited for; matrix products, arithmetic and copies ran while one was open for 4% of the time, Pallas kernels for 13%

profile of v8, /device:TPU:1, one launch (start us, length us, event | category | flops | bytes accessed | tf_op | source)
XLA Modules:
  0.0 202.1 jit_solution(8150428129165397979)
XLA Ops:
  4.7 1.7 collective-permute-start.1
  6.5 2.1 %collective-permute-start.2 = (bf16[512,640]{1,0:T(8,128)(2,1)S(1)}, bf16[512,640]{1,0:T(8,128)(2,1)S(1)}, u32[]{:S(2)}, u32[]{:S(2)}) collective-permute-start(bf16[512,640]{1,0:T(8,128)(2,1)S(1)} %lay.1.refs_0_), channel_id=1, source_target_pairs={{0,6},{2,0},{4,2},{6,4},{1,7},{3,1},{5,3},{7,5},{8,14},{10,8},{12,... | collective-permute-start | bytes 1966088 | tf_op jit(solution)/shard_map/ppermute | solution.py:27
  9.9 13.5 %collective-permute-done.1.refs_1_ = bf16[512,640]{1,0:T(8,128)(2,1)S(1)} collective-permute-done((bf16[512,640]{1,0:T(8,128)(2,1)S(1)}, bf16[512,640]{1,0:T(8,128)(2,1)S(1)}, u32[]{:S(2)}, u32[]{:S(2)}) %collective-permute-start.1) | collective-permute-done | bytes 655392 | tf_op jit(solution)/shard_map/ppermute | solution.py:27
  26.0 2.3 %collective-permute-start.6 = (bf16[512,640]{1,0:T(8,128)(2,1)}, bf16[512,640]{1,0:T(8,128)(2,1)S(1)}, u32[]{:S(2)}, u32[]{:S(2)}) collective-permute-start(bf16[512,640]{1,0:T(8,128)(2,1)} %collective-permute-done.3.refs_3_), channel_id=1, source_target_pairs={{0,6},{2,0},{4,2},{6,4},{1,7},{3,1},{5,3},{7,5},{8,14},{10,8},{12,... | collective-permute-start | bytes 1966088 | tf_op jit(solution)/shard_map/ppermute | solution.py:27
  30.1 2.7 %collective-permute-done.8 = s32[4,64]{1,0:T(4,128)S(1)} collective-permute-done((s32[4,64]{1,0:T(4,128)S(1)}, s32[4,64]{1,0:T(4,128)S(1)}, u32[]{:S(2)}, u32[]{:S(2)}) %collective-permute-start.8) | collective-permute-done | bytes 1056 | tf_op jit(solution)/shard_map/ppermute | solution.py:27
  32.8 1.5 collective-permute-start.9
  34.4 2.4 %collective-permute-done.9 = s32[4,64]{1,0:T(4,128)S(1)} collective-permute-done((s32[4,64]{1,0:T(4,128)S(1)}, s32[4,64]{1,0:T(4,128)S(1)}, u32[]{:S(2)}, u32[]{:S(2)}) %collective-permute-start.9) | collective-permute-done | bytes 1056 | tf_op jit(solution)/shard_map/ppermute | solution.py:27
  43.1 2.5 %collective-permute-start.12 = (bf16[512,256]{1,0:T(8,128)(2,1)}, bf16[512,256]{1,0:T(8,128)(2,1)}, u32[]{:S(2)}, u32[]{:S(2)}) collective-permute-start(bf16[512,256]{1,0:T(8,128)(2,1)} %slice.20), channel_id=1, source_target_pairs={{0,6},{2,0},{4,2},{6,4},{1,7},{3,1},{5,3},{7,5},{8,14},{10,8},{12,... | collective-permute-start | bytes 786440 | tf_op jit(solution)/shard_map/ppermute | solution.py:27
  48.4 3.3 %collective-permute-done.13.refs_9_ = bf16[512,128]{1,0:T(8,128)(2,1)} collective-permute-done((bf16[512,128]{1,0:T(8,128)(2,1)}, bf16[512,128]{1,0:T(8,128)(2,1)}, u32[]{:S(2)}, u32[]{:S(2)}) %collective-permute-start.13) | collective-permute-done | bytes 131104 | tf_op jit(solution)/shard_map/ppermute | solution.py:27
  52.4 21.3 %project.1 = (bf16[256,512]{1,0:T(8,128)(2,1)}, bf16[128,512]{1,0:T(8,128)(2,1)}, bf16[256,512]{1,0:T(8,128)(2,1)}, bf16[128,512]{1,0:T(8,128)(2,1)}, bf16[256,5...) custom-call(s32[8]{0:T(128)} %stack.94.chips, ...), custom_call_target="tpu_custom_call" | custom-call | flops 8053063680 | bytes 20971520 | tf_op jit(solution)/shard_map/project/pallas_call | solution.py:144
  76.5 2.9 %collective-permute-start.17 = (bf16[256,512]{1,0:T(8,128)(2,1)}, bf16[256,512]{1,0:T(8,128)(2,1)S(1)}, u32[]{:S(2)}, u32[]{:S(2)}) collective-permute-start(bf16[256,512]{1,0:T(8,128)(2,1)} %get-tuple-element.60.refs_4_), channel_id=1, source_target_pairs={{0,64},{64,0},{1,65},{65,1},{2,66},{66,2},{3,67},{67,3},{4,68},{68... | collective-permute-start | bytes 786440 | tf_op jit(solution)/shard_map/ppermute | solution.py:27
  80.1 2.7 %collective-permute-start.19 = (bf16[128,512]{1,0:T(8,128)(2,1)}, bf16[128,512]{1,0:T(8,128)(2,1)S(1)}, u32[]{:S(2)}, u32[]{:S(2)}) collective-permute-start(bf16[128,512]{1,0:T(8,128)(2,1)} %get-tuple-element.62), channel_id=1, source_target_pairs={{0,48},{16,0},{32,16},{48,32},{1,49},{17,1},{33,17},{49,33},{2,50}... | collective-permute-start | bytes 393224 | tf_op jit(solution)/shard_map/ppermute | solution.py:27
  82.8 4.3 %collective-permute-done.18.refs_16_ = bf16[128,512]{1,0:T(8,128)(2,1)S(1)} collective-permute-done((bf16[128,512]{1,0:T(8,128)(2,1)}, bf16[128,512]{1,0:T(8,128)(2,1)S(1)}, u32[]{:S(2)}, u32[]{:S(2)}) %collective-permute-start.18) | collective-permute-done | bytes 131104 | tf_op jit(solution)/shard_map/ppermute | solution.py:27
  88.1 5.0 %collective-permute-start.23 = (bf16[768,512]{1,0:T(8,128)(2,1)S(1)}, bf16[768,512]{1,0:T(8,128)(2,1)S(1)}, u32[]{:S(2)}, u32[]{:S(2)}) collective-permute-start(bf16[768,512]{1,0:T(8,128)(2,1)S(1)} %pad_maximum_fusion), channel_id=1, source_target_pairs={{0,1},{1,0},{2,3},{3,2},{4,5},{5,4},{6,7},{7,6},{8,9},{9,8},{10,11... | collective-permute-start | bytes 2359304 | tf_op jit(solution)/shard_map/ppermute | solution.py:27
  94.5 1.6 collective-permute-start.20
  98.7 8.0 %collective-permute-done.22.refs_17_ = bf16[128,512]{1,0:T(8,128)(2,1)S(1)} collective-permute-done((bf16[128,512]{1,0:T(8,128)(2,1)}, bf16[128,512]{1,0:T(8,128)(2,1)S(1)}, u32[]{:S(2)}, u32[]{:S(2)}) %collective-permute-start.22) | collective-permute-done | bytes 131104 | tf_op jit(solution)/shard_map/ppermute | solution.py:27
  106.7 1.8 collective-permute-done.21.refs_8_
  109.1 7.9 %collective-permute-done.25.refs_9_ = bf16[256,512]{1,0:T(8,128)(2,1)S(1)} collective-permute-done((bf16[256,512]{1,0:T(8,128)(2,1)S(1)}, bf16[256,512]{1,0:T(8,128)(2,1)S(1)}, u32[]{:S(2)}, u32[]{:S(2)}) %collective-permute-start.25) | collective-permute-done | bytes 262176 | tf_op jit(solution)/shard_map/ppermute | solution.py:27
  117.0 1.7 collective-permute-start.26
  119.2 5.0 %collective-permute-done.27.refs_11_ = bf16[256,512]{1,0:T(8,128)(2,1)S(1)} collective-permute-done((bf16[256,512]{1,0:T(8,128)(2,1)S(1)}, bf16[256,512]{1,0:T(8,128)(2,1)S(1)}, u32[]{:S(2)}, u32[]{:S(2)}) %collective-permute-start.27) | collective-permute-done | bytes 262176 | tf_op jit(solution)/shard_map/ppermute | solution.py:27
  126.5 14.3 %attend.1 = (bf16[512,128]{1,0:T(8,128)(2,1)S(1)}, bf16[512,128]{1,0:T(8,128)(2,1)S(1)}, bf16[512,128]{1,0:T(8,128)(2,1)S(1)}, bf16[512,128]{1,0:T(8,128)(2,1)S(1)}) custom-call(s32[16,64]{1,0:T(8,128)S(1)} %select_reduce_fusion.2.refs_0_, s32[16]{0:T(128)S(1)} %get-tuple-element.93.refs_1_, s32[17]{0:T(128)S(1)} %select_reduce_fusion.5.refs_2_, ...), custom_call_target="tpu_custom_call" | custom-call | flops 2147483648 | bytes 4194304 | tf_op jit(solution)/shard_map/attend/pallas_call | solution.py:286
  140.9 3.4 %collective-permute-start.31 = (bf16[512,128]{1,0:T(8,128)(2,1)S(1)}, bf16[512,128]{1,0:T(8,128)(2,1)S(1)}, u32[]{:S(2)}, u32[]{:S(2)}) collective-permute-start(bf16[512,128]{1,0:T(8,128)(2,1)S(1)} %get-tuple-element.72), channel_id=1, source_target_pairs={{0,32},{16,48},{32,0},{48,16},{1,33},{17,49},{33,1},{49,17},{2,34}... | collective-permute-start | bytes 393224 | tf_op jit(solution)/shard_map/ppermute | solution.py:27
  144.8 2.7 %collective-permute-done.31.refs_6_ = bf16[512,128]{1,0:T(8,128)(2,1)S(1)} collective-permute-done((bf16[512,128]{1,0:T(8,128)(2,1)S(1)}, bf16[512,128]{1,0:T(8,128)(2,1)S(1)}, u32[]{:S(2)}, u32[]{:S(2)}) %collective-permute-start.31) | collective-permute-done | bytes 131104 | tf_op jit(solution)/shard_map/ppermute | solution.py:27
  147.5 4.2 %collective-permute-done.32.refs_7_ = bf16[512,128]{1,0:T(8,128)(2,1)S(1)} collective-permute-done((bf16[512,128]{1,0:T(8,128)(2,1)S(1)}, bf16[512,128]{1,0:T(8,128)(2,1)S(1)}, u32[]{:S(2)}, u32[]{:S(2)}) %collective-permute-start.32) | collective-permute-done | bytes 131104 | tf_op jit(solution)/shard_map/ppermute | solution.py:27
  151.7 2.8 %leave.3 = (bf16[512,256]{1,0:T(8,128)(2,1)S(1)}, bf16[512,256]{1,0:T(8,128)(2,1)S(1)}, bf16[512,128]{1,0:T(8,128)(2,1)S(1)}) custom-call(s32[1]{0:T(128)} %bitcast.12.refs_0_, s32[4]{0:T(128)S(1)} %pad_add_fusion.1.refs_1_, bf16[256,5120]{1,0:T(8,128)(2,1)S(1)} %copy-done, bf16[256,5120]{1,0:T(8,128)(2,1)} %collective-permute-done.26.refs_3_, ...), custom_call_target="tpu_custom_call" | custom-call | flops 335544320 | bytes 1310720 | tf_op jit(solution)/shard_map/leave/pallas_call | solution.py:352
  154.7 2.7 %collective-permute-start.35 = (bf16[512,128]{1,0:T(8,128)(2,1)S(1)}, bf16[512,128]{1,0:T(8,128)(2,1)S(1)}, u32[]{:S(2)}, u32[]{:S(2)}) collective-permute-start(bf16[512,128]{1,0:T(8,128)(2,1)S(1)} %get-tuple-element.76), channel_id=1, source_target_pairs={{0,6},{2,0},{4,2},{6,4},{1,7},{3,1},{5,3},{7,5},{8,14},{10,8},{12,... | collective-permute-start | bytes 393224 | tf_op jit(solution)/shard_map/ppermute | solution.py:27
  157.4 4.6 %leave.5 = (bf16[512,640]{1,0:T(8,128)(2,1)S(1)}, bf16[512,640]{1,0:T(8,128)(2,1)S(1)}, bf16[512,640]{1,0:T(8,128)(2,1)S(1)}) custom-call(s32[3]{0:T(128)S(1)} %pad_add_fusion.3.refs_0_, s32[4]{0:T(128)S(1)} %pad_add_fusion.1.refs_1_, bf16[256,5120]{1,0:T(8,128)(2,1)S(1)} %copy-done, bf16[256,5120]{1,0:T(8,128)(2,1)} %collective-permute-done.26.refs_3_, ...), custom_call_target="tpu_custom_call" | custom-call | flops 1006632960 | bytes 3932160 | tf_op jit(solution)/shard_map/leave/pallas_call | solution.py:352
  166.2 6.2 %leave.4 = (bf16[512,640]{1,0:T(8,128)(2,1)S(1)}, bf16[512,640]{1,0:T(8,128)(2,1)}, bf16[512,640]{1,0:T(8,128)(2,1)S(1)}, bf16[512,640]{1,0:T(8,128)(2,1)S(1)}) custom-call(s32[4]{0:T(128)S(1)} %pad_add_fusion.refs_0_, s32[4]{0:T(128)S(1)} %pad_add_fusion.1.refs_1_, bf16[256,5120]{1,0:T(8,128)(2,1)S(1)} %copy-done, ...), custom_call_target="tpu_custom_call" | custom-call | flops 1342177280 | bytes 5242880 | tf_op jit(solution)/shard_map/leave/pallas_call | solution.py:352
  172.5 5.4 %collective-permute-done.36.refs_1_ = bf16[512,640]{1,0:T(8,128)(2,1)S(1)} collective-permute-done((bf16[512,640]{1,0:T(8,128)(2,1)S(1)}, bf16[512,640]{1,0:T(8,128)(2,1)S(1)}, u32[]{:S(2)}, u32[]{:S(2)}) %collective-permute-start.36) | collective-permute-done | bytes 655392 | tf_op jit(solution)/shard_map/ppermute | solution.py:27
  177.9 2.4 %collective-permute-done.38.refs_4_ = bf16[512,640]{1,0:T(8,128)(2,1)S(1)} collective-permute-done((bf16[512,640]{1,0:T(8,128)(2,1)S(1)}, bf16[512,640]{1,0:T(8,128)(2,1)S(1)}, u32[]{:S(2)}, u32[]{:S(2)}) %collective-permute-start.38) | collective-permute-done | bytes 655392 | tf_op jit(solution)/shard_map/ppermute | solution.py:27
  181.1 13.2 %collective-permute-done.40.refs_2_ = bf16[512,640]{1,0:T(8,128)(2,1)S(1)} collective-permute-done((bf16[512,640]{1,0:T(8,128)(2,1)}, bf16[512,640]{1,0:T(8,128)(2,1)S(1)}, u32[]{:S(2)}, u32[]{:S(2)}) %collective-permute-start.40) | collective-permute-done | bytes 655392 | tf_op jit(solution)/shard_map/ppermute | solution.py:27
  195.9 3.7 %collective-permute-start.42 = (bf16[320,512]{1,0:T(8,128)(2,1)S(1)}, bf16[320,512]{1,0:T(8,128)(2,1)S(1)}, u32[]{:S(2)}, u32[]{:S(2)}) collective-permute-start(bf16[320,512]{1,0:T(8,128)(2,1)S(1)} %constant_dynamic-slice_fusion), channel_id=1, source_target_pairs={{0,1},{1,0},{2,3},{3,2},{4,5},{5,4},{6,7},{7,6},{8,9},{9,8},{10,11... | collective-permute-start | bytes 983048 | tf_op jit(solution)/shard_map/ppermute | solution.py:27
  (126 shorter events, 42.1 us)
Async XLA Ops:
  4.6 47.1 %collective-permute-start.14 = (bf16[3,5120,256]{2,1,0:T(8,128)(2,1)}, bf16[3,5120,256]{2,1,0:T(8,128)(2,1)}, u32[]{:S(2)}, u32[]{:S(2)}) collective-permute-start(bf16[3,5120,256]{2,1,0:T(8,128)(2,1)} %refs_11_.1), channel_id=1, source_target_pairs={{0,1},{1,0},{2,3},{3,2},{4,5},{5,4},{6,7},{7,6},{8,9},{9,8},{10,11... | collective-permute-start | bytes 23592968 | tf_op jit(solution)/shard_map/ppermute | solution.py:27
  4.7 18.7 %collective-permute-start.1 = (bf16[512,640]{1,0:T(8,128)(2,1)S(1)}, bf16[512,640]{1,0:T(8,128)(2,1)S(1)}, u32[]{:S(2)}, u32[]{:S(2)}) collective-permute-start(bf16[512,640]{1,0:T(8,128)(2,1)S(1)} %lay.1.refs_0_), channel_id=1, source_target_pairs={{0,2},{2,4},{4,6},{6,0},{1,3},{3,5},{5,7},{7,1},{8,10},{10,12},{12... | collective-permute-start | bytes 1966088 | tf_op jit(solution)/shard_map/ppermute | solution.py:27
  6.5 17.0 %collective-permute-start.2 = (bf16[512,640]{1,0:T(8,128)(2,1)S(1)}, bf16[512,640]{1,0:T(8,128)(2,1)S(1)}, u32[]{:S(2)}, u32[]{:S(2)}) collective-permute-start(bf16[512,640]{1,0:T(8,128)(2,1)S(1)} %lay.1.refs_0_), channel_id=1, source_target_pairs={{0,6},{2,0},{4,2},{6,4},{1,7},{3,1},{5,3},{7,5},{8,14},{10,8},{12,... | collective-permute-start | bytes 1966088 | tf_op jit(solution)/shard_map/ppermute | solution.py:27
  8.6 15.8 %collective-permute-start.3 = (bf16[512,640]{1,0:T(8,128)(2,1)S(1)}, bf16[512,640]{1,0:T(8,128)(2,1)}, u32[]{:S(2)}, u32[]{:S(2)}) collective-permute-start(bf16[512,640]{1,0:T(8,128)(2,1)S(1)} %lay.1.refs_0_), channel_id=1, source_target_pairs={{0,8},{8,0},{1,9},{9,1},{2,10},{10,2},{3,11},{11,3},{4,12},{12,4},... | collective-permute-start | bytes 1966088 | tf_op jit(solution)/shard_map/ppermute | solution.py:27
  24.3 15.9 %collective-permute-start.4 = (bf16[512,640]{1,0:T(8,128)(2,1)S(1)}, bf16[512,640]{1,0:T(8,128)(2,1)S(1)}, u32[]{:S(2)}, u32[]{:S(2)}) collective-permute-start(bf16[512,640]{1,0:T(8,128)(2,1)S(1)} %collective-permute-done.1.refs_1_), channel_id=1, source_target_pairs={{0,2},{2,4},{4,6},{6,0},{1,3},{3,5},{5,7},{7,1},{8,10},{10,12},{12... | collective-permute-start | bytes 1966088 | tf_op jit(solution)/shard_map/ppermute | solution.py:27
  24.7 15.6 %collective-permute-start.5 = (bf16[512,640]{1,0:T(8,128)(2,1)S(1)}, bf16[512,640]{1,0:T(8,128)(2,1)S(1)}, u32[]{:S(2)}, u32[]{:S(2)}) collective-permute-start(bf16[512,640]{1,0:T(8,128)(2,1)S(1)} %collective-permute-done.1.refs_1_), channel_id=1, source_target_pairs={{0,8},{8,0},{1,9},{9,1},{2,10},{10,2},{3,11},{11,3},{4,12},{12,4},... | collective-permute-start | bytes 1966088 | tf_op jit(solution)/shard_map/ppermute | solution.py:27
  26.0 14.6 %collective-permute-start.6 = (bf16[512,640]{1,0:T(8,128)(2,1)}, bf16[512,640]{1,0:T(8,128)(2,1)S(1)}, u32[]{:S(2)}, u32[]{:S(2)}) collective-permute-start(bf16[512,640]{1,0:T(8,128)(2,1)} %collective-permute-done.3.refs_3_), channel_id=1, source_target_pairs={{0,6},{2,0},{4,2},{6,4},{1,7},{3,1},{5,3},{7,5},{8,14},{10,8},{12,... | collective-permute-start | bytes 1966088 | tf_op jit(solution)/shard_map/ppermute | solution.py:27
  41.5 10.2 %collective-permute-start.11 = (bf16[512,256]{1,0:T(8,128)(2,1)}, bf16[512,256]{1,0:T(8,128)(2,1)S(1)}, u32[]{:S(2)}, u32[]{:S(2)}) collective-permute-start(bf16[512,256]{1,0:T(8,128)(2,1)} %slice.19), channel_id=1, source_target_pairs={{0,8},{8,0},{1,9},{9,1},{2,10},{10,2},{3,11},{11,3},{4,12},{12,4},... | collective-permute-start | bytes 786440 | tf_op jit(solution)/shard_map/ppermute | solution.py:27
  43.1 8.5 %collective-permute-start.12 = (bf16[512,256]{1,0:T(8,128)(2,1)}, bf16[512,256]{1,0:T(8,128)(2,1)}, u32[]{:S(2)}, u32[]{:S(2)}) collective-permute-start(bf16[512,256]{1,0:T(8,128)(2,1)} %slice.20), channel_id=1, source_target_pairs={{0,6},{2,0},{4,2},{6,4},{1,7},{3,1},{5,3},{7,5},{8,14},{10,8},{12,... | collective-permute-start | bytes 786440 | tf_op jit(solution)/shard_map/ppermute | solution.py:27
  73.7 13.4 %collective-permute-start.15 = (bf16[256,512]{1,0:T(8,128)(2,1)}, bf16[256,512]{1,0:T(8,128)(2,1)S(1)}, u32[]{:S(2)}, u32[]{:S(2)}) collective-permute-start(bf16[256,512]{1,0:T(8,128)(2,1)} %get-tuple-element.58), channel_id=1, source_target_pairs={{0,16},{16,32},{32,48},{48,0},{1,17},{17,33},{33,49},{49,1},{2,18}... | collective-permute-start | bytes 786440 | tf_op jit(solution)/shard_map/ppermute | solution.py:27
  75.0 12.1 %collective-permute-start.16 = (bf16[256,512]{1,0:T(8,128)(2,1)}, bf16[256,512]{1,0:T(8,128)(2,1)S(1)}, u32[]{:S(2)}, u32[]{:S(2)}) collective-permute-start(bf16[256,512]{1,0:T(8,128)(2,1)} %get-tuple-element.59), channel_id=1, source_target_pairs={{0,48},{16,0},{32,16},{48,32},{1,49},{17,1},{33,17},{49,33},{2,50}... | collective-permute-start | bytes 786440 | tf_op jit(solution)/shard_map/ppermute | solution.py:27
  76.5 10.6 %collective-permute-start.17 = (bf16[256,512]{1,0:T(8,128)(2,1)}, bf16[256,512]{1,0:T(8,128)(2,1)S(1)}, u32[]{:S(2)}, u32[]{:S(2)}) collective-permute-start(bf16[256,512]{1,0:T(8,128)(2,1)} %get-tuple-element.60.refs_4_), channel_id=1, source_target_pairs={{0,64},{64,0},{1,65},{65,1},{2,66},{66,2},{3,67},{67,3},{4,68},{68... | collective-permute-start | bytes 786440 | tf_op jit(solution)/shard_map/ppermute | solution.py:27
  80.0 7.0 %collective-permute-start.18 = (bf16[128,512]{1,0:T(8,128)(2,1)}, bf16[128,512]{1,0:T(8,128)(2,1)S(1)}, u32[]{:S(2)}, u32[]{:S(2)}) collective-permute-start(bf16[128,512]{1,0:T(8,128)(2,1)} %get-tuple-element.61), channel_id=1, source_target_pairs={{0,16},{16,32},{32,48},{48,0},{1,17},{17,33},{33,49},{49,1},{2,18}... | collective-permute-start | bytes 393224 | tf_op jit(solution)/shard_map/ppermute | solution.py:27
  80.1 7.0 %collective-permute-start.19 = (bf16[128,512]{1,0:T(8,128)(2,1)}, bf16[128,512]{1,0:T(8,128)(2,1)S(1)}, u32[]{:S(2)}, u32[]{:S(2)}) collective-permute-start(bf16[128,512]{1,0:T(8,128)(2,1)} %get-tuple-element.62), channel_id=1, source_target_pairs={{0,48},{16,0},{32,16},{48,32},{1,49},{17,1},{33,17},{49,33},{2,50}... | collective-permute-start | bytes 393224 | tf_op jit(solution)/shard_map/ppermute | solution.py:27
  88.1 20.4 %collective-permute-start.23 = (bf16[768,512]{1,0:T(8,128)(2,1)S(1)}, bf16[768,512]{1,0:T(8,128)(2,1)S(1)}, u32[]{:S(2)}, u32[]{:S(2)}) collective-permute-start(bf16[768,512]{1,0:T(8,128)(2,1)S(1)} %pad_maximum_fusion), channel_id=1, source_target_pairs={{0,1},{1,0},{2,3},{3,2},{4,5},{5,4},{6,7},{7,6},{8,9},{9,8},{10,11... | collective-permute-start | bytes 2359304 | tf_op jit(solution)/shard_map/ppermute | solution.py:27
  93.2 15.3 %collective-permute-start.21 = (bf16[512,512]{1,0:T(8,128)(2,1)S(1)}, bf16[512,512]{1,0:T(8,128)(2,1)S(1)}, u32[]{:S(2)}, u32[]{:S(2)}) collective-permute-start(bf16[512,512]{1,0:T(8,128)(2,1)S(1)} %constant_dynamic-update-slice_fusion.refs_5_), channel_id=1, source_target_pairs={{0,64},{64,0},{1,65},{65,1},{2,66},{66,2},{3,67},{67,3},{4,68},{68... | collective-permute-start | bytes 1572872 | tf_op jit(solution)/shard_map/ppermute | solution.py:27
  94.5 12.2 %collective-permute-start.20 = (bf16[256,512]{1,0:T(8,128)(2,1)}, bf16[256,512]{1,0:T(8,128)(2,1)S(1)}, u32[]{:S(2)}, u32[]{:S(2)}) collective-permute-start(bf16[256,512]{1,0:T(8,128)(2,1)} %get-tuple-element.64), channel_id=1, source_target_pairs={{0,32},{16,48},{32,0},{48,16},{1,33},{17,49},{33,1},{49,17},{2,34}... | collective-permute-start | bytes 786440 | tf_op jit(solution)/shard_map/ppermute | solution.py:27
  96.1 10.6 %collective-permute-start.24 = (bf16[256,512]{1,0:T(8,128)(2,1)S(1)}, bf16[256,512]{1,0:T(8,128)(2,1)S(1)}, u32[]{:S(2)}, u32[]{:S(2)}) collective-permute-start(bf16[256,512]{1,0:T(8,128)(2,1)S(1)} %collective-permute-done.17.refs_7_), channel_id=1, source_target_pairs={{0,1},{1,0},{2,3},{3,2},{4,5},{5,4},{6,7},{7,6},{8,9},{9,8},{10,11... | collective-permute-start | bytes 786440 | tf_op jit(solution)/shard_map/ppermute | solution.py:27
  96.8 9.8 %collective-permute-start.22 = (bf16[128,512]{1,0:T(8,128)(2,1)}, bf16[128,512]{1,0:T(8,128)(2,1)S(1)}, u32[]{:S(2)}, u32[]{:S(2)}) collective-permute-start(bf16[128,512]{1,0:T(8,128)(2,1)} %get-tuple-element.66), channel_id=1, source_target_pairs={{0,32},{16,48},{32,0},{48,16},{1,33},{17,49},{33,1},{49,17},{2,34}... | collective-permute-start | bytes 393224 | tf_op jit(solution)/shard_map/ppermute | solution.py:27
  108.5 8.5 %collective-permute-start.25 = (bf16[256,512]{1,0:T(8,128)(2,1)S(1)}, bf16[256,512]{1,0:T(8,128)(2,1)S(1)}, u32[]{:S(2)}, u32[]{:S(2)}) collective-permute-start(bf16[256,512]{1,0:T(8,128)(2,1)S(1)} %collective-permute-done.20.refs_6_), channel_id=1, source_target_pairs={{0,64},{64,0},{1,65},{65,1},{2,66},{66,2},{3,67},{67,3},{4,68},{68... | collective-permute-start | bytes 786440 | tf_op jit(solution)/shard_map/ppermute | solution.py:27
  117.0 34.7 %collective-permute-start.26 = (bf16[256,5120]{1,0:T(8,128)(2,1)S(1)}, bf16[256,5120]{1,0:T(8,128)(2,1)}, u32[]{:S(2)}, u32[]{:S(2)}) collective-permute-start(bf16[256,5120]{1,0:T(8,128)(2,1)S(1)} %copy-done), channel_id=1, source_target_pairs={{0,1},{1,0},{2,3},{3,2},{4,5},{5,4},{6,7},{7,6},{8,9},{9,8},{10,11... | collective-permute-start | bytes 7864328 | tf_op jit(solution)/shard_map/ppermute | solution.py:27
  140.9 6.6 %collective-permute-start.31 = (bf16[512,128]{1,0:T(8,128)(2,1)S(1)}, bf16[512,128]{1,0:T(8,128)(2,1)S(1)}, u32[]{:S(2)}, u32[]{:S(2)}) collective-permute-start(bf16[512,128]{1,0:T(8,128)(2,1)S(1)} %get-tuple-element.72), channel_id=1, source_target_pairs={{0,32},{16,48},{32,0},{48,16},{1,33},{17,49},{33,1},{49,17},{2,34}... | collective-permute-start | bytes 393224 | tf_op jit(solution)/shard_map/ppermute | solution.py:27
  144.2 7.5 %collective-permute-start.32 = (bf16[512,128]{1,0:T(8,128)(2,1)S(1)}, bf16[512,128]{1,0:T(8,128)(2,1)S(1)}, u32[]{:S(2)}, u32[]{:S(2)}) collective-permute-start(bf16[512,128]{1,0:T(8,128)(2,1)S(1)} %get-tuple-element.73), channel_id=1, source_target_pairs={{0,16},{16,32},{32,48},{48,0},{1,17},{17,33},{33,49},{49,1},{2,18}... | collective-permute-start | bytes 393224 | tf_op jit(solution)/shard_map/ppermute | solution.py:27
  154.5 7.5 %collective-permute-start.33 = (bf16[512,256]{1,0:T(8,128)(2,1)S(1)}, bf16[512,256]{1,0:T(8,128)(2,1)S(1)}, u32[]{:S(2)}, u32[]{:S(2)}) collective-permute-start(bf16[512,256]{1,0:T(8,128)(2,1)S(1)} %get-tuple-element.74), channel_id=1, source_target_pairs={{0,8},{8,0},{1,9},{9,1},{2,10},{10,2},{3,11},{11,3},{4,12},{12,4},... | collective-permute-start | bytes 786440 | tf_op jit(solution)/shard_map/ppermute | solution.py:27
  154.7 8.3 %collective-permute-start.34 = (bf16[512,256]{1,0:T(8,128)(2,1)S(1)}, bf16[512,256]{1,0:T(8,128)(2,1)S(1)}, u32[]{:S(2)}, u32[]{:S(2)}) collective-permute-start(bf16[512,256]{1,0:T(8,128)(2,1)S(1)} %get-tuple-element.75), channel_id=1, source_target_pairs={{0,2},{2,4},{4,6},{6,0},{1,3},{3,5},{5,7},{7,1},{8,10},{10,12},{12... | collective-permute-start | bytes 786440 | tf_op jit(solution)/shard_map/ppermute | solution.py:27
  154.7 7.3 %collective-permute-start.35 = (bf16[512,128]{1,0:T(8,128)(2,1)S(1)}, bf16[512,128]{1,0:T(8,128)(2,1)S(1)}, u32[]{:S(2)}, u32[]{:S(2)}) collective-permute-start(bf16[512,128]{1,0:T(8,128)(2,1)S(1)} %get-tuple-element.76), channel_id=1, source_target_pairs={{0,6},{2,0},{4,2},{6,4},{1,7},{3,1},{5,3},{7,5},{8,14},{10,8},{12,... | collective-permute-start | bytes 393224 | tf_op jit(solution)/shard_map/ppermute | solution.py:27
  163.2 14.7 %collective-permute-start.36 = (bf16[512,640]{1,0:T(8,128)(2,1)S(1)}, bf16[512,640]{1,0:T(8,128)(2,1)S(1)}, u32[]{:S(2)}, u32[]{:S(2)}) collective-permute-start(bf16[512,640]{1,0:T(8,128)(2,1)S(1)} %get-tuple-element.86), channel_id=1, source_target_pairs={{0,6},{2,0},{4,2},{6,4},{1,7},{3,1},{5,3},{7,5},{8,14},{10,8},{12,... | collective-permute-start | bytes 1966088 | tf_op jit(solution)/shard_map/ppermute | solution.py:27
  163.3 14.6 %collective-permute-start.37 = (bf16[512,640]{1,0:T(8,128)(2,1)S(1)}, bf16[512,640]{1,0:T(8,128)(2,1)S(1)}, u32[]{:S(2)}, u32[]{:S(2)}) collective-permute-start(bf16[512,640]{1,0:T(8,128)(2,1)S(1)} %get-tuple-element.87), channel_id=1, source_target_pairs={{0,8},{8,0},{1,9},{9,1},{2,10},{10,2},{3,11},{11,3},{4,12},{12,4},... | collective-permute-start | bytes 1966088 | tf_op jit(solution)/shard_map/ppermute | solution.py:27
  164.8 15.5 %collective-permute-start.38 = (bf16[512,640]{1,0:T(8,128)(2,1)S(1)}, bf16[512,640]{1,0:T(8,128)(2,1)S(1)}, u32[]{:S(2)}, u32[]{:S(2)}) collective-permute-start(bf16[512,640]{1,0:T(8,128)(2,1)S(1)} %get-tuple-element.89), channel_id=1, source_target_pairs={{0,2},{2,4},{4,6},{6,0},{1,3},{3,5},{5,7},{7,1},{8,10},{10,12},{12... | collective-permute-start | bytes 1966088 | tf_op jit(solution)/shard_map/ppermute | solution.py:27
  172.4 21.9 %collective-permute-start.40 = (bf16[512,640]{1,0:T(8,128)(2,1)}, bf16[512,640]{1,0:T(8,128)(2,1)S(1)}, u32[]{:S(2)}, u32[]{:S(2)}) collective-permute-start(bf16[512,640]{1,0:T(8,128)(2,1)} %get-tuple-element.91), channel_id=1, source_target_pairs={{0,2},{2,4},{4,6},{6,0},{1,3},{3,5},{5,7},{7,1},{8,10},{10,12},{12... | collective-permute-start | bytes 1966088 | tf_op jit(solution)/shard_map/ppermute | solution.py:27
  180.7 13.6 %collective-permute-start.39 = (bf16[512,640]{1,0:T(8,128)(2,1)S(1)}, bf16[512,640]{1,0:T(8,128)(2,1)S(1)}, u32[]{:S(2)}, u32[]{:S(2)}) collective-permute-start(bf16[512,640]{1,0:T(8,128)(2,1)S(1)} %get-tuple-element.90), channel_id=1, source_target_pairs={{0,6},{2,0},{4,2},{6,4},{1,7},{3,1},{5,3},{7,5},{8,14},{10,8},{12,... | collective-permute-start | bytes 1966088 | tf_op jit(solution)/shard_map/ppermute | solution.py:27
  180.8 13.6 %collective-permute-start.41 = (bf16[512,640]{1,0:T(8,128)(2,1)S(1)}, bf16[512,640]{1,0:T(8,128)(2,1)S(1)}, u32[]{:S(2)}, u32[]{:S(2)}) collective-permute-start(bf16[512,640]{1,0:T(8,128)(2,1)S(1)} %get-tuple-element.92), channel_id=1, source_target_pairs={{0,8},{8,0},{1,9},{9,1},{2,10},{10,2},{3,11},{11,3},{4,12},{12,4},... | collective-permute-start | bytes 1966088 | tf_op jit(solution)/shard_map/ppermute | solution.py:27
  (27 other events, 239.3 us)

commit v9 on v8

--- a/solution.py
+++ b/solution.py
@@ -15,7 +15,7 @@
 FRAME = ("yh", "x")
 HEAD = ("yl", "z", "core")
 MIB = 1 << 20
-PAIRS = 8
+PAIRS = 12
 CUTS = ((0, 256), (256, 512), (512, 640))
 
 
@@ -61,6 +61,7 @@
 
 
 ROWS = 64
+NEAR = {1: 4, 3: 5}
 
 
 def project_kernel(chips, heads, *refs):
@@ -122,7 +123,10 @@
     @pl.when(step == pl.num_programs(0) - 1)
     def _():
         for index in range(4):
-            kv, q = outs[2 * index], outs[2 * index + 1]
+            if index % 2:
+                kv, q = outs[NEAR[index]], outs[NEAR[index]].at[2 * BLK :]
+            else:
+                kv, q = outs[index : index + 2]
             base = heads[index]
             q[...] = total[base].T.astype(jnp.bfloat16)
             keys = total[base + 2]
@@ -140,7 +144,7 @@
         pl.BlockSpec((parts, deep, inner), lambda k, chips, heads, i=i: (0, chips[2 * k + i], 0))
         for i in range(2)
     ]
-    shapes = [(2 * BLK, count), (BLK, count)] * 4
+    shapes = [(2 * BLK, count), (BLK, count)] * 2 + [(3 * BLK, count)] * 2
     return pl.pallas_call(
         project_kernel,
         grid_spec=pltpu.PrefetchScalarGridSpec(
@@ -493,32 +497,31 @@
     slots = [head_slot(steps) for steps in range(4)]
     bases = jnp.stack([side * 3 * heads_here + slot for side, slot in slots]).astype(jnp.int32)
     made = project(chips, bases, xs, qkv_weight, other_weight, modulation)
-    kv, queries = made[::2], made[1::2]
-    one, three = shift(kv[1], "x", 1), shift(kv[3], "x", 3)
-    away_kv = swap(kv[0], "yh")
-    q_one, q_three = shift(queries[1], "x", 1), shift(queries[3], "x", 3)
-    one, three = together((one, three), (away_kv, q_one, q_three))
-    both = jnp.concatenate([one, three], axis=0)
+    kv, query, kv_two, q_two, *packed = made
+    one, three = shift(packed[0], "x", 1), shift(packed[1], "x", 3)
+    away_kv = swap(kv, "yh")
+    one, three = together((one, three), (away_kv,))
+    both = jnp.concatenate([one[: 2 * BLK], three[: 2 * BLK]], axis=0)
     away_both = swap(both, "yh")
-    kv_two, q_two = together((kv[2], queries[2]), (one,))
+    kv_two, q_two = together((kv_two, q_two), (one,))
     two, q_two = shift(kv_two, "x", 2), shift(q_two, "x", 2)
-    near = swap(jnp.concatenate([kv[0], both], axis=0), "core")
     away_kv_other = swap(away_kv, "core")
-    (two,) = together((two,), (away_both, q_two, *lists, near, away_kv_other))
+    two, kv, both = together((two, kv, both), (away_both, q_two, *lists, away_kv_other))
     away_two = swap(two, "yh")
-    (out_own,) = together((out_weight,), (away_two,))
-    leaving = out_weight, swap(out_own, "core")
-    arrays = [kv[0], both, two, away_kv, away_both, away_two, near, swap(two, "core")]
+    near = swap(jnp.concatenate([kv, both], axis=0), "core")
+    arrays = [kv, both, two, away_kv, away_both, away_two, near, swap(two, "core")]
     arrays += [away_kv_other, swap(away_both, "core"), swap(away_two, "core")]
-    arrays += [queries[0], q_one, q_two, q_three]
+    arrays += [query, one, q_two, three]
     step = 2 * BLK
     plan = []
     for index, array in ((0, 0), (4, 3), (12, 8)):
         plan += [("kv", index, array, 0), ("kv", index + 1, array + 1, 0)]
         plan += [("kv", index + 3, array + 1, step), ("kv", index + 2, array + 2, 0)]
     plan += [("kv", 8, 6, 0), ("kv", 9, 6, step), ("kv", 11, 6, 2 * step), ("kv", 10, 7, 0)]
-    plan += [("q", index, 11 + index, 0) for index in range(4)]
+    plan += [("q", index, 11 + index, index % 2 * step) for index in range(4)]
     heads = attend(factor, lists, plan, arrays, half)
+    (out_own,) = together((out_weight,), (heads[0],))
+    leaving = out_weight, swap(out_own, "core")
     heads = [heads[0]] + [shift(heads[steps], "x", -steps) for steps in (1, 2, 3)]
 
     columns = jnp.stack([side * heads_here + slot for side, slot in slots]).astype(jnp.int32)

time: 204 us -> 195 us (0.956); the launches traced: 202 us -> 196 us
  starting transfers between devices: 52.5 us -> 62.5 us
  waiting for transfers between devices: 82.4 us -> 76.6 us
  Pallas kernels: 50.4 us -> 45.4 us
  local copies, waits for them, and re-layouts: 10.3 us -> 7.65 us
  other arithmetic: 6.04 us -> 3.84 us
    ppermute x43 -> x41, starting transfers between devices: 52.5 us -> 62.5 us  [shift(): lax.ppermute(value, axis, [(i, (i + steps) % count) for i in range(count)])]
    ppermute x43 -> x41, waiting for transfers between devices: 82.4 us -> 76.6 us  [shift(): lax.ppermute(value, axis, [(i, (i + steps) % count) for i in range(count)])]
    pallas_call x1, Pallas kernels: 14.3 us -> 9.24 us  [attend(): pl.pallas_call(kernel, in_specs=[pl.BlockSpec(memory_space=pltpu.SMEM)] *...]
    unnamed x33 -> x40, local copies, waits for them, and re-layouts: 4.53 us -> 2.65 us
  transfers between devices with their start and end apart: 43 -> 41, of which waited for: 24 -> 21; matrix products, arithmetic and copies ran while one was open for 4% -> 3% of each run, Pallas kernels for 13% -> 6%
where the time goes in v9:
time: 195 us; the launch traced here: 196 us
  waiting for transfers between devices  76.6 us (39%)
  starting transfers between devices  62.5 us (32%)
  Pallas kernels  45.4 us (23%)
  local copies, waits for them, and re-layouts  7.65 us (4%)
  other arithmetic  3.84 us (2%)
    ppermute x41, waiting for transfers between devices, shift(): lax.ppermute(value, axis, [(i, (i + steps) % count) for i in range(count)])  76.6 us
    ppermute x41, starting transfers between devices, shift(): lax.ppermute(value, axis, [(i, (i + steps) % count) for i in range(count)])  62.5 us
    pallas_call x1, Pallas kernels, project(): pl.pallas_call(project_kernel, grid_spec=pltpu.PrefetchScalarGridSpec(num...  21.3 us
    pallas_call x3, Pallas kernels, leave(): pl.pallas_call(kernel, grid_spec=pltpu.PrefetchScalarGridSpec(num_scalar_...  13.5 us
    pallas_call x1, Pallas kernels, attend(): pl.pallas_call(kernel, in_specs=[pl.BlockSpec(memory_space=pltpu.SMEM)] *...  9.24 us
  transfers between devices with their start and end apart: 41, of which 21 were waited for; matrix products, arithmetic and copies ran while one was open for 3% of the time, Pallas kernels for 6%

profile of v9, /device:TPU:1, one launch (start us, length us, event | category | flops | bytes accessed | tf_op | source)
XLA Modules:
  0.0 196.5 jit_solution(2672043064507541927)
XLA Ops:
  1.1 1.5 collective-permute-start.4
  4.6 1.7 collective-permute-start.5
  6.4 2.1 %collective-permute-start.6 = (bf16[512,640]{1,0:T(8,128)(2,1)S(1)}, bf16[512,640]{1,0:T(8,128)(2,1)S(1)}, u32[]{:S(2)}, u32[]{:S(2)}) collective-permute-start(bf16[512,640]{1,0:T(8,128)(2,1)S(1)} %lay.1.refs_0_), channel_id=1, source_target_pairs={{0,6},{2,0},{4,2},{6,4},{1,7},{3,1},{5,3},{7,5},{8,14},{10,8},{12,... | collective-permute-start | bytes 1966088 | tf_op jit(solution)/shard_map/ppermute | solution.py:27
  9.8 13.7 %collective-permute-done.5.refs_1_ = bf16[512,640]{1,0:T(8,128)(2,1)S(1)} collective-permute-done((bf16[512,640]{1,0:T(8,128)(2,1)S(1)}, bf16[512,640]{1,0:T(8,128)(2,1)S(1)}, u32[]{:S(2)}, u32[]{:S(2)}) %collective-permute-start.5) | collective-permute-done | bytes 655392 | tf_op jit(solution)/shard_map/ppermute | solution.py:27
  26.1 2.3 %collective-permute-start.10 = (bf16[512,640]{1,0:T(8,128)(2,1)}, bf16[512,640]{1,0:T(8,128)(2,1)S(1)}, u32[]{:S(2)}, u32[]{:S(2)}) collective-permute-start(bf16[512,640]{1,0:T(8,128)(2,1)} %collective-permute-done.7.refs_3_), channel_id=1, source_target_pairs={{0,6},{2,0},{4,2},{6,4},{1,7},{3,1},{5,3},{7,5},{8,14},{10,8},{12,... | collective-permute-start | bytes 1966088 | tf_op jit(solution)/shard_map/ppermute | solution.py:27
  28.4 2.5 %collective-permute-start.3 = (s32[4,64]{1,0:T(4,128)S(1)}, s32[4,64]{1,0:T(4,128)S(1)}, u32[]{:S(2)}, u32[]{:S(2)}) collective-permute-start(s32[4,64]{1,0:T(4,128)S(1)} %get-tuple-element.102), channel_id=1, source_target_pairs={{0,48},{16,0},{32,16},{48,32},{1,49},{17,1},{33,17},{49,33},{2,50}... | collective-permute-start | bytes 3080 | tf_op jit(solution)/shard_map/ppermute | solution.py:27
  31.7 2.3 %collective-permute-start.2 = (s32[4,64]{1,0:T(4,128)S(1)}, s32[4,64]{1,0:T(4,128)S(1)}, u32[]{:S(2)}, u32[]{:S(2)}) collective-permute-start(s32[4,64]{1,0:T(4,128)S(1)} %get-tuple-element.101), channel_id=1, source_target_pairs={{0,32},{16,48},{32,0},{48,16},{1,33},{17,49},{33,1},{49,17},{2,34}... | collective-permute-start | bytes 3080 | tf_op jit(solution)/shard_map/ppermute | solution.py:27
  34.0 1.7 collective-permute-done.2
  36.8 3.3 %collective-permute-done.1 = s32[4,64]{1,0:T(4,128)S(1)} collective-permute-done((s32[4,64]{1,0:T(4,128)S(1)}, s32[4,64]{1,0:T(4,128)S(1)}, u32[]{:S(2)}, u32[]{:S(2)}) %collective-permute-start.1) | collective-permute-done | bytes 1056 | tf_op jit(solution)/shard_map/ppermute | solution.py:27
  43.5 2.4 %collective-permute-start.12 = (bf16[512,256]{1,0:T(8,128)(2,1)}, bf16[512,256]{1,0:T(8,128)(2,1)}, u32[]{:S(2)}, u32[]{:S(2)}) collective-permute-start(bf16[512,256]{1,0:T(8,128)(2,1)} %slice.28), channel_id=1, source_target_pairs={{0,6},{2,0},{4,2},{6,4},{1,7},{3,1},{5,3},{7,5},{8,14},{10,8},{12,... | collective-permute-start | bytes 786440 | tf_op jit(solution)/shard_map/ppermute | solution.py:27
  48.0 4.1 %collective-permute-done.13.refs_9_ = bf16[512,128]{1,0:T(8,128)(2,1)} collective-permute-done((bf16[512,128]{1,0:T(8,128)(2,1)}, bf16[512,128]{1,0:T(8,128)(2,1)}, u32[]{:S(2)}, u32[]{:S(2)}) %collective-permute-start.13) | collective-permute-done | bytes 131104 | tf_op jit(solution)/shard_map/ppermute | solution.py:27
  52.7 21.3 %project.1 = (bf16[256,512]{1,0:T(8,128)(2,1)}, bf16[128,512]{1,0:T(8,128)(2,1)}, bf16[256,512]{1,0:T(8,128)(2,1)}, bf16[128,512]{1,0:T(8,128)(2,1)}, bf16[384,5...) custom-call(s32[8]{0:T(128)} %stack.97.chips, s32[4]{0:T(128)} %pad_add_fusion.2.heads, bf16[512,640]{1,0:T(8,128)(2,1)} %copy-done.1, ...), custom_call_target="tpu_custom_call" | custom-call | flops 8053063680 | bytes 20971520 | tf_op jit(solution)/shard_map/project/pallas_call | solution.py:148
  75.3 1.5 collective-permute-start.16
  76.8 3.0 %collective-permute-start.17 = (bf16[256,512]{1,0:T(8,128)(2,1)}, bf16[256,512]{1,0:T(8,128)(2,1)S(1)}, u32[]{:S(2)}, u32[]{:S(2)}) collective-permute-start(bf16[256,512]{1,0:T(8,128)(2,1)} %get-tuple-element.65.refs_4_), channel_id=1, source_target_pairs={{0,64},{64,0},{1,65},{65,1},{2,66},{66,2},{3,67},{67,3},{4,68},{68... | collective-permute-start | bytes 786440 | tf_op jit(solution)/shard_map/ppermute | solution.py:27
  80.5 3.4 %collective-permute-done.17.refs_7_ = bf16[256,512]{1,0:T(8,128)(2,1)S(1)} collective-permute-done((bf16[256,512]{1,0:T(8,128)(2,1)}, bf16[256,512]{1,0:T(8,128)(2,1)S(1)}, u32[]{:S(2)}, u32[]{:S(2)}) %collective-permute-start.17) | collective-permute-done | bytes 262176 | tf_op jit(solution)/shard_map/ppermute | solution.py:27
  83.9 3.3 %collective-permute-start.19 = (bf16[512,512]{1,0:T(8,128)(2,1)S(1)}, bf16[512,512]{1,0:T(8,128)(2,1)S(1)}, u32[]{:S(2)}, u32[]{:S(2)}) collective-permute-start(bf16[512,512]{1,0:T(8,128)(2,1)S(1)} %pad_maximum_fusion.1.refs_5_), channel_id=1, source_target_pairs={{0,64},{64,0},{1,65},{65,1},{2,66},{66,2},{3,67},{67,3},{4,68},{68... | collective-permute-start | bytes 1572872 | tf_op jit(solution)/shard_map/ppermute | solution.py:27
  87.6 7.3 %collective-permute-start.21 = (bf16[256,512]{1,0:T(8,128)(2,1)S(1)}, bf16[256,512]{1,0:T(8,128)(2,1)S(1)}, u32[]{:S(2)}, u32[]{:S(2)}) collective-permute-start(bf16[256,512]{1,0:T(8,128)(2,1)S(1)} %collective-permute-done.17.refs_7_), channel_id=1, source_target_pairs={{0,1},{1,0},{2,3},{3,2},{4,5},{5,4},{6,7},{7,6},{8,9},{9,8},{10,11... | collective-permute-start | bytes 786440 | tf_op jit(solution)/shard_map/ppermute | solution.py:27
  94.9 1.9 collective-permute-start.18
  98.7 8.4 %collective-permute-done.20.refs_17_ = bf16[128,512]{1,0:T(8,128)(2,1)S(1)} collective-permute-done((bf16[128,512]{1,0:T(8,128)(2,1)S(1)}, bf16[128,512]{1,0:T(8,128)(2,1)S(1)}, u32[]{:S(2)}, u32[]{:S(2)}) %collective-permute-start.20) | collective-permute-done | bytes 131104 | tf_op jit(solution)/shard_map/ppermute | solution.py:27
  108.7 8.7 %collective-permute-done.22.refs_9_ = bf16[256,512]{1,0:T(8,128)(2,1)S(1)} collective-permute-done((bf16[256,512]{1,0:T(8,128)(2,1)S(1)}, bf16[256,512]{1,0:T(8,128)(2,1)S(1)}, u32[]{:S(2)}, u32[]{:S(2)}) %collective-permute-start.22) | collective-permute-done | bytes 262176 | tf_op jit(solution)/shard_map/ppermute | solution.py:27
  119.5 9.2 %attend.1 = (bf16[512,128]{1,0:T(8,128)(2,1)S(1)}, bf16[512,128]{1,0:T(8,128)(2,1)S(1)}, bf16[512,128]{1,0:T(8,128)(2,1)S(1)}, bf16[512,128]{1,0:T(8,128)(2,1)S(1)}) custom-call(s32[16,64]{1,0:T(8,128)S(1)} %select_reduce_fusion.2.refs_0_, s32[16]{0:T(128)S(1)} %get-tuple-element.93.refs_1_, s32[17]{0:T(128)S(1)} %select_reduce_fusion.5.refs_2_, ...), custom_call_target="tpu_custom_call" | custom-call | flops 2147483648 | bytes 4194304 | tf_op jit(solution)/shard_map/attend/pallas_call | solution.py:290
  129.2 8.4 %collective-permute-start.28 = (bf16[512,128]{1,0:T(8,128)(2,1)S(1)}, bf16[512,128]{1,0:T(8,128)(2,1)S(1)}, u32[]{:S(2)}, u32[]{:S(2)}) collective-permute-start(bf16[512,128]{1,0:T(8,128)(2,1)S(1)} %get-tuple-element.71), channel_id=1, source_target_pairs={{0,48},{16,0},{32,16},{48,32},{1,49},{17,1},{33,17},{49,33},{2,50}... | collective-permute-start | bytes 393224 | tf_op jit(solution)/shard_map/ppermute | solution.py:27
  138.3 5.2 %collective-permute-done.28.refs_5_ = bf16[512,128]{1,0:T(8,128)(2,1)S(1)} collective-permute-done((bf16[512,128]{1,0:T(8,128)(2,1)S(1)}, bf16[512,128]{1,0:T(8,128)(2,1)S(1)}, u32[]{:S(2)}, u32[]{:S(2)}) %collective-permute-start.28) | collective-permute-done | bytes 131104 | tf_op jit(solution)/shard_map/ppermute | solution.py:27
  144.0 2.9 %collective-permute-done.30.refs_7_ = bf16[512,128]{1,0:T(8,128)(2,1)S(1)} collective-permute-done((bf16[512,128]{1,0:T(8,128)(2,1)S(1)}, bf16[512,128]{1,0:T(8,128)(2,1)S(1)}, u32[]{:S(2)}, u32[]{:S(2)}) %collective-permute-start.30) | collective-permute-done | bytes 131104 | tf_op jit(solution)/shard_map/ppermute | solution.py:27
  146.9 2.8 %leave.3 = (bf16[512,256]{1,0:T(8,128)(2,1)S(1)}, bf16[512,256]{1,0:T(8,128)(2,1)S(1)}, bf16[512,128]{1,0:T(8,128)(2,1)S(1)}) custom-call(s32[1]{0:T(128)} %bitcast.18.refs_0_, s32[4]{0:T(128)S(1)} %pad_add_fusion.1.refs_1_, bf16[256,5120]{1,0:T(8,128)(2,1)S(1)} %copy-done, bf16[256,5120]{1,0:T(8,128)(2,1)} %collective-permute-done.27.refs_3_, ...), custom_call_target="tpu_custom_call" | custom-call | flops 335544320 | bytes 1310720 | tf_op jit(solution)/shard_map/leave/pallas_call | solution.py:356
  149.8 2.7 %collective-permute-start.33 = (bf16[512,128]{1,0:T(8,128)(2,1)S(1)}, bf16[512,128]{1,0:T(8,128)(2,1)S(1)}, u32[]{:S(2)}, u32[]{:S(2)}) collective-permute-start(bf16[512,128]{1,0:T(8,128)(2,1)S(1)} %get-tuple-element.76), channel_id=1, source_target_pairs={{0,6},{2,0},{4,2},{6,4},{1,7},{3,1},{5,3},{7,5},{8,14},{10,8},{12,... | collective-permute-start | bytes 393224 | tf_op jit(solution)/shard_map/ppermute | solution.py:27
  152.6 4.6 %leave.5 = (bf16[512,640]{1,0:T(8,128)(2,1)S(1)}, bf16[512,640]{1,0:T(8,128)(2,1)S(1)}, bf16[512,640]{1,0:T(8,128)(2,1)S(1)}) custom-call(s32[3]{0:T(128)S(1)} %pad_add_fusion.3.refs_0_, s32[4]{0:T(128)S(1)} %pad_add_fusion.1.refs_1_, bf16[256,5120]{1,0:T(8,128)(2,1)S(1)} %copy-done, bf16[256,5120]{1,0:T(8,128)(2,1)} %collective-permute-done.27.refs_3_, ...), custom_call_target="tpu_custom_call" | custom-call | flops 1006632960 | bytes 3932160 | tf_op jit(solution)/shard_map/leave/pallas_call | solution.py:356
  159.6 1.4 collective-permute-start.36
  161.0 6.2 %leave.4 = (bf16[512,640]{1,0:T(8,128)(2,1)S(1)}, bf16[512,640]{1,0:T(8,128)(2,1)}, bf16[512,640]{1,0:T(8,128)(2,1)S(1)}, bf16[512,640]{1,0:T(8,128)(2,1)S(1)}) custom-call(s32[4]{0:T(128)S(1)} %pad_add_fusion.refs_0_, s32[4]{0:T(128)S(1)} %pad_add_fusion.1.refs_1_, bf16[256,5120]{1,0:T(8,128)(2,1)S(1)} %copy-done, ...), custom_call_target="tpu_custom_call" | custom-call | flops 1342177280 | bytes 5242880 | tf_op jit(solution)/shard_map/leave/pallas_call | solution.py:356
  167.3 5.7 %collective-permute-done.34.refs_1_ = bf16[512,640]{1,0:T(8,128)(2,1)S(1)} collective-permute-done((bf16[512,640]{1,0:T(8,128)(2,1)S(1)}, bf16[512,640]{1,0:T(8,128)(2,1)S(1)}, u32[]{:S(2)}, u32[]{:S(2)}) %collective-permute-start.34) | collective-permute-done | bytes 655392 | tf_op jit(solution)/shard_map/ppermute | solution.py:27
  175.9 12.5 %collective-permute-done.38.refs_2_ = bf16[512,640]{1,0:T(8,128)(2,1)S(1)} collective-permute-done((bf16[512,640]{1,0:T(8,128)(2,1)}, bf16[512,640]{1,0:T(8,128)(2,1)S(1)}, u32[]{:S(2)}, u32[]{:S(2)}) %collective-permute-start.38) | collective-permute-done | bytes 655392 | tf_op jit(solution)/shard_map/ppermute | solution.py:27
  190.0 4.0 %collective-permute-start.40 = (bf16[320,512]{1,0:T(8,128)(2,1)S(1)}, bf16[320,512]{1,0:T(8,128)(2,1)S(1)}, u32[]{:S(2)}, u32[]{:S(2)}) collective-permute-start(bf16[320,512]{1,0:T(8,128)(2,1)S(1)} %constant_dynamic-slice_fusion), channel_id=1, source_target_pairs={{0,1},{1,0},{2,3},{3,2},{4,5},{5,4},{6,7},{7,6},{8,9},{9,8},{10,11... | collective-permute-start | bytes 983048 | tf_op jit(solution)/shard_map/ppermute | solution.py:27
  (131 shorter events, 34.3 us)
Async XLA Ops:
  4.2 47.8 %collective-permute-start.14 = (bf16[3,5120,256]{2,1,0:T(8,128)(2,1)}, bf16[3,5120,256]{2,1,0:T(8,128)(2,1)}, u32[]{:S(2)}, u32[]{:S(2)}) collective-permute-start(bf16[3,5120,256]{2,1,0:T(8,128)(2,1)} %refs_11_.1), channel_id=1, source_target_pairs={{0,1},{1,0},{2,3},{3,2},{4,5},{5,4},{6,7},{7,6},{8,9},{9,8},{10,11... | collective-permute-start | bytes 23592968 | tf_op jit(solution)/shard_map/ppermute | solution.py:27
  4.6 18.8 %collective-permute-start.5 = (bf16[512,640]{1,0:T(8,128)(2,1)S(1)}, bf16[512,640]{1,0:T(8,128)(2,1)S(1)}, u32[]{:S(2)}, u32[]{:S(2)}) collective-permute-start(bf16[512,640]{1,0:T(8,128)(2,1)S(1)} %lay.1.refs_0_), channel_id=1, source_target_pairs={{0,2},{2,4},{4,6},{6,0},{1,3},{3,5},{5,7},{7,1},{8,10},{10,12},{12... | collective-permute-start | bytes 1966088 | tf_op jit(solution)/shard_map/ppermute | solution.py:27
  6.4 17.1 %collective-permute-start.6 = (bf16[512,640]{1,0:T(8,128)(2,1)S(1)}, bf16[512,640]{1,0:T(8,128)(2,1)S(1)}, u32[]{:S(2)}, u32[]{:S(2)}) collective-permute-start(bf16[512,640]{1,0:T(8,128)(2,1)S(1)} %lay.1.refs_0_), channel_id=1, source_target_pairs={{0,6},{2,0},{4,2},{6,4},{1,7},{3,1},{5,3},{7,5},{8,14},{10,8},{12,... | collective-permute-start | bytes 1966088 | tf_op jit(solution)/shard_map/ppermute | solution.py:27
  8.5 16.0 %collective-permute-start.7 = (bf16[512,640]{1,0:T(8,128)(2,1)S(1)}, bf16[512,640]{1,0:T(8,128)(2,1)}, u32[]{:S(2)}, u32[]{:S(2)}) collective-permute-start(bf16[512,640]{1,0:T(8,128)(2,1)S(1)} %lay.1.refs_0_), channel_id=1, source_target_pairs={{0,8},{8,0},{1,9},{9,1},{2,10},{10,2},{3,11},{11,3},{4,12},{12,4},... | collective-permute-start | bytes 1966088 | tf_op jit(solution)/shard_map/ppermute | solution.py:27
  24.4 16.2 %collective-permute-start.8 = (bf16[512,640]{1,0:T(8,128)(2,1)S(1)}, bf16[512,640]{1,0:T(8,128)(2,1)S(1)}, u32[]{:S(2)}, u32[]{:S(2)}) collective-permute-start(bf16[512,640]{1,0:T(8,128)(2,1)S(1)} %collective-permute-done.5.refs_1_), channel_id=1, source_target_pairs={{0,2},{2,4},{4,6},{6,0},{1,3},{3,5},{5,7},{7,1},{8,10},{10,12},{12... | collective-permute-start | bytes 1966088 | tf_op jit(solution)/shard_map/ppermute | solution.py:27
  24.8 15.8 %collective-permute-start.9 = (bf16[512,640]{1,0:T(8,128)(2,1)S(1)}, bf16[512,640]{1,0:T(8,128)(2,1)S(1)}, u32[]{:S(2)}, u32[]{:S(2)}) collective-permute-start(bf16[512,640]{1,0:T(8,128)(2,1)S(1)} %collective-permute-done.5.refs_1_), channel_id=1, source_target_pairs={{0,8},{8,0},{1,9},{9,1},{2,10},{10,2},{3,11},{11,3},{4,12},{12,4},... | collective-permute-start | bytes 1966088 | tf_op jit(solution)/shard_map/ppermute | solution.py:27
  26.1 14.8 %collective-permute-start.10 = (bf16[512,640]{1,0:T(8,128)(2,1)}, bf16[512,640]{1,0:T(8,128)(2,1)S(1)}, u32[]{:S(2)}, u32[]{:S(2)}) collective-permute-start(bf16[512,640]{1,0:T(8,128)(2,1)} %collective-permute-done.7.refs_3_), channel_id=1, source_target_pairs={{0,6},{2,0},{4,2},{6,4},{1,7},{3,1},{5,3},{7,5},{8,14},{10,8},{12,... | collective-permute-start | bytes 1966088 | tf_op jit(solution)/shard_map/ppermute | solution.py:27
  41.8 10.2 %collective-permute-start.11 = (bf16[512,256]{1,0:T(8,128)(2,1)}, bf16[512,256]{1,0:T(8,128)(2,1)S(1)}, u32[]{:S(2)}, u32[]{:S(2)}) collective-permute-start(bf16[512,256]{1,0:T(8,128)(2,1)} %slice.27), channel_id=1, source_target_pairs={{0,8},{8,0},{1,9},{9,1},{2,10},{10,2},{3,11},{11,3},{4,12},{12,4},... | collective-permute-start | bytes 786440 | tf_op jit(solution)/shard_map/ppermute | solution.py:27
  43.5 8.5 %collective-permute-start.12 = (bf16[512,256]{1,0:T(8,128)(2,1)}, bf16[512,256]{1,0:T(8,128)(2,1)}, u32[]{:S(2)}, u32[]{:S(2)}) collective-permute-start(bf16[512,256]{1,0:T(8,128)(2,1)} %slice.28), channel_id=1, source_target_pairs={{0,6},{2,0},{4,2},{6,4},{1,7},{3,1},{5,3},{7,5},{8,14},{10,8},{12,... | collective-permute-start | bytes 786440 | tf_op jit(solution)/shard_map/ppermute | solution.py:27
  74.1 9.8 %collective-permute-start.15 = (bf16[384,512]{1,0:T(8,128)(2,1)}, bf16[384,512]{1,0:T(8,128)(2,1)S(1)}, u32[]{:S(2)}, u32[]{:S(2)}) collective-permute-start(bf16[384,512]{1,0:T(8,128)(2,1)} %get-tuple-element.58), channel_id=1, source_target_pairs={{0,16},{16,32},{32,48},{48,0},{1,17},{17,33},{33,49},{49,1},{2,18}... | collective-permute-start | bytes 1179656 | tf_op jit(solution)/shard_map/ppermute | solution.py:27
  75.3 8.5 %collective-permute-start.16 = (bf16[384,512]{1,0:T(8,128)(2,1)}, bf16[384,512]{1,0:T(8,128)(2,1)S(1)}, u32[]{:S(2)}, u32[]{:S(2)}) collective-permute-start(bf16[384,512]{1,0:T(8,128)(2,1)} %get-tuple-element.59), channel_id=1, source_target_pairs={{0,48},{16,0},{32,16},{48,32},{1,49},{17,1},{33,17},{49,33},{2,50}... | collective-permute-start | bytes 1179656 | tf_op jit(solution)/shard_map/ppermute | solution.py:27
  76.8 7.0 %collective-permute-start.17 = (bf16[256,512]{1,0:T(8,128)(2,1)}, bf16[256,512]{1,0:T(8,128)(2,1)S(1)}, u32[]{:S(2)}, u32[]{:S(2)}) collective-permute-start(bf16[256,512]{1,0:T(8,128)(2,1)} %get-tuple-element.65.refs_4_), channel_id=1, source_target_pairs={{0,64},{64,0},{1,65},{65,1},{2,66},{66,2},{3,67},{67,3},{4,68},{68... | collective-permute-start | bytes 786440 | tf_op jit(solution)/shard_map/ppermute | solution.py:27
  83.9 23.1 %collective-permute-start.19 = (bf16[512,512]{1,0:T(8,128)(2,1)S(1)}, bf16[512,512]{1,0:T(8,128)(2,1)S(1)}, u32[]{:S(2)}, u32[]{:S(2)}) collective-permute-start(bf16[512,512]{1,0:T(8,128)(2,1)S(1)} %pad_maximum_fusion.1.refs_5_), channel_id=1, source_target_pairs={{0,64},{64,0},{1,65},{65,1},{2,66},{66,2},{3,67},{67,3},{4,68},{68... | collective-permute-start | bytes 1572872 | tf_op jit(solution)/shard_map/ppermute | solution.py:27
  87.6 19.5 %collective-permute-start.21 = (bf16[256,512]{1,0:T(8,128)(2,1)S(1)}, bf16[256,512]{1,0:T(8,128)(2,1)S(1)}, u32[]{:S(2)}, u32[]{:S(2)}) collective-permute-start(bf16[256,512]{1,0:T(8,128)(2,1)S(1)} %collective-permute-done.17.refs_7_), channel_id=1, source_target_pairs={{0,1},{1,0},{2,3},{3,2},{4,5},{5,4},{6,7},{7,6},{8,9},{9,8},{10,11... | collective-permute-start | bytes 786440 | tf_op jit(solution)/shard_map/ppermute | solution.py:27
  94.9 12.2 %collective-permute-start.18 = (bf16[256,512]{1,0:T(8,128)(2,1)S(1)}, bf16[256,512]{1,0:T(8,128)(2,1)S(1)}, u32[]{:S(2)}, u32[]{:S(2)}) collective-permute-start(bf16[256,512]{1,0:T(8,128)(2,1)S(1)} %copy-done.18), channel_id=1, source_target_pairs={{0,32},{16,48},{32,0},{48,16},{1,33},{17,49},{33,1},{49,17},{2,34}... | collective-permute-start | bytes 786440 | tf_op jit(solution)/shard_map/ppermute | solution.py:27
  96.9 10.1 %collective-permute-start.20 = (bf16[128,512]{1,0:T(8,128)(2,1)S(1)}, bf16[128,512]{1,0:T(8,128)(2,1)S(1)}, u32[]{:S(2)}, u32[]{:S(2)}) collective-permute-start(bf16[128,512]{1,0:T(8,128)(2,1)S(1)} %copy-done.19), channel_id=1, source_target_pairs={{0,32},{16,48},{32,0},{48,16},{1,33},{17,49},{33,1},{49,17},{2,34}... | collective-permute-start | bytes 393224 | tf_op jit(solution)/shard_map/ppermute | solution.py:27
  107.1 12.4 %collective-permute-start.23 = (bf16[768,512]{1,0:T(8,128)(2,1)S(1)}, bf16[768,512]{1,0:T(8,128)(2,1)S(1)}, u32[]{:S(2)}, u32[]{:S(2)}) collective-permute-start(bf16[768,512]{1,0:T(8,128)(2,1)S(1)} %pad_maximum_fusion), channel_id=1, source_target_pairs={{0,1},{1,0},{2,3},{3,2},{4,5},{5,4},{6,7},{7,6},{8,9},{9,8},{10,11... | collective-permute-start | bytes 2359304 | tf_op jit(solution)/shard_map/ppermute | solution.py:27
  108.1 9.4 %collective-permute-start.22 = (bf16[256,512]{1,0:T(8,128)(2,1)S(1)}, bf16[256,512]{1,0:T(8,128)(2,1)S(1)}, u32[]{:S(2)}, u32[]{:S(2)}) collective-permute-start(bf16[256,512]{1,0:T(8,128)(2,1)S(1)} %collective-permute-done.18.refs_6_), channel_id=1, source_target_pairs={{0,64},{64,0},{1,65},{65,1},{2,66},{66,2},{3,67},{67,3},{4,68},{68... | collective-permute-start | bytes 786440 | tf_op jit(solution)/shard_map/ppermute | solution.py:27
  108.2 10.1 %collective-permute-start.25 = (bf16[512,512]{1,0:T(8,128)(2,1)S(1)}, bf16[512,512]{1,0:T(8,128)(2,1)S(1)}, u32[]{:S(2)}, u32[]{:S(2)}) collective-permute-start(bf16[512,512]{1,0:T(8,128)(2,1)S(1)} %collective-permute-done.19.refs_8_), channel_id=1, source_target_pairs={{0,1},{1,0},{2,3},{3,2},{4,5},{5,4},{6,7},{7,6},{8,9},{9,8},{10,11... | collective-permute-start | bytes 1572872 | tf_op jit(solution)/shard_map/ppermute | solution.py:27
  108.6 9.8 %collective-permute-start.24 = (bf16[256,512]{1,0:T(8,128)(2,1)S(1)}, bf16[256,512]{1,0:T(8,128)(2,1)S(1)}, u32[]{:S(2)}, u32[]{:S(2)}) collective-permute-start(bf16[256,512]{1,0:T(8,128)(2,1)S(1)} %collective-permute-done.18.refs_6_), channel_id=1, source_target_pairs={{0,1},{1,0},{2,3},{3,2},{4,5},{5,4},{6,7},{7,6},{8,9},{9,8},{10,11... | collective-permute-start | bytes 786440 | tf_op jit(solution)/shard_map/ppermute | solution.py:27
  128.8 18.1 %collective-permute-start.27 = (bf16[256,5120]{1,0:T(8,128)(2,1)S(1)}, bf16[256,5120]{1,0:T(8,128)(2,1)}, u32[]{:S(2)}, u32[]{:S(2)}) collective-permute-start(bf16[256,5120]{1,0:T(8,128)(2,1)S(1)} %copy-done), channel_id=1, source_target_pairs={{0,1},{1,0},{2,3},{3,2},{4,5},{5,4},{6,7},{7,6},{8,9},{9,8},{10,11... | collective-permute-start | bytes 7864328 | tf_op jit(solution)/shard_map/ppermute | solution.py:27
  129.2 14.2 %collective-permute-start.28 = (bf16[512,128]{1,0:T(8,128)(2,1)S(1)}, bf16[512,128]{1,0:T(8,128)(2,1)S(1)}, u32[]{:S(2)}, u32[]{:S(2)}) collective-permute-start(bf16[512,128]{1,0:T(8,128)(2,1)S(1)} %get-tuple-element.71), channel_id=1, source_target_pairs={{0,48},{16,0},{32,16},{48,32},{1,49},{17,1},{33,17},{49,33},{2,50}... | collective-permute-start | bytes 393224 | tf_op jit(solution)/shard_map/ppermute | solution.py:27
  137.7 9.2 %collective-permute-start.30 = (bf16[512,128]{1,0:T(8,128)(2,1)S(1)}, bf16[512,128]{1,0:T(8,128)(2,1)S(1)}, u32[]{:S(2)}, u32[]{:S(2)}) collective-permute-start(bf16[512,128]{1,0:T(8,128)(2,1)S(1)} %get-tuple-element.73), channel_id=1, source_target_pairs={{0,16},{16,32},{32,48},{48,0},{1,17},{17,33},{33,49},{49,1},{2,18}... | collective-permute-start | bytes 393224 | tf_op jit(solution)/shard_map/ppermute | solution.py:27
  149.7 7.5 %collective-permute-start.31 = (bf16[512,256]{1,0:T(8,128)(2,1)S(1)}, bf16[512,256]{1,0:T(8,128)(2,1)S(1)}, u32[]{:S(2)}, u32[]{:S(2)}) collective-permute-start(bf16[512,256]{1,0:T(8,128)(2,1)S(1)} %get-tuple-element.74), channel_id=1, source_target_pairs={{0,8},{8,0},{1,9},{9,1},{2,10},{10,2},{3,11},{11,3},{4,12},{12,4},... | collective-permute-start | bytes 786440 | tf_op jit(solution)/shard_map/ppermute | solution.py:27
  149.8 8.4 %collective-permute-start.32 = (bf16[512,256]{1,0:T(8,128)(2,1)S(1)}, bf16[512,256]{1,0:T(8,128)(2,1)S(1)}, u32[]{:S(2)}, u32[]{:S(2)}) collective-permute-start(bf16[512,256]{1,0:T(8,128)(2,1)S(1)} %get-tuple-element.75), channel_id=1, source_target_pairs={{0,2},{2,4},{4,6},{6,0},{1,3},{3,5},{5,7},{7,1},{8,10},{10,12},{12... | collective-permute-start | bytes 786440 | tf_op jit(solution)/shard_map/ppermute | solution.py:27
  149.8 7.3 %collective-permute-start.33 = (bf16[512,128]{1,0:T(8,128)(2,1)S(1)}, bf16[512,128]{1,0:T(8,128)(2,1)S(1)}, u32[]{:S(2)}, u32[]{:S(2)}) collective-permute-start(bf16[512,128]{1,0:T(8,128)(2,1)S(1)} %get-tuple-element.76), channel_id=1, source_target_pairs={{0,6},{2,0},{4,2},{6,4},{1,7},{3,1},{5,3},{7,5},{8,14},{10,8},{12,... | collective-permute-start | bytes 393224 | tf_op jit(solution)/shard_map/ppermute | solution.py:27
  158.4 14.7 %collective-permute-start.34 = (bf16[512,640]{1,0:T(8,128)(2,1)S(1)}, bf16[512,640]{1,0:T(8,128)(2,1)S(1)}, u32[]{:S(2)}, u32[]{:S(2)}) collective-permute-start(bf16[512,640]{1,0:T(8,128)(2,1)S(1)} %get-tuple-element.86), channel_id=1, source_target_pairs={{0,6},{2,0},{4,2},{6,4},{1,7},{3,1},{5,3},{7,5},{8,14},{10,8},{12,... | collective-permute-start | bytes 1966088 | tf_op jit(solution)/shard_map/ppermute | solution.py:27
  158.4 14.6 %collective-permute-start.35 = (bf16[512,640]{1,0:T(8,128)(2,1)S(1)}, bf16[512,640]{1,0:T(8,128)(2,1)S(1)}, u32[]{:S(2)}, u32[]{:S(2)}) collective-permute-start(bf16[512,640]{1,0:T(8,128)(2,1)S(1)} %get-tuple-element.87), channel_id=1, source_target_pairs={{0,8},{8,0},{1,9},{9,1},{2,10},{10,2},{3,11},{11,3},{4,12},{12,4},... | collective-permute-start | bytes 1966088 | tf_op jit(solution)/shard_map/ppermute | solution.py:27
  159.6 14.8 %collective-permute-start.36 = (bf16[512,640]{1,0:T(8,128)(2,1)S(1)}, bf16[512,640]{1,0:T(8,128)(2,1)S(1)}, u32[]{:S(2)}, u32[]{:S(2)}) collective-permute-start(bf16[512,640]{1,0:T(8,128)(2,1)S(1)} %get-tuple-element.89), channel_id=1, source_target_pairs={{0,2},{2,4},{4,6},{6,0},{1,3},{3,5},{5,7},{7,1},{8,10},{10,12},{12... | collective-permute-start | bytes 1966088 | tf_op jit(solution)/shard_map/ppermute | solution.py:27
  167.2 21.2 %collective-permute-start.38 = (bf16[512,640]{1,0:T(8,128)(2,1)}, bf16[512,640]{1,0:T(8,128)(2,1)S(1)}, u32[]{:S(2)}, u32[]{:S(2)}) collective-permute-start(bf16[512,640]{1,0:T(8,128)(2,1)} %get-tuple-element.91), channel_id=1, source_target_pairs={{0,2},{2,4},{4,6},{6,0},{1,3},{3,5},{5,7},{7,1},{8,10},{10,12},{12... | collective-permute-start | bytes 1966088 | tf_op jit(solution)/shard_map/ppermute | solution.py:27
  174.8 13.6 %collective-permute-start.37 = (bf16[512,640]{1,0:T(8,128)(2,1)S(1)}, bf16[512,640]{1,0:T(8,128)(2,1)S(1)}, u32[]{:S(2)}, u32[]{:S(2)}) collective-permute-start(bf16[512,640]{1,0:T(8,128)(2,1)S(1)} %get-tuple-element.90), channel_id=1, source_target_pairs={{0,6},{2,0},{4,2},{6,4},{1,7},{3,1},{5,3},{7,5},{8,14},{10,8},{12,... | collective-permute-start | bytes 1966088 | tf_op jit(solution)/shard_map/ppermute | solution.py:27
  174.8 13.6 %collective-permute-start.39 = (bf16[512,640]{1,0:T(8,128)(2,1)S(1)}, bf16[512,640]{1,0:T(8,128)(2,1)S(1)}, u32[]{:S(2)}, u32[]{:S(2)}) collective-permute-start(bf16[512,640]{1,0:T(8,128)(2,1)S(1)} %get-tuple-element.92), channel_id=1, source_target_pairs={{0,8},{8,0},{1,9},{9,1},{2,10},{10,2},{3,11},{11,3},{4,12},{12,4},... | collective-permute-start | bytes 1966088 | tf_op jit(solution)/shard_map/ppermute | solution.py:27
  (29 other events, 349.0 us)

commit v10 on v9

--- a/solution.py
+++ b/solution.py
@@ -65,101 +65,100 @@
 
 
 def project_kernel(chips, heads, *refs):
-    xs, weights, modulation, rest = refs[:10], refs[10:14], refs[14], refs[15:]
-    outs, (held_x, normed, total, arrived) = rest[:-4], rest[-4:]
-    step = pl.program_id(0)
-    features = 8 * DEEP
-    count = normed.shape[1]
+    xs, weights, modulation, rest = refs[:10], refs[10:12], refs[12], refs[13:]
+    outs, (held_x, held_weight, normed, total, arrived, loaded) = rest[:-6], rest[-6:]
+    count, features = normed.shape
     tiles = [(piece, at) for piece in range(8) for at in range(0, DEEP, BLK)]
 
-    @pl.when(step == 0)
-    def _():
-        places = [held_x.at[piece] for piece in range(7)]
-        places += [held_x.at[7, :, cut[0] : cut[1]] for cut in CUTS]
-        copies = [
-            pltpu.make_async_copy(x, place, arrived.at[index])
-            for index, (x, place) in enumerate(zip(xs, places))
-        ]
-        for copy in copies:
-            copy.start()
-        for copy in copies:
-            copy.wait()
-        total[...] = jnp.zeros_like(total)
-
-        def norm(i, _):
-            rows = pl.ds(pl.multiple_of(i * ROWS, ROWS), ROWS)
-
-            def load(piece, at):
-                return held_x[piece, rows, at : at + BLK].astype(jnp.float32)
-
-            summed = jnp.zeros((ROWS, BLK), jnp.float32)
-            for tile in tiles:
-                summed = summed + load(*tile)
-            center = jnp.sum(summed, axis=1, keepdims=True) / features
-            center = jnp.broadcast_to(center, (ROWS, BLK))
-            summed = jnp.zeros((ROWS, BLK), jnp.float32)
-            for tile in tiles:
-                summed = summed + jnp.square(load(*tile) - center)
-            spread = jnp.sum(summed, axis=1, keepdims=True) / features
-            rate = jnp.broadcast_to(lax.rsqrt(spread + EPSILON), (ROWS, BLK))
-            for piece, at in tiles:
-                place = pl.ds(pl.multiple_of(chips[piece] * DEEP + at, BLK), BLK)
-                gain = 1.0 + modulation[1:2, place]
-                value = (load(piece, at) - center) * rate * gain + modulation[0:1, place]
-                column = piece % 2 * DEEP + at
-                normed[piece // 2, rows, column : column + BLK] = value.astype(jnp.bfloat16)
-            return 0
-
-        lax.fori_loop(0, count // ROWS, norm, 0)
-
-    held = normed[step]
+    places = [held_x.at[piece] for piece in range(7)]
+    places += [held_x.at[7, :, cut[0] : cut[1]] for cut in CUTS]
+    copies = [
+        pltpu.make_async_copy(x, place, arrived.at[index])
+        for index, (x, place) in enumerate(zip(xs, places))
+    ]
+    for copy in copies:
+        copy.start()
+    loads = []
+    for side, weight in enumerate(weights):
+        for piece in range(8):
+            rows = pl.ds(pl.multiple_of(chips[piece] * DEEP, BLK), DEEP)
+            loads.append(
+                pltpu.make_async_copy(
+                    weight.at[:, rows, :],
+                    held_weight.at[side, :, piece * DEEP : (piece + 1) * DEEP, :],
+                    loaded.at[side * 8 + piece],
+                )
+            )
+    for copy in copies:
+        copy.wait()
+    for copy in loads:
+        copy.start()
+
+    def norm(i, _):
+        rows = pl.ds(pl.multiple_of(i * ROWS, ROWS), ROWS)
+
+        def load(piece, at):
+            return held_x[piece, rows, at : at + BLK].astype(jnp.float32)
+
+        summed = jnp.zeros((ROWS, BLK), jnp.float32)
+        for tile in tiles:
+            summed = summed + load(*tile)
+        center = jnp.sum(summed, axis=1, keepdims=True) / features
+        center = jnp.broadcast_to(center, (ROWS, BLK))
+        summed = jnp.zeros((ROWS, BLK), jnp.float32)
+        for tile in tiles:
+            summed = summed + jnp.square(load(*tile) - center)
+        spread = jnp.sum(summed, axis=1, keepdims=True) / features
+        rate = jnp.broadcast_to(lax.rsqrt(spread + EPSILON), (ROWS, BLK))
+        for piece, at in tiles:
+            place = pl.ds(pl.multiple_of(chips[piece] * DEEP + at, BLK), BLK)
+            gain = 1.0 + modulation[1:2, place]
+            value = (load(piece, at) - center) * rate * gain + modulation[0:1, place]
+            column = piece * DEEP + at
+            normed[rows, column : column + BLK] = value.astype(jnp.bfloat16)
+        return 0
+
+    lax.fori_loop(0, count // ROWS, norm, 0)
+    for copy in loads:
+        copy.wait()
     for side in range(2):
         for part in range(3):
-            weight = jnp.concatenate([w[part] for w in weights[2 * side : 2 * side + 2]], axis=0)
-            made = jnp.dot(held, weight, preferred_element_type=jnp.float32)
+            made = jnp.dot(
+                normed[...], held_weight[side, part], preferred_element_type=jnp.float32
+            )
             for slot in range(2):
-                total[side * 6 + part * 2 + slot] += made[:, slot * BLK : (slot + 1) * BLK]
-
-    @pl.when(step == pl.num_programs(0) - 1)
-    def _():
-        for index in range(4):
-            if index % 2:
-                kv, q = outs[NEAR[index]], outs[NEAR[index]].at[2 * BLK :]
-            else:
-                kv, q = outs[index : index + 2]
-            base = heads[index]
-            q[...] = total[base].T.astype(jnp.bfloat16)
-            keys = total[base + 2]
-            for part in range(count // BLK):
-                rows = slice(part * BLK, (part + 1) * BLK)
-                kv[:BLK, rows] = keys[rows].astype(jnp.bfloat16)
-            kv[BLK : 2 * BLK, :] = total[base + 4].T.astype(jnp.bfloat16)
+                total[side * 6 + part * 2 + slot] = made[:, slot * BLK : (slot + 1) * BLK]
+    for index in range(4):
+        if index % 2:
+            kv, q = outs[NEAR[index]], outs[NEAR[index]].at[2 * BLK :]
+        else:
+            kv, q = outs[index : index + 2]
+        base = heads[index]
+        q[...] = total[base].T.astype(jnp.bfloat16)
+        for part in range(count // BLK):
+            rows = slice(part * BLK, (part + 1) * BLK)
+            kv[:BLK, rows] = total[base + 2, rows].astype(jnp.bfloat16)
+        kv[BLK : 2 * BLK, :] = total[base + 4].T.astype(jnp.bfloat16)
 
 
 def project(chips, heads, xs, own, other, modulation):
     parts, features, inner = own.shape
     count, deep = xs[0].shape
-    whole = lambda shape: pl.BlockSpec(shape, lambda k, *_: (0, 0))
-    blocks = [
-        pl.BlockSpec((parts, deep, inner), lambda k, chips, heads, i=i: (0, chips[2 * k + i], 0))
-        for i in range(2)
-    ]
     shapes = [(2 * BLK, count), (BLK, count)] * 2 + [(3 * BLK, count)] * 2
     return pl.pallas_call(
         project_kernel,
-        grid_spec=pltpu.PrefetchScalarGridSpec(
-            num_scalar_prefetch=2,
-            grid=(features // deep // 2,),
-            in_specs=[pl.BlockSpec(memory_space=pl.ANY)] * len(xs)
-            + [*blocks, *blocks, whole(modulation.shape)],
-            out_specs=[whole(s) for s in shapes],
-            scratch_shapes=[
-                pltpu.VMEM((features // deep, count, deep), jnp.bfloat16),
-                pltpu.VMEM((features // deep // 2, count, 2 * deep), jnp.bfloat16),
-                pltpu.VMEM((2 * parts * inner // BLK, count, BLK), jnp.float32),
-                pltpu.SemaphoreType.DMA((len(xs),)),
-            ],
-        ),
+        in_specs=[pl.BlockSpec(memory_space=pltpu.SMEM)] * 2
+        + [pl.BlockSpec(memory_space=pl.ANY)] * (len(xs) + 2)
+        + [pl.BlockSpec(memory_space=pltpu.VMEM)],
+        out_specs=[pl.BlockSpec(memory_space=pltpu.VMEM)] * len(shapes),
+        scratch_shapes=[
+            pltpu.VMEM((features // deep, count, deep), jnp.bfloat16),
+            pltpu.VMEM((2, parts, features, inner), jnp.bfloat16),
+            pltpu.VMEM((count, features), jnp.bfloat16),
+            pltpu.VMEM((2 * parts * inner // BLK, count, BLK), jnp.float32),
+            pltpu.SemaphoreType.DMA((len(xs),)),
+            pltpu.SemaphoreType.DMA((2 * features // deep,)),
+        ],
         out_shape=[jax.ShapeDtypeStruct(s, jnp.bfloat16) for s in shapes],
         compiler_params=pltpu.CompilerParams(vmem_limit_bytes=56 * MIB),
         cost_estimate=pl.CostEstimate(
@@ -168,7 +167,7 @@
             transcendentals=0,
         ),
         name="project",
-    )(chips, heads, *xs, own, own, other, other, modulation)
+    )(chips, heads, *xs, own, other, modulation)
 
 
 def attend_kernel(factor, unroll, plan, places, counts, first, owner, *refs):

time: 195 us -> 190 us (0.974)
  starting transfers between devices: 62.5 us -> 55.7 us
  local copies, waits for them, and re-layouts: 7.65 us -> 4.49 us
    ppermute x41, starting transfers between devices: 62.5 us -> 55.7 us  [shift(): lax.ppermute(value, axis, [(i, (i + steps) % count) for i in range(count)])]
    pallas_call x1, Pallas kernels: 9.24 us -> 13.8 us  [attend(): pl.pallas_call(kernel, in_specs=[pl.BlockSpec(memory_space=pltpu.SMEM)] *...]
    pallas_call x1, Pallas kernels: 21.3 us -> 18.6 us  [project(): pl.pallas_call(project_kernel, in_specs=[pl.BlockSpec(memory_space=pltpu....]
  transfers between devices with their start and end apart: 41 -> 41, of which waited for: 21 -> 21; matrix products, arithmetic and copies ran while one was open for 3% -> 2% of each run, Pallas kernels for 6% -> 6%
where the time goes in v10:
time: 190 us
  waiting for transfers between devices  78.1 us (41%)
  starting transfers between devices  55.7 us (29%)
  Pallas kernels  47.2 us (25%)
  local copies, waits for them, and re-layouts  4.49 us (2%)
  other arithmetic  3.83 us (2%)
    ppermute x41, waiting for transfers between devices, shift(): lax.ppermute(value, axis, [(i, (i + steps) % count) for i in range(count)])  78.1 us
    ppermute x41, starting transfers between devices, shift(): lax.ppermute(value, axis, [(i, (i + steps) % count) for i in range(count)])  55.7 us
    pallas_call x1, Pallas kernels, project(): pl.pallas_call(project_kernel, in_specs=[pl.BlockSpec(memory_space=pltpu....  18.6 us
    pallas_call x1, Pallas kernels, attend(): pl.pallas_call(kernel, in_specs=[pl.BlockSpec(memory_space=pltpu.SMEM)] *...  13.8 us
    pallas_call x3, Pallas kernels, leave(): pl.pallas_call(kernel, grid_spec=pltpu.PrefetchScalarGridSpec(num_scalar_...  13.5 us
  transfers between devices with their start and end apart: 41, of which 21 were waited for; matrix products, arithmetic and copies ran while one was open for 2% of the time, Pallas kernels for 6%

profile of v10, /device:TPU:1, one launch (start us, length us, event | category | flops | bytes accessed | tf_op | source)
XLA Modules:
  0.0 189.7 jit_solution(11724642972183442082)
XLA Ops:
  1.1 1.5 collective-permute-start.4
  4.6 1.7 collective-permute-start.5
  6.4 2.1 %collective-permute-start.6 = (bf16[512,640]{1,0:T(8,128)(2,1)S(1)}, bf16[512,640]{1,0:T(8,128)(2,1)S(1)}, u32[]{:S(2)}, u32[]{:S(2)}) collective-permute-start(bf16[512,640]{1,0:T(8,128)(2,1)S(1)} %lay.1.refs_0_), channel_id=1, source_target_pairs={{0,6},{2,0},{4,2},{6,4},{1,7},{3,1},{5,3},{7,5},{8,14},{10,8},{12,... | collective-permute-start | bytes 1966088 | tf_op jit(solution)/shard_map/ppermute | solution.py:27
  9.8 13.8 %collective-permute-done.5.refs_1_ = bf16[512,640]{1,0:T(8,128)(2,1)} collective-permute-done((bf16[512,640]{1,0:T(8,128)(2,1)S(1)}, bf16[512,640]{1,0:T(8,128)(2,1)}, u32[]{:S(2)}, u32[]{:S(2)}) %collective-permute-start.5) | collective-permute-done | bytes 655392 | tf_op jit(solution)/shard_map/ppermute | solution.py:27
  25.8 2.7 %collective-permute-start.10 = (bf16[512,640]{1,0:T(8,128)(2,1)}, bf16[512,640]{1,0:T(8,128)(2,1)S(1)}, u32[]{:S(2)}, u32[]{:S(2)}) collective-permute-start(bf16[512,640]{1,0:T(8,128)(2,1)} %collective-permute-done.7.refs_3_), channel_id=1, source_target_pairs={{0,6},{2,0},{4,2},{6,4},{1,7},{3,1},{5,3},{7,5},{8,14},{10,8},{12,... | collective-permute-start | bytes 1966088 | tf_op jit(solution)/shard_map/ppermute | solution.py:27
  28.5 2.5 %collective-permute-start.3 = (s32[4,64]{1,0:T(4,128)S(1)}, s32[4,64]{1,0:T(4,128)S(1)}, u32[]{:S(2)}, u32[]{:S(2)}) collective-permute-start(s32[4,64]{1,0:T(4,128)S(1)} %get-tuple-element.102), channel_id=1, source_target_pairs={{0,48},{16,0},{32,16},{48,32},{1,49},{17,1},{33,17},{49,33},{2,50}... | collective-permute-start | bytes 3080 | tf_op jit(solution)/shard_map/ppermute | solution.py:27
  31.7 2.3 %collective-permute-start.2 = (s32[4,64]{1,0:T(4,128)S(1)}, s32[4,64]{1,0:T(4,128)S(1)}, u32[]{:S(2)}, u32[]{:S(2)}) collective-permute-start(s32[4,64]{1,0:T(4,128)S(1)} %get-tuple-element.101), channel_id=1, source_target_pairs={{0,32},{16,48},{32,0},{48,16},{1,33},{17,49},{33,1},{49,17},{2,34}... | collective-permute-start | bytes 3080 | tf_op jit(solution)/shard_map/ppermute | solution.py:27
  34.0 1.7 collective-permute-done.2
  36.8 3.3 %collective-permute-done.1 = s32[4,64]{1,0:T(4,128)S(1)} collective-permute-done((s32[4,64]{1,0:T(4,128)S(1)}, s32[4,64]{1,0:T(4,128)S(1)}, u32[]{:S(2)}, u32[]{:S(2)}) %collective-permute-start.1) | collective-permute-done | bytes 1056 | tf_op jit(solution)/shard_map/ppermute | solution.py:27
  42.3 2.3 %collective-permute-start.12 = (bf16[512,256]{1,0:T(8,128)(2,1)S(1)}, bf16[512,256]{1,0:T(8,128)(2,1)}, u32[]{:S(2)}, u32[]{:S(2)}) collective-permute-start(bf16[512,256]{1,0:T(8,128)(2,1)S(1)} %slice.28), channel_id=1, source_target_pairs={{0,6},{2,0},{4,2},{6,4},{1,7},{3,1},{5,3},{7,5},{8,14},{10,8},{12,... | collective-permute-start | bytes 786440 | tf_op jit(solution)/shard_map/ppermute | solution.py:27
  46.2 3.8 %collective-permute-done.13.refs_9_ = bf16[512,128]{1,0:T(8,128)(2,1)S(1)} collective-permute-done((bf16[512,128]{1,0:T(8,128)(2,1)S(1)}, bf16[512,128]{1,0:T(8,128)(2,1)S(1)}, u32[]{:S(2)}, u32[]{:S(2)}) %collective-permute-start.13) | collective-permute-done | bytes 131104 | tf_op jit(solution)/shard_map/ppermute | solution.py:27
  50.6 18.6 %project.1 = (bf16[256,512]{1,0:T(8,128)(2,1)}, bf16[128,512]{1,0:T(8,128)(2,1)}, bf16[256,512]{1,0:T(8,128)(2,1)}, bf16[128,512]{1,0:T(8,128)(2,1)}, bf16[384,5...) custom-call(s32[8]{0:T(128)} %stack.97.chips, s32[4]{0:T(128)} %pad_add_fusion.2.heads, bf16[512,640]{1,0:T(8,128)(2,1)} %copy-done.1, ...), custom_call_target="tpu_custom_call" | custom-call | flops 8053063680 | bytes 20971520 | tf_op jit(solution)/shard_map/project/pallas_call | solution.py:148
  70.6 1.5 collective-permute-start.16
  72.0 3.0 %collective-permute-start.17 = (bf16[256,512]{1,0:T(8,128)(2,1)}, bf16[256,512]{1,0:T(8,128)(2,1)S(1)}, u32[]{:S(2)}, u32[]{:S(2)}) collective-permute-start(bf16[256,512]{1,0:T(8,128)(2,1)} %get-tuple-element.65.refs_4_), channel_id=1, source_target_pairs={{0,64},{64,0},{1,65},{65,1},{2,66},{66,2},{3,67},{67,3},{4,68},{68... | collective-permute-start | bytes 786440 | tf_op jit(solution)/shard_map/ppermute | solution.py:27
  75.7 3.4 %collective-permute-done.17.refs_7_ = bf16[256,512]{1,0:T(8,128)(2,1)S(1)} collective-permute-done((bf16[256,512]{1,0:T(8,128)(2,1)}, bf16[256,512]{1,0:T(8,128)(2,1)S(1)}, u32[]{:S(2)}, u32[]{:S(2)}) %collective-permute-start.17) | collective-permute-done | bytes 262176 | tf_op jit(solution)/shard_map/ppermute | solution.py:27
  79.2 3.3 %collective-permute-start.19 = (bf16[512,512]{1,0:T(8,128)(2,1)S(1)}, bf16[512,512]{1,0:T(8,128)(2,1)S(1)}, u32[]{:S(2)}, u32[]{:S(2)}) collective-permute-start(bf16[512,512]{1,0:T(8,128)(2,1)S(1)} %pad_maximum_fusion.1.refs_5_), channel_id=1, source_target_pairs={{0,64},{64,0},{1,65},{65,1},{2,66},{66,2},{3,67},{67,3},{4,68},{68... | collective-permute-start | bytes 1572872 | tf_op jit(solution)/shard_map/ppermute | solution.py:27
  82.8 7.3 %collective-permute-start.21 = (bf16[256,512]{1,0:T(8,128)(2,1)S(1)}, bf16[256,512]{1,0:T(8,128)(2,1)S(1)}, u32[]{:S(2)}, u32[]{:S(2)}) collective-permute-start(bf16[256,512]{1,0:T(8,128)(2,1)S(1)} %collective-permute-done.17.refs_7_), channel_id=1, source_target_pairs={{0,1},{1,0},{2,3},{3,2},{4,5},{5,4},{6,7},{7,6},{8,9},{9,8},{10,11... | collective-permute-start | bytes 786440 | tf_op jit(solution)/shard_map/ppermute | solution.py:27
  90.1 1.9 collective-permute-start.18
  93.7 8.6 %collective-permute-done.20.refs_17_ = bf16[128,512]{1,0:T(8,128)(2,1)S(1)} collective-permute-done((bf16[128,512]{1,0:T(8,128)(2,1)S(1)}, bf16[128,512]{1,0:T(8,128)(2,1)S(1)}, u32[]{:S(2)}, u32[]{:S(2)}) %collective-permute-start.20) | collective-permute-done | bytes 131104 | tf_op jit(solution)/shard_map/ppermute | solution.py:27
  103.9 8.7 %collective-permute-done.22.refs_9_ = bf16[256,512]{1,0:T(8,128)(2,1)S(1)} collective-permute-done((bf16[256,512]{1,0:T(8,128)(2,1)S(1)}, bf16[256,512]{1,0:T(8,128)(2,1)S(1)}, u32[]{:S(2)}, u32[]{:S(2)}) %collective-permute-start.22) | collective-permute-done | bytes 262176 | tf_op jit(solution)/shard_map/ppermute | solution.py:27
  114.7 13.8 %attend.1 = (bf16[512,128]{1,0:T(8,128)(2,1)S(1)}, bf16[512,128]{1,0:T(8,128)(2,1)S(1)}, bf16[512,128]{1,0:T(8,128)(2,1)S(1)}, bf16[512,128]{1,0:T(8,128)(2,1)S(1)}) custom-call(s32[16,64]{1,0:T(8,128)S(1)} %select_reduce_fusion.2.refs_0_, s32[16]{0:T(128)S(1)} %get-tuple-element.93.refs_1_, s32[17]{0:T(128)S(1)} %select_reduce_fusion.5.refs_2_, ...), custom_call_target="tpu_custom_call" | custom-call | flops 2147483648 | bytes 4194304 | tf_op jit(solution)/shard_map/attend/pallas_call | solution.py:289
  129.0 1.6 collective-permute-start.28
  131.2 2.8 %collective-permute-done.28.refs_5_ = bf16[512,128]{1,0:T(8,128)(2,1)S(1)} collective-permute-done((bf16[512,128]{1,0:T(8,128)(2,1)S(1)}, bf16[512,128]{1,0:T(8,128)(2,1)S(1)}, u32[]{:S(2)}, u32[]{:S(2)}) %collective-permute-start.28) | collective-permute-done | bytes 131104 | tf_op jit(solution)/shard_map/ppermute | solution.py:27
  134.0 2.8 %collective-permute-done.29.refs_6_ = bf16[512,128]{1,0:T(8,128)(2,1)S(1)} collective-permute-done((bf16[512,128]{1,0:T(8,128)(2,1)S(1)}, bf16[512,128]{1,0:T(8,128)(2,1)S(1)}, u32[]{:S(2)}, u32[]{:S(2)}) %collective-permute-start.29) | collective-permute-done | bytes 131104 | tf_op jit(solution)/shard_map/ppermute | solution.py:27
  136.8 2.9 %collective-permute-done.30.refs_7_ = bf16[512,128]{1,0:T(8,128)(2,1)S(1)} collective-permute-done((bf16[512,128]{1,0:T(8,128)(2,1)S(1)}, bf16[512,128]{1,0:T(8,128)(2,1)S(1)}, u32[]{:S(2)}, u32[]{:S(2)}) %collective-permute-start.30) | collective-permute-done | bytes 131104 | tf_op jit(solution)/shard_map/ppermute | solution.py:27
  139.7 2.8 %leave.3 = (bf16[512,256]{1,0:T(8,128)(2,1)S(1)}, bf16[512,256]{1,0:T(8,128)(2,1)S(1)}, bf16[512,128]{1,0:T(8,128)(2,1)S(1)}) custom-call(s32[1]{0:T(128)} %bitcast.18.refs_0_, s32[4]{0:T(128)S(1)} %pad_add_fusion.1.refs_1_, bf16[256,5120]{1,0:T(8,128)(2,1)S(1)} %copy-done, bf16[256,5120]{1,0:T(8,128)(2,1)} %collective-permute-done.27.refs_3_, ...), custom_call_target="tpu_custom_call" | custom-call | flops 335544320 | bytes 1310720 | tf_op jit(solution)/shard_map/leave/pallas_call | solution.py:355
  143.9 2.7 %collective-permute-start.33 = (bf16[512,128]{1,0:T(8,128)(2,1)S(1)}, bf16[512,128]{1,0:T(8,128)(2,1)S(1)}, u32[]{:S(2)}, u32[]{:S(2)}) collective-permute-start(bf16[512,128]{1,0:T(8,128)(2,1)S(1)} %get-tuple-element.76), channel_id=1, source_target_pairs={{0,6},{2,0},{4,2},{6,4},{1,7},{3,1},{5,3},{7,5},{8,14},{10,8},{12,... | collective-permute-start | bytes 393224 | tf_op jit(solution)/shard_map/ppermute | solution.py:27
  146.6 4.6 %leave.5 = (bf16[512,640]{1,0:T(8,128)(2,1)S(1)}, bf16[512,640]{1,0:T(8,128)(2,1)S(1)}, bf16[512,640]{1,0:T(8,128)(2,1)S(1)}) custom-call(s32[3]{0:T(128)S(1)} %pad_add_fusion.3.refs_0_, s32[4]{0:T(128)S(1)} %pad_add_fusion.1.refs_1_, bf16[256,5120]{1,0:T(8,128)(2,1)S(1)} %copy-done, bf16[256,5120]{1,0:T(8,128)(2,1)} %collective-permute-done.27.refs_3_, ...), custom_call_target="tpu_custom_call" | custom-call | flops 1006632960 | bytes 3932160 | tf_op jit(solution)/shard_map/leave/pallas_call | solution.py:355
  153.9 6.2 %leave.4 = (bf16[512,640]{1,0:T(8,128)(2,1)S(1)}, bf16[512,640]{1,0:T(8,128)(2,1)}, bf16[512,640]{1,0:T(8,128)(2,1)S(1)}, bf16[512,640]{1,0:T(8,128)(2,1)S(1)}) custom-call(s32[4]{0:T(128)S(1)} %pad_add_fusion.refs_0_, s32[4]{0:T(128)S(1)} %pad_add_fusion.1.refs_1_, bf16[256,5120]{1,0:T(8,128)(2,1)S(1)} %copy-done, ...), custom_call_target="tpu_custom_call" | custom-call | flops 1342177280 | bytes 5242880 | tf_op jit(solution)/shard_map/leave/pallas_call | solution.py:355
  160.2 6.2 %collective-permute-done.34.refs_1_ = bf16[512,640]{1,0:T(8,128)(2,1)S(1)} collective-permute-done((bf16[512,640]{1,0:T(8,128)(2,1)S(1)}, bf16[512,640]{1,0:T(8,128)(2,1)S(1)}, u32[]{:S(2)}, u32[]{:S(2)}) %collective-permute-start.34) | collective-permute-done | bytes 655392 | tf_op jit(solution)/shard_map/ppermute | solution.py:27
  169.0 12.9 %collective-permute-done.38.refs_2_ = bf16[512,640]{1,0:T(8,128)(2,1)S(1)} collective-permute-done((bf16[512,640]{1,0:T(8,128)(2,1)}, bf16[512,640]{1,0:T(8,128)(2,1)S(1)}, u32[]{:S(2)}, u32[]{:S(2)}) %collective-permute-start.38) | collective-permute-done | bytes 655392 | tf_op jit(solution)/shard_map/ppermute | solution.py:27
  183.5 3.7 %collective-permute-start.40 = (bf16[320,512]{1,0:T(8,128)(2,1)S(1)}, bf16[320,512]{1,0:T(8,128)(2,1)S(1)}, u32[]{:S(2)}, u32[]{:S(2)}) collective-permute-start(bf16[320,512]{1,0:T(8,128)(2,1)S(1)} %constant_dynamic-slice_fusion), channel_id=1, source_target_pairs={{0,1},{1,0},{2,3},{3,2},{4,5},{5,4},{6,7},{7,6},{8,9},{9,8},{10,11... | collective-permute-start | bytes 983048 | tf_op jit(solution)/shard_map/ppermute | solution.py:27
  (121 shorter events, 32.5 us)
Async XLA Ops:
  4.2 45.8 %collective-permute-start.14 = (bf16[3,5120,256]{2,1,0:T(8,128)(2,1)}, bf16[3,5120,256]{2,1,0:T(8,128)(2,1)}, u32[]{:S(2)}, u32[]{:S(2)}) collective-permute-start(bf16[3,5120,256]{2,1,0:T(8,128)(2,1)} %refs_10_.1), channel_id=1, source_target_pairs={{0,1},{1,0},{2,3},{3,2},{4,5},{5,4},{6,7},{7,6},{8,9},{9,8},{10,11... | collective-permute-start | bytes 23592968 | tf_op jit(solution)/shard_map/ppermute | solution.py:27
  4.6 18.9 %collective-permute-start.5 = (bf16[512,640]{1,0:T(8,128)(2,1)S(1)}, bf16[512,640]{1,0:T(8,128)(2,1)}, u32[]{:S(2)}, u32[]{:S(2)}) collective-permute-start(bf16[512,640]{1,0:T(8,128)(2,1)S(1)} %lay.1.refs_0_), channel_id=1, source_target_pairs={{0,2},{2,4},{4,6},{6,0},{1,3},{3,5},{5,7},{7,1},{8,10},{10,12},{12... | collective-permute-start | bytes 1966088 | tf_op jit(solution)/shard_map/ppermute | solution.py:27
  6.4 17.2 %collective-permute-start.6 = (bf16[512,640]{1,0:T(8,128)(2,1)S(1)}, bf16[512,640]{1,0:T(8,128)(2,1)S(1)}, u32[]{:S(2)}, u32[]{:S(2)}) collective-permute-start(bf16[512,640]{1,0:T(8,128)(2,1)S(1)} %lay.1.refs_0_), channel_id=1, source_target_pairs={{0,6},{2,0},{4,2},{6,4},{1,7},{3,1},{5,3},{7,5},{8,14},{10,8},{12,... | collective-permute-start | bytes 1966088 | tf_op jit(solution)/shard_map/ppermute | solution.py:27
  8.5 16.0 %collective-permute-start.7 = (bf16[512,640]{1,0:T(8,128)(2,1)S(1)}, bf16[512,640]{1,0:T(8,128)(2,1)}, u32[]{:S(2)}, u32[]{:S(2)}) collective-permute-start(bf16[512,640]{1,0:T(8,128)(2,1)S(1)} %lay.1.refs_0_), channel_id=1, source_target_pairs={{0,8},{8,0},{1,9},{9,1},{2,10},{10,2},{3,11},{11,3},{4,12},{12,4},... | collective-permute-start | bytes 1966088 | tf_op jit(solution)/shard_map/ppermute | solution.py:27
  24.4 16.4 %collective-permute-start.8 = (bf16[512,640]{1,0:T(8,128)(2,1)}, bf16[512,640]{1,0:T(8,128)(2,1)S(1)}, u32[]{:S(2)}, u32[]{:S(2)}) collective-permute-start(bf16[512,640]{1,0:T(8,128)(2,1)} %collective-permute-done.5.refs_1_), channel_id=1, source_target_pairs={{0,2},{2,4},{4,6},{6,0},{1,3},{3,5},{5,7},{7,1},{8,10},{10,12},{12... | collective-permute-start | bytes 1966088 | tf_op jit(solution)/shard_map/ppermute | solution.py:27
  24.5 16.4 %collective-permute-start.9 = (bf16[512,640]{1,0:T(8,128)(2,1)}, bf16[512,640]{1,0:T(8,128)(2,1)S(1)}, u32[]{:S(2)}, u32[]{:S(2)}) collective-permute-start(bf16[512,640]{1,0:T(8,128)(2,1)} %collective-permute-done.5.refs_1_), channel_id=1, source_target_pairs={{0,8},{8,0},{1,9},{9,1},{2,10},{10,2},{3,11},{11,3},{4,12},{12,4},... | collective-permute-start | bytes 1966088 | tf_op jit(solution)/shard_map/ppermute | solution.py:27
  25.8 15.2 %collective-permute-start.10 = (bf16[512,640]{1,0:T(8,128)(2,1)}, bf16[512,640]{1,0:T(8,128)(2,1)S(1)}, u32[]{:S(2)}, u32[]{:S(2)}) collective-permute-start(bf16[512,640]{1,0:T(8,128)(2,1)} %collective-permute-done.7.refs_3_), channel_id=1, source_target_pairs={{0,6},{2,0},{4,2},{6,4},{1,7},{3,1},{5,3},{7,5},{8,14},{10,8},{12,... | collective-permute-start | bytes 1966088 | tf_op jit(solution)/shard_map/ppermute | solution.py:27
  40.9 9.0 %collective-permute-start.11 = (bf16[512,256]{1,0:T(8,128)(2,1)S(1)}, bf16[512,256]{1,0:T(8,128)(2,1)}, u32[]{:S(2)}, u32[]{:S(2)}) collective-permute-start(bf16[512,256]{1,0:T(8,128)(2,1)S(1)} %slice.27), channel_id=1, source_target_pairs={{0,8},{8,0},{1,9},{9,1},{2,10},{10,2},{3,11},{11,3},{4,12},{12,4},... | collective-permute-start | bytes 786440 | tf_op jit(solution)/shard_map/ppermute | solution.py:27
  42.3 7.7 %collective-permute-start.12 = (bf16[512,256]{1,0:T(8,128)(2,1)S(1)}, bf16[512,256]{1,0:T(8,128)(2,1)}, u32[]{:S(2)}, u32[]{:S(2)}) collective-permute-start(bf16[512,256]{1,0:T(8,128)(2,1)S(1)} %slice.28), channel_id=1, source_target_pairs={{0,6},{2,0},{4,2},{6,4},{1,7},{3,1},{5,3},{7,5},{8,14},{10,8},{12,... | collective-permute-start | bytes 786440 | tf_op jit(solution)/shard_map/ppermute | solution.py:27
  69.3 9.8 %collective-permute-start.15 = (bf16[384,512]{1,0:T(8,128)(2,1)}, bf16[384,512]{1,0:T(8,128)(2,1)S(1)}, u32[]{:S(2)}, u32[]{:S(2)}) collective-permute-start(bf16[384,512]{1,0:T(8,128)(2,1)} %get-tuple-element.58), channel_id=1, source_target_pairs={{0,16},{16,32},{32,48},{48,0},{1,17},{17,33},{33,49},{49,1},{2,18}... | collective-permute-start | bytes 1179656 | tf_op jit(solution)/shard_map/ppermute | solution.py:27
  70.6 8.5 %collective-permute-start.16 = (bf16[384,512]{1,0:T(8,128)(2,1)}, bf16[384,512]{1,0:T(8,128)(2,1)S(1)}, u32[]{:S(2)}, u32[]{:S(2)}) collective-permute-start(bf16[384,512]{1,0:T(8,128)(2,1)} %get-tuple-element.59), channel_id=1, source_target_pairs={{0,48},{16,0},{32,16},{48,32},{1,49},{17,1},{33,17},{49,33},{2,50}... | collective-permute-start | bytes 1179656 | tf_op jit(solution)/shard_map/ppermute | solution.py:27
  72.0 7.0 %collective-permute-start.17 = (bf16[256,512]{1,0:T(8,128)(2,1)}, bf16[256,512]{1,0:T(8,128)(2,1)S(1)}, u32[]{:S(2)}, u32[]{:S(2)}) collective-permute-start(bf16[256,512]{1,0:T(8,128)(2,1)} %get-tuple-element.65.refs_4_), channel_id=1, source_target_pairs={{0,64},{64,0},{1,65},{65,1},{2,66},{66,2},{3,67},{67,3},{4,68},{68... | collective-permute-start | bytes 786440 | tf_op jit(solution)/shard_map/ppermute | solution.py:27
  79.2 23.1 %collective-permute-start.19 = (bf16[512,512]{1,0:T(8,128)(2,1)S(1)}, bf16[512,512]{1,0:T(8,128)(2,1)S(1)}, u32[]{:S(2)}, u32[]{:S(2)}) collective-permute-start(bf16[512,512]{1,0:T(8,128)(2,1)S(1)} %pad_maximum_fusion.1.refs_5_), channel_id=1, source_target_pairs={{0,64},{64,0},{1,65},{65,1},{2,66},{66,2},{3,67},{67,3},{4,68},{68... | collective-permute-start | bytes 1572872 | tf_op jit(solution)/shard_map/ppermute | solution.py:27
  82.8 19.5 %collective-permute-start.21 = (bf16[256,512]{1,0:T(8,128)(2,1)S(1)}, bf16[256,512]{1,0:T(8,128)(2,1)S(1)}, u32[]{:S(2)}, u32[]{:S(2)}) collective-permute-start(bf16[256,512]{1,0:T(8,128)(2,1)S(1)} %collective-permute-done.17.refs_7_), channel_id=1, source_target_pairs={{0,1},{1,0},{2,3},{3,2},{4,5},{5,4},{6,7},{7,6},{8,9},{9,8},{10,11... | collective-permute-start | bytes 786440 | tf_op jit(solution)/shard_map/ppermute | solution.py:27
  90.1 12.2 %collective-permute-start.18 = (bf16[256,512]{1,0:T(8,128)(2,1)S(1)}, bf16[256,512]{1,0:T(8,128)(2,1)S(1)}, u32[]{:S(2)}, u32[]{:S(2)}) collective-permute-start(bf16[256,512]{1,0:T(8,128)(2,1)S(1)} %copy-done.12), channel_id=1, source_target_pairs={{0,32},{16,48},{32,0},{48,16},{1,33},{17,49},{33,1},{49,17},{2,34}... | collective-permute-start | bytes 786440 | tf_op jit(solution)/shard_map/ppermute | solution.py:27
  92.1 10.1 %collective-permute-start.20 = (bf16[128,512]{1,0:T(8,128)(2,1)S(1)}, bf16[128,512]{1,0:T(8,128)(2,1)S(1)}, u32[]{:S(2)}, u32[]{:S(2)}) collective-permute-start(bf16[128,512]{1,0:T(8,128)(2,1)S(1)} %copy-done.14), channel_id=1, source_target_pairs={{0,32},{16,48},{32,0},{48,16},{1,33},{17,49},{33,1},{49,17},{2,34}... | collective-permute-start | bytes 393224 | tf_op jit(solution)/shard_map/ppermute | solution.py:27
  102.3 12.4 %collective-permute-start.23 = (bf16[768,512]{1,0:T(8,128)(2,1)S(1)}, bf16[768,512]{1,0:T(8,128)(2,1)S(1)}, u32[]{:S(2)}, u32[]{:S(2)}) collective-permute-start(bf16[768,512]{1,0:T(8,128)(2,1)S(1)} %pad_maximum_fusion), channel_id=1, source_target_pairs={{0,1},{1,0},{2,3},{3,2},{4,5},{5,4},{6,7},{7,6},{8,9},{9,8},{10,11... | collective-permute-start | bytes 2359304 | tf_op jit(solution)/shard_map/ppermute | solution.py:27
  103.3 9.4 %collective-permute-start.22 = (bf16[256,512]{1,0:T(8,128)(2,1)S(1)}, bf16[256,512]{1,0:T(8,128)(2,1)S(1)}, u32[]{:S(2)}, u32[]{:S(2)}) collective-permute-start(bf16[256,512]{1,0:T(8,128)(2,1)S(1)} %collective-permute-done.18.refs_6_), channel_id=1, source_target_pairs={{0,64},{64,0},{1,65},{65,1},{2,66},{66,2},{3,67},{67,3},{4,68},{68... | collective-permute-start | bytes 786440 | tf_op jit(solution)/shard_map/ppermute | solution.py:27
  103.4 10.1 %collective-permute-start.25 = (bf16[512,512]{1,0:T(8,128)(2,1)S(1)}, bf16[512,512]{1,0:T(8,128)(2,1)S(1)}, u32[]{:S(2)}, u32[]{:S(2)}) collective-permute-start(bf16[512,512]{1,0:T(8,128)(2,1)S(1)} %collective-permute-done.19.refs_8_), channel_id=1, source_target_pairs={{0,1},{1,0},{2,3},{3,2},{4,5},{5,4},{6,7},{7,6},{8,9},{9,8},{10,11... | collective-permute-start | bytes 1572872 | tf_op jit(solution)/shard_map/ppermute | solution.py:27
  103.8 9.8 %collective-permute-start.24 = (bf16[256,512]{1,0:T(8,128)(2,1)S(1)}, bf16[256,512]{1,0:T(8,128)(2,1)S(1)}, u32[]{:S(2)}, u32[]{:S(2)}) collective-permute-start(bf16[256,512]{1,0:T(8,128)(2,1)S(1)} %collective-permute-done.18.refs_6_), channel_id=1, source_target_pairs={{0,1},{1,0},{2,3},{3,2},{4,5},{5,4},{6,7},{7,6},{8,9},{9,8},{10,11... | collective-permute-start | bytes 786440 | tf_op jit(solution)/shard_map/ppermute | solution.py:27
  128.5 11.2 %collective-permute-start.27 = (bf16[256,5120]{1,0:T(8,128)(2,1)S(1)}, bf16[256,5120]{1,0:T(8,128)(2,1)}, u32[]{:S(2)}, u32[]{:S(2)}) collective-permute-start(bf16[256,5120]{1,0:T(8,128)(2,1)S(1)} %copy-done), channel_id=1, source_target_pairs={{0,1},{1,0},{2,3},{3,2},{4,5},{5,4},{6,7},{7,6},{8,9},{9,8},{10,11... | collective-permute-start | bytes 7864328 | tf_op jit(solution)/shard_map/ppermute | solution.py:27
  130.6 6.3 %collective-permute-start.29 = (bf16[512,128]{1,0:T(8,128)(2,1)S(1)}, bf16[512,128]{1,0:T(8,128)(2,1)S(1)}, u32[]{:S(2)}, u32[]{:S(2)}) collective-permute-start(bf16[512,128]{1,0:T(8,128)(2,1)S(1)} %get-tuple-element.72), channel_id=1, source_target_pairs={{0,32},{16,48},{32,0},{48,16},{1,33},{17,49},{33,1},{49,17},{2,34}... | collective-permute-start | bytes 393224 | tf_op jit(solution)/shard_map/ppermute | solution.py:27
  130.6 9.2 %collective-permute-start.30 = (bf16[512,128]{1,0:T(8,128)(2,1)S(1)}, bf16[512,128]{1,0:T(8,128)(2,1)S(1)}, u32[]{:S(2)}, u32[]{:S(2)}) collective-permute-start(bf16[512,128]{1,0:T(8,128)(2,1)S(1)} %get-tuple-element.73), channel_id=1, source_target_pairs={{0,16},{16,32},{32,48},{48,0},{1,17},{17,33},{33,49},{49,1},{2,18}... | collective-permute-start | bytes 393224 | tf_op jit(solution)/shard_map/ppermute | solution.py:27
  142.5 8.7 %collective-permute-start.31 = (bf16[512,256]{1,0:T(8,128)(2,1)S(1)}, bf16[512,256]{1,0:T(8,128)(2,1)S(1)}, u32[]{:S(2)}, u32[]{:S(2)}) collective-permute-start(bf16[512,256]{1,0:T(8,128)(2,1)S(1)} %get-tuple-element.74), channel_id=1, source_target_pairs={{0,8},{8,0},{1,9},{9,1},{2,10},{10,2},{3,11},{11,3},{4,12},{12,4},... | collective-permute-start | bytes 786440 | tf_op jit(solution)/shard_map/ppermute | solution.py:27
  143.9 8.0 %collective-permute-start.32 = (bf16[512,256]{1,0:T(8,128)(2,1)S(1)}, bf16[512,256]{1,0:T(8,128)(2,1)S(1)}, u32[]{:S(2)}, u32[]{:S(2)}) collective-permute-start(bf16[512,256]{1,0:T(8,128)(2,1)S(1)} %get-tuple-element.75), channel_id=1, source_target_pairs={{0,2},{2,4},{4,6},{6,0},{1,3},{3,5},{5,7},{7,1},{8,10},{10,12},{12... | collective-permute-start | bytes 786440 | tf_op jit(solution)/shard_map/ppermute | solution.py:27
  143.9 7.3 %collective-permute-start.33 = (bf16[512,128]{1,0:T(8,128)(2,1)S(1)}, bf16[512,128]{1,0:T(8,128)(2,1)S(1)}, u32[]{:S(2)}, u32[]{:S(2)}) collective-permute-start(bf16[512,128]{1,0:T(8,128)(2,1)S(1)} %get-tuple-element.76), channel_id=1, source_target_pairs={{0,6},{2,0},{4,2},{6,4},{1,7},{3,1},{5,3},{7,5},{8,14},{10,8},{12,... | collective-permute-start | bytes 393224 | tf_op jit(solution)/shard_map/ppermute | solution.py:27
  152.1 14.3 %collective-permute-start.34 = (bf16[512,640]{1,0:T(8,128)(2,1)S(1)}, bf16[512,640]{1,0:T(8,128)(2,1)S(1)}, u32[]{:S(2)}, u32[]{:S(2)}) collective-permute-start(bf16[512,640]{1,0:T(8,128)(2,1)S(1)} %get-tuple-element.86), channel_id=1, source_target_pairs={{0,6},{2,0},{4,2},{6,4},{1,7},{3,1},{5,3},{7,5},{8,14},{10,8},{12,... | collective-permute-start | bytes 1966088 | tf_op jit(solution)/shard_map/ppermute | solution.py:27
  152.2 14.3 %collective-permute-start.35 = (bf16[512,640]{1,0:T(8,128)(2,1)S(1)}, bf16[512,640]{1,0:T(8,128)(2,1)S(1)}, u32[]{:S(2)}, u32[]{:S(2)}) collective-permute-start(bf16[512,640]{1,0:T(8,128)(2,1)S(1)} %get-tuple-element.87), channel_id=1, source_target_pairs={{0,8},{8,0},{1,9},{9,1},{2,10},{10,2},{3,11},{11,3},{4,12},{12,4},... | collective-permute-start | bytes 1966088 | tf_op jit(solution)/shard_map/ppermute | solution.py:27
  152.9 14.9 %collective-permute-start.36 = (bf16[512,640]{1,0:T(8,128)(2,1)S(1)}, bf16[512,640]{1,0:T(8,128)(2,1)S(1)}, u32[]{:S(2)}, u32[]{:S(2)}) collective-permute-start(bf16[512,640]{1,0:T(8,128)(2,1)S(1)} %get-tuple-element.89), channel_id=1, source_target_pairs={{0,2},{2,4},{4,6},{6,0},{1,3},{3,5},{5,7},{7,1},{8,10},{10,12},{12... | collective-permute-start | bytes 1966088 | tf_op jit(solution)/shard_map/ppermute | solution.py:27
  160.1 21.8 %collective-permute-start.38 = (bf16[512,640]{1,0:T(8,128)(2,1)}, bf16[512,640]{1,0:T(8,128)(2,1)S(1)}, u32[]{:S(2)}, u32[]{:S(2)}) collective-permute-start(bf16[512,640]{1,0:T(8,128)(2,1)} %get-tuple-element.91), channel_id=1, source_target_pairs={{0,2},{2,4},{4,6},{6,0},{1,3},{3,5},{5,7},{7,1},{8,10},{10,12},{12... | collective-permute-start | bytes 1966088 | tf_op jit(solution)/shard_map/ppermute | solution.py:27
  168.3 13.6 %collective-permute-start.37 = (bf16[512,640]{1,0:T(8,128)(2,1)S(1)}, bf16[512,640]{1,0:T(8,128)(2,1)S(1)}, u32[]{:S(2)}, u32[]{:S(2)}) collective-permute-start(bf16[512,640]{1,0:T(8,128)(2,1)S(1)} %get-tuple-element.90), channel_id=1, source_target_pairs={{0,6},{2,0},{4,2},{6,4},{1,7},{3,1},{5,3},{7,5},{8,14},{10,8},{12,... | collective-permute-start | bytes 1966088 | tf_op jit(solution)/shard_map/ppermute | solution.py:27
  168.3 13.6 %collective-permute-start.39 = (bf16[512,640]{1,0:T(8,128)(2,1)S(1)}, bf16[512,640]{1,0:T(8,128)(2,1)S(1)}, u32[]{:S(2)}, u32[]{:S(2)}) collective-permute-start(bf16[512,640]{1,0:T(8,128)(2,1)S(1)} %get-tuple-element.92), channel_id=1, source_target_pairs={{0,8},{8,0},{1,9},{9,1},{2,10},{10,2},{3,11},{11,3},{4,12},{12,4},... | collective-permute-start | bytes 1966088 | tf_op jit(solution)/shard_map/ppermute | solution.py:27
  (24 other events, 251.4 us)

commit v11 on v10

--- a/solution.py
+++ b/solution.py
@@ -16,6 +16,7 @@
 HEAD = ("yl", "z", "core")
 MIB = 1 << 20
 PAIRS = 12
+FIT = 192
 CUTS = ((0, 256), (256, 512), (512, 640))
 
 
@@ -251,14 +252,25 @@
             sums[row] += summed
         return 0
 
-    for index in range(len(outs)):
-        low, high = first[index * per_piece], first[(index + 1) * per_piece]
+    whole = first[rows] <= FIT
+    size = jnp.where(whole, rows, per_piece)
+
+    def segment(index, _):
+        begin = index * size
+        low, high = first[begin], first[begin + size]
         steps = (high - low + unroll - 1) // unroll
         lax.fori_loop(0, steps, functools.partial(rate, low, high), 0)
-        for row in range(index * per_piece, (index + 1) * per_piece):
+
+        def settle(row, _):
             top = jnp.max(tops[row], axis=0, keepdims=True) * factor
             tops[row] = jnp.broadcast_to(top, tops.shape[1:])
+            return 0
+
+        lax.fori_loop(begin, begin + size, settle, 0)
         lax.fori_loop(0, steps, functools.partial(gather, low, high), 0)
+        return 0
+
+    lax.fori_loop(0, jnp.where(whole, 1, len(outs)), segment, 0)
 
     for index, out in enumerate(outs):
         for part in range(per_piece):
@@ -296,13 +308,13 @@
             pltpu.VMEM((pieces, 2 * BLK, count), jnp.bfloat16),
             pltpu.VMEM((asking, *shape), jnp.bfloat16),
             pltpu.VMEM((rows, BLK, BLK), jnp.bfloat16),
-            pltpu.VMEM((rows * most // 2 // asking + PAIRS, 2 * BLK, BLK), jnp.float32),
+            pltpu.VMEM((max(rows * most // 2 // asking, FIT) + PAIRS, 2 * BLK, BLK), jnp.float32),
             pltpu.VMEM((rows, 8, BLK), jnp.float32),
             pltpu.VMEM((rows, 8, BLK), jnp.float32),
             pltpu.VMEM((rows, BLK, BLK), jnp.float32),
             pltpu.SemaphoreType.DMA((len(plan),)),
         ],
-        compiler_params=pltpu.CompilerParams(vmem_limit_bytes=32 * MIB),
+        compiler_params=pltpu.CompilerParams(vmem_limit_bytes=42 * MIB),
         cost_estimate=pl.CostEstimate(
             flops=rows * BLK * most * BLK * BLK,
             bytes_accessed=4 * most * BLK * BLK,

time: 190 us -> 189 us (level)
  no operation moved by 1% of the time
where the time goes in v11:
time: 189 us; the launch traced here: 188 us
  waiting for transfers between devices  77 us (41%)
  starting transfers between devices  56.5 us (30%)
  Pallas kernels  45.4 us (24%)
  local copies, waits for them, and re-layouts  4.49 us (2%)
  other arithmetic  3.83 us (2%)
    ppermute x41, waiting for transfers between devices, shift(): lax.ppermute(value, axis, [(i, (i + steps) % count) for i in range(count)])  77 us
    ppermute x41, starting transfers between devices, shift(): lax.ppermute(value, axis, [(i, (i + steps) % count) for i in range(count)])  56.5 us
    pallas_call x1, Pallas kernels, project(): pl.pallas_call(project_kernel, in_specs=[pl.BlockSpec(memory_space=pltpu....  18.6 us
    pallas_call x3, Pallas kernels, leave(): pl.pallas_call(kernel, grid_spec=pltpu.PrefetchScalarGridSpec(num_scalar_...  13.5 us
    pallas_call x1, Pallas kernels, attend(): pl.pallas_call(kernel, in_specs=[pl.BlockSpec(memory_space=pltpu.SMEM)] *...  11.9 us
  transfers between devices with their start and end apart: 41, of which 21 were waited for; matrix products, arithmetic and copies ran while one was open for 2% of the time, Pallas kernels for 6%

profile of v11, /device:TPU:1, one launch (start us, length us, event | category | flops | bytes accessed | tf_op | source)
XLA Modules:
  0.0 187.6 jit_solution(10609807668176127493)
XLA Ops:
  1.1 1.5 collective-permute-start.4
  4.6 1.7 collective-permute-start.5
  6.4 2.1 %collective-permute-start.6 = (bf16[512,640]{1,0:T(8,128)(2,1)S(1)}, bf16[512,640]{1,0:T(8,128)(2,1)S(1)}, u32[]{:S(2)}, u32[]{:S(2)}) collective-permute-start(bf16[512,640]{1,0:T(8,128)(2,1)S(1)} %lay.1.refs_0_), channel_id=1, source_target_pairs={{0,6},{2,0},{4,2},{6,4},{1,7},{3,1},{5,3},{7,5},{8,14},{10,8},{12,... | collective-permute-start | bytes 1966088 | tf_op jit(solution)/shard_map/ppermute | solution.py:28
  9.8 13.8 %collective-permute-done.5.refs_1_ = bf16[512,640]{1,0:T(8,128)(2,1)} collective-permute-done((bf16[512,640]{1,0:T(8,128)(2,1)S(1)}, bf16[512,640]{1,0:T(8,128)(2,1)}, u32[]{:S(2)}, u32[]{:S(2)}) %collective-permute-start.5) | collective-permute-done | bytes 655392 | tf_op jit(solution)/shard_map/ppermute | solution.py:28
  25.8 2.7 %collective-permute-start.10 = (bf16[512,640]{1,0:T(8,128)(2,1)}, bf16[512,640]{1,0:T(8,128)(2,1)S(1)}, u32[]{:S(2)}, u32[]{:S(2)}) collective-permute-start(bf16[512,640]{1,0:T(8,128)(2,1)} %collective-permute-done.7.refs_3_), channel_id=1, source_target_pairs={{0,6},{2,0},{4,2},{6,4},{1,7},{3,1},{5,3},{7,5},{8,14},{10,8},{12,... | collective-permute-start | bytes 1966088 | tf_op jit(solution)/shard_map/ppermute | solution.py:28
  28.5 2.5 %collective-permute-start.3 = (s32[4,64]{1,0:T(4,128)S(1)}, s32[4,64]{1,0:T(4,128)S(1)}, u32[]{:S(2)}, u32[]{:S(2)}) collective-permute-start(s32[4,64]{1,0:T(4,128)S(1)} %get-tuple-element.102), channel_id=1, source_target_pairs={{0,48},{16,0},{32,16},{48,32},{1,49},{17,1},{33,17},{49,33},{2,50}... | collective-permute-start | bytes 3080 | tf_op jit(solution)/shard_map/ppermute | solution.py:28
  31.7 2.3 %collective-permute-start.2 = (s32[4,64]{1,0:T(4,128)S(1)}, s32[4,64]{1,0:T(4,128)S(1)}, u32[]{:S(2)}, u32[]{:S(2)}) collective-permute-start(s32[4,64]{1,0:T(4,128)S(1)} %get-tuple-element.101), channel_id=1, source_target_pairs={{0,32},{16,48},{32,0},{48,16},{1,33},{17,49},{33,1},{49,17},{2,34}... | collective-permute-start | bytes 3080 | tf_op jit(solution)/shard_map/ppermute | solution.py:28
  34.0 1.7 collective-permute-done.2
  36.8 3.3 %collective-permute-done.1 = s32[4,64]{1,0:T(4,128)S(1)} collective-permute-done((s32[4,64]{1,0:T(4,128)S(1)}, s32[4,64]{1,0:T(4,128)S(1)}, u32[]{:S(2)}, u32[]{:S(2)}) %collective-permute-start.1) | collective-permute-done | bytes 1056 | tf_op jit(solution)/shard_map/ppermute | solution.py:28
  42.3 2.3 %collective-permute-start.12 = (bf16[512,256]{1,0:T(8,128)(2,1)S(1)}, bf16[512,256]{1,0:T(8,128)(2,1)}, u32[]{:S(2)}, u32[]{:S(2)}) collective-permute-start(bf16[512,256]{1,0:T(8,128)(2,1)S(1)} %slice.28), channel_id=1, source_target_pairs={{0,6},{2,0},{4,2},{6,4},{1,7},{3,1},{5,3},{7,5},{8,14},{10,8},{12,... | collective-permute-start | bytes 786440 | tf_op jit(solution)/shard_map/ppermute | solution.py:28
  46.2 3.8 %collective-permute-done.13.refs_9_ = bf16[512,128]{1,0:T(8,128)(2,1)S(1)} collective-permute-done((bf16[512,128]{1,0:T(8,128)(2,1)S(1)}, bf16[512,128]{1,0:T(8,128)(2,1)S(1)}, u32[]{:S(2)}, u32[]{:S(2)}) %collective-permute-start.13) | collective-permute-done | bytes 131104 | tf_op jit(solution)/shard_map/ppermute | solution.py:28
  50.6 18.6 %project.1 = (bf16[256,512]{1,0:T(8,128)(2,1)}, bf16[128,512]{1,0:T(8,128)(2,1)}, bf16[256,512]{1,0:T(8,128)(2,1)}, bf16[128,512]{1,0:T(8,128)(2,1)}, bf16[384,5...) custom-call(s32[8]{0:T(128)} %stack.97.chips, s32[4]{0:T(128)} %pad_add_fusion.2.heads, bf16[512,640]{1,0:T(8,128)(2,1)} %copy-done.1, ...), custom_call_target="tpu_custom_call" | custom-call | flops 8053063680 | bytes 20971520 | tf_op jit(solution)/shard_map/project/pallas_call | solution.py:149
  70.6 1.5 collective-permute-start.16
  72.0 3.0 %collective-permute-start.17 = (bf16[256,512]{1,0:T(8,128)(2,1)}, bf16[256,512]{1,0:T(8,128)(2,1)S(1)}, u32[]{:S(2)}, u32[]{:S(2)}) collective-permute-start(bf16[256,512]{1,0:T(8,128)(2,1)} %get-tuple-element.65.refs_4_), channel_id=1, source_target_pairs={{0,64},{64,0},{1,65},{65,1},{2,66},{66,2},{3,67},{67,3},{4,68},{68... | collective-permute-start | bytes 786440 | tf_op jit(solution)/shard_map/ppermute | solution.py:28
  75.7 3.4 %collective-permute-done.17.refs_7_ = bf16[256,512]{1,0:T(8,128)(2,1)S(1)} collective-permute-done((bf16[256,512]{1,0:T(8,128)(2,1)}, bf16[256,512]{1,0:T(8,128)(2,1)S(1)}, u32[]{:S(2)}, u32[]{:S(2)}) %collective-permute-start.17) | collective-permute-done | bytes 262176 | tf_op jit(solution)/shard_map/ppermute | solution.py:28
  79.2 3.3 %collective-permute-start.19 = (bf16[512,512]{1,0:T(8,128)(2,1)S(1)}, bf16[512,512]{1,0:T(8,128)(2,1)S(1)}, u32[]{:S(2)}, u32[]{:S(2)}) collective-permute-start(bf16[512,512]{1,0:T(8,128)(2,1)S(1)} %pad_maximum_fusion.1.refs_5_), channel_id=1, source_target_pairs={{0,64},{64,0},{1,65},{65,1},{2,66},{66,2},{3,67},{67,3},{4,68},{68... | collective-permute-start | bytes 1572872 | tf_op jit(solution)/shard_map/ppermute | solution.py:28
  82.8 7.3 %collective-permute-start.21 = (bf16[256,512]{1,0:T(8,128)(2,1)S(1)}, bf16[256,512]{1,0:T(8,128)(2,1)S(1)}, u32[]{:S(2)}, u32[]{:S(2)}) collective-permute-start(bf16[256,512]{1,0:T(8,128)(2,1)S(1)} %collective-permute-done.17.refs_7_), channel_id=1, source_target_pairs={{0,1},{1,0},{2,3},{3,2},{4,5},{5,4},{6,7},{7,6},{8,9},{9,8},{10,11... | collective-permute-start | bytes 786440 | tf_op jit(solution)/shard_map/ppermute | solution.py:28
  90.1 1.9 collective-permute-start.18
  93.7 8.6 %collective-permute-done.20.refs_17_ = bf16[128,512]{1,0:T(8,128)(2,1)S(1)} collective-permute-done((bf16[128,512]{1,0:T(8,128)(2,1)S(1)}, bf16[128,512]{1,0:T(8,128)(2,1)S(1)}, u32[]{:S(2)}, u32[]{:S(2)}) %collective-permute-start.20) | collective-permute-done | bytes 131104 | tf_op jit(solution)/shard_map/ppermute | solution.py:28
  103.9 8.7 %collective-permute-done.22.refs_9_ = bf16[256,512]{1,0:T(8,128)(2,1)S(1)} collective-permute-done((bf16[256,512]{1,0:T(8,128)(2,1)S(1)}, bf16[256,512]{1,0:T(8,128)(2,1)S(1)}, u32[]{:S(2)}, u32[]{:S(2)}) %collective-permute-start.22) | collective-permute-done | bytes 262176 | tf_op jit(solution)/shard_map/ppermute | solution.py:28
  114.7 11.9 %attend.1 = (bf16[512,128]{1,0:T(8,128)(2,1)S(1)}, bf16[512,128]{1,0:T(8,128)(2,1)S(1)}, bf16[512,128]{1,0:T(8,128)(2,1)S(1)}, bf16[512,128]{1,0:T(8,128)(2,1)S(1)}) custom-call(s32[16,64]{1,0:T(8,128)S(1)} %select_reduce_fusion.2.refs_0_, s32[16]{0:T(128)S(1)} %get-tuple-element.93.refs_1_, s32[17]{0:T(128)S(1)} %select_reduce_fusion.5.refs_2_, ...), custom_call_target="tpu_custom_call" | custom-call | flops 2147483648 | bytes 4194304 | tf_op jit(solution)/shard_map/attend/pallas_call | solution.py:301
  127.1 1.6 collective-permute-start.28
  129.3 2.9 %collective-permute-done.28.refs_5_ = bf16[512,128]{1,0:T(8,128)(2,1)S(1)} collective-permute-done((bf16[512,128]{1,0:T(8,128)(2,1)S(1)}, bf16[512,128]{1,0:T(8,128)(2,1)S(1)}, u32[]{:S(2)}, u32[]{:S(2)}) %collective-permute-start.28) | collective-permute-done | bytes 131104 | tf_op jit(solution)/shard_map/ppermute | solution.py:28
  132.2 2.8 %collective-permute-done.29.refs_6_ = bf16[512,128]{1,0:T(8,128)(2,1)S(1)} collective-permute-done((bf16[512,128]{1,0:T(8,128)(2,1)S(1)}, bf16[512,128]{1,0:T(8,128)(2,1)S(1)}, u32[]{:S(2)}, u32[]{:S(2)}) %collective-permute-start.29) | collective-permute-done | bytes 131104 | tf_op jit(solution)/shard_map/ppermute | solution.py:28
  135.0 2.9 %collective-permute-done.30.refs_7_ = bf16[512,128]{1,0:T(8,128)(2,1)S(1)} collective-permute-done((bf16[512,128]{1,0:T(8,128)(2,1)S(1)}, bf16[512,128]{1,0:T(8,128)(2,1)S(1)}, u32[]{:S(2)}, u32[]{:S(2)}) %collective-permute-start.30) | collective-permute-done | bytes 131104 | tf_op jit(solution)/shard_map/ppermute | solution.py:28
  137.9 2.8 %leave.3 = (bf16[512,256]{1,0:T(8,128)(2,1)S(1)}, bf16[512,256]{1,0:T(8,128)(2,1)S(1)}, bf16[512,128]{1,0:T(8,128)(2,1)S(1)}) custom-call(s32[1]{0:T(128)} %bitcast.18.refs_0_, s32[4]{0:T(128)S(1)} %pad_add_fusion.1.refs_1_, bf16[256,5120]{1,0:T(8,128)(2,1)S(1)} %copy-done, bf16[256,5120]{1,0:T(8,128)(2,1)} %collective-permute-done.27.refs_3_, ...), custom_call_target="tpu_custom_call" | custom-call | flops 335544320 | bytes 1310720 | tf_op jit(solution)/shard_map/leave/pallas_call | solution.py:367
  141.3 2.7 %collective-permute-start.33 = (bf16[512,128]{1,0:T(8,128)(2,1)S(1)}, bf16[512,128]{1,0:T(8,128)(2,1)S(1)}, u32[]{:S(2)}, u32[]{:S(2)}) collective-permute-start(bf16[512,128]{1,0:T(8,128)(2,1)S(1)} %get-tuple-element.76), channel_id=1, source_target_pairs={{0,6},{2,0},{4,2},{6,4},{1,7},{3,1},{5,3},{7,5},{8,14},{10,8},{12,... | collective-permute-start | bytes 393224 | tf_op jit(solution)/shard_map/ppermute | solution.py:28
  144.1 4.6 %leave.5 = (bf16[512,640]{1,0:T(8,128)(2,1)S(1)}, bf16[512,640]{1,0:T(8,128)(2,1)S(1)}, bf16[512,640]{1,0:T(8,128)(2,1)S(1)}) custom-call(s32[3]{0:T(128)S(1)} %pad_add_fusion.3.refs_0_, s32[4]{0:T(128)S(1)} %pad_add_fusion.1.refs_1_, bf16[256,5120]{1,0:T(8,128)(2,1)S(1)} %copy-done, bf16[256,5120]{1,0:T(8,128)(2,1)} %collective-permute-done.27.refs_3_, ...), custom_call_target="tpu_custom_call" | custom-call | flops 1006632960 | bytes 3932160 | tf_op jit(solution)/shard_map/leave/pallas_call | solution.py:367
  152.1 6.2 %leave.4 = (bf16[512,640]{1,0:T(8,128)(2,1)S(1)}, bf16[512,640]{1,0:T(8,128)(2,1)}, bf16[512,640]{1,0:T(8,128)(2,1)S(1)}, bf16[512,640]{1,0:T(8,128)(2,1)S(1)}) custom-call(s32[4]{0:T(128)S(1)} %pad_add_fusion.refs_0_, s32[4]{0:T(128)S(1)} %pad_add_fusion.1.refs_1_, bf16[256,5120]{1,0:T(8,128)(2,1)S(1)} %copy-done, ...), custom_call_target="tpu_custom_call" | custom-call | flops 1342177280 | bytes 5242880 | tf_op jit(solution)/shard_map/leave/pallas_call | solution.py:367
  158.3 6.2 %collective-permute-done.34.refs_1_ = bf16[512,640]{1,0:T(8,128)(2,1)S(1)} collective-permute-done((bf16[512,640]{1,0:T(8,128)(2,1)S(1)}, bf16[512,640]{1,0:T(8,128)(2,1)S(1)}, u32[]{:S(2)}, u32[]{:S(2)}) %collective-permute-start.34) | collective-permute-done | bytes 655392 | tf_op jit(solution)/shard_map/ppermute | solution.py:28
  167.5 12.0 %collective-permute-done.38.refs_2_ = bf16[512,640]{1,0:T(8,128)(2,1)S(1)} collective-permute-done((bf16[512,640]{1,0:T(8,128)(2,1)}, bf16[512,640]{1,0:T(8,128)(2,1)S(1)}, u32[]{:S(2)}, u32[]{:S(2)}) %collective-permute-start.38) | collective-permute-done | bytes 655392 | tf_op jit(solution)/shard_map/ppermute | solution.py:28
  181.0 4.0 %collective-permute-start.40 = (bf16[320,512]{1,0:T(8,128)(2,1)S(1)}, bf16[320,512]{1,0:T(8,128)(2,1)S(1)}, u32[]{:S(2)}, u32[]{:S(2)}) collective-permute-start(bf16[320,512]{1,0:T(8,128)(2,1)S(1)} %constant_dynamic-slice_fusion), channel_id=1, source_target_pairs={{0,1},{1,0},{2,3},{3,2},{4,5},{5,4},{6,7},{7,6},{8,9},{9,8},{10,11... | collective-permute-start | bytes 983048 | tf_op jit(solution)/shard_map/ppermute | solution.py:28
  (121 shorter events, 32.9 us)
Async XLA Ops:
  4.2 45.8 %collective-permute-start.14 = (bf16[3,5120,256]{2,1,0:T(8,128)(2,1)}, bf16[3,5120,256]{2,1,0:T(8,128)(2,1)}, u32[]{:S(2)}, u32[]{:S(2)}) collective-permute-start(bf16[3,5120,256]{2,1,0:T(8,128)(2,1)} %refs_10_.1), channel_id=1, source_target_pairs={{0,1},{1,0},{2,3},{3,2},{4,5},{5,4},{6,7},{7,6},{8,9},{9,8},{10,11... | collective-permute-start | bytes 23592968 | tf_op jit(solution)/shard_map/ppermute | solution.py:28
  4.6 18.9 %collective-permute-start.5 = (bf16[512,640]{1,0:T(8,128)(2,1)S(1)}, bf16[512,640]{1,0:T(8,128)(2,1)}, u32[]{:S(2)}, u32[]{:S(2)}) collective-permute-start(bf16[512,640]{1,0:T(8,128)(2,1)S(1)} %lay.1.refs_0_), channel_id=1, source_target_pairs={{0,2},{2,4},{4,6},{6,0},{1,3},{3,5},{5,7},{7,1},{8,10},{10,12},{12... | collective-permute-start | bytes 1966088 | tf_op jit(solution)/shard_map/ppermute | solution.py:28
  6.4 17.2 %collective-permute-start.6 = (bf16[512,640]{1,0:T(8,128)(2,1)S(1)}, bf16[512,640]{1,0:T(8,128)(2,1)S(1)}, u32[]{:S(2)}, u32[]{:S(2)}) collective-permute-start(bf16[512,640]{1,0:T(8,128)(2,1)S(1)} %lay.1.refs_0_), channel_id=1, source_target_pairs={{0,6},{2,0},{4,2},{6,4},{1,7},{3,1},{5,3},{7,5},{8,14},{10,8},{12,... | collective-permute-start | bytes 1966088 | tf_op jit(solution)/shard_map/ppermute | solution.py:28
  8.5 16.0 %collective-permute-start.7 = (bf16[512,640]{1,0:T(8,128)(2,1)S(1)}, bf16[512,640]{1,0:T(8,128)(2,1)}, u32[]{:S(2)}, u32[]{:S(2)}) collective-permute-start(bf16[512,640]{1,0:T(8,128)(2,1)S(1)} %lay.1.refs_0_), channel_id=1, source_target_pairs={{0,8},{8,0},{1,9},{9,1},{2,10},{10,2},{3,11},{11,3},{4,12},{12,4},... | collective-permute-start | bytes 1966088 | tf_op jit(solution)/shard_map/ppermute | solution.py:28
  24.4 16.4 %collective-permute-start.8 = (bf16[512,640]{1,0:T(8,128)(2,1)}, bf16[512,640]{1,0:T(8,128)(2,1)S(1)}, u32[]{:S(2)}, u32[]{:S(2)}) collective-permute-start(bf16[512,640]{1,0:T(8,128)(2,1)} %collective-permute-done.5.refs_1_), channel_id=1, source_target_pairs={{0,2},{2,4},{4,6},{6,0},{1,3},{3,5},{5,7},{7,1},{8,10},{10,12},{12... | collective-permute-start | bytes 1966088 | tf_op jit(solution)/shard_map/ppermute | solution.py:28
  24.5 16.4 %collective-permute-start.9 = (bf16[512,640]{1,0:T(8,128)(2,1)}, bf16[512,640]{1,0:T(8,128)(2,1)S(1)}, u32[]{:S(2)}, u32[]{:S(2)}) collective-permute-start(bf16[512,640]{1,0:T(8,128)(2,1)} %collective-permute-done.5.refs_1_), channel_id=1, source_target_pairs={{0,8},{8,0},{1,9},{9,1},{2,10},{10,2},{3,11},{11,3},{4,12},{12,4},... | collective-permute-start | bytes 1966088 | tf_op jit(solution)/shard_map/ppermute | solution.py:28
  25.8 15.2 %collective-permute-start.10 = (bf16[512,640]{1,0:T(8,128)(2,1)}, bf16[512,640]{1,0:T(8,128)(2,1)S(1)}, u32[]{:S(2)}, u32[]{:S(2)}) collective-permute-start(bf16[512,640]{1,0:T(8,128)(2,1)} %collective-permute-done.7.refs_3_), channel_id=1, source_target_pairs={{0,6},{2,0},{4,2},{6,4},{1,7},{3,1},{5,3},{7,5},{8,14},{10,8},{12,... | collective-permute-start | bytes 1966088 | tf_op jit(solution)/shard_map/ppermute | solution.py:28
  40.9 9.0 %collective-permute-start.11 = (bf16[512,256]{1,0:T(8,128)(2,1)S(1)}, bf16[512,256]{1,0:T(8,128)(2,1)}, u32[]{:S(2)}, u32[]{:S(2)}) collective-permute-start(bf16[512,256]{1,0:T(8,128)(2,1)S(1)} %slice.27), channel_id=1, source_target_pairs={{0,8},{8,0},{1,9},{9,1},{2,10},{10,2},{3,11},{11,3},{4,12},{12,4},... | collective-permute-start | bytes 786440 | tf_op jit(solution)/shard_map/ppermute | solution.py:28
  42.3 7.7 %collective-permute-start.12 = (bf16[512,256]{1,0:T(8,128)(2,1)S(1)}, bf16[512,256]{1,0:T(8,128)(2,1)}, u32[]{:S(2)}, u32[]{:S(2)}) collective-permute-start(bf16[512,256]{1,0:T(8,128)(2,1)S(1)} %slice.28), channel_id=1, source_target_pairs={{0,6},{2,0},{4,2},{6,4},{1,7},{3,1},{5,3},{7,5},{8,14},{10,8},{12,... | collective-permute-start | bytes 786440 | tf_op jit(solution)/shard_map/ppermute | solution.py:28
  69.3 9.8 %collective-permute-start.15 = (bf16[384,512]{1,0:T(8,128)(2,1)}, bf16[384,512]{1,0:T(8,128)(2,1)S(1)}, u32[]{:S(2)}, u32[]{:S(2)}) collective-permute-start(bf16[384,512]{1,0:T(8,128)(2,1)} %get-tuple-element.58), channel_id=1, source_target_pairs={{0,16},{16,32},{32,48},{48,0},{1,17},{17,33},{33,49},{49,1},{2,18}... | collective-permute-start | bytes 1179656 | tf_op jit(solution)/shard_map/ppermute | solution.py:28
  70.6 8.5 %collective-permute-start.16 = (bf16[384,512]{1,0:T(8,128)(2,1)}, bf16[384,512]{1,0:T(8,128)(2,1)S(1)}, u32[]{:S(2)}, u32[]{:S(2)}) collective-permute-start(bf16[384,512]{1,0:T(8,128)(2,1)} %get-tuple-element.59), channel_id=1, source_target_pairs={{0,48},{16,0},{32,16},{48,32},{1,49},{17,1},{33,17},{49,33},{2,50}... | collective-permute-start | bytes 1179656 | tf_op jit(solution)/shard_map/ppermute | solution.py:28
  72.0 7.0 %collective-permute-start.17 = (bf16[256,512]{1,0:T(8,128)(2,1)}, bf16[256,512]{1,0:T(8,128)(2,1)S(1)}, u32[]{:S(2)}, u32[]{:S(2)}) collective-permute-start(bf16[256,512]{1,0:T(8,128)(2,1)} %get-tuple-element.65.refs_4_), channel_id=1, source_target_pairs={{0,64},{64,0},{1,65},{65,1},{2,66},{66,2},{3,67},{67,3},{4,68},{68... | collective-permute-start | bytes 786440 | tf_op jit(solution)/shard_map/ppermute | solution.py:28
  79.2 23.1 %collective-permute-start.19 = (bf16[512,512]{1,0:T(8,128)(2,1)S(1)}, bf16[512,512]{1,0:T(8,128)(2,1)S(1)}, u32[]{:S(2)}, u32[]{:S(2)}) collective-permute-start(bf16[512,512]{1,0:T(8,128)(2,1)S(1)} %pad_maximum_fusion.1.refs_5_), channel_id=1, source_target_pairs={{0,64},{64,0},{1,65},{65,1},{2,66},{66,2},{3,67},{67,3},{4,68},{68... | collective-permute-start | bytes 1572872 | tf_op jit(solution)/shard_map/ppermute | solution.py:28
  82.8 19.5 %collective-permute-start.21 = (bf16[256,512]{1,0:T(8,128)(2,1)S(1)}, bf16[256,512]{1,0:T(8,128)(2,1)S(1)}, u32[]{:S(2)}, u32[]{:S(2)}) collective-permute-start(bf16[256,512]{1,0:T(8,128)(2,1)S(1)} %collective-permute-done.17.refs_7_), channel_id=1, source_target_pairs={{0,1},{1,0},{2,3},{3,2},{4,5},{5,4},{6,7},{7,6},{8,9},{9,8},{10,11... | collective-permute-start | bytes 786440 | tf_op jit(solution)/shard_map/ppermute | solution.py:28
  90.1 12.2 %collective-permute-start.18 = (bf16[256,512]{1,0:T(8,128)(2,1)S(1)}, bf16[256,512]{1,0:T(8,128)(2,1)S(1)}, u32[]{:S(2)}, u32[]{:S(2)}) collective-permute-start(bf16[256,512]{1,0:T(8,128)(2,1)S(1)} %copy-done.12), channel_id=1, source_target_pairs={{0,32},{16,48},{32,0},{48,16},{1,33},{17,49},{33,1},{49,17},{2,34}... | collective-permute-start | bytes 786440 | tf_op jit(solution)/shard_map/ppermute | solution.py:28
  92.1 10.1 %collective-permute-start.20 = (bf16[128,512]{1,0:T(8,128)(2,1)S(1)}, bf16[128,512]{1,0:T(8,128)(2,1)S(1)}, u32[]{:S(2)}, u32[]{:S(2)}) collective-permute-start(bf16[128,512]{1,0:T(8,128)(2,1)S(1)} %copy-done.14), channel_id=1, source_target_pairs={{0,32},{16,48},{32,0},{48,16},{1,33},{17,49},{33,1},{49,17},{2,34}... | collective-permute-start | bytes 393224 | tf_op jit(solution)/shard_map/ppermute | solution.py:28
  102.3 12.4 %collective-permute-start.23 = (bf16[768,512]{1,0:T(8,128)(2,1)S(1)}, bf16[768,512]{1,0:T(8,128)(2,1)S(1)}, u32[]{:S(2)}, u32[]{:S(2)}) collective-permute-start(bf16[768,512]{1,0:T(8,128)(2,1)S(1)} %pad_maximum_fusion), channel_id=1, source_target_pairs={{0,1},{1,0},{2,3},{3,2},{4,5},{5,4},{6,7},{7,6},{8,9},{9,8},{10,11... | collective-permute-start | bytes 2359304 | tf_op jit(solution)/shard_map/ppermute | solution.py:28
  103.3 9.4 %collective-permute-start.22 = (bf16[256,512]{1,0:T(8,128)(2,1)S(1)}, bf16[256,512]{1,0:T(8,128)(2,1)S(1)}, u32[]{:S(2)}, u32[]{:S(2)}) collective-permute-start(bf16[256,512]{1,0:T(8,128)(2,1)S(1)} %collective-permute-done.18.refs_6_), channel_id=1, source_target_pairs={{0,64},{64,0},{1,65},{65,1},{2,66},{66,2},{3,67},{67,3},{4,68},{68... | collective-permute-start | bytes 786440 | tf_op jit(solution)/shard_map/ppermute | solution.py:28
  103.4 10.1 %collective-permute-start.25 = (bf16[512,512]{1,0:T(8,128)(2,1)S(1)}, bf16[512,512]{1,0:T(8,128)(2,1)S(1)}, u32[]{:S(2)}, u32[]{:S(2)}) collective-permute-start(bf16[512,512]{1,0:T(8,128)(2,1)S(1)} %collective-permute-done.19.refs_8_), channel_id=1, source_target_pairs={{0,1},{1,0},{2,3},{3,2},{4,5},{5,4},{6,7},{7,6},{8,9},{9,8},{10,11... | collective-permute-start | bytes 1572872 | tf_op jit(solution)/shard_map/ppermute | solution.py:28
  103.8 9.8 %collective-permute-start.24 = (bf16[256,512]{1,0:T(8,128)(2,1)S(1)}, bf16[256,512]{1,0:T(8,128)(2,1)S(1)}, u32[]{:S(2)}, u32[]{:S(2)}) collective-permute-start(bf16[256,512]{1,0:T(8,128)(2,1)S(1)} %collective-permute-done.18.refs_6_), channel_id=1, source_target_pairs={{0,1},{1,0},{2,3},{3,2},{4,5},{5,4},{6,7},{7,6},{8,9},{9,8},{10,11... | collective-permute-start | bytes 786440 | tf_op jit(solution)/shard_map/ppermute | solution.py:28
  126.6 11.2 %collective-permute-start.27 = (bf16[256,5120]{1,0:T(8,128)(2,1)S(1)}, bf16[256,5120]{1,0:T(8,128)(2,1)}, u32[]{:S(2)}, u32[]{:S(2)}) collective-permute-start(bf16[256,5120]{1,0:T(8,128)(2,1)S(1)} %copy-done), channel_id=1, source_target_pairs={{0,1},{1,0},{2,3},{3,2},{4,5},{5,4},{6,7},{7,6},{8,9},{9,8},{10,11... | collective-permute-start | bytes 7864328 | tf_op jit(solution)/shard_map/ppermute | solution.py:28
  128.7 6.3 %collective-permute-start.29 = (bf16[512,128]{1,0:T(8,128)(2,1)S(1)}, bf16[512,128]{1,0:T(8,128)(2,1)S(1)}, u32[]{:S(2)}, u32[]{:S(2)}) collective-permute-start(bf16[512,128]{1,0:T(8,128)(2,1)S(1)} %get-tuple-element.72), channel_id=1, source_target_pairs={{0,32},{16,48},{32,0},{48,16},{1,33},{17,49},{33,1},{49,17},{2,34}... | collective-permute-start | bytes 393224 | tf_op jit(solution)/shard_map/ppermute | solution.py:28
  128.7 9.2 %collective-permute-start.30 = (bf16[512,128]{1,0:T(8,128)(2,1)S(1)}, bf16[512,128]{1,0:T(8,128)(2,1)S(1)}, u32[]{:S(2)}, u32[]{:S(2)}) collective-permute-start(bf16[512,128]{1,0:T(8,128)(2,1)S(1)} %get-tuple-element.73), channel_id=1, source_target_pairs={{0,16},{16,32},{32,48},{48,0},{1,17},{17,33},{33,49},{49,1},{2,18}... | collective-permute-start | bytes 393224 | tf_op jit(solution)/shard_map/ppermute | solution.py:28
  140.7 8.0 %collective-permute-start.31 = (bf16[512,256]{1,0:T(8,128)(2,1)S(1)}, bf16[512,256]{1,0:T(8,128)(2,1)S(1)}, u32[]{:S(2)}, u32[]{:S(2)}) collective-permute-start(bf16[512,256]{1,0:T(8,128)(2,1)S(1)} %get-tuple-element.74), channel_id=1, source_target_pairs={{0,8},{8,0},{1,9},{9,1},{2,10},{10,2},{3,11},{11,3},{4,12},{12,4},... | collective-permute-start | bytes 786440 | tf_op jit(solution)/shard_map/ppermute | solution.py:28
  141.3 8.3 %collective-permute-start.32 = (bf16[512,256]{1,0:T(8,128)(2,1)S(1)}, bf16[512,256]{1,0:T(8,128)(2,1)S(1)}, u32[]{:S(2)}, u32[]{:S(2)}) collective-permute-start(bf16[512,256]{1,0:T(8,128)(2,1)S(1)} %get-tuple-element.75), channel_id=1, source_target_pairs={{0,2},{2,4},{4,6},{6,0},{1,3},{3,5},{5,7},{7,1},{8,10},{10,12},{12... | collective-permute-start | bytes 786440 | tf_op jit(solution)/shard_map/ppermute | solution.py:28
  141.3 7.3 %collective-permute-start.33 = (bf16[512,128]{1,0:T(8,128)(2,1)S(1)}, bf16[512,128]{1,0:T(8,128)(2,1)S(1)}, u32[]{:S(2)}, u32[]{:S(2)}) collective-permute-start(bf16[512,128]{1,0:T(8,128)(2,1)S(1)} %get-tuple-element.76), channel_id=1, source_target_pairs={{0,6},{2,0},{4,2},{6,4},{1,7},{3,1},{5,3},{7,5},{8,14},{10,8},{12,... | collective-permute-start | bytes 393224 | tf_op jit(solution)/shard_map/ppermute | solution.py:28
  149.9 14.7 %collective-permute-start.34 = (bf16[512,640]{1,0:T(8,128)(2,1)S(1)}, bf16[512,640]{1,0:T(8,128)(2,1)S(1)}, u32[]{:S(2)}, u32[]{:S(2)}) collective-permute-start(bf16[512,640]{1,0:T(8,128)(2,1)S(1)} %get-tuple-element.86), channel_id=1, source_target_pairs={{0,6},{2,0},{4,2},{6,4},{1,7},{3,1},{5,3},{7,5},{8,14},{10,8},{12,... | collective-permute-start | bytes 1966088 | tf_op jit(solution)/shard_map/ppermute | solution.py:28
  150.0 14.6 %collective-permute-start.35 = (bf16[512,640]{1,0:T(8,128)(2,1)S(1)}, bf16[512,640]{1,0:T(8,128)(2,1)S(1)}, u32[]{:S(2)}, u32[]{:S(2)}) collective-permute-start(bf16[512,640]{1,0:T(8,128)(2,1)S(1)} %get-tuple-element.87), channel_id=1, source_target_pairs={{0,8},{8,0},{1,9},{9,1},{2,10},{10,2},{3,11},{11,3},{4,12},{12,4},... | collective-permute-start | bytes 1966088 | tf_op jit(solution)/shard_map/ppermute | solution.py:28
  150.6 14.8 %collective-permute-start.36 = (bf16[512,640]{1,0:T(8,128)(2,1)S(1)}, bf16[512,640]{1,0:T(8,128)(2,1)S(1)}, u32[]{:S(2)}, u32[]{:S(2)}) collective-permute-start(bf16[512,640]{1,0:T(8,128)(2,1)S(1)} %get-tuple-element.89), channel_id=1, source_target_pairs={{0,2},{2,4},{4,6},{6,0},{1,3},{3,5},{5,7},{7,1},{8,10},{10,12},{12... | collective-permute-start | bytes 1966088 | tf_op jit(solution)/shard_map/ppermute | solution.py:28
  158.2 21.2 %collective-permute-start.38 = (bf16[512,640]{1,0:T(8,128)(2,1)}, bf16[512,640]{1,0:T(8,128)(2,1)S(1)}, u32[]{:S(2)}, u32[]{:S(2)}) collective-permute-start(bf16[512,640]{1,0:T(8,128)(2,1)} %get-tuple-element.91), channel_id=1, source_target_pairs={{0,2},{2,4},{4,6},{6,0},{1,3},{3,5},{5,7},{7,1},{8,10},{10,12},{12... | collective-permute-start | bytes 1966088 | tf_op jit(solution)/shard_map/ppermute | solution.py:28
  165.8 13.6 %collective-permute-start.37 = (bf16[512,640]{1,0:T(8,128)(2,1)S(1)}, bf16[512,640]{1,0:T(8,128)(2,1)S(1)}, u32[]{:S(2)}, u32[]{:S(2)}) collective-permute-start(bf16[512,640]{1,0:T(8,128)(2,1)S(1)} %get-tuple-element.90), channel_id=1, source_target_pairs={{0,6},{2,0},{4,2},{6,4},{1,7},{3,1},{5,3},{7,5},{8,14},{10,8},{12,... | collective-permute-start | bytes 1966088 | tf_op jit(solution)/shard_map/ppermute | solution.py:28
  166.3 13.2 %collective-permute-start.39 = (bf16[512,640]{1,0:T(8,128)(2,1)S(1)}, bf16[512,640]{1,0:T(8,128)(2,1)S(1)}, u32[]{:S(2)}, u32[]{:S(2)}) collective-permute-start(bf16[512,640]{1,0:T(8,128)(2,1)S(1)} %get-tuple-element.92), channel_id=1, source_target_pairs={{0,8},{8,0},{1,9},{9,1},{2,10},{10,2},{3,11},{11,3},{4,12},{12,4},... | collective-permute-start | bytes 1966088 | tf_op jit(solution)/shard_map/ppermute | solution.py:28
  (24 other events, 249.5 us)

commit v12 on v11

--- a/solution.py
+++ b/solution.py
@@ -175,9 +175,8 @@
     arrays, outs, rest = refs[: -4 - 8], refs[-4 - 8 : -8], refs[-8:]
     kv, query, asked, scores, tops, totals, sums, arrived = rest
     copies = []
-    for kind, index, array, start in plan:
-        to = (kv if kind == "kv" else query).at[index]
-        rows = to.shape[0]
+    for kind, index, array, start, rows in plan:
+        to = kv.at[index * 2 * BLK : index * 2 * BLK + rows] if kind == "kv" else query.at[index]
         copies.append(
             pltpu.make_async_copy(
                 arrays[array].at[start : start + rows], to, arrived.at[len(copies)]
@@ -185,7 +184,7 @@
         )
     for copy in copies:
         copy.start()
-    per_piece = kv.shape[2] // BLK
+    per_piece = kv.shape[1] // BLK
     rows = len(outs) * per_piece
     tops[...] = jnp.full_like(tops, NEGATIVE)
     totals[...] = jnp.zeros_like(totals)
@@ -210,7 +209,8 @@
 
     def held(where, part):
         start = pl.multiple_of((where & (per_piece - 1)) * BLK, BLK)
-        return kv[where >> 2, part * BLK : (part + 1) * BLK, pl.ds(start, BLK)]
+        row = pl.multiple_of((where >> 2) * (2 * BLK) + part * BLK, BLK)
+        return kv[pl.ds(row, BLK), pl.ds(start, BLK)]
 
     def fold(op, value):
         return op(value.reshape(BLK // 8, 8, BLK), axis=0)
@@ -305,7 +305,7 @@
         out_specs=[pl.BlockSpec(memory_space=pltpu.VMEM)] * asking,
         out_shape=[jax.ShapeDtypeStruct((count, BLK), jnp.bfloat16)] * asking,
         scratch_shapes=[
-            pltpu.VMEM((pieces, 2 * BLK, count), jnp.bfloat16),
+            pltpu.VMEM((pieces * 2 * BLK, count), jnp.bfloat16),
             pltpu.VMEM((asking, *shape), jnp.bfloat16),
             pltpu.VMEM((rows, BLK, BLK), jnp.bfloat16),
             pltpu.VMEM((max(rows * most // 2 // asking, FIT) + PAIRS, 2 * BLK, BLK), jnp.float32),
@@ -492,7 +492,8 @@
     per_core = half // BLK
     piece, inside = blocks // per_core, blocks % per_core
     from_core, from_y = core ^ (piece // 8), frame_y ^ (piece // 4 % 2)
-    from_x = (frame_x - piece % 4) % 4
+    order = piece % 4
+    from_x = (frame_x - jnp.where(order < 2, order, 5 - order)) % 4
     origin = (from_y * 4 + from_x) * (2 * per_core) + from_core * per_core + inside
     same = origin[:, None] == blocks[None, :]
     keep = jnp.sum(jnp.where(same[None] & keep[:, None, :], 1, 0), axis=2)
@@ -526,10 +527,10 @@
     step = 2 * BLK
     plan = []
     for index, array in ((0, 0), (4, 3), (12, 8)):
-        plan += [("kv", index, array, 0), ("kv", index + 1, array + 1, 0)]
-        plan += [("kv", index + 3, array + 1, step), ("kv", index + 2, array + 2, 0)]
-    plan += [("kv", 8, 6, 0), ("kv", 9, 6, step), ("kv", 11, 6, 2 * step), ("kv", 10, 7, 0)]
-    plan += [("q", index, 11 + index, index % 2 * step) for index in range(4)]
+        plan += [("kv", index, array, 0, step), ("kv", index + 1, array + 1, 0, 2 * step)]
+        plan += [("kv", index + 3, array + 2, 0, step)]
+    plan += [("kv", 8, 6, 0, 3 * step), ("kv", 11, 7, 0, step)]
+    plan += [("q", index, 11 + index, index % 2 * step, BLK) for index in range(4)]
     heads = attend(factor, lists, plan, arrays, half)
     (out_own,) = together((out_weight,), (heads[0],))
     leaving = out_weight, swap(out_own, "core")

time: 189 us -> 189 us (level)
  Pallas kernels: 45.4 us -> 42 us
  starting transfers between devices: 56.5 us -> 59.6 us
    pallas_call x1, Pallas kernels: 11.9 us -> 8.46 us  [attend(): pl.pallas_call(kernel, in_specs=[pl.BlockSpec(memory_space=pltpu.SMEM)] *...]
    ppermute x41, starting transfers between devices: 56.5 us -> 59.6 us  [shift(): lax.ppermute(value, axis, [(i, (i + steps) % count) for i in range(count)])]
where the time goes in v12:
time: 189 us
  waiting for transfers between devices  78.7 us (42%)
  starting transfers between devices  59.6 us (32%)
  Pallas kernels  42 us (22%)
  local copies, waits for them, and re-layouts  4.49 us (2%)
  other arithmetic  3.83 us (2%)
    ppermute x41, waiting for transfers between devices, shift(): lax.ppermute(value, axis, [(i, (i + steps) % count) for i in range(count)])  78.7 us
    ppermute x41, starting transfers between devices, shift(): lax.ppermute(value, axis, [(i, (i + steps) % count) for i in range(count)])  59.6 us
    pallas_call x1, Pallas kernels, project(): pl.pallas_call(project_kernel, in_specs=[pl.BlockSpec(memory_space=pltpu....  18.6 us
    pallas_call x3, Pallas kernels, leave(): pl.pallas_call(kernel, grid_spec=pltpu.PrefetchScalarGridSpec(num_scalar_...  13.5 us
    pallas_call x1, Pallas kernels, attend(): pl.pallas_call(kernel, in_specs=[pl.BlockSpec(memory_space=pltpu.SMEM)] *...  8.46 us
  transfers between devices with their start and end apart: 41, of which 21 were waited for; matrix products, arithmetic and copies ran while one was open for 2% of the time, Pallas kernels for 6%

profile of v12, /device:TPU:1, one launch (start us, length us, event | category | flops | bytes accessed | tf_op | source)
XLA Modules:
  0.0 189.0 jit_solution(5003661504860860464)
XLA Ops:
  4.6 1.7 collective-permute-start.5
  6.4 2.1 %collective-permute-start.6 = (bf16[512,640]{1,0:T(8,128)(2,1)S(1)}, bf16[512,640]{1,0:T(8,128)(2,1)S(1)}, u32[]{:S(2)}, u32[]{:S(2)}) collective-permute-start(bf16[512,640]{1,0:T(8,128)(2,1)S(1)} %lay.1.refs_0_), channel_id=1, source_target_pairs={{0,6},{2,0},{4,2},{6,4},{1,7},{3,1},{5,3},{7,5},{8,14},{10,8},{12,... | collective-permute-start | bytes 1966088 | tf_op jit(solution)/shard_map/ppermute | solution.py:28
  9.8 13.8 %collective-permute-done.5.refs_1_ = bf16[512,640]{1,0:T(8,128)(2,1)} collective-permute-done((bf16[512,640]{1,0:T(8,128)(2,1)S(1)}, bf16[512,640]{1,0:T(8,128)(2,1)}, u32[]{:S(2)}, u32[]{:S(2)}) %collective-permute-start.5) | collective-permute-done | bytes 655392 | tf_op jit(solution)/shard_map/ppermute | solution.py:28
  25.8 2.7 %collective-permute-start.10 = (bf16[512,640]{1,0:T(8,128)(2,1)}, bf16[512,640]{1,0:T(8,128)(2,1)S(1)}, u32[]{:S(2)}, u32[]{:S(2)}) collective-permute-start(bf16[512,640]{1,0:T(8,128)(2,1)} %collective-permute-done.7.refs_3_), channel_id=1, source_target_pairs={{0,6},{2,0},{4,2},{6,4},{1,7},{3,1},{5,3},{7,5},{8,14},{10,8},{12,... | collective-permute-start | bytes 1966088 | tf_op jit(solution)/shard_map/ppermute | solution.py:28
  28.5 2.5 %collective-permute-start.3 = (s32[4,64]{1,0:T(4,128)S(1)}, s32[4,64]{1,0:T(4,128)S(1)}, u32[]{:S(2)}, u32[]{:S(2)}) collective-permute-start(s32[4,64]{1,0:T(4,128)S(1)} %get-tuple-element.102), channel_id=1, source_target_pairs={{0,48},{16,0},{32,16},{48,32},{1,49},{17,1},{33,17},{49,33},{2,50}... | collective-permute-start | bytes 3080 | tf_op jit(solution)/shard_map/ppermute | solution.py:28
  31.7 2.3 %collective-permute-start.2 = (s32[4,64]{1,0:T(4,128)S(1)}, s32[4,64]{1,0:T(4,128)S(1)}, u32[]{:S(2)}, u32[]{:S(2)}) collective-permute-start(s32[4,64]{1,0:T(4,128)S(1)} %get-tuple-element.101), channel_id=1, source_target_pairs={{0,32},{16,48},{32,0},{48,16},{1,33},{17,49},{33,1},{49,17},{2,34}... | collective-permute-start | bytes 3080 | tf_op jit(solution)/shard_map/ppermute | solution.py:28
  34.0 1.7 collective-permute-done.2
  36.8 3.3 %collective-permute-done.1 = s32[4,64]{1,0:T(4,128)S(1)} collective-permute-done((s32[4,64]{1,0:T(4,128)S(1)}, s32[4,64]{1,0:T(4,128)S(1)}, u32[]{:S(2)}, u32[]{:S(2)}) %collective-permute-start.1) | collective-permute-done | bytes 1056 | tf_op jit(solution)/shard_map/ppermute | solution.py:28
  42.3 2.3 %collective-permute-start.12 = (bf16[512,256]{1,0:T(8,128)(2,1)S(1)}, bf16[512,256]{1,0:T(8,128)(2,1)}, u32[]{:S(2)}, u32[]{:S(2)}) collective-permute-start(bf16[512,256]{1,0:T(8,128)(2,1)S(1)} %slice.28), channel_id=1, source_target_pairs={{0,6},{2,0},{4,2},{6,4},{1,7},{3,1},{5,3},{7,5},{8,14},{10,8},{12,... | collective-permute-start | bytes 786440 | tf_op jit(solution)/shard_map/ppermute | solution.py:28
  46.2 3.8 %collective-permute-done.13.refs_9_ = bf16[512,128]{1,0:T(8,128)(2,1)S(1)} collective-permute-done((bf16[512,128]{1,0:T(8,128)(2,1)S(1)}, bf16[512,128]{1,0:T(8,128)(2,1)S(1)}, u32[]{:S(2)}, u32[]{:S(2)}) %collective-permute-start.13) | collective-permute-done | bytes 131104 | tf_op jit(solution)/shard_map/ppermute | solution.py:28
  50.6 18.6 %project.1 = (bf16[256,512]{1,0:T(8,128)(2,1)}, bf16[128,512]{1,0:T(8,128)(2,1)}, bf16[256,512]{1,0:T(8,128)(2,1)}, bf16[128,512]{1,0:T(8,128)(2,1)}, bf16[384,5...) custom-call(s32[8]{0:T(128)} %stack.97.chips, s32[4]{0:T(128)} %pad_add_fusion.2.heads, bf16[512,640]{1,0:T(8,128)(2,1)} %copy-done.1, ...), custom_call_target="tpu_custom_call" | custom-call | flops 8053063680 | bytes 20971520 | tf_op jit(solution)/shard_map/project/pallas_call | solution.py:149
  72.0 3.0 %collective-permute-start.17 = (bf16[256,512]{1,0:T(8,128)(2,1)}, bf16[256,512]{1,0:T(8,128)(2,1)S(1)}, u32[]{:S(2)}, u32[]{:S(2)}) collective-permute-start(bf16[256,512]{1,0:T(8,128)(2,1)} %get-tuple-element.65.refs_4_), channel_id=1, source_target_pairs={{0,64},{64,0},{1,65},{65,1},{2,66},{66,2},{3,67},{67,3},{4,68},{68... | collective-permute-start | bytes 786440 | tf_op jit(solution)/shard_map/ppermute | solution.py:28
  75.7 3.4 %collective-permute-done.17.refs_7_ = bf16[256,512]{1,0:T(8,128)(2,1)S(1)} collective-permute-done((bf16[256,512]{1,0:T(8,128)(2,1)}, bf16[256,512]{1,0:T(8,128)(2,1)S(1)}, u32[]{:S(2)}, u32[]{:S(2)}) %collective-permute-start.17) | collective-permute-done | bytes 262176 | tf_op jit(solution)/shard_map/ppermute | solution.py:28
  79.2 3.3 %collective-permute-start.19 = (bf16[512,512]{1,0:T(8,128)(2,1)S(1)}, bf16[512,512]{1,0:T(8,128)(2,1)S(1)}, u32[]{:S(2)}, u32[]{:S(2)}) collective-permute-start(bf16[512,512]{1,0:T(8,128)(2,1)S(1)} %pad_maximum_fusion.1.refs_5_), channel_id=1, source_target_pairs={{0,64},{64,0},{1,65},{65,1},{2,66},{66,2},{3,67},{67,3},{4,68},{68... | collective-permute-start | bytes 1572872 | tf_op jit(solution)/shard_map/ppermute | solution.py:28
  82.8 7.3 %collective-permute-start.21 = (bf16[256,512]{1,0:T(8,128)(2,1)S(1)}, bf16[256,512]{1,0:T(8,128)(2,1)S(1)}, u32[]{:S(2)}, u32[]{:S(2)}) collective-permute-start(bf16[256,512]{1,0:T(8,128)(2,1)S(1)} %collective-permute-done.17.refs_7_), channel_id=1, source_target_pairs={{0,1},{1,0},{2,3},{3,2},{4,5},{5,4},{6,7},{7,6},{8,9},{9,8},{10,11... | collective-permute-start | bytes 786440 | tf_op jit(solution)/shard_map/ppermute | solution.py:28
  90.1 1.9 collective-permute-start.18
  93.7 8.6 %collective-permute-done.20.refs_17_ = bf16[128,512]{1,0:T(8,128)(2,1)S(1)} collective-permute-done((bf16[128,512]{1,0:T(8,128)(2,1)S(1)}, bf16[128,512]{1,0:T(8,128)(2,1)S(1)}, u32[]{:S(2)}, u32[]{:S(2)}) %collective-permute-start.20) | collective-permute-done | bytes 131104 | tf_op jit(solution)/shard_map/ppermute | solution.py:28
  103.9 8.7 %collective-permute-done.22.refs_9_ = bf16[256,512]{1,0:T(8,128)(2,1)S(1)} collective-permute-done((bf16[256,512]{1,0:T(8,128)(2,1)S(1)}, bf16[256,512]{1,0:T(8,128)(2,1)S(1)}, u32[]{:S(2)}, u32[]{:S(2)}) %collective-permute-start.22) | collective-permute-done | bytes 262176 | tf_op jit(solution)/shard_map/ppermute | solution.py:28
  114.7 8.5 %attend.1 = (bf16[512,128]{1,0:T(8,128)(2,1)S(1)}, bf16[512,128]{1,0:T(8,128)(2,1)S(1)}, bf16[512,128]{1,0:T(8,128)(2,1)S(1)}, bf16[512,128]{1,0:T(8,128)(2,1)S(1)}) custom-call(s32[16,64]{1,0:T(8,128)S(1)} %select_reduce_fusion.2.refs_0_, s32[16]{0:T(128)S(1)} %get-tuple-element.93.refs_1_, s32[17]{0:T(128)S(1)} %select_reduce_fusion.5.refs_2_, ...), custom_call_target="tpu_custom_call" | custom-call | flops 2147483648 | bytes 4194304 | tf_op jit(solution)/shard_map/attend/pallas_call | solution.py:301
  123.7 1.6 collective-permute-start.28
  126.4 2.3 %collective-permute-done.28.refs_5_ = bf16[512,128]{1,0:T(8,128)(2,1)S(1)} collective-permute-done((bf16[512,128]{1,0:T(8,128)(2,1)S(1)}, bf16[512,128]{1,0:T(8,128)(2,1)S(1)}, u32[]{:S(2)}, u32[]{:S(2)}) %collective-permute-start.28) | collective-permute-done | bytes 131104 | tf_op jit(solution)/shard_map/ppermute | solution.py:28
  128.7 2.7 %collective-permute-done.29.refs_6_ = bf16[512,128]{1,0:T(8,128)(2,1)S(1)} collective-permute-done((bf16[512,128]{1,0:T(8,128)(2,1)S(1)}, bf16[512,128]{1,0:T(8,128)(2,1)S(1)}, u32[]{:S(2)}, u32[]{:S(2)}) %collective-permute-start.29) | collective-permute-done | bytes 131104 | tf_op jit(solution)/shard_map/ppermute | solution.py:28
  131.4 3.6 %collective-permute-done.30.refs_7_ = bf16[512,128]{1,0:T(8,128)(2,1)S(1)} collective-permute-done((bf16[512,128]{1,0:T(8,128)(2,1)S(1)}, bf16[512,128]{1,0:T(8,128)(2,1)S(1)}, u32[]{:S(2)}, u32[]{:S(2)}) %collective-permute-start.30) | collective-permute-done | bytes 131104 | tf_op jit(solution)/shard_map/ppermute | solution.py:28
  135.0 2.8 %leave.3 = (bf16[512,256]{1,0:T(8,128)(2,1)S(1)}, bf16[512,256]{1,0:T(8,128)(2,1)S(1)}, bf16[512,128]{1,0:T(8,128)(2,1)S(1)}) custom-call(s32[1]{0:T(128)} %bitcast.18.refs_0_, s32[4]{0:T(128)S(1)} %pad_add_fusion.1.refs_1_, bf16[256,5120]{1,0:T(8,128)(2,1)S(1)} %copy-done, bf16[256,5120]{1,0:T(8,128)(2,1)} %collective-permute-done.27.refs_3_, ...), custom_call_target="tpu_custom_call" | custom-call | flops 335544320 | bytes 1310720 | tf_op jit(solution)/shard_map/leave/pallas_call | solution.py:367
  137.8 4.4 %collective-permute-start.31 = (bf16[512,256]{1,0:T(8,128)(2,1)S(1)}, bf16[512,256]{1,0:T(8,128)(2,1)S(1)}, u32[]{:S(2)}, u32[]{:S(2)}) collective-permute-start(bf16[512,256]{1,0:T(8,128)(2,1)S(1)} %get-tuple-element.74), channel_id=1, source_target_pairs={{0,8},{8,0},{1,9},{9,1},{2,10},{10,2},{3,11},{11,3},{4,12},{12,4},... | collective-permute-start | bytes 786440 | tf_op jit(solution)/shard_map/ppermute | solution.py:28
  142.2 2.7 %collective-permute-start.33 = (bf16[512,128]{1,0:T(8,128)(2,1)S(1)}, bf16[512,128]{1,0:T(8,128)(2,1)S(1)}, u32[]{:S(2)}, u32[]{:S(2)}) collective-permute-start(bf16[512,128]{1,0:T(8,128)(2,1)S(1)} %get-tuple-element.76), channel_id=1, source_target_pairs={{0,6},{2,0},{4,2},{6,4},{1,7},{3,1},{5,3},{7,5},{8,14},{10,8},{12,... | collective-permute-start | bytes 393224 | tf_op jit(solution)/shard_map/ppermute | solution.py:28
  145.0 4.6 %leave.5 = (bf16[512,640]{1,0:T(8,128)(2,1)S(1)}, bf16[512,640]{1,0:T(8,128)(2,1)S(1)}, bf16[512,640]{1,0:T(8,128)(2,1)S(1)}) custom-call(s32[3]{0:T(128)S(1)} %pad_add_fusion.3.refs_0_, s32[4]{0:T(128)S(1)} %pad_add_fusion.1.refs_1_, bf16[256,5120]{1,0:T(8,128)(2,1)S(1)} %copy-done, bf16[256,5120]{1,0:T(8,128)(2,1)} %collective-permute-done.27.refs_3_, ...), custom_call_target="tpu_custom_call" | custom-call | flops 1006632960 | bytes 3932160 | tf_op jit(solution)/shard_map/leave/pallas_call | solution.py:367
  152.8 6.2 %leave.4 = (bf16[512,640]{1,0:T(8,128)(2,1)S(1)}, bf16[512,640]{1,0:T(8,128)(2,1)}, bf16[512,640]{1,0:T(8,128)(2,1)S(1)}, bf16[512,640]{1,0:T(8,128)(2,1)S(1)}) custom-call(s32[4]{0:T(128)S(1)} %pad_add_fusion.refs_0_, s32[4]{0:T(128)S(1)} %pad_add_fusion.1.refs_1_, bf16[256,5120]{1,0:T(8,128)(2,1)S(1)} %copy-done, ...), custom_call_target="tpu_custom_call" | custom-call | flops 1342177280 | bytes 5242880 | tf_op jit(solution)/shard_map/leave/pallas_call | solution.py:367
  159.0 6.4 %collective-permute-done.34.refs_1_ = bf16[512,640]{1,0:T(8,128)(2,1)S(1)} collective-permute-done((bf16[512,640]{1,0:T(8,128)(2,1)S(1)}, bf16[512,640]{1,0:T(8,128)(2,1)S(1)}, u32[]{:S(2)}, u32[]{:S(2)}) %collective-permute-start.34) | collective-permute-done | bytes 655392 | tf_op jit(solution)/shard_map/ppermute | solution.py:28
  165.4 1.7 collective-permute-done.36.refs_4_
  168.3 12.8 %collective-permute-done.38.refs_2_ = bf16[512,640]{1,0:T(8,128)(2,1)S(1)} collective-permute-done((bf16[512,640]{1,0:T(8,128)(2,1)}, bf16[512,640]{1,0:T(8,128)(2,1)S(1)}, u32[]{:S(2)}, u32[]{:S(2)}) %collective-permute-start.38) | collective-permute-done | bytes 655392 | tf_op jit(solution)/shard_map/ppermute | solution.py:28
  182.7 3.7 %collective-permute-start.40 = (bf16[320,512]{1,0:T(8,128)(2,1)S(1)}, bf16[320,512]{1,0:T(8,128)(2,1)S(1)}, u32[]{:S(2)}, u32[]{:S(2)}) collective-permute-start(bf16[320,512]{1,0:T(8,128)(2,1)S(1)} %constant_dynamic-slice_fusion), channel_id=1, source_target_pairs={{0,1},{1,0},{2,3},{3,2},{4,5},{5,4},{6,7},{7,6},{8,9},{9,8},{10,11... | collective-permute-start | bytes 983048 | tf_op jit(solution)/shard_map/ppermute | solution.py:28
  (121 shorter events, 33.8 us)
Async XLA Ops:
  4.2 45.8 %collective-permute-start.14 = (bf16[3,5120,256]{2,1,0:T(8,128)(2,1)}, bf16[3,5120,256]{2,1,0:T(8,128)(2,1)}, u32[]{:S(2)}, u32[]{:S(2)}) collective-permute-start(bf16[3,5120,256]{2,1,0:T(8,128)(2,1)} %refs_10_.1), channel_id=1, source_target_pairs={{0,1},{1,0},{2,3},{3,2},{4,5},{5,4},{6,7},{7,6},{8,9},{9,8},{10,11... | collective-permute-start | bytes 23592968 | tf_op jit(solution)/shard_map/ppermute | solution.py:28
  4.6 18.9 %collective-permute-start.5 = (bf16[512,640]{1,0:T(8,128)(2,1)S(1)}, bf16[512,640]{1,0:T(8,128)(2,1)}, u32[]{:S(2)}, u32[]{:S(2)}) collective-permute-start(bf16[512,640]{1,0:T(8,128)(2,1)S(1)} %lay.1.refs_0_), channel_id=1, source_target_pairs={{0,2},{2,4},{4,6},{6,0},{1,3},{3,5},{5,7},{7,1},{8,10},{10,12},{12... | collective-permute-start | bytes 1966088 | tf_op jit(solution)/shard_map/ppermute | solution.py:28
  6.4 17.2 %collective-permute-start.6 = (bf16[512,640]{1,0:T(8,128)(2,1)S(1)}, bf16[512,640]{1,0:T(8,128)(2,1)S(1)}, u32[]{:S(2)}, u32[]{:S(2)}) collective-permute-start(bf16[512,640]{1,0:T(8,128)(2,1)S(1)} %lay.1.refs_0_), channel_id=1, source_target_pairs={{0,6},{2,0},{4,2},{6,4},{1,7},{3,1},{5,3},{7,5},{8,14},{10,8},{12,... | collective-permute-start | bytes 1966088 | tf_op jit(solution)/shard_map/ppermute | solution.py:28
  8.5 16.0 %collective-permute-start.7 = (bf16[512,640]{1,0:T(8,128)(2,1)S(1)}, bf16[512,640]{1,0:T(8,128)(2,1)}, u32[]{:S(2)}, u32[]{:S(2)}) collective-permute-start(bf16[512,640]{1,0:T(8,128)(2,1)S(1)} %lay.1.refs_0_), channel_id=1, source_target_pairs={{0,8},{8,0},{1,9},{9,1},{2,10},{10,2},{3,11},{11,3},{4,12},{12,4},... | collective-permute-start | bytes 1966088 | tf_op jit(solution)/shard_map/ppermute | solution.py:28
  24.4 16.4 %collective-permute-start.8 = (bf16[512,640]{1,0:T(8,128)(2,1)}, bf16[512,640]{1,0:T(8,128)(2,1)S(1)}, u32[]{:S(2)}, u32[]{:S(2)}) collective-permute-start(bf16[512,640]{1,0:T(8,128)(2,1)} %collective-permute-done.5.refs_1_), channel_id=1, source_target_pairs={{0,2},{2,4},{4,6},{6,0},{1,3},{3,5},{5,7},{7,1},{8,10},{10,12},{12... | collective-permute-start | bytes 1966088 | tf_op jit(solution)/shard_map/ppermute | solution.py:28
  24.5 16.4 %collective-permute-start.9 = (bf16[512,640]{1,0:T(8,128)(2,1)}, bf16[512,640]{1,0:T(8,128)(2,1)S(1)}, u32[]{:S(2)}, u32[]{:S(2)}) collective-permute-start(bf16[512,640]{1,0:T(8,128)(2,1)} %collective-permute-done.5.refs_1_), channel_id=1, source_target_pairs={{0,8},{8,0},{1,9},{9,1},{2,10},{10,2},{3,11},{11,3},{4,12},{12,4},... | collective-permute-start | bytes 1966088 | tf_op jit(solution)/shard_map/ppermute | solution.py:28
  25.8 15.2 %collective-permute-start.10 = (bf16[512,640]{1,0:T(8,128)(2,1)}, bf16[512,640]{1,0:T(8,128)(2,1)S(1)}, u32[]{:S(2)}, u32[]{:S(2)}) collective-permute-start(bf16[512,640]{1,0:T(8,128)(2,1)} %collective-permute-done.7.refs_3_), channel_id=1, source_target_pairs={{0,6},{2,0},{4,2},{6,4},{1,7},{3,1},{5,3},{7,5},{8,14},{10,8},{12,... | collective-permute-start | bytes 1966088 | tf_op jit(solution)/shard_map/ppermute | solution.py:28
  40.9 9.0 %collective-permute-start.11 = (bf16[512,256]{1,0:T(8,128)(2,1)S(1)}, bf16[512,256]{1,0:T(8,128)(2,1)}, u32[]{:S(2)}, u32[]{:S(2)}) collective-permute-start(bf16[512,256]{1,0:T(8,128)(2,1)S(1)} %slice.27), channel_id=1, source_target_pairs={{0,8},{8,0},{1,9},{9,1},{2,10},{10,2},{3,11},{11,3},{4,12},{12,4},... | collective-permute-start | bytes 786440 | tf_op jit(solution)/shard_map/ppermute | solution.py:28
  42.3 7.7 %collective-permute-start.12 = (bf16[512,256]{1,0:T(8,128)(2,1)S(1)}, bf16[512,256]{1,0:T(8,128)(2,1)}, u32[]{:S(2)}, u32[]{:S(2)}) collective-permute-start(bf16[512,256]{1,0:T(8,128)(2,1)S(1)} %slice.28), channel_id=1, source_target_pairs={{0,6},{2,0},{4,2},{6,4},{1,7},{3,1},{5,3},{7,5},{8,14},{10,8},{12,... | collective-permute-start | bytes 786440 | tf_op jit(solution)/shard_map/ppermute | solution.py:28
  69.3 9.8 %collective-permute-start.15 = (bf16[384,512]{1,0:T(8,128)(2,1)}, bf16[384,512]{1,0:T(8,128)(2,1)S(1)}, u32[]{:S(2)}, u32[]{:S(2)}) collective-permute-start(bf16[384,512]{1,0:T(8,128)(2,1)} %get-tuple-element.58), channel_id=1, source_target_pairs={{0,16},{16,32},{32,48},{48,0},{1,17},{17,33},{33,49},{49,1},{2,18}... | collective-permute-start | bytes 1179656 | tf_op jit(solution)/shard_map/ppermute | solution.py:28
  70.6 8.5 %collective-permute-start.16 = (bf16[384,512]{1,0:T(8,128)(2,1)}, bf16[384,512]{1,0:T(8,128)(2,1)S(1)}, u32[]{:S(2)}, u32[]{:S(2)}) collective-permute-start(bf16[384,512]{1,0:T(8,128)(2,1)} %get-tuple-element.59), channel_id=1, source_target_pairs={{0,48},{16,0},{32,16},{48,32},{1,49},{17,1},{33,17},{49,33},{2,50}... | collective-permute-start | bytes 1179656 | tf_op jit(solution)/shard_map/ppermute | solution.py:28
  72.0 7.0 %collective-permute-start.17 = (bf16[256,512]{1,0:T(8,128)(2,1)}, bf16[256,512]{1,0:T(8,128)(2,1)S(1)}, u32[]{:S(2)}, u32[]{:S(2)}) collective-permute-start(bf16[256,512]{1,0:T(8,128)(2,1)} %get-tuple-element.65.refs_4_), channel_id=1, source_target_pairs={{0,64},{64,0},{1,65},{65,1},{2,66},{66,2},{3,67},{67,3},{4,68},{68... | collective-permute-start | bytes 786440 | tf_op jit(solution)/shard_map/ppermute | solution.py:28
  79.2 23.1 %collective-permute-start.19 = (bf16[512,512]{1,0:T(8,128)(2,1)S(1)}, bf16[512,512]{1,0:T(8,128)(2,1)S(1)}, u32[]{:S(2)}, u32[]{:S(2)}) collective-permute-start(bf16[512,512]{1,0:T(8,128)(2,1)S(1)} %pad_maximum_fusion.1.refs_5_), channel_id=1, source_target_pairs={{0,64},{64,0},{1,65},{65,1},{2,66},{66,2},{3,67},{67,3},{4,68},{68... | collective-permute-start | bytes 1572872 | tf_op jit(solution)/shard_map/ppermute | solution.py:28
  82.8 19.5 %collective-permute-start.21 = (bf16[256,512]{1,0:T(8,128)(2,1)S(1)}, bf16[256,512]{1,0:T(8,128)(2,1)S(1)}, u32[]{:S(2)}, u32[]{:S(2)}) collective-permute-start(bf16[256,512]{1,0:T(8,128)(2,1)S(1)} %collective-permute-done.17.refs_7_), channel_id=1, source_target_pairs={{0,1},{1,0},{2,3},{3,2},{4,5},{5,4},{6,7},{7,6},{8,9},{9,8},{10,11... | collective-permute-start | bytes 786440 | tf_op jit(solution)/shard_map/ppermute | solution.py:28
  90.1 12.2 %collective-permute-start.18 = (bf16[256,512]{1,0:T(8,128)(2,1)S(1)}, bf16[256,512]{1,0:T(8,128)(2,1)S(1)}, u32[]{:S(2)}, u32[]{:S(2)}) collective-permute-start(bf16[256,512]{1,0:T(8,128)(2,1)S(1)} %copy-done.12), channel_id=1, source_target_pairs={{0,32},{16,48},{32,0},{48,16},{1,33},{17,49},{33,1},{49,17},{2,34}... | collective-permute-start | bytes 786440 | tf_op jit(solution)/shard_map/ppermute | solution.py:28
  92.1 10.1 %collective-permute-start.20 = (bf16[128,512]{1,0:T(8,128)(2,1)S(1)}, bf16[128,512]{1,0:T(8,128)(2,1)S(1)}, u32[]{:S(2)}, u32[]{:S(2)}) collective-permute-start(bf16[128,512]{1,0:T(8,128)(2,1)S(1)} %copy-done.14), channel_id=1, source_target_pairs={{0,32},{16,48},{32,0},{48,16},{1,33},{17,49},{33,1},{49,17},{2,34}... | collective-permute-start | bytes 393224 | tf_op jit(solution)/shard_map/ppermute | solution.py:28
  102.3 12.4 %collective-permute-start.23 = (bf16[768,512]{1,0:T(8,128)(2,1)S(1)}, bf16[768,512]{1,0:T(8,128)(2,1)S(1)}, u32[]{:S(2)}, u32[]{:S(2)}) collective-permute-start(bf16[768,512]{1,0:T(8,128)(2,1)S(1)} %pad_maximum_fusion), channel_id=1, source_target_pairs={{0,1},{1,0},{2,3},{3,2},{4,5},{5,4},{6,7},{7,6},{8,9},{9,8},{10,11... | collective-permute-start | bytes 2359304 | tf_op jit(solution)/shard_map/ppermute | solution.py:28
  103.3 9.4 %collective-permute-start.22 = (bf16[256,512]{1,0:T(8,128)(2,1)S(1)}, bf16[256,512]{1,0:T(8,128)(2,1)S(1)}, u32[]{:S(2)}, u32[]{:S(2)}) collective-permute-start(bf16[256,512]{1,0:T(8,128)(2,1)S(1)} %collective-permute-done.18.refs_6_), channel_id=1, source_target_pairs={{0,64},{64,0},{1,65},{65,1},{2,66},{66,2},{3,67},{67,3},{4,68},{68... | collective-permute-start | bytes 786440 | tf_op jit(solution)/shard_map/ppermute | solution.py:28
  103.4 10.1 %collective-permute-start.25 = (bf16[512,512]{1,0:T(8,128)(2,1)S(1)}, bf16[512,512]{1,0:T(8,128)(2,1)S(1)}, u32[]{:S(2)}, u32[]{:S(2)}) collective-permute-start(bf16[512,512]{1,0:T(8,128)(2,1)S(1)} %collective-permute-done.19.refs_8_), channel_id=1, source_target_pairs={{0,1},{1,0},{2,3},{3,2},{4,5},{5,4},{6,7},{7,6},{8,9},{9,8},{10,11... | collective-permute-start | bytes 1572872 | tf_op jit(solution)/shard_map/ppermute | solution.py:28
  103.8 9.8 %collective-permute-start.24 = (bf16[256,512]{1,0:T(8,128)(2,1)S(1)}, bf16[256,512]{1,0:T(8,128)(2,1)S(1)}, u32[]{:S(2)}, u32[]{:S(2)}) collective-permute-start(bf16[256,512]{1,0:T(8,128)(2,1)S(1)} %collective-permute-done.18.refs_6_), channel_id=1, source_target_pairs={{0,1},{1,0},{2,3},{3,2},{4,5},{5,4},{6,7},{7,6},{8,9},{9,8},{10,11... | collective-permute-start | bytes 786440 | tf_op jit(solution)/shard_map/ppermute | solution.py:28
  123.2 11.8 %collective-permute-start.27 = (bf16[256,5120]{1,0:T(8,128)(2,1)S(1)}, bf16[256,5120]{1,0:T(8,128)(2,1)}, u32[]{:S(2)}, u32[]{:S(2)}) collective-permute-start(bf16[256,5120]{1,0:T(8,128)(2,1)S(1)} %copy-done), channel_id=1, source_target_pairs={{0,1},{1,0},{2,3},{3,2},{4,5},{5,4},{6,7},{7,6},{8,9},{9,8},{10,11... | collective-permute-start | bytes 7864328 | tf_op jit(solution)/shard_map/ppermute | solution.py:28
  125.2 6.2 %collective-permute-start.29 = (bf16[512,128]{1,0:T(8,128)(2,1)S(1)}, bf16[512,128]{1,0:T(8,128)(2,1)S(1)}, u32[]{:S(2)}, u32[]{:S(2)}) collective-permute-start(bf16[512,128]{1,0:T(8,128)(2,1)S(1)} %get-tuple-element.72), channel_id=1, source_target_pairs={{0,32},{16,48},{32,0},{48,16},{1,33},{17,49},{33,1},{49,17},{2,34}... | collective-permute-start | bytes 393224 | tf_op jit(solution)/shard_map/ppermute | solution.py:28
  125.8 9.2 %collective-permute-start.30 = (bf16[512,128]{1,0:T(8,128)(2,1)S(1)}, bf16[512,128]{1,0:T(8,128)(2,1)S(1)}, u32[]{:S(2)}, u32[]{:S(2)}) collective-permute-start(bf16[512,128]{1,0:T(8,128)(2,1)S(1)} %get-tuple-element.73), channel_id=1, source_target_pairs={{0,16},{16,32},{32,48},{48,0},{1,17},{17,33},{33,49},{49,1},{2,18}... | collective-permute-start | bytes 393224 | tf_op jit(solution)/shard_map/ppermute | solution.py:28
  137.8 11.8 %collective-permute-start.31 = (bf16[512,256]{1,0:T(8,128)(2,1)S(1)}, bf16[512,256]{1,0:T(8,128)(2,1)S(1)}, u32[]{:S(2)}, u32[]{:S(2)}) collective-permute-start(bf16[512,256]{1,0:T(8,128)(2,1)S(1)} %get-tuple-element.74), channel_id=1, source_target_pairs={{0,8},{8,0},{1,9},{9,1},{2,10},{10,2},{3,11},{11,3},{4,12},{12,4},... | collective-permute-start | bytes 786440 | tf_op jit(solution)/shard_map/ppermute | solution.py:28
  142.2 8.3 %collective-permute-start.32 = (bf16[512,256]{1,0:T(8,128)(2,1)S(1)}, bf16[512,256]{1,0:T(8,128)(2,1)S(1)}, u32[]{:S(2)}, u32[]{:S(2)}) collective-permute-start(bf16[512,256]{1,0:T(8,128)(2,1)S(1)} %get-tuple-element.75), channel_id=1, source_target_pairs={{0,2},{2,4},{4,6},{6,0},{1,3},{3,5},{5,7},{7,1},{8,10},{10,12},{12... | collective-permute-start | bytes 786440 | tf_op jit(solution)/shard_map/ppermute | solution.py:28
  142.2 7.3 %collective-permute-start.33 = (bf16[512,128]{1,0:T(8,128)(2,1)S(1)}, bf16[512,128]{1,0:T(8,128)(2,1)S(1)}, u32[]{:S(2)}, u32[]{:S(2)}) collective-permute-start(bf16[512,128]{1,0:T(8,128)(2,1)S(1)} %get-tuple-element.76), channel_id=1, source_target_pairs={{0,6},{2,0},{4,2},{6,4},{1,7},{3,1},{5,3},{7,5},{8,14},{10,8},{12,... | collective-permute-start | bytes 393224 | tf_op jit(solution)/shard_map/ppermute | solution.py:28
  150.8 14.7 %collective-permute-start.34 = (bf16[512,640]{1,0:T(8,128)(2,1)S(1)}, bf16[512,640]{1,0:T(8,128)(2,1)S(1)}, u32[]{:S(2)}, u32[]{:S(2)}) collective-permute-start(bf16[512,640]{1,0:T(8,128)(2,1)S(1)} %get-tuple-element.86), channel_id=1, source_target_pairs={{0,6},{2,0},{4,2},{6,4},{1,7},{3,1},{5,3},{7,5},{8,14},{10,8},{12,... | collective-permute-start | bytes 1966088 | tf_op jit(solution)/shard_map/ppermute | solution.py:28
  150.9 14.6 %collective-permute-start.35 = (bf16[512,640]{1,0:T(8,128)(2,1)S(1)}, bf16[512,640]{1,0:T(8,128)(2,1)S(1)}, u32[]{:S(2)}, u32[]{:S(2)}) collective-permute-start(bf16[512,640]{1,0:T(8,128)(2,1)S(1)} %get-tuple-element.87), channel_id=1, source_target_pairs={{0,8},{8,0},{1,9},{9,1},{2,10},{10,2},{3,11},{11,3},{4,12},{12,4},... | collective-permute-start | bytes 1966088 | tf_op jit(solution)/shard_map/ppermute | solution.py:28
  151.3 15.8 %collective-permute-start.36 = (bf16[512,640]{1,0:T(8,128)(2,1)S(1)}, bf16[512,640]{1,0:T(8,128)(2,1)S(1)}, u32[]{:S(2)}, u32[]{:S(2)}) collective-permute-start(bf16[512,640]{1,0:T(8,128)(2,1)S(1)} %get-tuple-element.89), channel_id=1, source_target_pairs={{0,2},{2,4},{4,6},{6,0},{1,3},{3,5},{5,7},{7,1},{8,10},{10,12},{12... | collective-permute-start | bytes 1966088 | tf_op jit(solution)/shard_map/ppermute | solution.py:28
  159.0 22.2 %collective-permute-start.38 = (bf16[512,640]{1,0:T(8,128)(2,1)}, bf16[512,640]{1,0:T(8,128)(2,1)S(1)}, u32[]{:S(2)}, u32[]{:S(2)}) collective-permute-start(bf16[512,640]{1,0:T(8,128)(2,1)} %get-tuple-element.91), channel_id=1, source_target_pairs={{0,2},{2,4},{4,6},{6,0},{1,3},{3,5},{5,7},{7,1},{8,10},{10,12},{12... | collective-permute-start | bytes 1966088 | tf_op jit(solution)/shard_map/ppermute | solution.py:28
  167.5 13.6 %collective-permute-start.37 = (bf16[512,640]{1,0:T(8,128)(2,1)S(1)}, bf16[512,640]{1,0:T(8,128)(2,1)S(1)}, u32[]{:S(2)}, u32[]{:S(2)}) collective-permute-start(bf16[512,640]{1,0:T(8,128)(2,1)S(1)} %get-tuple-element.90), channel_id=1, source_target_pairs={{0,6},{2,0},{4,2},{6,4},{1,7},{3,1},{5,3},{7,5},{8,14},{10,8},{12,... | collective-permute-start | bytes 1966088 | tf_op jit(solution)/shard_map/ppermute | solution.py:28
  167.6 13.6 %collective-permute-start.39 = (bf16[512,640]{1,0:T(8,128)(2,1)S(1)}, bf16[512,640]{1,0:T(8,128)(2,1)S(1)}, u32[]{:S(2)}, u32[]{:S(2)}) collective-permute-start(bf16[512,640]{1,0:T(8,128)(2,1)S(1)} %get-tuple-element.92), channel_id=1, source_target_pairs={{0,8},{8,0},{1,9},{9,1},{2,10},{10,2},{3,11},{11,3},{4,12},{12,4},... | collective-permute-start | bytes 1966088 | tf_op jit(solution)/shard_map/ppermute | solution.py:28
  (24 other events, 246.5 us)
